TPU v7x, 32 devices: a whole 2x2x4 slice. The times are simulated.
32 devices in a mesh: dp: 16 (over z, x, core), head: 2 (over y).
Axes of the slice: x: 2, y: 2, z: 4, core: 2. Of those that a mesh axis runs over, the one named last changes fastest.
Arguments:
- block_in: bfloat16 [16, 1024, 768], P('dp', 'head'), may hold values from -8 to 8
- text: bfloat16 [16, 256, 1024], P('dp'), may hold values from -6 to 6
- timesteps: int32 [16], P('dp'), may hold values from 0 to 999
- frame_mask: int32 [16, 1024], P('dp'), may hold values from 0 to 1, as said below
- text_mask: int32 [16, 256], P('dp'), may hold values from 0 to 1, as said below
- cotangent: bfloat16 [16, 1024, 768], P('dp', 'head'), may hold values from -6 to 6
- w_ada: float32 [768, 4608], P(('dp', 'head')), may hold values from -0.625 to 0.625
- w_qkv: float32 [768, 2304], P(('dp', 'head')), may hold values from -0.21875 to 0.21875
- w_out: float32 [768, 768], P(('dp', 'head')), may hold values from -3.5 to 3.5
- w_cq: float32 [768, 768], P(('dp', 'head')), may hold values from -0.21875 to 0.21875
- w_cout: float32 [768, 768], P(('dp', 'head')), may hold values from -1.75 to 1.75
- w_ckv: float32 [1024, 2, 768], P('dp', None, 'head'), may hold values from -0.1875 to 0.1875
- w_fc1: float32 [768, 3072], P('dp', 'head'), may hold values from -0.21875 to 0.21875
- w_fc2: float32 [3072, 768], P('head', 'dp'), may hold values from -0.109375 to 0.109375
- row_state: float32 [8704], replicated, may hold values from 2.2439396e-08 to 5.983839e-07, as said below
- col_state: float32 [14592], replicated, may hold values from 2.2439396e-08 to 5.983839e-07, as said below
Outputs:
- block_out: bfloat16 [16, 1024, 768], P('dp', 'head')
- input_grad: bfloat16 [16, 1024, 768], P('dp', 'head')
- grad_norm: float32 [], replicated
- row_new: float32 [8704], replicated
- col_new: float32 [14592], replicated
- grad_ada: float32 [768, 4608], P(('dp', 'head'))
- grad_qkv: float32 [768, 2304], P(('dp', 'head'))
- grad_out: float32 [768, 768], P(('dp', 'head'))
- grad_cq: float32 [768, 768], P(('dp', 'head'))
- grad_cout: float32 [768, 768], P(('dp', 'head'))
- grad_ckv: float32 [1024, 2, 768], P('dp', None, 'head')
- grad_fc1: float32 [768, 3072], P('dp', 'head')
- grad_fc2: float32 [3072, 768], P('head', 'dp')
- new_ada: float32 [768, 4608], P(('dp', 'head'))
- new_qkv: float32 [768, 2304], P(('dp', 'head'))
- new_out: float32 [768, 768], P(('dp', 'head'))
- new_cq: float32 [768, 768], P(('dp', 'head'))
- new_cout: float32 [768, 768], P(('dp', 'head'))
- new_ckv: float32 [1024, 2, 768], P('dp', None, 'head')
- new_fc1: float32 [768, 3072], P('dp', 'head')
- new_fc2: float32 [3072, 768], P('head', 'dp')
Inputs may be any that keep to these rules, and one draw needn't show every extreme that they name: `frame_mask`: each clip's frame mask is 1 on a prefix of 256 to 1024 frames and 0 after it; in each aligned block of 4 clips, one clip has all 1024 frames. `text_mask`: each clip's text mask is 1 on a prefix of 77 to 256 tokens and 0 after it; some clip has 77 tokens and some has 256. `row_state`: Positive. `col_state`: Positive.
All inputs are finite; a program needn't handle non-finite values.
Results may differ from a plain program's by a relative error of at most 0.023.
The roundings to bfloat16 on the way count: a program that leaves them out, or rounds other values in their place, can miss the bound.
Values may be sent and summed in bfloat16 or wider, within the bound.
No kernel may reach another device: no remote copies, remote signals or barrier semaphores. Data moves between devices by JAX's collectives and lax.ppermute only.
A program may use at most 192 MiB of HBM per device.

v0:
```python
import jax
import jax.numpy as jnp
from jax import lax
from jax.sharding import PartitionSpec as P

D = 768
FF = 3072
DT = 1024
HD = 64


PRECISE = lax.Precision.HIGHEST
FLOAT = jnp.float32
BFLOAT = jnp.bfloat16
EPS_NORM = 1e-06
EPS_FACTOR = 1e-30
CLIP_NORM = 1.0
CLIP_UPDATE = 0.25
DECAY_RATE = 0.5
RELATIVE_RATE = 4.0
SCALE_FLOOR = 0.001
SCORE_SCALE = 0.125
MASKED_SCORE = -1e30


def embed(timestep, model_width):
    halfway = model_width // 2
    freqs = jnp.exp(-jnp.log(10000.0) * jnp.arange(halfway, dtype=jnp.float32) / halfway)
    angles = timestep.astype(jnp.float32)[..., None] * freqs
    return jnp.concatenate([jnp.cos(angles), jnp.sin(angles)], axis=-1)


def layer_norm(values):
    centered = values - jnp.mean(values, axis=-1, keepdims=True)
    variance = jnp.mean(centered * centered, axis=-1, keepdims=True)
    return centered * lax.rsqrt(variance + EPS_NORM)


def modulate(values, shift, scale):
    return layer_norm(values) * (1.0 + scale[:, None, :]) + shift[:, None, :]


def heads_of(tensor):
    clip_count, length, breadth = tensor.shape
    return (
        tensor.reshape(clip_count, length, breadth // HD, HD)
        .transpose(0, 2, 1, 3)
        .reshape(clip_count * (breadth // HD), length, HD)
    )


def frames_of(tensor, clip_count):
    items, length, depth = tensor.shape
    per_clip = items // clip_count
    return (
        tensor.reshape(clip_count, per_clip, length, depth)
        .transpose(0, 2, 1, 3)
        .reshape(clip_count, length, per_clip * depth)
    )


def to_heads(stacked):
    return lax.all_to_all(stacked, "head", split_axis=3, concat_axis=2, tiled=True)


def to_frames(stacked):
    return lax.all_to_all(stacked, "head", split_axis=2, concat_axis=3, tiled=True)


def join_rows(values):
    return lax.all_gather(values, "head", axis=1, tiled=True)


def part_rows(values):
    return lax.psum_scatter(
        values.astype(jnp.bfloat16), "head", scatter_dimension=1, tiled=True
    ).astype(jnp.float32)


def attend_item(pieces):
    queries, keys, values, allowed = pieces
    scores = jnp.einsum("qd,kd->qk", queries, keys, preferred_element_type=FLOAT) * SCORE_SCALE
    scores = jnp.where(allowed[None, :], scores, MASKED_SCORE)
    peak = jnp.max(scores, axis=-1, keepdims=True)
    exponent = jnp.exp(scores - peak)
    totals = jnp.sum(exponent, axis=-1, keepdims=True)
    probs = (exponent / totals).astype(BFLOAT)
    result = jnp.dot(probs, values, preferred_element_type=FLOAT)
    return (result, (peak + jnp.log(totals))[:, 0])


def attend_back(pieces):
    queries, keys, values, allowed, out_grad, log_total = pieces
    scores = jnp.einsum("qd,kd->qk", queries, keys, preferred_element_type=FLOAT) * SCORE_SCALE
    scores = jnp.where(allowed[None, :], scores, MASKED_SCORE)
    probs = jnp.exp(scores - log_total[:, None])
    prob_grad = jnp.einsum("qd,kd->qk", out_grad, values, preferred_element_type=FLOAT)
    inner = jnp.sum(probs * prob_grad, axis=-1, keepdims=True)
    score_grad = (probs * (prob_grad - inner)).astype(BFLOAT)
    query_grad = (
        jnp.einsum("qk,kd->qd", score_grad, keys, preferred_element_type=FLOAT) * SCORE_SCALE
    )
    key_grad = (
        jnp.einsum("qk,qd->kd", score_grad, queries, preferred_element_type=FLOAT) * SCORE_SCALE
    )
    value_grad = jnp.einsum(
        "qk,qd->kd", probs.astype(BFLOAT), out_grad, preferred_element_type=FLOAT
    )
    return (query_grad.astype(BFLOAT), key_grad.astype(BFLOAT), value_grad.astype(BFLOAT))


def run_attention(queries, keys, values, allowed_rows, clip_count):
    allowed_items = jnp.repeat(allowed_rows, queries.shape[2] // HD, axis=0)
    outputs, log_totals = lax.map(
        attend_item, (heads_of(queries), heads_of(keys), heads_of(values), allowed_items)
    )
    return (frames_of(outputs, clip_count), log_totals)


def run_backward(queries, keys, values, allowed_rows, out_grad, log_totals, clip_count):
    allowed_items = jnp.repeat(allowed_rows, queries.shape[2] // HD, axis=0)
    query_grad, key_grad, value_grad = lax.map(
        attend_back,
        (
            heads_of(queries),
            heads_of(keys),
            heads_of(values),
            allowed_items,
            heads_of(out_grad),
            log_totals,
        ),
    )
    return (
        frames_of(query_grad, clip_count),
        frames_of(key_grad, clip_count),
        frames_of(value_grad, clip_count),
    )


def spread(piece, total_len, offset):
    return lax.dynamic_update_slice(jnp.zeros((total_len,), FLOAT), piece, (offset,))


def stat_parts(squares, row_starts, col_starts, full_rows, full_cols):
    row_list, col_list = ([], [])
    for square, row_start, col_start, rows_len, cols_len in zip(
        squares, row_starts, col_starts, full_rows, full_cols
    ):
        if square.ndim == 3:
            row_list.append(spread(jnp.sum(square, axis=(1, 2)), rows_len, row_start))
            col_piece = jnp.sum(square, axis=0)
            placed = lax.dynamic_update_slice(
                jnp.zeros((2, cols_len // 2), FLOAT), col_piece, (0, col_start)
            )
            col_list.append(placed.reshape(-1))
        else:
            row_list.append(spread(jnp.sum(square, axis=1), rows_len, row_start))
            col_list.append(spread(jnp.sum(square, axis=0), cols_len, col_start))
    return (jnp.concatenate(row_list), jnp.concatenate(col_list))


def factored_update(shard, row_segment, col_segment, row_start, col_start):
    row_here = lax.dynamic_slice_in_dim(row_segment, row_start, shard.shape[0])
    row_mean = jnp.mean(row_segment)
    if shard.ndim == 3:
        col_here = lax.dynamic_slice(
            col_segment.reshape(2, -1), (0, col_start), (2, shard.shape[2])
        )
        estimate = row_here[:, None, None] * col_here[None, :, :] / row_mean
    else:
        col_here = lax.dynamic_slice_in_dim(col_segment, col_start, shard.shape[1])
        estimate = row_here[:, None] * col_here[None, :] / row_mean
    return shard * lax.rsqrt(estimate)


def per_device(
    block_in,
    text,
    timesteps,
    frame_mask,
    text_mask,
    cotangent,
    w_ada,
    w_qkv,
    w_out,
    w_cq,
    w_cout,
    w_ckv,
    w_fc1,
    w_fc2,
    row_state,
    col_state,
):
    ada_full, qkv_full, out_full, cq_full, cout_full = (
        lax.all_gather(w_ada.astype(BFLOAT), ("dp", "head"), axis=0, tiled=True),
        lax.all_gather(w_qkv.astype(BFLOAT), ("dp", "head"), axis=0, tiled=True),
        lax.all_gather(w_out.astype(BFLOAT), ("dp", "head"), axis=0, tiled=True),
        lax.all_gather(w_cq.astype(BFLOAT), ("dp", "head"), axis=0, tiled=True),
        lax.all_gather(w_cout.astype(BFLOAT), ("dp", "head"), axis=0, tiled=True),
    )
    ckv_half, fc1_half, fc2_half = (
        lax.all_gather(w_ckv.astype(BFLOAT), "dp", axis=0, tiled=True),
        lax.all_gather(w_fc1.astype(BFLOAT), "dp", axis=0, tiled=True),
        lax.all_gather(w_fc2.astype(BFLOAT), "dp", axis=1, tiled=True),
    )
    clip_count = block_in.shape[0]
    inputs = block_in.astype(FLOAT)
    condition = jax.nn.silu(embed(timesteps, D)).astype(BFLOAT)
    modulation = jnp.dot(condition, ada_full, preferred_element_type=FLOAT)
    shift_self, scale_self, gate_self, shift_mlp, scale_mlp, gate_mlp = jnp.split(
        modulation, 6, axis=-1
    )
    self_input = modulate(inputs, shift_self, scale_self).astype(BFLOAT)
    qkv_three = qkv_full.reshape(D, 3, D)
    projected = jnp.einsum(
        "cfd,dke->kcfe", self_input, qkv_three, preferred_element_type=FLOAT
    ).astype(BFLOAT)
    self_heads = to_heads(projected)
    frames_allowed = frame_mask > 0
    self_out, self_logs = run_attention(
        self_heads[0], self_heads[1], self_heads[2], frames_allowed, clip_count
    )
    self_frames = to_frames(self_out.astype(BFLOAT)[None])[0]
    self_branch = jnp.einsum("cfd,de->cfe", self_frames, out_full, preferred_element_type=FLOAT)
    after_self = inputs + gate_self[:, None, :] * self_branch
    cross_input = layer_norm(after_self).astype(BFLOAT)
    cross_query = jnp.einsum(
        "cfd,de->cfe", cross_input, cq_full, preferred_element_type=FLOAT
    ).astype(BFLOAT)
    query_heads = to_heads(cross_query[None])[0]
    text_pair = jnp.einsum("cld,dke->kcle", text, ckv_half, preferred_element_type=FLOAT).astype(
        BFLOAT
    )
    tokens_allowed = text_mask > 0
    cross_out, cross_logs = run_attention(
        query_heads, text_pair[0], text_pair[1], tokens_allowed, clip_count
    )
    cross_frames = to_frames(cross_out.astype(BFLOAT)[None])[0]
    cross_branch = jnp.einsum("cfd,de->cfe", cross_frames, cout_full, preferred_element_type=FLOAT)
    after_cross = after_self + cross_branch
    mlp_input = modulate(after_cross, shift_mlp, scale_mlp).astype(BFLOAT)
    joined = join_rows(mlp_input)
    hidden_pre = jnp.einsum("cfd,dh->cfh", joined, fc1_half, preferred_element_type=FLOAT)
    hidden_act = jax.nn.gelu(hidden_pre).astype(BFLOAT)
    mlp_branch = part_rows(
        jnp.einsum("cfh,hd->cfd", hidden_act, fc2_half, preferred_element_type=FLOAT)
    )
    block_out = (after_cross + gate_mlp[:, None, :] * mlp_branch).astype(BFLOAT)
    out_grad = cotangent.astype(FLOAT)
    gate_mlp_grad = jnp.sum(out_grad * mlp_branch, axis=1)
    mlp_grad = (gate_mlp[:, None, :] * out_grad).astype(BFLOAT)
    mlp_grad_all = join_rows(mlp_grad)
    grad_fc2_part = jnp.einsum(
        "cfh,cfd->hd", hidden_act, mlp_grad_all, preferred_element_type=FLOAT
    )
    act_grad = jnp.einsum("cfd,hd->cfh", mlp_grad_all, fc2_half, preferred_element_type=FLOAT)
    gelu_back = jax.vjp(jax.nn.gelu, hidden_pre)[1]
    pre_grad = gelu_back(act_grad)[0].astype(BFLOAT)
    grad_fc1_part = jnp.einsum("cfd,cfh->dh", joined, pre_grad, preferred_element_type=FLOAT)
    mlp_in_grad = part_rows(
        jnp.einsum("cfh,dh->cfd", pre_grad, fc1_half, preferred_element_type=FLOAT)
    )
    mlp_back = jax.vjp(modulate, after_cross, shift_mlp, scale_mlp)[1]
    cross_res_grad, shift_mlp_grad, scale_mlp_grad = mlp_back(mlp_in_grad)
    cross_res_grad = out_grad + cross_res_grad
    cross_out_grad = cross_res_grad.astype(BFLOAT)
    grad_cout_part = jnp.einsum(
        "cfd,cfe->de", cross_frames, cross_out_grad, preferred_element_type=FLOAT
    )
    cross_attn_grad = jnp.einsum(
        "cfe,de->cfd", cross_out_grad, cout_full, preferred_element_type=FLOAT
    ).astype(BFLOAT)
    cross_grad_heads = to_heads(cross_attn_grad[None])[0]
    cross_query_grad, text_key_grad, text_value_grad = run_backward(
        query_heads,
        text_pair[0],
        text_pair[1],
        tokens_allowed,
        cross_grad_heads,
        cross_logs,
        clip_count,
    )
    text_pair_grad = jnp.stack([text_key_grad, text_value_grad])
    grad_ckv_part = jnp.einsum("cld,kcle->dke", text, text_pair_grad, preferred_element_type=FLOAT)
    cross_query_frames = to_frames(cross_query_grad[None])[0]
    grad_cq_part = jnp.einsum(
        "cfd,cfe->de", cross_input, cross_query_frames, preferred_element_type=FLOAT
    )
    cross_in_grad = jnp.einsum(
        "cfe,de->cfd", cross_query_frames, cq_full, preferred_element_type=FLOAT
    )
    norm_back = jax.vjp(layer_norm, after_self)[1]
    self_res_grad = cross_res_grad + norm_back(cross_in_grad)[0]
    gate_self_grad = jnp.sum(self_res_grad * self_branch, axis=1)
    self_out_grad = (gate_self[:, None, :] * self_res_grad).astype(BFLOAT)
    grad_out_part = jnp.einsum(
        "cfd,cfe->de", self_frames, self_out_grad, preferred_element_type=FLOAT
    )
    self_attn_grad = jnp.einsum(
        "cfe,de->cfd", self_out_grad, out_full, preferred_element_type=FLOAT
    ).astype(BFLOAT)
    self_grad_heads = to_heads(self_attn_grad[None])[0]
    query_grad, key_grad, value_grad = run_backward(
        self_heads[0],
        self_heads[1],
        self_heads[2],
        frames_allowed,
        self_grad_heads,
        self_logs,
        clip_count,
    )
    projected_grad = to_frames(jnp.stack([query_grad, key_grad, value_grad]))
    grad_qkv_part = jnp.einsum(
        "cfd,kcfe->dke", self_input, projected_grad, preferred_element_type=FLOAT
    ).reshape(D, 3 * D)
    in_grad_normed = jnp.einsum(
        "kcfe,dke->cfd", projected_grad, qkv_three, preferred_element_type=FLOAT
    )
    self_back = jax.vjp(modulate, inputs, shift_self, scale_self)[1]
    input_res_grad, shift_self_grad, scale_self_grad = self_back(in_grad_normed)
    input_grad = (self_res_grad + input_res_grad).astype(BFLOAT)
    modulation_grad = jnp.concatenate(
        [
            shift_self_grad,
            scale_self_grad,
            gate_self_grad,
            shift_mlp_grad,
            scale_mlp_grad,
            gate_mlp_grad,
        ],
        axis=-1,
    )
    flat_at = lax.axis_index("dp") * lax.axis_size("head") + lax.axis_index("head")
    data_at = lax.axis_index("dp")
    head_at = lax.axis_index("head")
    condition_wide = condition.astype(FLOAT)
    grad_ada_part = jnp.einsum("cr,cx->rx", condition_wide, modulation_grad, precision=PRECISE)
    grad_ada_raw, grad_qkv_raw, grad_out_raw, grad_cq_raw, grad_cout_raw = (
        lax.psum_scatter(grad_ada_part, ("dp", "head"), scatter_dimension=0, tiled=True),
        lax.psum_scatter(grad_qkv_part, ("dp", "head"), scatter_dimension=0, tiled=True),
        lax.psum_scatter(grad_out_part, ("dp", "head"), scatter_dimension=0, tiled=True),
        lax.psum_scatter(grad_cq_part, ("dp", "head"), scatter_dimension=0, tiled=True),
        lax.psum_scatter(grad_cout_part, ("dp", "head"), scatter_dimension=0, tiled=True),
    )
    grad_ckv_raw, grad_fc1_raw, grad_fc2_raw = (
        lax.psum_scatter(grad_ckv_part, "dp", scatter_dimension=0, tiled=True),
        lax.psum_scatter(grad_fc1_part, "dp", scatter_dimension=0, tiled=True),
        lax.psum_scatter(grad_fc2_part, "dp", scatter_dimension=1, tiled=True),
    )
    raw_grads = [
        grad_ada_raw,
        grad_qkv_raw,
        grad_out_raw,
        grad_cq_raw,
        grad_cout_raw,
        grad_ckv_raw,
        grad_fc1_raw,
        grad_fc2_raw,
    ]
    masters = [w_ada, w_qkv, w_out, w_cq, w_cout, w_ckv, w_fc1, w_fc2]
    full_rows = [D, D, D, D, D, DT, D, FF]
    full_cols = [6 * D, 3 * D, D, D, D, 2 * D, FF, D]
    row_starts = [flat_at * grad.shape[0] for grad in raw_grads[:5]] + [
        data_at * grad_ckv_raw.shape[0],
        data_at * grad_fc1_raw.shape[0],
        head_at * grad_fc2_raw.shape[0],
    ]
    col_starts = [
        0,
        0,
        0,
        0,
        0,
        head_at * grad_ckv_raw.shape[2],
        head_at * grad_fc1_raw.shape[1],
        data_at * grad_fc2_raw.shape[1],
    ]
    raw_squares = [grad * grad for grad in raw_grads]
    square_local = sum((jnp.sum(square) for square in raw_squares))
    weight_local = jnp.stack([jnp.sum(master * master) for master in masters])
    square_total, weight_total = lax.psum((square_local, weight_local), ("dp", "head"))
    grad_norm = jnp.sqrt(square_total)
    factor = 1.0 / jnp.maximum(1.0, grad_norm / CLIP_NORM)
    clipped = [grad * factor for grad in raw_grads]
    row_local, col_local = stat_parts(
        [grad * grad for grad in clipped], row_starts, col_starts, full_rows, full_cols
    )
    row_sums, col_sums = lax.psum((row_local, col_local), ("dp", "head"))
    row_divisor = jnp.concatenate(
        [
            jnp.full((rows_len,), float(cols_len), FLOAT)
            for rows_len, cols_len in zip(full_rows, full_cols)
        ]
    )
    col_divisor = jnp.concatenate(
        [
            jnp.full((cols_len,), float(rows_len), FLOAT)
            for rows_len, cols_len in zip(full_rows, full_cols)
        ]
    )
    row_new = DECAY_RATE * row_state + (1.0 - DECAY_RATE) * (row_sums / row_divisor + EPS_FACTOR)
    col_new = DECAY_RATE * col_state + (1.0 - DECAY_RATE) * (col_sums / col_divisor + EPS_FACTOR)
    updates = []
    row_at, col_at = (0, 0)
    for shard, row_start, col_start, rows_len, cols_len in zip(
        clipped, row_starts, col_starts, full_rows, full_cols
    ):
        row_segment = row_new[row_at : row_at + rows_len]
        col_segment = col_new[col_at : col_at + cols_len]
        updates.append(factored_update(shard, row_segment, col_segment, row_start, col_start))
        row_at = row_at + rows_len
        col_at = col_at + cols_len
    update_local = jnp.stack([jnp.sum(update * update) for update in updates])
    update_total = lax.psum(update_local, ("dp", "head"))
    entry_counts = jnp.array(
        [float(rows_len * cols_len) for rows_len, cols_len in zip(full_rows, full_cols)], FLOAT
    )
    limits = jnp.maximum(1.0, jnp.sqrt(update_total / entry_counts) / CLIP_UPDATE)
    rates = RELATIVE_RATE * jnp.maximum(SCALE_FLOOR, jnp.sqrt(weight_total / entry_counts))
    updated = [
        master - rates[place] * (update / limits[place])
        for place, (master, update) in enumerate(zip(masters, updates))
    ]
    grad_ada, grad_qkv, grad_out, grad_cq, grad_cout, grad_ckv, grad_fc1, grad_fc2 = clipped
    new_ada, new_qkv, new_out, new_cq, new_cout, new_ckv, new_fc1, new_fc2 = updated
    return (
        block_out,
        input_grad,
        grad_norm,
        row_new,
        col_new,
        grad_ada,
        grad_qkv,
        grad_out,
        grad_cq,
        grad_cout,
        grad_ckv,
        grad_fc1,
        grad_fc2,
        new_ada,
        new_qkv,
        new_out,
        new_cq,
        new_cout,
        new_ckv,
        new_fc1,
        new_fc2,
    )


def solution(mesh):
    return jax.shard_map(
        per_device,
        mesh=mesh,
        in_specs=(
            P("dp", "head", None),
            P("dp", None, None),
            P("dp"),
            P("dp", None),
            P("dp", None),
            P("dp", "head", None),
            P(("dp", "head"), None),
            P(("dp", "head"), None),
            P(("dp", "head"), None),
            P(("dp", "head"), None),
            P(("dp", "head"), None),
            P("dp", None, "head"),
            P("dp", "head"),
            P("head", "dp"),
            P(),
            P(),
        ),
        out_specs=(
            P("dp", "head", None),
            P("dp", "head", None),
            P(),
            P(),
            P(),
            P(("dp", "head"), None),
            P(("dp", "head"), None),
            P(("dp", "head"), None),
            P(("dp", "head"), None),
            P(("dp", "head"), None),
            P("dp", None, "head"),
            P("dp", "head"),
            P("head", "dp"),
            P(("dp", "head"), None),
            P(("dp", "head"), None),
            P(("dp", "head"), None),
            P(("dp", "head"), None),
            P(("dp", "head"), None),
            P("dp", None, "head"),
            P("dp", "head"),
            P("head", "dp"),
        ),
        check_vma=False,
    )
```

profile of v0, /device:TPU:0, one launch (start us, length us, event | category | flops | bytes accessed | tf_op | source)
XLA Modules:
  0.0 1864.6 jit_solution(11720379872005244072)
XLA Ops:
  19.5 55.0 %all-gather.13.cloned.1.call-done = bf16[768,2304]{1,0:T(8,128)(2,1)} async-done(((bf16[24,2304]{1,0:T(8,128)(2,1)}), bf16[768,2304]{1,0:T(8,128)(2,1)}) %all-gather.13.cloned.1.call-update) | async-done | bytes 3538960 | tf_op jit(solution)/shard_map/all_gather | solution.py:196
  74.5 5.7 copy.206
  80.2 69.2 %all-gather.11.cloned.1.call-done = bf16[768,4608]{1,0:T(8,128)(2,1)} async-done(((bf16[24,4608]{1,0:T(8,128)(2,1)}), bf16[768,4608]{1,0:T(8,128)(2,1)}) %all-gather.11.cloned.1.call-update) | async-done | bytes 7077904 | tf_op jit(solution)/shard_map/all_gather | solution.py:195
  158.5 6.0 copy.208
  164.5 5.3 all-to-all-start
  171.4 37.9 %all-to-all-done = bf16[3,1,512,768]{2,0,1,3:T(4,128)(2,1)} async-done(((bf16[3,1,512,768]{2,0,1,3:T(4,128)(2,1)}), bf16[3,1,512,768]{2,0,1,3:T(4,128)(2,1)}, u32[]{:S(2)}, u32[]{:S(2)}) %all-to-all-start) | async-done | bytes 2359328 | tf_op jit(solution)/shard_map/all_to_all | solution.py:63
  232.1 34.1 %while.52 = (s32[]{:T(128)}, bf16[6,1024,64]{1,2,0:T(8,128)(2,1)}, f32[6,1024]{1,0:T(8,128)S(1)}, pred[6,1024]{1,0:T(8,128)(4,1)S(1)}, bf16[6,1024,64]{2,1,0:T(8...) while((s32[]{:T(128)}, bf16[6,1024,64]{1,2,0:T(8,128)(2,1)}, ...), condition=%wide.region_5.6_spmd, body=%wide.region_2.5_spmd.sunk | while | flops 281017344 | bytes 13679725 | solution.py:114
  266.3 5.4 copy.213
  272.2 7.3 reduce.44
  287.2 9.3 all-to-all-done.1
  310.6 6.4 reduce.45
  339.7 16.6 while.53
  359.4 6.4 reduce.46
  366.8 12.3 all_to_all.120
  393.0 12.6 all-gather.25.cloned.1.call-done
  405.6 28.1 %all-gather.23.cloned.1.call-done = bf16[1,1024,768]{2,1,0:T(8,128)(2,1)} async-done(((bf16[1,512,768]{2,1,0:T(8,128)(2,1)}), bf16[1,1024,768]{2,1,0:T(8,128)(2,1)}) %all-gather.23.cloned.1.call-update) | async-done | bytes 1572880 | tf_op jit(solution)/shard_map/all_gather | solution.py:71
  433.7 7.4 fusion.139
  441.1 37.8 %all-gather.27.cloned.1.call-done = bf16[1536,768]{0,1:T(8,128)(2,1)} async-done(((bf16[1536,48]{0,1:T(8,128)(2,1)}), bf16[1536,768]{0,1:T(8,128)(2,1)}) %all-gather.27.cloned.1.call-update) | async-done | bytes 2359312 | tf_op jit(solution)/shard_map/all_gather | solution.py:204
  478.9 28.0 %all-gather.29.cloned.1.call-done = bf16[1,1024,768]{2,1,0:T(8,128)(2,1)} async-done(((bf16[1,512,768]{2,1,0:T(8,128)(2,1)}), bf16[1,1024,768]{2,1,0:T(8,128)(2,1)}) %all-gather.29.cloned.1.call-update) | async-done | bytes 1572880 | tf_op jit(solution)/shard_map/all_gather | solution.py:71
  506.9 8.6 fusion.109
  520.9 8.4 fusion.141
  529.3 17.7 reduce-scatter.12.cloned.1.call-done
  550.0 25.4 %reduce-scatter.10.cloned.1.call-done = bf16[1,512,768]{2,1,0:T(8,128)(2,1)} async-done(((bf16[1,1024,768]{2,1,0:T(8,128)(2,1)}), bf16[1,512,768]{2,1,0:T(8,128)(2,1)}) %reduce-scatter.10.cloned.1.call-update) | async-done | bytes 786448 | tf_op jit(solution)/shard_map/reduce_scatter | solution.py:75
  583.4 5.1 copy.223
  588.6 7.3 reduce.47
  602.6 11.1 all-to-all-done.4
  623.8 40.9 %while.54 = (s32[]{:T(128)}, bf16[6,1024,64]{1,2,0:T(8,128)(2,1)}, bf16[6,256,64]{1,2,0:T(8,128)(2,1)S(1)}, bf16[6,256,64]{1,2,0:T(8,128)(2,1)}, pred[6,256]{1,0...) while((s32[]{:T(128)}, bf16[6,1024,64]{1,2,0:T(8,128)(2,1)}, ...), condition=%wide.region_20.21_spmd, body=%wide.region_18.20_spmd.sunk | while | flops 170310656 | bytes 9070717 | solution.py:122
  667.9 5.9 copy.240
  682.4 7.3 reduce.48
  691.7 14.6 all_to_all.121
  726.9 6.4 fusion.137
  740.3 5.4 reduce.49
  750.7 8.1 fusion.131
  763.8 67.1 %while.55 = (s32[]{:T(128)}, bf16[6,1024,64]{1,2,0:T(8,128)(2,1)S(1)}, bf16[6,1024,64]{1,2,0:T(8,128)(2,1)S(1)}, bf16[6,1024,64]{1,2,0:T(8,128)(2,1)S(1)}, pred[...) while((s32[]{:T(128)}, ...), condition=%wide.region_25.26_spmd, body=%wide.region_23.25_spmd.sunk | while | flops 687143936 | bytes 33462396 | solution.py:122
  837.9 40.8 %all_to_all.122 = bf16[3,1,1024,384]{3,0,1,2:T(4,128)(2,1)S(1)} all-to-all(bf16[3,1,1024,384]{3,0,1,2:T(4,128)(2,1)} %copy.235), channel_id=1, replica_groups=mesh['dp'=16,'head'=2] {'head'}, dimensions={2} | all-to-all | bytes 4718592 | tf_op jit(solution)/shard_map/all_to_all | solution.py:67
  888.7 6.8 fusion.152
  902.7 6.8 broadcast_multiply_fusion
  915.4 71.1 %reduce-scatter.18.cloned.1.call-done = f32[24,768]{1,0:T(8,128)} async-done(((f32[768,768]{1,0:T(8,128)}), f32[24,768]{1,0:T(8,128)}) %reduce-scatter.18.cloned.1.call-update) | async-done | bytes 73744 | tf_op jit(solution)/shard_map/reduce_scatter | solution.py:341
  988.0 101.8 %reduce-scatter.20.cloned.1.call-done = f32[24,768]{1,0:T(8,128)} async-done(((f32[768,768]{1,0:T(8,128)}), f32[24,768]{1,0:T(8,128)}) %reduce-scatter.20.cloned.1.call-update) | async-done | bytes 73744 | tf_op jit(solution)/shard_map/reduce_scatter | solution.py:342
  1091.3 77.2 %reduce-scatter.24.cloned.1.call-done = f32[48,1536]{1,0:T(8,128)} async-done(((f32[768,1536]{1,0:T(8,128)}), f32[48,1536]{1,0:T(8,128)}) %reduce-scatter.24.cloned.1.call-update) | async-done | bytes 294928 | tf_op jit(solution)/shard_map/reduce_scatter | solution.py:347
  1170.2 76.7 %reduce-scatter.26.cloned.1.call-done = f32[1536,48]{0,1:T(8,128)} async-done(((f32[1536,768]{0,1:T(8,128)}), f32[1536,48]{0,1:T(8,128)}) %reduce-scatter.26.cloned.1.call-update) | async-done | bytes 294928 | tf_op jit(solution)/shard_map/reduce_scatter | solution.py:348
  1248.5 123.2 %reduce-scatter.16.cloned.1.call-done = f32[24,2304]{1,0:T(8,128)} async-done(((f32[768,2304]{1,0:T(8,128)}), f32[24,2304]{1,0:T(8,128)}) %reduce-scatter.16.cloned.1.call-update) | async-done | bytes 221200 | tf_op jit(solution)/shard_map/reduce_scatter | solution.py:340
  1373.4 166.4 %reduce-scatter.14.cloned.1.call-done = f32[24,4608]{1,0:T(8,128)} async-done(((f32[768,4608]{1,0:T(8,128)}), f32[24,4608]{1,0:T(8,128)}) %reduce-scatter.14.cloned.1.call-update) | async-done | bytes 442384 | tf_op jit(solution)/shard_map/reduce_scatter | solution.py:339
  1546.7 5.8 stack.70
  1552.5 39.5 %psum.35 = f32[]{:T(128)} all-reduce(f32[]{:T(128)S(6)} %add.293), channel_id=1, replica_groups=mesh['dp'=16,'head'=2] {'dp','head'}, use_global_device_ids=true, to_apply=%region_50.51 | all-reduce | flops 1 | bytes 8 | tf_op jit(solution)/shard_map/psum | solution.py:381
  1631.3 119.5 %all-reduce.8.cloned.1.call-done = (f32[8704]{0:T(1024)}, f32[14592]{0:T(1024)}) async-done(((f32[8704]{0:T(1024)}, f32[14592]{0:T(1024)}), (f32[8704]{0:T(1024)}, f32[14592]{0:T(1024)})) %all-reduce.8.cloned.1.call-update) | async-done | bytes 93200 | tf_op jit(solution)/shard_map/psum | solution.py:388
  1788.1 5.1 stack.79
  1796.3 41.1 %all-reduce.1 = (f32[8]{0:T(128)S(1)}, f32[8]{0:T(128)S(1)}) all-reduce(f32[8]{0:T(128)S(1)} %stack.79, f32[8]{0:T(128)S(1)} %copy-done.90), channel_id=1, replica_groups=mesh['dp'=16,'head'=2] {'dp','head'}, use_global_device_ids=true, to_apply=%region_94.95 | all-reduce | flops 16 | bytes 128 | tf_op jit(solution)/shard_map/psum | solution.py:414
  (636 shorter events, 481.5 us)
Async XLA Ops:
  7.2 314.7 %copy-start = (bf16[1,256,1024]{2,1,0:T(8,128)(2,1)S(1)}, bf16[1,256,1024]{2,1,0:T(8,128)(2,1)}, u32[]{:S(2)}) copy-start(bf16[1,256,1024]{2,1,0:T(8,128)(2,1)} %param.26) | copy-start | bytes 1572868
  7.2 67.3 %all-gather.13.cloned.1.call-start = ((), (), s32[]{:S(2)}) async-start(), calls=%async_computation.18 | async-start | bytes 3649536 | tf_op jit(solution)/shard_map/all_gather | solution.py:196
  9.7 139.7 %all-gather.11.cloned.1.call-start = ((), (), s32[]{:S(2)}) async-start(), calls=%async_computation.17 | async-start | bytes 7299072 | tf_op jit(solution)/shard_map/all_gather | solution.py:195
  12.3 289.3 %all-gather.15.cloned.1.call-start = ((), (), s32[]{:S(2)}) async-start(), calls=%async_computation.19 | async-start | bytes 1216512 | tf_op jit(solution)/shard_map/all_gather | solution.py:197
  14.6 290.9 %all-gather.17.cloned.1.call-start = ((), (), s32[]{:S(2)}) async-start(), calls=%async_computation.20 | async-start | bytes 1216512 | tf_op jit(solution)/shard_map/all_gather | solution.py:198
  16.9 305.0 %all-gather.19.cloned.1.call-start = ((), (), s32[]{:S(2)}) async-start(), calls=%async_computation.21 | async-start | bytes 1671168 | tf_op jit(solution)/shard_map/all_gather | solution.py:202
  19.1 135.1 %copy-start.57 = (f32[512]{0:T(512)}, f32[512]{0:T(512)S(1)}, u32[]{:S(2)}) copy-start(f32[512]{0:T(512)S(1)} %broadcast_multiply_fusion.10) | copy-start | bytes 6148
  19.5 60.7 %copy-start.69 = (f32[512]{0:T(512)}, f32[512]{0:T(512)S(1)}, u32[]{:S(2)}) copy-start(f32[512]{0:T(512)S(1)} %fusion.124) | copy-start | bytes 6148
  19.5 134.7 %copy-start.65 = (f32[512]{0:T(512)}, f32[512]{0:T(512)S(1)}, u32[]{:S(2)}) copy-start(f32[512]{0:T(512)S(1)} %fusion.165) | copy-start | bytes 6148
  154.2 147.3 %copy-start.62 = (f32[768]{0:T(1024)}, f32[768]{0:T(1024)S(1)}, u32[]{:S(2)}) copy-start(f32[768]{0:T(1024)S(1)} %get-tuple-element.534) | copy-start | bytes 9220
  164.5 44.8 %all-to-all-start = ((bf16[3,1,512,768]{2,0,1,3:T(4,128)(2,1)}), bf16[3,1,512,768]{2,0,1,3:T(4,128)(2,1)}, u32[]{:S(2)}, u32[]{:S(2)}) async-start(bf16[3,1,512,768]{2,0,1,3:T(4,128)(2,1)} %copy.208), calls=%async_computation | async-start | bytes 6291456 | tf_op jit(solution)/shard_map/all_to_all | solution.py:63
  169.8 214.7 %all-gather.21.cloned.1.call-start = ((), (), s32[]{:S(2)}) async-start(), calls=%async_computation.22 | async-start | bytes 1216512 | tf_op jit(solution)/shard_map/all_gather | solution.py:199
  281.5 15.0 all-to-all-start.1
  285.9 119.7 %all-gather.25.cloned.1.call-start = ((), (), s32[]{:S(2)}) async-start(), calls=%async_computation.24 | async-start | bytes 2506752 | tf_op jit(solution)/shard_map/all_gather | solution.py:203
  318.3 13.2 all-to-all-start.2
  321.8 111.9 %all-gather.23.cloned.1.call-start = ((), (), s32[]{:S(2)}) async-start(), calls=%async_computation.23 | async-start | bytes 2359296 | tf_op jit(solution)/shard_map/all_gather | solution.py:71
  389.4 89.5 %all-gather.27.cloned.1.call-start = ((), (), s32[]{:S(2)}) async-start(), calls=%async_computation.25 | async-start | bytes 2506752 | tf_op jit(solution)/shard_map/all_gather | solution.py:204
  391.8 115.1 %all-gather.29.cloned.1.call-start = ((), (), s32[]{:S(2)}) async-start(), calls=%async_computation.27 | async-start | bytes 2359296 | tf_op jit(solution)/shard_map/all_gather | solution.py:71
  392.9 154.1 %reduce-scatter.12.cloned.1.call-start = ((), (), s32[]{:S(2)}) async-start(), calls=%async_computation.28 | async-start | bytes 2359296 | tf_op jit(solution)/shard_map/reduce_scatter | solution.py:75
  520.9 54.5 %reduce-scatter.10.cloned.1.call-start = ((), (), s32[]{:S(2)}) async-start(), calls=%async_computation.26 | async-start | bytes 2359296 | tf_op jit(solution)/shard_map/reduce_scatter | solution.py:75
  598.2 15.5 all-to-all-start.4
  602.5 309.6 %all-reduce.6.cloned.1.call-start = ((), (), s32[]{:S(2)}) async-start(), calls=%async_computation.36 | async-start | bytes 6291456
  673.8 240.1 %reduce-scatter.22.cloned.1.call-start = ((), (), s32[]{:S(2)}) async-start(), calls=%async_computation.33 | async-start | bytes 2433024 | tf_op jit(solution)/shard_map/reduce_scatter | solution.py:343
  677.4 309.1 %reduce-scatter.18.cloned.1.call-start = ((), (), s32[]{:S(2)}) async-start(), calls=%async_computation.31 | async-start | bytes 2433024 | tf_op jit(solution)/shard_map/reduce_scatter | solution.py:341
  721.9 367.9 %reduce-scatter.20.cloned.1.call-start = ((), (), s32[]{:S(2)}) async-start(), calls=%async_computation.32 | async-start | bytes 2433024 | tf_op jit(solution)/shard_map/reduce_scatter | solution.py:342
  725.5 443.1 %reduce-scatter.24.cloned.1.call-start = ((), (), s32[]{:S(2)}) async-start(), calls=%async_computation.34 | async-start | bytes 5013504 | tf_op jit(solution)/shard_map/reduce_scatter | solution.py:347
  747.1 12.9 all-to-all-start.6
  750.6 496.3 %reduce-scatter.26.cloned.1.call-start = ((), (), s32[]{:S(2)}) async-start(), calls=%async_computation.35 | async-start | bytes 5013504 | tf_op jit(solution)/shard_map/reduce_scatter | solution.py:348
  758.8 612.9 %reduce-scatter.16.cloned.1.call-start = ((), (), s32[]{:S(2)}) async-start(), calls=%async_computation.30 | async-start | bytes 7299072 | tf_op jit(solution)/shard_map/reduce_scatter | solution.py:340
  895.5 644.3 %reduce-scatter.14.cloned.1.call-start = ((), (), s32[]{:S(2)}) async-start(), calls=%async_computation.29 | async-start | bytes 14598144 | tf_op jit(solution)/shard_map/reduce_scatter | solution.py:339
  909.5 841.3 %all-reduce.8.cloned.1.call-start = ((), (), s32[]{:S(2)}) async-start(), calls=%async_computation.37 | async-start | bytes 196608 | tf_op jit(solution)/shard_map/psum | solution.py:388
  1170.2 436.7 %copy-start.47 = (f32[24,768]{1,0:T(8,128)S(1)}, f32[24,768]{1,0:T(8,128)}, u32[]{:S(2)}) copy-start(f32[24,768]{1,0:T(8,128)} %reduce-scatter.22.cloned.1.call-done) | copy-start | bytes 221188
  1371.7 225.9 %copy-start.37 = (f32[24,2304]{1,0:T(8,128)S(1)}, f32[24,2304]{1,0:T(8,128)}, u32[]{:S(2)}) copy-start(f32[24,2304]{1,0:T(8,128)} %reduce-scatter.16.cloned.1.call-done) | copy-start | bytes 663556
  1594.2 189.6 %copy-start.38 = (f32[64,2,384]{2,1,0:T(2,128)}, f32[64,2,384]{2,1,0:T(2,128)S(1)}, u32[]{:S(2)}) copy-start(f32[64,2,384]{2,1,0:T(2,128)S(1)} %get-tuple-element.612) | copy-start | bytes 589828
  1596.0 242.8 %copy-start.15 = (f32[24,4608]{1,0:T(8,128)}, f32[24,4608]{1,0:T(8,128)S(1)}, u32[]{:S(2)}) copy-start(f32[24,4608]{1,0:T(8,128)S(1)} %get-tuple-element.617) | copy-start | bytes 1327108
  1598.3 242.8 %copy-start.26 = (f32[24,2304]{1,0:T(8,128)}, f32[24,2304]{1,0:T(8,128)S(1)}, u32[]{:S(2)}) copy-start(f32[24,2304]{1,0:T(8,128)S(1)} %get-tuple-element.616) | copy-start | bytes 663556
  1612.2 175.1 %copy-start.22 = (f32[48,1536]{1,0:T(8,128)}, f32[48,1536]{1,0:T(8,128)S(1)}, u32[]{:S(2)}) copy-start(f32[48,1536]{1,0:T(8,128)S(1)} %get-tuple-element.611) | copy-start | bytes 884740
  1796.2 50.0 %copy-start.41 = (f32[24,768]{1,0:T(8,128)S(1)}, f32[24,768]{1,0:T(8,128)}, u32[]{:S(2)}) copy-start(f32[24,768]{1,0:T(8,128)} %get-tuple-element.614) | copy-start | bytes 221188
  1796.2 50.0 %copy-start.44 = (f32[24,768]{1,0:T(8,128)S(1)}, f32[24,768]{1,0:T(8,128)}, u32[]{:S(2)}) copy-start(f32[24,768]{1,0:T(8,128)} %param.34) | copy-start | bytes 221188
  1796.2 50.0 %copy-start.60 = (f32[768]{0:T(1024)S(1)}, f32[768]{0:T(1024)}, u32[]{:S(2)}) copy-start(f32[768]{0:T(1024)} %get-tuple-element.659) | copy-start | bytes 9220
  1796.3 50.0 %copy-start.86 = (f32[24]{0:T(128)S(1)}, f32[24]{0:T(128)}, u32[]{:S(2)}) copy-start(f32[24]{0:T(128)} %dynamic_slice.101) | copy-start | bytes 292
  1796.3 52.0 %copy-start.42 = (f32[24,768]{1,0:T(8,128)S(1)}, f32[24,768]{1,0:T(8,128)}, u32[]{:S(2)}) copy-start(f32[24,768]{1,0:T(8,128)} %get-tuple-element.613) | copy-start | bytes 221188
  1796.3 52.0 %copy-start.46 = (f32[24,768]{1,0:T(8,128)S(1)}, f32[24,768]{1,0:T(8,128)}, u32[]{:S(2)}) copy-start(f32[24,768]{1,0:T(8,128)} %param.35) | copy-start | bytes 221188
  1796.3 52.0 %copy-start.59 = (f32[768]{0:T(1024)S(1)}, f32[768]{0:T(1024)}, u32[]{:S(2)}) copy-start(f32[768]{0:T(1024)} %get-tuple-element.658) | copy-start | bytes 9220
  1796.3 52.0 %copy-start.85 = (f32[24]{0:T(128)S(1)}, f32[24]{0:T(128)}, u32[]{:S(2)}) copy-start(f32[24]{0:T(128)} %dynamic_slice.102) | copy-start | bytes 292
  1796.3 54.0 %copy-start.23 = (f32[48,1536]{1,0:T(8,128)S(1)}, f32[48,1536]{1,0:T(8,128)}, u32[]{:S(2)}) copy-start(f32[48,1536]{1,0:T(8,128)} %copy-done.22) | copy-start | bytes 884740
  1796.3 54.0 %copy-start.33 = (f32[48,1536]{1,0:T(8,128)S(1)}, f32[48,1536]{1,0:T(8,128)}, u32[]{:S(2)}) copy-start(f32[48,1536]{1,0:T(8,128)} %param.37) | copy-start | bytes 884740
  1796.3 54.0 %copy-start.84 = (f32[48]{0:T(128)S(1)}, f32[48]{0:T(128)}, u32[]{:S(2)}) copy-start(f32[48]{0:T(128)} %dynamic_slice.105) | copy-start | bytes 580
  (73 other events, 682.7 us)
Sparse Core Ops, SparseCore 0:
  11.6 62.8 all-gather.12
  78.0 71.3 all-gather.10
  152.9 54.0 all-gather.14
  210.4 53.1 all-gather.16
  266.2 38.6 all-gather.18
  308.3 53.1 all-gather.20
  364.3 41.2 all-gather.24
  407.7 25.9 all-gather.22
  436.6 42.3 all-gather.26
  480.9 25.9 all-gather.28
  521.0 26.0 reduce-scatter.11
  549.3 26.0 reduce-scatter.9
  673.9 103.6 all-reduce.5
  782.8 99.6 reduce-scatter.21
  888.4 98.0 reduce-scatter.17
  991.7 98.1 reduce-scatter.19
  1094.0 74.4 reduce-scatter.23
  1172.2 74.5 reduce-scatter.25
  1253.5 118.1 reduce-scatter.15
  1377.6 162.1 reduce-scatter.13
  1630.2 120.5 all-reduce.7
where the time goes:
time: 1880 us; the launch traced here: 1860 us
  waiting for transfers between devices  1070 us (57%)
  matrix products  228 us (12%)
  local copies, waits for them, and re-layouts  202 us (11%)
  other arithmetic  160 us (9%)
  blocking collectives  148 us (8%)
  between operations  29 us (2%)
  starting transfers between devices  22.1 us (1%)
    reduce_scatter x1, waiting for transfers between devices, per_device(): lax.psum_scatter(grad_ada_part, ('dp', 'head'), scatter_dimension=0, tile...  166 us
    reduce_scatter x1, waiting for transfers between devices, per_device(): lax.psum_scatter(grad_qkv_part, ('dp', 'head'), scatter_dimension=0, tile...  123 us
    psum x1, waiting for transfers between devices, per_device(): row_sums, col_sums = lax.psum((row_local, col_local), ('dp', 'head'))  119 us
    reduce_scatter x1, waiting for transfers between devices, per_device(): lax.psum_scatter(grad_cq_part, ('dp', 'head'), scatter_dimension=0, tiled...  102 us
    reduce_scatter x1, waiting for transfers between devices, per_device(): lax.psum_scatter(grad_fc1_part, 'dp', scatter_dimension=0, tiled=True)  77.2 us
    reduce_scatter x1, waiting for transfers between devices, per_device(): lax.psum_scatter(grad_fc2_part, 'dp', scatter_dimension=1, tiled=True)  76.7 us
    reduce_scatter x1, waiting for transfers between devices, per_device(): lax.psum_scatter(grad_out_part, ('dp', 'head'), scatter_dimension=0, tile...  71.1 us
    all_gather x1, waiting for transfers between devices, per_device(): lax.all_gather(w_ada.astype(BFLOAT), ('dp', 'head'), axis=0, tiled=True)  69.2 us
  transfers between devices with their start and end apart: 26, of which 20 were waited for; matrix products, arithmetic and copies ran while one was open for 20% of the time, Pallas kernels for 0%

commit v1 on v0

v1 whole, which is shorter than its diff:
```python
import functools

import jax
import jax.numpy as jnp
from jax import lax
from jax.experimental import pallas as pl
from jax.experimental.pallas import tpu as pltpu
from jax.sharding import PartitionSpec as P

D = 768
FF = 3072
DT = 1024
HD = 64
HALF = FF // 2

PRECISE = lax.Precision.HIGHEST
FLOAT = jnp.float32
BFLOAT = jnp.bfloat16
EPS_NORM = 1e-06
EPS_FACTOR = 1e-30
CLIP_NORM = 1.0
CLIP_UPDATE = 0.25
DECAY_RATE = 0.5
RELATIVE_RATE = 4.0
SCALE_FLOOR = 0.001
SCORE_SCALE = 0.125
MASKED_SCORE = -1e30
ALL = ("dp", "head")
PAIR = 2 * HD
PAIRS = D // PAIR


def embed_part(steps, first, count):
    halfway = D // 2
    place = first + jnp.arange(count)
    freqs = jnp.exp(-jnp.log(10000.0) * (place % halfway).astype(FLOAT) / halfway)
    angles = steps.astype(FLOAT)[:, None] * freqs
    waves = jnp.where(place < halfway, jnp.cos(angles), jnp.sin(angles))
    return jax.nn.silu(waves).astype(BFLOAT)


def layer_norm(values):
    centered = values - jnp.mean(values, axis=-1, keepdims=True)
    variance = jnp.mean(centered * centered, axis=-1, keepdims=True)
    return centered * lax.rsqrt(variance + EPS_NORM)


def modulate(values, shift, scale):
    return layer_norm(values) * (1.0 + scale) + shift


def core_link():
    return ("dp", 1)


def row_link():
    return ("head", 1)


def far_links():
    masks, mask = [], 2
    while mask < lax.axis_size("dp"):
        masks.append(mask)
        mask = mask * 2
    return [("dp", mask) for mask in masks]


def dp_bits():
    return lax.axis_size("dp").bit_length() - 1


def bit_of(link):
    return (lax.axis_index(link[0]) // link[1]) % 2


def cross(values, link):
    pairs = [(place, place ^ link[1]) for place in range(lax.axis_size(link[0]))]
    return lax.ppermute(values, link[0], pairs)


def dim_of(link, head_first):
    if link[0] == "head":
        return 0 if head_first else dp_bits()
    return (1 if head_first else 0) + dp_bits() - link[1].bit_length()


def grow(block, link, head_first):
    other = cross(block, link)
    upper = bit_of(link) == 1
    low = jnp.where(upper, other, block)
    high = jnp.where(upper, block, other)
    return jnp.concatenate([low, high], axis=dim_of(link, head_first))


def shrink(block, link, head_first, kind=BFLOAT):
    dim, bit = dim_of(link, head_first), bit_of(link)
    kept = lax.dynamic_slice_in_dim(block, bit, 1, axis=dim)
    sent = lax.dynamic_slice_in_dim(block, 1 - bit, 1, axis=dim)
    return (kept.astype(FLOAT) + cross(sent.astype(BFLOAT), link).astype(FLOAT)).astype(kind)


def gather_shard(shard, head_first, row_early):
    block = shard.reshape((1,) * (dp_bits() + 1) + shard.shape)
    far = far_links()
    plane = [row_link(), far[0]] if row_early else [far[0], row_link()]
    for link in far[1:] + plane + [core_link()]:
        block = grow(block, link, head_first)
    return block


def scatter_sum(block, head_first, row_early):
    far = far_links()
    plane = [far[0], row_link()] if row_early else [row_link(), far[0]]
    order = [core_link()] + plane + far[:0:-1]
    for place, link in enumerate(order):
        block = shrink(block, link, head_first, FLOAT if place == len(order) - 1 else BFLOAT)
    return block.reshape(block.shape[dp_bits() + 1 :])


def split_rows(matrix):
    bits = dp_bits() + 1
    return matrix.reshape((2,) * bits + (matrix.shape[0] // 2**bits, matrix.shape[1]))


def split_halves(matrices):
    bits = dp_bits()
    return matrices.reshape(
        (2,) * (bits + 1) + (matrices.shape[1] // 2**bits, matrices.shape[2])
    )


def sum_all(values):
    for link in [core_link(), row_link()] + far_links():
        values = values + cross(values, link)
    return values


def swap_place(values):
    pairs = []
    for place in range(lax.axis_size("dp")):
        for head in range(2):
            pairs.append((place * 2 + head, ((place & ~1) | head) * 2 + (place & 1)))
    return lax.ppermute(values, ALL, pairs)


def from_clip_core(values):
    pairs = []
    for place in range(0, lax.axis_size("dp"), 2):
        for head in range(2):
            pairs.append(((place + head) * 2 + head, (place + 1 - head) * 2 + head))
    own = bit_of(core_link()) == bit_of(row_link())
    return jnp.where(own, values, lax.ppermute(values, ALL, pairs))


def nt(left, right):
    return lax.dot_general(left, right, (((1,), (1,)), ((), ())), preferred_element_type=FLOAT)


def nn(left, right):
    return lax.dot_general(left, right, (((1,), (0,)), ((), ())), preferred_element_type=FLOAT)


def lanes_of(length):
    return lax.broadcasted_iota(jnp.int32, (length, PAIR), 1)


def with_spare(pair, head, spare):
    lane = lanes_of(pair.shape[0])
    rest = jnp.where(lane == HD * (1 - head), spare, jnp.zeros_like(pair))
    return jnp.where(lane // HD == head, pair, rest)


def attend_kernel(blocks, *refs):
    query_ref = refs[0]
    key_refs, value_refs, bias_refs = refs[1 : 1 + 3 * blocks : 3], refs[2 : 2 + 3 * blocks : 3], refs[3 : 3 + 3 * blocks : 3]
    out_ref, log_ref = refs[1 + 3 * blocks :]
    queries = query_ref[...] * jnp.asarray(SCORE_SCALE, BFLOAT)
    one = jnp.ones((1, 1), BFLOAT)
    values_t = [ref[...].T for ref in value_refs]
    results, logs = [], []
    for head in range(2):
        query = with_spare(queries, head, one)
        scores = [
            nt(with_spare(key_ref[...], head, bias_ref[...]), query)
            for key_ref, bias_ref in zip(key_refs, bias_refs)
        ]
        peak = functools.reduce(
            jnp.maximum, [jnp.max(score, axis=0, keepdims=True) for score in scores]
        )
        total = None
        for score, value_t in zip(scores, values_t):
            probs = jnp.exp(score - peak).astype(BFLOAT)
            row = lax.broadcasted_iota(jnp.int32, value_t.shape, 0)
            term = nn(jnp.where(row // HD == head, value_t, one), probs)
            total = term if total is None else total + term
        weight = total[HD * (1 - head) : HD * (1 - head) + 1, :]
        results.append(total[HD * head : HD * (head + 1), :] / weight)
        logs.append(peak + jnp.log(weight))
    out_ref[...] = jnp.concatenate(results, axis=0).T.astype(BFLOAT)
    log_ref[0] = jnp.concatenate(logs, axis=0)


def back_kernel(blocks, *refs):
    query_ref, out_ref, grad_ref, log_ref = refs[:4]
    ins = refs[4 : 4 + 3 * blocks]
    key_refs, value_refs, bias_refs = ins[0::3], ins[1::3], ins[2::3]
    query_grad_ref = refs[4 + 3 * blocks]
    pair_grad_refs = refs[5 + 3 * blocks :]
    queries = query_ref[...] * jnp.asarray(SCORE_SCALE, BFLOAT)
    out_grad = grad_ref[...]
    zero = jnp.zeros((1, 1), BFLOAT)
    one = jnp.ones((1, 1), BFLOAT)
    product = out_ref[...].astype(FLOAT) * out_grad.astype(FLOAT)
    chooser = (
        lax.broadcasted_iota(jnp.int32, (8, PAIR), 1) // HD
        == lax.broadcasted_iota(jnp.int32, (8, PAIR), 0)
    ).astype(FLOAT)
    inner = lax.dot_general(
        chooser, product, (((1,), (1,)), ((), ())), precision=PRECISE, preferred_element_type=FLOAT
    )
    keys_t = [ref[...].T for ref in key_refs]
    query_parts = [None, None]
    for block in range(blocks):
        key_grad, value_grad = None, None
        for head in range(2):
            grad_here = with_spare(out_grad, head, zero)
            score = nt(
                with_spare(key_refs[block][...], head, bias_refs[block][...]),
                with_spare(queries, head, one),
            )
            probs = jnp.exp(score - log_ref[0, head : head + 1, :])
            prob_grad = nt(value_refs[block][...], grad_here)
            score_grad = (probs * (prob_grad - inner[head : head + 1, :])).astype(BFLOAT)
            value_term = nn(probs.astype(BFLOAT), grad_here)
            key_term = nn(score_grad, with_spare(queries, head, zero))
            query_term = nn(keys_t[block][HD * head : HD * (head + 1), :], score_grad)
            value_grad = value_term if value_grad is None else value_grad + value_term
            key_grad = key_term if key_grad is None else key_grad + key_term
            query_parts[head] = (
                query_term if query_parts[head] is None else query_parts[head] + query_term
            )
        pair_grad_refs[block][0] = key_grad.astype(BFLOAT)
        pair_grad_refs[block][1] = value_grad.astype(BFLOAT)
    joined = jnp.concatenate(query_parts, axis=0) * SCORE_SCALE
    query_grad_ref[...] = joined.T.astype(BFLOAT)


def column_block(length):
    return pl.BlockSpec((length, PAIR), lambda pair: (0, pair))


def value_block(length):
    return pl.BlockSpec((length, PAIR), lambda pair: (0, pair + PAIRS))


def whole_block(shape):
    return pl.BlockSpec(shape, lambda pair: (0,) * len(shape))


def log_block(frames):
    return pl.BlockSpec((1, 2, frames), lambda pair: (pair, 0, 0))


def key_specs(key_values):
    specs, operands = [], []
    for joint, bias in key_values:
        length = joint.shape[0]
        specs += [column_block(length), value_block(length), whole_block((length, PAIR))]
        operands += [joint, joint, bias]
    return specs, operands


def attend(queries, key_values):
    frames, blocks = queries.shape[0], len(key_values)
    length = sum(joint.shape[0] for joint, _ in key_values)
    specs, operands = key_specs(key_values)
    return pl.pallas_call(
        functools.partial(attend_kernel, blocks),
        grid=(PAIRS,),
        in_specs=[column_block(frames)] + specs,
        out_specs=[column_block(frames), log_block(frames)],
        out_shape=[
            jax.ShapeDtypeStruct((frames, D), BFLOAT),
            jax.ShapeDtypeStruct((PAIRS, 2, frames), FLOAT),
        ],
        compiler_params=pltpu.CompilerParams(vmem_limit_bytes=48 * 1024 * 1024),
        cost_estimate=pl.CostEstimate(
            flops=16 * frames * length * D,
            bytes_accessed=4 * frames * D + 4 * length * D,
            transcendentals=12 * frames * length,
        ),
    )(queries, *operands)


def attend_back(queries, out, out_grad, logs, key_values):
    frames, blocks = queries.shape[0], len(key_values)
    length = sum(joint.shape[0] for joint, _ in key_values)
    specs, operands = key_specs(key_values)
    return pl.pallas_call(
        functools.partial(back_kernel, blocks),
        grid=(PAIRS,),
        in_specs=[column_block(frames)] * 3 + [log_block(frames)] + specs,
        out_specs=[column_block(frames)]
        + [
            pl.BlockSpec((2, joint.shape[0], PAIR), lambda pair: (0, 0, pair))
            for joint, _ in key_values
        ],
        out_shape=[jax.ShapeDtypeStruct((frames, D), BFLOAT)]
        + [jax.ShapeDtypeStruct((2, joint.shape[0], D), BFLOAT) for joint, _ in key_values],
        compiler_params=pltpu.CompilerParams(vmem_limit_bytes=48 * 1024 * 1024),
        cost_estimate=pl.CostEstimate(
            flops=40 * frames * length * D,
            bytes_accessed=8 * frames * D + 8 * length * D,
            transcendentals=12 * frames * length,
        ),
    )(queries, out, out_grad, logs, *operands)


def bias_of(allowed):
    column = jnp.where(allowed > 0, 0.0, MASKED_SCORE).astype(BFLOAT)
    return jnp.broadcast_to(column[:, None], (allowed.shape[0], PAIR))


def spread(piece, total_len, offset):
    return lax.dynamic_update_slice(jnp.zeros((total_len,), FLOAT), piece, (offset,))


def per_device(
    block_in,
    text,
    timesteps,
    frame_mask,
    text_mask,
    cotangent,
    w_ada,
    w_qkv,
    w_out,
    w_cq,
    w_cout,
    w_ckv,
    w_fc1,
    w_fc2,
    row_state,
    col_state,
):
    clips = lax.axis_size("dp")
    devices = clips * 2
    data_at = lax.axis_index("dp")
    head_at = lax.axis_index("head")
    flat_at = data_at * 2 + head_at
    frames = block_in.shape[1]
    rows = w_qkv.shape[0]

    mlp_shard = jnp.concatenate([w_fc1.astype(BFLOAT), w_fc2.T.astype(BFLOAT)], axis=0)
    mlp_all = lax.all_gather(mlp_shard, ALL, axis=0, tiled=False)
    query_out = gather_shard(
        jnp.concatenate([w_qkv[:, :D], w_out], axis=1).astype(BFLOAT), False, False
    ).reshape(D, 2 * D)
    w_key_value = gather_shard(w_qkv[:, D:].astype(BFLOAT), False, True).reshape(D, 2 * D)
    w_query, w_project = query_out[:, :D], query_out[:, D:]

    inputs = swap_place(block_in[0]).astype(FLOAT)
    out_grad = swap_place(cotangent[0]).astype(FLOAT)
    masks = from_clip_core(jnp.concatenate([frame_mask[0], text_mask[0]]))
    clip_text = from_clip_core(text[0])
    core_at = data_at % 2
    own_allowed = lax.dynamic_slice_in_dim(masks, core_at * frames, frames)
    other_allowed = lax.dynamic_slice_in_dim(masks, (1 - core_at) * frames, frames)
    own_bias, other_bias = bias_of(own_allowed), bias_of(other_allowed)
    text_bias = bias_of(masks[2 * frames :])

    steps = lax.dynamic_update_slice(jnp.zeros((clips,), jnp.int32), timesteps, (data_at,))
    for link in [core_link()] + far_links():
        steps = steps + cross(steps, link)
    condition = embed_part(steps, flat_at * rows, rows)
    modulation = jnp.dot(condition, w_ada.astype(BFLOAT), preferred_element_type=FLOAT)
    modulation = modulation.reshape(clips // 2, 2, 6 * D)
    kept = lax.dynamic_slice_in_dim(modulation, head_at, 1, axis=1)
    sent = lax.dynamic_slice_in_dim(modulation, 1 - head_at, 1, axis=1)
    modulation = (kept + cross(sent, row_link())).reshape(clips // 2, 6 * D)
    for link in far_links():
        bit = bit_of(link)
        halves = modulation.reshape(-1, 2, 6 * D)
        kept = lax.dynamic_slice_in_dim(halves, bit, 1, axis=1)
        sent = lax.dynamic_slice_in_dim(halves, 1 - bit, 1, axis=1)
        modulation = (kept + cross(sent, link)).reshape(-1, 6 * D)
    modulation = modulation + cross(modulation, core_link())
    shift_self, scale_self, gate_self, shift_mlp, scale_mlp, gate_mlp = jnp.split(
        modulation, 6, axis=-1
    )

    self_input = modulate(inputs, shift_self, scale_self).astype(BFLOAT)
    key_value = nn(self_input, w_key_value).astype(BFLOAT)
    query = nn(self_input, w_query).astype(BFLOAT)
    other_key_value = cross(key_value, core_link())

    cross_pair = gather_shard(
        jnp.concatenate([w_cq, w_cout], axis=1).astype(BFLOAT), False, False
    ).reshape(D, 2 * D)
    w_cross_query, w_cross_project = cross_pair[:, :D], cross_pair[:, D:]
    w_text = gather_shard(
        w_ckv.astype(BFLOAT).reshape(w_ckv.shape[0], D), True, True
    ).reshape(2, DT, D)

    self_keys = [(key_value, own_bias), (other_key_value, other_bias)]
    self_attn, self_logs = attend(query, self_keys)
    self_branch = nn(self_attn, w_project)
    after_self = inputs + gate_self * self_branch

    text_halves = jnp.einsum(
        "ld,hde->hle", clip_text, w_text, preferred_element_type=FLOAT
    ).astype(BFLOAT)
    text_pair = (
        text_halves.reshape(2, clip_text.shape[0], 2, D // 2)
        .transpose(1, 2, 0, 3)
        .reshape(clip_text.shape[0], 2 * D)
    )
    cross_input = layer_norm(after_self).astype(BFLOAT)
    cross_query = nn(cross_input, w_cross_query).astype(BFLOAT)
    text_keys = [(text_pair, text_bias)]
    cross_attn, cross_logs = attend(cross_query, text_keys)
    after_cross = after_self + nn(cross_attn, w_cross_project)

    mlp_input = modulate(after_cross, shift_mlp, scale_mlp).astype(BFLOAT)
    mlp_all = mlp_all.reshape(clips, 2, 2, rows * 2, HALF).transpose(2, 1, 0, 3, 4)
    fc1_halves, fc2_halves = mlp_all.reshape(2, 2, D, HALF)
    hidden_pre = jnp.einsum("fd,hdk->hfk", mlp_input, fc1_halves, preferred_element_type=FLOAT)
    hidden_act = jax.nn.gelu(hidden_pre).astype(BFLOAT)
    mlp_branch = jnp.einsum("hfk,hdk->fd", hidden_act, fc2_halves, preferred_element_type=FLOAT)
    block_out = swap_place((after_cross + gate_mlp * mlp_branch).astype(BFLOAT))

    gate_mlp_grad = jnp.sum(out_grad * mlp_branch, axis=0, keepdims=True)
    mlp_grad = (gate_mlp * out_grad).astype(BFLOAT)
    grad_fc2_part = jnp.einsum(
        "fd,hfk->hdk", mlp_grad, hidden_act, preferred_element_type=FLOAT
    ).astype(BFLOAT)
    act_grad = jnp.einsum("fd,hdk->hfk", mlp_grad, fc2_halves, preferred_element_type=FLOAT)
    gelu_back = jax.vjp(jax.nn.gelu, hidden_pre)[1]
    pre_grad = gelu_back(act_grad)[0].astype(BFLOAT)
    grad_fc1_part = jnp.einsum(
        "fd,hfk->hdk", mlp_input, pre_grad, preferred_element_type=FLOAT
    ).astype(BFLOAT)
    mlp_parts = jnp.stack([grad_fc1_part, grad_fc2_part]).reshape(2, 2, clips, rows * 2, HALF)
    mlp_raw = lax.psum_scatter(
        mlp_parts.transpose(2, 1, 0, 3, 4).reshape(devices, 2, rows * 2, HALF),
        ALL,
        scatter_dimension=0,
        tiled=False,
    ).astype(FLOAT)
    mlp_in_grad = jnp.einsum("hfk,hdk->fd", pre_grad, fc1_halves, preferred_element_type=FLOAT)
    mlp_back = jax.vjp(modulate, after_cross, shift_mlp, scale_mlp)[1]
    cross_res_grad, shift_mlp_grad, scale_mlp_grad = mlp_back(mlp_in_grad)
    cross_res_grad = out_grad + cross_res_grad

    cross_out_grad = cross_res_grad.astype(BFLOAT)
    grad_cout_part = jnp.einsum(
        "fd,fe->de", cross_attn, cross_out_grad, preferred_element_type=FLOAT
    ).astype(BFLOAT)
    cross_attn_grad = nt(cross_out_grad, w_cross_project).astype(BFLOAT)
    cross_query_grad, text_pair_grad = attend_back(
        cross_query, cross_attn, cross_attn_grad, cross_logs, text_keys
    )
    text_grad_halves = text_pair_grad.reshape(2, -1, 2, D // 2).transpose(2, 1, 0, 3)
    grad_ckv_part = jnp.einsum(
        "ld,hle->hde",
        clip_text,
        text_grad_halves.reshape(2, -1, D),
        preferred_element_type=FLOAT,
    ).astype(BFLOAT)
    grad_cq_part = jnp.einsum(
        "fd,fe->de", cross_input, cross_query_grad, preferred_element_type=FLOAT
    ).astype(BFLOAT)
    cross_raw = scatter_sum(
        split_rows(jnp.concatenate([grad_cq_part, grad_cout_part], axis=1)), False, False
    )
    ckv_raw = scatter_sum(split_halves(grad_ckv_part), True, True)
    cross_in_grad = nt(cross_query_grad, w_cross_query)
    norm_back = jax.vjp(layer_norm, after_self)[1]
    self_res_grad = cross_res_grad + norm_back(cross_in_grad)[0]

    gate_self_grad = jnp.sum(self_res_grad * self_branch, axis=0, keepdims=True)
    self_out_grad = (gate_self * self_res_grad).astype(BFLOAT)
    grad_out_part = jnp.einsum(
        "fd,fe->de", self_attn, self_out_grad, preferred_element_type=FLOAT
    ).astype(BFLOAT)
    self_attn_grad = nt(self_out_grad, w_project).astype(BFLOAT)
    query_grad, own_pair_grad, other_pair_grad = attend_back(
        query, self_attn, self_attn_grad, self_logs, self_keys
    )
    pair_grad = (
        own_pair_grad.astype(FLOAT) + cross(other_pair_grad, core_link()).astype(FLOAT)
    ).astype(BFLOAT)
    grad_query_part = jnp.einsum(
        "fd,fe->de", self_input, query_grad, preferred_element_type=FLOAT
    ).astype(BFLOAT)
    grad_pair_part = jnp.einsum(
        "fd,kfe->dke", self_input, pair_grad, preferred_element_type=FLOAT
    ).astype(BFLOAT)
    query_out_raw = scatter_sum(
        split_rows(jnp.concatenate([grad_query_part, grad_out_part], axis=1)), False, False
    )
    pair_raw = scatter_sum(split_rows(grad_pair_part.reshape(D, 2 * D)), False, True)
    in_grad_normed = nt(query_grad, w_query) + jnp.einsum(
        "kfe,dke->fd", pair_grad, w_key_value.reshape(D, 2, D), preferred_element_type=FLOAT
    )
    self_back = jax.vjp(modulate, inputs, shift_self, scale_self)[1]
    input_res_grad, shift_self_grad, scale_self_grad = self_back(in_grad_normed)
    input_grad = swap_place((self_res_grad + input_res_grad).astype(BFLOAT))

    modulation_grad = jnp.concatenate(
        [
            shift_self_grad,
            scale_self_grad,
            gate_self_grad,
            shift_mlp_grad,
            scale_mlp_grad,
            gate_mlp_grad,
        ],
        axis=-1,
    )
    modulation_grad = modulation_grad + cross(modulation_grad, core_link())
    modulation_grad = modulation_grad.reshape((1,) * dp_bits() + (6 * D,))
    for link in far_links()[::-1] + [row_link()]:
        other = cross(modulation_grad, link)
        upper = bit_of(link) == 1
        dim = dp_bits() - 1 if link[0] == "head" else dp_bits() - link[1].bit_length()
        modulation_grad = jnp.concatenate(
            [
                jnp.where(upper, other, modulation_grad),
                jnp.where(upper, modulation_grad, other),
            ],
            axis=dim,
        )
    ada_raw = jnp.einsum(
        "cr,cx->rx",
        condition.astype(FLOAT),
        modulation_grad.reshape(clips, 6 * D),
        precision=PRECISE,
    )

    qkv_raw = jnp.concatenate([query_out_raw[:, :D], pair_raw], axis=1)
    raw_grads = [
        ada_raw,
        qkv_raw,
        query_out_raw[:, D:],
        cross_raw[:, :D],
        cross_raw[:, D:],
        ckv_raw,
        mlp_raw[0],
        mlp_raw[1],
    ]
    masters = [
        w_ada,
        w_qkv,
        w_out,
        w_cq,
        w_cout,
        w_ckv.reshape(w_ckv.shape[0], D),
        w_fc1,
        w_fc2.T,
    ]
    full_rows = [D, D, D, D, D, DT, D, FF]
    full_cols = [6 * D, 3 * D, D, D, D, 2 * D, FF, D]
    squares = [grad * grad for grad in raw_grads]
    across = [jnp.sum(square, axis=1) for square in squares]
    down = [jnp.sum(square, axis=0) for square in squares]
    row_list = [spread(piece, D, flat_at * rows) for piece in across[:5]] + [
        spread(across[5], DT, data_at * across[5].shape[0]),
        spread(across[6], D, data_at * across[6].shape[0]),
        spread(down[7], FF, head_at * HALF),
    ]
    text_down = lax.dynamic_update_slice(
        jnp.zeros((2, D), FLOAT), down[5].reshape(2, D // 2), (0, head_at * (D // 2))
    )
    col_list = down[:5] + [
        text_down.reshape(-1),
        spread(down[6], FF, head_at * HALF),
        spread(across[7], D, data_at * across[7].shape[0]),
    ]
    weight_local = jnp.stack([jnp.sum(master * master) for master in masters])
    sums = sum_all(jnp.concatenate(row_list + col_list + [weight_local]))
    row_total, col_total = sum(full_rows), sum(full_cols)
    row_sums = sums[:row_total]
    col_sums = sums[row_total : row_total + col_total]
    weight_total = sums[row_total + col_total :]
    grad_norm = jnp.sqrt(jnp.sum(row_sums))
    factor = 1.0 / jnp.maximum(1.0, grad_norm / CLIP_NORM)
    row_divisor = jnp.concatenate(
        [
            jnp.full((rows_len,), float(cols_len), FLOAT)
            for rows_len, cols_len in zip(full_rows, full_cols)
        ]
    )
    col_divisor = jnp.concatenate(
        [
            jnp.full((cols_len,), float(rows_len), FLOAT)
            for rows_len, cols_len in zip(full_rows, full_cols)
        ]
    )
    square_factor = factor * factor
    row_new = DECAY_RATE * row_state + (1.0 - DECAY_RATE) * (
        square_factor * row_sums / row_divisor + EPS_FACTOR
    )
    col_new = DECAY_RATE * col_state + (1.0 - DECAY_RATE) * (
        square_factor * col_sums / col_divisor + EPS_FACTOR
    )
    clipped = [grad * factor for grad in raw_grads]
    updates = []
    row_at, col_at = (0, 0)
    for place, shard in enumerate(clipped):
        row_segment = row_new[row_at : row_at + full_rows[place]]
        col_segment = col_new[col_at : col_at + full_cols[place]]
        row_at = row_at + full_rows[place]
        col_at = col_at + full_cols[place]
        if place < 5:
            row_here = lax.dynamic_slice_in_dim(row_segment, flat_at * rows, rows)
            col_here = col_segment
        elif place == 5:
            length = shard.shape[0]
            row_here = lax.dynamic_slice_in_dim(row_segment, data_at * length, length)
            col_here = lax.dynamic_slice(
                col_segment.reshape(2, D), (0, head_at * (D // 2)), (2, D // 2)
            ).reshape(-1)
        elif place == 6:
            length = shard.shape[0]
            row_here = lax.dynamic_slice_in_dim(row_segment, data_at * length, length)
            col_here = lax.dynamic_slice_in_dim(col_segment, head_at * HALF, HALF)
        else:
            length = shard.shape[0]
            row_here = lax.dynamic_slice_in_dim(col_segment, data_at * length, length)
            col_here = lax.dynamic_slice_in_dim(row_segment, head_at * HALF, HALF)
        estimate = row_here[:, None] * col_here[None, :] / jnp.mean(row_segment)
        updates.append(shard * lax.rsqrt(estimate))
    update_total = sum_all(jnp.stack([jnp.sum(update * update) for update in updates]))
    entry_counts = jnp.array(
        [float(rows_len * cols_len) for rows_len, cols_len in zip(full_rows, full_cols)], FLOAT
    )
    limits = jnp.maximum(1.0, jnp.sqrt(update_total / entry_counts) / CLIP_UPDATE)
    rates = RELATIVE_RATE * jnp.maximum(SCALE_FLOOR, jnp.sqrt(weight_total / entry_counts))
    updated = [
        master - rates[place] * (update / limits[place])
        for place, (master, update) in enumerate(zip(masters, updates))
    ]
    clipped[5] = clipped[5].reshape(w_ckv.shape)
    updated[5] = updated[5].reshape(w_ckv.shape)
    clipped[7] = clipped[7].T
    updated[7] = updated[7].T
    return (
        block_out[None],
        input_grad[None],
        grad_norm,
        row_new,
        col_new,
        *clipped,
        *updated,
    )


def solution(mesh):
    return jax.shard_map(
        per_device,
        mesh=mesh,
        in_specs=(
            P("dp", "head", None),
            P("dp", None, None),
            P("dp"),
            P("dp", None),
            P("dp", None),
            P("dp", "head", None),
            P(("dp", "head"), None),
            P(("dp", "head"), None),
            P(("dp", "head"), None),
            P(("dp", "head"), None),
            P(("dp", "head"), None),
            P("dp", None, "head"),
            P("dp", "head"),
            P("head", "dp"),
            P(),
            P(),
        ),
        out_specs=(
            P("dp", "head", None),
            P("dp", "head", None),
            P(),
            P(),
            P(),
            P(("dp", "head"), None),
            P(("dp", "head"), None),
            P(("dp", "head"), None),
            P(("dp", "head"), None),
            P(("dp", "head"), None),
            P("dp", None, "head"),
            P("dp", "head"),
            P("head", "dp"),
            P(("dp", "head"), None),
            P(("dp", "head"), None),
            P(("dp", "head"), None),
            P(("dp", "head"), None),
            P(("dp", "head"), None),
            P("dp", None, "head"),
            P("dp", "head"),
            P("head", "dp"),
        ),
        check_vma=False,
    )
```

time: 1880 us -> 647 us (0.34)
  waiting for transfers between devices: 1070 us -> 226 us
  matrix products: 228 us -> 69.8 us
  blocking collectives: 148 us -> 0 us
  local copies, waits for them, and re-layouts: 202 us -> 91.3 us
  other arithmetic: 160 us -> 85.7 us
  starting transfers between devices: 22.1 us -> 90.2 us
  Pallas kernels: 0 us -> 48.6 us
    reduce_scatter x9 -> x1, waiting for transfers between devices: 660 us -> 0.01 us  [per_device(): lax.psum_scatter(mlp_parts.transpose(2, 1, 0, 3, 4).reshape(devices, 2, r...]
    all_gather x10 -> x1, waiting for transfers between devices: 231 us -> 0.02 us  [per_device(): mlp_all = lax.all_gather(mlp_shard, ALL, axis=0, tiled=False)]
    ppermute x0 -> x72, waiting for transfers between devices: none -> 226 us  [the longest x66 226 us: cross(): return lax.ppermute(values, link[0], pairs)]
    dot_general x105 -> x25, matrix products: 228 us -> 69.8 us  [the longest x1 8.52 us: per_device(): jnp.einsum('fd,hfk->hdk', mlp_grad, hidden_act, preferred_element_type=FL...]
    psum x1 -> x0, waiting for transfers between devices: 119 us -> none  [per_device(): row_sums, col_sums = lax.psum((row_local, col_local), ('dp', 'head'))]
    ppermute x0 -> x72, starting transfers between devices: none -> 90.1 us  [the longest x66 62 us: cross(): return lax.ppermute(values, link[0], pairs)]
    psum x2 -> x0, blocking collectives: 80.6 us -> none  [the longest x1 41.1 us: per_device(): update_total = lax.psum(update_local, ('dp', 'head'))]
    all_to_all x3 -> x0, blocking collectives: 67.7 us -> none  [to_frames(): lax.all_to_all(stacked, 'head', split_axis=2, concat_axis=3, tiled=True)]
  transfers between devices with their start and end apart: 26 -> 74, of which waited for: 20 -> 44; matrix products, arithmetic and copies ran while one was open for 20% -> 27% of each run, Pallas kernels for 0% -> 6%
where the time goes in v1:
time: 647 us; the launch traced here: 636 us
  waiting for transfers between devices  226 us (35%)
  local copies, waits for them, and re-layouts  91.3 us (14%)
  starting transfers between devices  90.2 us (14%)
  other arithmetic  85.7 us (13%)
  matrix products  69.8 us (11%)
  Pallas kernels  48.6 us (8%)
  between operations  24.6 us (4%)
    ppermute x66, waiting for transfers between devices, cross(): return lax.ppermute(values, link[0], pairs)  226 us
    ppermute x66, starting transfers between devices, cross(): return lax.ppermute(values, link[0], pairs)  62 us
    pallas_call x2, Pallas kernels, attend_back(): pl.pallas_call(functools.partial(back_kernel, blocks), grid=(PAIRS,), in_...  29.2 us
    ppermute x4, starting transfers between devices, swap_place(): return lax.ppermute(values, ALL, pairs)  24.2 us
    pallas_call x2, Pallas kernels, attend(): pl.pallas_call(functools.partial(attend_kernel, blocks), grid=(PAIRS,), i...  19.3 us
    sub x7, other arithmetic, per_device(): master - rates[place] * (update / limits[place])  14.8 us
    convert_element_type x16, other arithmetic, shrink(): (kept.astype(FLOAT) + cross(sent.astype(BFLOAT), link).astype(FLOAT)).ast...  14.2 us
    dynamic_slice x20, local copies, waits for them, and re-layouts, shrink(): sent = lax.dynamic_slice_in_dim(block, 1 - bit, 1, axis=dim)  13.3 us
  transfers between devices with their start and end apart: 74, of which 44 were waited for; matrix products, arithmetic and copies ran while one was open for 27% of the time, Pallas kernels for 6%

profile of v1, /device:TPU:0, one launch (start us, length us, event | category | flops | bytes accessed | tf_op | source)
XLA Modules:
  0.0 636.0 jit_solution(4051690448326011373)
XLA Ops:
  7.2 7.6 %collective-permute-start.34 = (bf16[512,768]{1,0:T(8,128)(2,1)}, bf16[512,768]{1,0:T(8,128)(2,1)}, u32[]{:S(2)}, u32[]{:S(2)}) collective-permute-start(bf16[512,768]{1,0:T(8,128)(2,1)} %bitcast.253), channel_id=1, source_target_pairs={{0,0},{1,2},{2,1},{3,3},{4,4},{5,6},{6,5},{7,7},{8,8},{9,10},{10,9... | collective-permute-start | bytes 2359304 | tf_op jit(solution)/shard_map/ppermute | solution.py:143
  62.5 13.6 %collective-permute-done.23 = bf16[1,2,1,1,1,24,1536]{6,5,4,3,2,1,0:T(8,128)(2,1)S(1)} collective-permute-done((bf16[1,2,1,1,1,24,1536]{6,5,4,3,2,1,0:T(8,128)(2,1)S(1)}, bf16[1,2,1,1,1,24,1536]{6,5,4,3,2,1,0:T(8,128)(2,1)S(1)}, u32[]{:S(2)}, u32[]{:S(2)}) %collective-permute-start.23) | collective-permute-done | bytes 147488 | tf_op jit(solution)/shard_map/ppermute | solution.py:78
  76.1 12.1 %collective-permute-done.16 = bf16[1,2,1,1,1,24,1536]{6,5,4,3,2,1,0:T(8,128)(2,1)S(1)} collective-permute-done((bf16[1,2,1,1,1,24,1536]{6,5,4,3,2,1,0:T(8,128)(2,1)S(1)}, bf16[1,2,1,1,1,24,1536]{6,5,4,3,2,1,0:T(8,128)(2,1)S(1)}, u32[]{:S(2)}, u32[]{:S(2)}) %collective-permute-start.16) | collective-permute-done | bytes 147488 | tf_op jit(solution)/shard_map/ppermute | solution.py:78
  96.1 3.9 collective-permute-start.7
  100.0 4.1 collective-permute-done.7
  112.7 3.8 collective-permute-start.17
  117.1 4.9 collective-permute-done.12
  122.3 7.6 %collective-permute-done.24 = bf16[2,2,1,1,1,24,1536]{6,5,4,3,2,1,0:T(8,128)(2,1)S(1)} collective-permute-done((bf16[2,2,1,1,1,24,1536]{6,5,4,3,2,1,0:T(8,128)(2,1)S(1)}, bf16[2,2,1,1,1,24,1536]{6,5,4,3,2,1,0:T(8,128)(2,1)S(1)}, u32[]{:S(2)}, u32[]{:S(2)}) %collective-permute-start.24) | collective-permute-done | bytes 294944 | tf_op jit(solution)/shard_map/ppermute | solution.py:78
  132.3 9.7 %collective-permute-done.29 = bf16[1,2,2,1,1,64,768]{6,5,4,3,2,1,0:T(8,128)(2,1)S(1)} collective-permute-done((bf16[1,2,2,1,1,64,768]{6,5,4,3,2,1,0:T(8,128)(2,1)S(1)}, bf16[1,2,2,1,1,64,768]{6,5,4,3,2,1,0:T(8,128)(2,1)S(1)}, u32[]{:S(2)}, u32[]{:S(2)}) %collective-permute-start.29) | collective-permute-done | bytes 393248 | tf_op jit(solution)/shard_map/ppermute | solution.py:78
  144.8 9.9 %collective-permute-done.13 = bf16[2,2,2,1,1,24,1536]{6,5,4,3,2,1,0:T(8,128)(2,1)S(1)} collective-permute-done((bf16[2,2,2,1,1,24,1536]{6,5,4,3,2,1,0:T(8,128)(2,1)S(1)}, bf16[2,2,2,1,1,24,1536]{6,5,4,3,2,1,0:T(8,128)(2,1)S(1)}, u32[]{:S(2)}, u32[]{:S(2)}) %collective-permute-start.13) | collective-permute-done | bytes 589856 | tf_op jit(solution)/shard_map/ppermute | solution.py:78
  155.5 9.0 %collective-permute-done.25 = bf16[2,2,2,1,1,24,1536]{6,5,4,3,2,1,0:T(8,128)(2,1)S(1)} collective-permute-done((bf16[2,2,2,1,1,24,1536]{6,5,4,3,2,1,0:T(8,128)(2,1)S(1)}, bf16[2,2,2,1,1,24,1536]{6,5,4,3,2,1,0:T(8,128)(2,1)S(1)}, u32[]{:S(2)}, u32[]{:S(2)}) %collective-permute-start.25) | collective-permute-done | bytes 589856 | tf_op jit(solution)/shard_map/ppermute | solution.py:78
  164.7 4.0 collective-permute-done.30
  176.2 6.1 reshape_reshape.19
  194.3 13.4 %shard_map.328 = (bf16[512,768]{1,0:T(8,128)(2,1)S(1)}, f32[6,2,512]{2,1,0:T(2,128)S(1)}) custom-call(bf16[512,768]{1,0:T(8,128)(2,1)S(1)} %copy-done.5, bf16[512,1536]{1,0:T(8,128)(2,1)S(1)} %convolution_convert_fusion.2.refs_1_.refs_2_.refs_4_.refs_5_, bf16[512,1536]{1,0:T(8,128)(2,1)S(1)} %convolution_convert_fusion.2.refs_1_.refs_2_.refs_4_.refs_5_, ...), custom_call_target="tpu_custom_call" | custom-call | flops 6442450944 | bytes 4718592 | tf_op jit(solution)/shard_map/pallas_call | solution.py:277
  210.9 6.0 shard_map.329
  219.3 6.8 %fusion.118 = (bf16[1,2,16,48,1536]{4,3,0,1,2:T(8,128)(2,1)}, bf16[1,2,16,48,1536]{4,3,0,1,2:T(8,128)(2,1)S(1)}) fusion(bf16[2,2,16,48,1536]{4,3,0,1,2:T(8,128)(2,1)} %bitcast.223), kind=kLoop, calls=%fused_computation.382 | loop fusion | bytes 18874368 | tf_op jit(solution)/shard_map/unstack | solution.py:426
  233.1 8.3 %fusion.6 = bf16[2,512,1536]{1,2,0:T(8,128)(2,1)S(1)} fusion(f32[2,1536,512]{2,1,0:T(8,128)S(1)} %fusion.103, bf16[2,768,1536]{2,1,0:T(8,128)(2,1)S(1)} %bitcast.238, bf16[512,768]{1,0:T(8,128)(2,1)} %collective-permute-done.34, f32[768]{0:T(1024)S(1)} %copy-done.85), kind=kOutput, calls=%fused_computation.9 | convolution fusion | flops 2448556032 | bytes 14945280 | tf_op jit(solution)/shard_map/fd,hdk->hfk/dot_general | solution.py:437
  241.4 4.7 fusion.26
  246.2 7.6 %fusion.25 = (f32[768]{0:T(1024)}, bf16[512,768]{1,0:T(8,128)(2,1)}, f32[512]{0:T(512)S(1)}, f32[512,768]{1,0:T(8,128)S(1)}) fusion(bf16[512,768]{1,0:T(8,128)(2,1)} %collective-permute-done.34, f32[512,768]{1,0:T(8,128)S(1)} %copy-done.28, f32[768]{0:T(1024)S(1)} %copy-done.85, f32[512]{0:T(512)S(1)} %multiply_multiply_fusion.4, ...), kind=kOutput, calls=%fused_computation.56 | convolution fusion | flops 2435185408 | bytes 17318912 | tf_op jit(solution)/shard_map/hfk,hdk->fd/dot_general | solution.py:429
  256.8 7.7 %shard_map.330 = (bf16[512,768]{1,0:T(8,128)(2,1)S(1)}, bf16[2,256,768]{2,1,0:T(8,128)(2,1)S(1)}) custom-call(bf16[512,768]{1,0:T(8,128)(2,1)S(1)} %copy-done.2, bf16[512,768]{1,0:T(8,128)(2,1)S(1)} %get-tuple-element.31.refs_1_, bf16[512,768]{1,0:T(8,128)(2,1)S(1)} %convolution_convert_fusion.9.refs_2_, f32[6,2,512]{2,1,0:T(2,128)S(1)} %get-tuple-element.32.refs_3_, ...), custom_call_target="tpu_custom_call" | custom-call | flops 4026531840 | bytes 4718592 | tf_op jit(solution)/shard_map/pallas_call | solution.py:299
  274.5 7.4 %collective-permute-start.33 = (bf16[512,768]{1,0:T(8,128)(2,1)}, bf16[512,768]{1,0:T(8,128)(2,1)}, u32[]{:S(2)}, u32[]{:S(2)}) collective-permute-start(bf16[512,768]{1,0:T(8,128)(2,1)} %get-tuple-element.106), channel_id=1, source_target_pairs={{0,0},{1,2},{2,1},{3,3},{4,4},{5,6},{6,5},{7,7},{8,8},{9,10},{10,9... | collective-permute-start | bytes 2359304 | tf_op jit(solution)/shard_map/ppermute | solution.py:143
  281.9 21.5 %shard_map.331 = (bf16[512,768]{1,0:T(8,128)(2,1)S(1)}, bf16[2,512,768]{2,1,0:T(8,128)(2,1)S(1)}, bf16[2,512,768]{2,1,0:T(8,128)(2,1)}) custom-call(bf16[512,768]{1,0:T(8,128)(2,1)S(1)} %copy-done.6, bf16[512,768]{1,0:T(8,128)(2,1)S(1)} %get-tuple-element.30.refs_1_, bf16[512,768]{1,0:T(8,128)(2,1)S(1)} %convolution_convert_fusion.8.refs_2_, ...), custom_call_target="tpu_custom_call" | custom-call | flops 16106127360 | bytes 9437184 | tf_op jit(solution)/shard_map/pallas_call | solution.py:299
  306.1 4.3 copy.87
  314.8 4.3 copy.90
  326.7 4.6 copy.92
  334.6 8.5 %convolution_convert_fusion = bf16[2,1536,768]{1,2,0:T(8,128)(2,1)} fusion(bf16[512,768]{1,0:T(8,128)(2,1)} %collective-permute-done.34, f32[768]{0:T(1024)S(1)} %copy-done.86, f32[2,1536,512]{2,1,0:T(8,128)} %copy-done.96), kind=kOutput, calls=%fused_computation.17 | convolution fusion | flops 2433613824 | bytes 11799552 | tf_op jit(solution)/shard_map/fd,hfk->hdk/dot_general | solution.py:434
  343.2 4.9 convolution_convert_fusion.1
  348.1 8.2 %maximum_bitcast_fusion = bf16[16,2,2,48,1536]{4,3,0,1,2:T(8,128)(2,1)} fusion(bf16[1,2,16,48,1536]{4,3,2,1,0:T(8,128)(2,1)} %bitcast.242, bf16[1,2,16,48,1536]{4,3,2,1,0:T(8,128)(2,1)} %bitcast.243), kind=kLoop, calls=%fused_computation | loop fusion | flops 4718592 | bytes 18874368 | tf_op jit(solution)/shard_map/transpose | solution.py:445
  356.4 8.2 %copy.97 = bf16[16,2,2,48,1536]{4,3,2,1,0:T(8,128)(2,1)} copy(bf16[16,2,2,48,1536]{4,3,0,1,2:T(8,128)(2,1)} %maximum_bitcast_fusion) | data formatting | bytes 18874368 | tf_op jit(solution)/shard_map/transpose | solution.py:445
  382.3 7.5 %collective-permute-start.36 = (bf16[512,768]{1,0:T(8,128)(2,1)}, bf16[512,768]{1,0:T(8,128)(2,1)}, u32[]{:S(2)}, u32[]{:S(2)}) collective-permute-start(bf16[512,768]{1,0:T(8,128)(2,1)} %add_convert_fusion.6), channel_id=1, source_target_pairs={{0,0},{1,2},{2,1},{3,3},{4,4},{5,6},{6,5},{7,7},{8,8},{9,10},{10,9... | collective-permute-start | bytes 2359304 | tf_op jit(solution)/shard_map/ppermute | solution.py:143
  395.9 3.8 copy.89
  399.7 5.6 reshape_reshape.20
  420.2 7.6 %collective-permute-done.41 = f32[2,2,2,1,4608]{4,3,2,1,0:T(1,128)S(1)} collective-permute-done((f32[2,2,2,1,4608]{4,3,2,1,0:T(1,128)S(1)}, f32[2,2,2,1,4608]{4,3,2,1,0:T(1,128)S(1)}, u32[]{:S(2)}, u32[]{:S(2)}) %collective-permute-start.41) | collective-permute-done | bytes 147488 | tf_op jit(solution)/shard_map/ppermute | solution.py:78
  435.6 19.2 %collective-permute-done.44 = bf16[2,2,1,1,1,24,1536]{6,5,4,3,2,1,0:T(8,128)(2,1)} collective-permute-done((bf16[2,2,1,1,1,24,1536]{6,5,4,3,2,1,0:T(8,128)(2,1)}, bf16[2,2,1,1,1,24,1536]{6,5,4,3,2,1,0:T(8,128)(2,1)}, u32[]{:S(2)}, u32[]{:S(2)}) %collective-permute-start.44) | collective-permute-done | bytes 294944 | tf_op jit(solution)/shard_map/ppermute | solution.py:78
  455.9 9.5 %collective-permute-done.54 = bf16[2,2,1,1,1,24,1536]{6,5,4,3,2,1,0:T(8,128)(2,1)S(1)} collective-permute-done((bf16[2,2,1,1,1,24,1536]{6,5,4,3,2,1,0:T(8,128)(2,1)}, bf16[2,2,1,1,1,24,1536]{6,5,4,3,2,1,0:T(8,128)(2,1)S(1)}, u32[]{:S(2)}, u32[]{:S(2)}) %collective-permute-start.54) | collective-permute-done | bytes 294944 | tf_op jit(solution)/shard_map/ppermute | solution.py:78
  465.6 9.4 %collective-permute-done.45 = bf16[1,2,1,1,1,24,1536]{6,5,4,3,2,1,0:T(8,128)(2,1)S(1)} collective-permute-done((bf16[1,2,1,1,1,24,1536]{6,5,4,3,2,1,0:T(8,128)(2,1)S(1)}, bf16[1,2,1,1,1,24,1536]{6,5,4,3,2,1,0:T(8,128)(2,1)S(1)}, u32[]{:S(2)}, u32[]{:S(2)}) %collective-permute-start.45) | collective-permute-done | bytes 147488 | tf_op jit(solution)/shard_map/ppermute | solution.py:78
  475.1 16.7 %collective-permute-done.55 = bf16[1,2,1,1,1,24,1536]{6,5,4,3,2,1,0:T(8,128)(2,1)S(1)} collective-permute-done((bf16[1,2,1,1,1,24,1536]{6,5,4,3,2,1,0:T(8,128)(2,1)S(1)}, bf16[1,2,1,1,1,24,1536]{6,5,4,3,2,1,0:T(8,128)(2,1)S(1)}, u32[]{:S(2)}, u32[]{:S(2)}) %collective-permute-start.55) | collective-permute-done | bytes 147488 | tf_op jit(solution)/shard_map/ppermute | solution.py:78
  491.8 5.1 collective-permute-done.46
  501.4 9.9 %collective-permute-done.59 = bf16[1,2,2,1,1,64,768]{6,5,4,3,2,1,0:T(8,128)(2,1)S(1)} collective-permute-done((bf16[1,2,2,1,1,64,768]{6,5,4,3,2,1,0:T(8,128)(2,1)S(1)}, bf16[1,2,2,1,1,64,768]{6,5,4,3,2,1,0:T(8,128)(2,1)S(1)}, u32[]{:S(2)}, u32[]{:S(2)}) %collective-permute-start.59) | collective-permute-done | bytes 393248 | tf_op jit(solution)/shard_map/ppermute | solution.py:78
  512.9 4.3 collective-permute-done.48
  519.3 3.7 collective-permute-done.60
  528.0 6.7 %collective-permute-done.50 = bf16[1,2,1,1,1,24,1536]{6,5,4,3,2,1,0:T(8,128)(2,1)S(1)} collective-permute-done((bf16[1,2,1,1,1,24,1536]{6,5,4,3,2,1,0:T(8,128)(2,1)S(1)}, bf16[1,2,1,1,1,24,1536]{6,5,4,3,2,1,0:T(8,128)(2,1)S(1)}, u32[]{:S(2)}, u32[]{:S(2)}) %collective-permute-start.50) | collective-permute-done | bytes 147488 | tf_op jit(solution)/shard_map/ppermute | solution.py:78
  535.1 4.0 collective-permute-done.51
  542.2 5.1 concatenate.160
  558.1 4.6 collective-permute-done.65
  562.8 5.9 collective-permute-done.66
  583.4 5.3 stack.79
  600.5 4.4 collective-permute-done.71
  (590 shorter events, 250.5 us)
Async XLA Ops:
  7.2 212.1 %all-gather.3.cloned.1.call-start = ((), (), s32[]{:S(2)}) async-start(), calls=%async_computation.2 | async-start | bytes 9732096 | tf_op jit(solution)/shard_map/all_gather | solution.py:355
  7.2 225.9 %collective-permute-start.34 = (bf16[512,768]{1,0:T(8,128)(2,1)}, bf16[512,768]{1,0:T(8,128)(2,1)}, u32[]{:S(2)}, u32[]{:S(2)}) collective-permute-start(bf16[512,768]{1,0:T(8,128)(2,1)} %bitcast.253), channel_id=1, source_target_pairs={{0,0},{1,2},{2,1},{3,3},{4,4},{5,6},{6,5},{7,7},{8,8},{9,10},{10,9... | collective-permute-start | bytes 2359304 | tf_op jit(solution)/shard_map/ppermute | solution.py:143
  15.6 16.7 %collective-permute-start.1 = (s32[16]{0:T(128)S(1)}, s32[16]{0:T(128)S(1)}, u32[]{:S(2)}, u32[]{:S(2)}) collective-permute-start(s32[16]{0:T(128)S(1)} %dynamic_update_slice.38), channel_id=1, source_target_pairs={{0,2},{2,0},{4,6},{6,4},{8,10},{10,8},{12,14},{14,12},{16,18},{18,... | collective-permute-start | bytes 200 | tf_op jit(solution)/shard_map/ppermute | solution.py:78
  15.6 126.8 %collective-permute-start = (bf16[512,768]{1,0:T(8,128)(2,1)}, bf16[512,768]{1,0:T(8,128)(2,1)S(1)}, u32[]{:S(2)}, u32[]{:S(2)}) collective-permute-start(bf16[512,768]{1,0:T(8,128)(2,1)} %bitcast.252), channel_id=1, source_target_pairs={{0,0},{1,2},{2,1},{3,3},{4,4},{5,6},{6,5},{7,7},{8,8},{9,10},{10,9... | collective-permute-start | bytes 2359304 | tf_op jit(solution)/shard_map/ppermute | solution.py:143
  20.7 27.4 %collective-permute-start.10 = (bf16[1,1,1,1,1,24,1536]{6,5,4,3,2,1,0:T(8,128)(2,1)S(1)}, bf16[1,1,1,1,1,24,1536]{6,5,4,3,2,1,0:T(8,128)(2,1)S(1)}, u32[]{:S(2)}, u32[]{:S(2)}) collective-permute-start(bf16[1,1,1,1,1,24,1536]{6,5,4,3,2,1,0:T(8,128)(2,1)S(1)} %pad_maximum_fusion.26), channel_id=1, source_target_pairs={{0,8},{2,10},{4,12},{6,14},{8,0},{10,2},{12,4},{14,6},{16,24},{18,... | collective-permute-start | bytes 221192 | tf_op jit(solution)/shard_map/ppermute | solution.py:78
  27.0 21.4 %collective-permute-start.22 = (bf16[1,1,1,1,1,24,1536]{6,5,4,3,2,1,0:T(8,128)(2,1)S(1)}, bf16[1,1,1,1,1,24,1536]{6,5,4,3,2,1,0:T(8,128)(2,1)S(1)}, u32[]{:S(2)}, u32[]{:S(2)}) collective-permute-start(bf16[1,1,1,1,1,24,1536]{6,5,4,3,2,1,0:T(8,128)(2,1)S(1)} %pad_maximum_fusion.27), channel_id=1, source_target_pairs={{0,8},{2,10},{4,12},{6,14},{8,0},{10,2},{12,4},{14,6},{16,24},{18,... | collective-permute-start | bytes 221192 | tf_op jit(solution)/shard_map/ppermute | solution.py:78
  29.6 509.9 %reduce-scatter.2.cloned.1.call-start = ((), (), s32[]{:S(2)}) async-start(), calls=%async_computation.1 | async-start | bytes 9732096 | tf_op jit(solution)/shard_map/reduce_scatter | solution.py:444
  46.1 6.4 %collective-permute-start.15 = (bf16[1,1,1,1,1,24,1536]{6,5,4,3,2,1,0:T(8,128)(2,1)S(1)}, bf16[1,1,1,1,1,24,1536]{6,5,4,3,2,1,0:T(8,128)(2,1)S(1)}, u32[]{:S(2)}, u32[]{:S(2)}) collective-permute-start(bf16[1,1,1,1,1,24,1536]{6,5,4,3,2,1,0:T(8,128)(2,1)S(1)} %slice_bitcast_fusion), channel_id=1, source_target_pairs={{0,8},{2,10},{4,12},{6,14},{8,0},{10,2},{12,4},{14,6},{16,24},{18,... | collective-permute-start | bytes 221192 | tf_op jit(solution)/shard_map/ppermute | solution.py:78
  48.2 7.9 %collective-permute-start.27 = (bf16[1,1,1,1,1,64,768]{6,5,4,3,2,1,0:T(8,128)(2,1)S(1)}, bf16[1,1,1,1,1,64,768]{6,5,4,3,2,1,0:T(8,128)(2,1)S(1)}, u32[]{:S(2)}, u32[]{:S(2)}) collective-permute-start(bf16[1,1,1,1,1,64,768]{6,5,4,3,2,1,0:T(8,128)(2,1)S(1)} %reshape_reshape.18), channel_id=1, source_target_pairs={{0,8},{2,10},{4,12},{6,14},{8,0},{10,2},{12,4},{14,6},{16,24},{18,... | collective-permute-start | bytes 294920 | tf_op jit(solution)/shard_map/ppermute | solution.py:78
  48.4 140.7 %collective-permute-start.32 = (bf16[256,1024]{1,0:T(8,128)(2,1)}, bf16[256,1024]{1,0:T(8,128)(2,1)}, u32[]{:S(2)}, u32[]{:S(2)}) collective-permute-start(bf16[256,1024]{1,0:T(8,128)(2,1)} %bitcast.13), channel_id=1, source_target_pairs={{0,2},{3,1},{4,6},{7,5},{8,10},{11,9},{12,14},{15,13},{16,18},{19,... | collective-permute-start | bytes 1572872 | tf_op jit(solution)/shard_map/ppermute | solution.py:152
  52.6 6.6 %collective-permute-start.5 = (f32[8,1,4608]{2,1,0:T(1,128)S(1)}, f32[8,1,4608]{2,1,0:T(1,128)S(1)}, u32[]{:S(2)}, u32[]{:S(2)}) collective-permute-start(f32[8,1,4608]{2,1,0:T(1,128)S(1)} %constant_dynamic-slice_fusion.24), channel_id=1, source_target_pairs={{0,1},{1,0},{2,3},{3,2},{4,5},{5,4},{6,7},{7,6},{8,9},{9,8},{10,11... | collective-permute-start | bytes 442376 | tf_op jit(solution)/shard_map/ppermute | solution.py:78
  56.1 20.0 %collective-permute-start.23 = (bf16[1,2,1,1,1,24,1536]{6,5,4,3,2,1,0:T(8,128)(2,1)S(1)}, bf16[1,2,1,1,1,24,1536]{6,5,4,3,2,1,0:T(8,128)(2,1)S(1)}, u32[]{:S(2)}, u32[]{:S(2)}) collective-permute-start(bf16[1,2,1,1,1,24,1536]{6,5,4,3,2,1,0:T(8,128)(2,1)S(1)} %pad_maximum_fusion.24), channel_id=1, source_target_pairs={{0,16},{2,18},{4,20},{6,22},{8,24},{10,26},{12,28},{14,30},{16,0},... | collective-permute-start | bytes 442376 | tf_op jit(solution)/shard_map/ppermute | solution.py:78
  59.2 29.0 %collective-permute-start.16 = (bf16[1,2,1,1,1,24,1536]{6,5,4,3,2,1,0:T(8,128)(2,1)S(1)}, bf16[1,2,1,1,1,24,1536]{6,5,4,3,2,1,0:T(8,128)(2,1)S(1)}, u32[]{:S(2)}, u32[]{:S(2)}) collective-permute-start(bf16[1,2,1,1,1,24,1536]{6,5,4,3,2,1,0:T(8,128)(2,1)S(1)} %pad_maximum_fusion.23), channel_id=1, source_target_pairs={{0,16},{2,18},{4,20},{6,22},{8,24},{10,26},{12,28},{14,30},{16,0},... | collective-permute-start | bytes 442376 | tf_op jit(solution)/shard_map/ppermute | solution.py:78
  76.1 15.2 %collective-permute-start.11 = (bf16[1,2,1,1,1,24,1536]{6,5,4,3,2,1,0:T(8,128)(2,1)S(1)}, bf16[1,2,1,1,1,24,1536]{6,5,4,3,2,1,0:T(8,128)(2,1)S(1)}, u32[]{:S(2)}, u32[]{:S(2)}) collective-permute-start(bf16[1,2,1,1,1,24,1536]{6,5,4,3,2,1,0:T(8,128)(2,1)S(1)} %pad_maximum_fusion.22), channel_id=1, source_target_pairs={{0,16},{2,18},{4,20},{6,22},{8,24},{10,26},{12,28},{14,30},{16,0},... | collective-permute-start | bytes 442376 | tf_op jit(solution)/shard_map/ppermute | solution.py:78
  88.2 23.2 %collective-permute-start.28 = (bf16[1,1,2,1,1,64,768]{6,5,4,3,2,1,0:T(8,128)(2,1)S(1)}, bf16[1,1,2,1,1,64,768]{6,5,4,3,2,1,0:T(8,128)(2,1)S(1)}, u32[]{:S(2)}, u32[]{:S(2)}) collective-permute-start(bf16[1,1,2,1,1,64,768]{6,5,4,3,2,1,0:T(8,128)(2,1)S(1)} %pad_maximum_fusion.21), channel_id=1, source_target_pairs={{0,16},{2,18},{4,20},{6,22},{8,24},{10,26},{12,28},{14,30},{16,0},... | collective-permute-start | bytes 589832 | tf_op jit(solution)/shard_map/ppermute | solution.py:78
  96.1 8.0 %collective-permute-start.7 = (f32[2,1,4608]{2,1,0:T(1,128)S(1)}, f32[2,1,4608]{2,1,0:T(1,128)S(1)}, u32[]{:S(2)}, u32[]{:S(2)}) collective-permute-start(f32[2,1,4608]{2,1,0:T(1,128)S(1)} %constant_dynamic-slice_fusion.22), channel_id=1, source_target_pairs={{0,8},{2,10},{4,12},{6,14},{8,0},{10,2},{12,4},{14,6},{16,24},{18,... | collective-permute-start | bytes 110600 | tf_op jit(solution)/shard_map/ppermute | solution.py:78
  109.7 12.3 %collective-permute-start.12 = (bf16[2,2,1,1,1,24,1536]{6,5,4,3,2,1,0:T(8,128)(2,1)S(1)}, bf16[2,2,1,1,1,24,1536]{6,5,4,3,2,1,0:T(8,128)(2,1)S(1)}, u32[]{:S(2)}, u32[]{:S(2)}) collective-permute-start(bf16[2,2,1,1,1,24,1536]{6,5,4,3,2,1,0:T(8,128)(2,1)S(1)} %pad_maximum_fusion.15), channel_id=1, source_target_pairs={{0,4},{2,6},{4,0},{6,2},{8,12},{10,14},{12,8},{14,10},{16,20},{18,... | collective-permute-start | bytes 884744 | tf_op jit(solution)/shard_map/ppermute | solution.py:78
  112.7 18.1 %collective-permute-start.17 = (bf16[2,2,1,1,1,24,1536]{6,5,4,3,2,1,0:T(8,128)(2,1)S(1)}, bf16[2,2,1,1,1,24,1536]{6,5,4,3,2,1,0:T(8,128)(2,1)S(1)}, u32[]{:S(2)}, u32[]{:S(2)}) collective-permute-start(bf16[2,2,1,1,1,24,1536]{6,5,4,3,2,1,0:T(8,128)(2,1)S(1)} %pad_maximum_fusion.16), channel_id=1, source_target_pairs={{0,1},{1,0},{2,3},{3,2},{4,5},{5,4},{6,7},{7,6},{8,9},{9,8},{10,11... | collective-permute-start | bytes 884744 | tf_op jit(solution)/shard_map/ppermute | solution.py:78
  122.0 8.0 %collective-permute-start.24 = (bf16[2,2,1,1,1,24,1536]{6,5,4,3,2,1,0:T(8,128)(2,1)S(1)}, bf16[2,2,1,1,1,24,1536]{6,5,4,3,2,1,0:T(8,128)(2,1)S(1)}, u32[]{:S(2)}, u32[]{:S(2)}) collective-permute-start(bf16[2,2,1,1,1,24,1536]{6,5,4,3,2,1,0:T(8,128)(2,1)S(1)} %pad_maximum_fusion.17), channel_id=1, source_target_pairs={{0,4},{2,6},{4,0},{6,2},{8,12},{10,14},{12,8},{14,10},{16,20},{18,... | collective-permute-start | bytes 884744 | tf_op jit(solution)/shard_map/ppermute | solution.py:78
  129.9 12.1 %collective-permute-start.29 = (bf16[1,2,2,1,1,64,768]{6,5,4,3,2,1,0:T(8,128)(2,1)S(1)}, bf16[1,2,2,1,1,64,768]{6,5,4,3,2,1,0:T(8,128)(2,1)S(1)}, u32[]{:S(2)}, u32[]{:S(2)}) collective-permute-start(bf16[1,2,2,1,1,64,768]{6,5,4,3,2,1,0:T(8,128)(2,1)S(1)} %pad_maximum_fusion.14), channel_id=1, source_target_pairs={{0,1},{1,0},{2,3},{3,2},{4,5},{5,4},{6,7},{7,6},{8,9},{9,8},{10,11... | collective-permute-start | bytes 1179656 | tf_op jit(solution)/shard_map/ppermute | solution.py:78
  130.7 23.9 %collective-permute-start.13 = (bf16[2,2,2,1,1,24,1536]{6,5,4,3,2,1,0:T(8,128)(2,1)S(1)}, bf16[2,2,2,1,1,24,1536]{6,5,4,3,2,1,0:T(8,128)(2,1)S(1)}, u32[]{:S(2)}, u32[]{:S(2)}) collective-permute-start(bf16[2,2,2,1,1,24,1536]{6,5,4,3,2,1,0:T(8,128)(2,1)S(1)} %pad_maximum_fusion.11), channel_id=1, source_target_pairs={{0,1},{1,0},{2,3},{3,2},{4,5},{5,4},{6,7},{7,6},{8,9},{9,8},{10,11... | collective-permute-start | bytes 1769480 | tf_op jit(solution)/shard_map/ppermute | solution.py:78
  142.0 13.2 %collective-permute-start.18 = (bf16[2,2,1,1,2,24,1536]{6,5,4,3,2,1,0:T(8,128)(2,1)S(1)}, bf16[2,2,1,1,2,24,1536]{6,5,4,3,2,1,0:T(8,128)(2,1)S(1)}, u32[]{:S(2)}, u32[]{:S(2)}) collective-permute-start(bf16[2,2,1,1,2,24,1536]{6,5,4,3,2,1,0:T(8,128)(2,1)S(1)} %pad_maximum_fusion.12), channel_id=1, source_target_pairs={{0,4},{2,6},{4,0},{6,2},{8,12},{10,14},{12,8},{14,10},{16,20},{18,... | collective-permute-start | bytes 1769480 | tf_op jit(solution)/shard_map/ppermute | solution.py:78
  142.4 22.0 %collective-permute-start.25 = (bf16[2,2,2,1,1,24,1536]{6,5,4,3,2,1,0:T(8,128)(2,1)S(1)}, bf16[2,2,2,1,1,24,1536]{6,5,4,3,2,1,0:T(8,128)(2,1)S(1)}, u32[]{:S(2)}, u32[]{:S(2)}) collective-permute-start(bf16[2,2,2,1,1,24,1536]{6,5,4,3,2,1,0:T(8,128)(2,1)S(1)} %pad_maximum_fusion.13), channel_id=1, source_target_pairs={{0,1},{1,0},{2,3},{3,2},{4,5},{5,4},{6,7},{7,6},{8,9},{9,8},{10,11... | collective-permute-start | bytes 1769480 | tf_op jit(solution)/shard_map/ppermute | solution.py:78
  154.6 14.1 %collective-permute-start.30 = (bf16[2,2,2,1,1,64,768]{6,5,4,3,2,1,0:T(8,128)(2,1)S(1)}, bf16[2,2,2,1,1,64,768]{6,5,4,3,2,1,0:T(8,128)(2,1)S(1)}, u32[]{:S(2)}, u32[]{:S(2)}) collective-permute-start(bf16[2,2,2,1,1,64,768]{6,5,4,3,2,1,0:T(8,128)(2,1)S(1)} %pad_maximum_fusion.10), channel_id=1, source_target_pairs={{0,4},{2,6},{4,0},{6,2},{8,12},{10,14},{12,8},{14,10},{16,20},{18,... | collective-permute-start | bytes 2359304 | tf_op jit(solution)/shard_map/ppermute | solution.py:78
  155.2 17.5 %collective-permute-start.14 = (bf16[2,2,2,1,2,24,1536]{6,5,4,3,2,1,0:T(8,128)(2,1)S(1)}, bf16[2,2,2,1,2,24,1536]{6,5,4,3,2,1,0:T(8,128)(2,1)S(1)}, u32[]{:S(2)}, u32[]{:S(2)}) collective-permute-start(bf16[2,2,2,1,2,24,1536]{6,5,4,3,2,1,0:T(8,128)(2,1)S(1)} %pad_maximum_fusion.7), channel_id=1, source_target_pairs={{0,2},{2,0},{4,6},{6,4},{8,10},{10,8},{12,14},{14,12},{16,18},{18,... | collective-permute-start | bytes 3538952 | tf_op jit(solution)/shard_map/ppermute | solution.py:78
  170.3 16.9 %collective-permute-start.31 = (bf16[2,2,2,2,1,64,768]{6,5,4,3,2,1,0:T(8,128)(2,1)}, bf16[2,2,2,2,1,64,768]{6,5,4,3,2,1,0:T(8,128)(2,1)}, u32[]{:S(2)}, u32[]{:S(2)}) collective-permute-start(bf16[2,2,2,2,1,64,768]{6,5,4,3,2,1,0:T(8,128)(2,1)} %pad_maximum_fusion.6), channel_id=1, source_target_pairs={{0,2},{2,0},{4,6},{6,4},{8,10},{10,8},{12,14},{14,12},{16,18},{18,... | collective-permute-start | bytes 4718600 | tf_op jit(solution)/shard_map/ppermute | solution.py:78
  172.7 20.1 %collective-permute-start.21 = (bf16[512,1536]{1,0:T(8,128)(2,1)S(1)}, bf16[512,1536]{1,0:T(8,128)(2,1)}, u32[]{:S(2)}, u32[]{:S(2)}) collective-permute-start(bf16[512,1536]{1,0:T(8,128)(2,1)S(1)} %convolution_convert_fusion.2.refs_1_.refs_2_.refs_4_.refs_5_), channel_id=1, source_target_pairs={{0,2},{2,0},{4,6},{6,4},{8,10},{10,8},{12,14},{14,12},{16,18},{18,... | collective-permute-start | bytes 4718600 | tf_op jit(solution)/shard_map/ppermute | solution.py:78
  274.5 288.3 %collective-permute-start.33 = (bf16[512,768]{1,0:T(8,128)(2,1)}, bf16[512,768]{1,0:T(8,128)(2,1)}, u32[]{:S(2)}, u32[]{:S(2)}) collective-permute-start(bf16[512,768]{1,0:T(8,128)(2,1)} %get-tuple-element.106), channel_id=1, source_target_pairs={{0,0},{1,2},{2,1},{3,3},{4,4},{5,6},{6,5},{7,7},{8,8},{9,10},{10,9... | collective-permute-start | bytes 2359304 | tf_op jit(solution)/shard_map/ppermute | solution.py:143
  303.4 68.8 %collective-permute-start.35 = (bf16[2,512,768]{2,1,0:T(8,128)(2,1)}, bf16[2,512,768]{2,1,0:T(8,128)(2,1)}, u32[]{:S(2)}, u32[]{:S(2)}) collective-permute-start(bf16[2,512,768]{2,1,0:T(8,128)(2,1)} %get-tuple-element.37), channel_id=1, source_target_pairs={{0,2},{2,0},{4,6},{6,4},{8,10},{10,8},{12,14},{14,12},{16,18},{18,... | collective-permute-start | bytes 4718600 | tf_op jit(solution)/shard_map/ppermute | solution.py:78
  312.9 51.7 %collective-permute-start.42 = (bf16[2,2,2,1,2,24,1536]{6,5,4,3,2,1,0:T(8,128)(2,1)}, bf16[2,2,2,1,2,24,1536]{6,5,4,3,2,1,0:T(8,128)(2,1)}, u32[]{:S(2)}, u32[]{:S(2)}) collective-permute-start(bf16[2,2,2,1,2,24,1536]{6,5,4,3,2,1,0:T(8,128)(2,1)} %constant_dynamic-slice_fusion.20), channel_id=1, source_target_pairs={{0,2},{2,0},{4,6},{6,4},{8,10},{10,8},{12,14},{14,12},{16,18},{18,... | collective-permute-start | bytes 3538952 | tf_op jit(solution)/shard_map/ppermute | solution.py:78
  321.5 46.5 %collective-permute-start.52 = (bf16[2,2,2,1,2,24,1536]{6,5,4,3,2,1,0:T(8,128)(2,1)}, bf16[2,2,2,1,2,24,1536]{6,5,4,3,2,1,0:T(8,128)(2,1)}, u32[]{:S(2)}, u32[]{:S(2)}) collective-permute-start(bf16[2,2,2,1,2,24,1536]{6,5,4,3,2,1,0:T(8,128)(2,1)} %constant_dynamic-slice_fusion.10), channel_id=1, source_target_pairs={{0,2},{2,0},{4,6},{6,4},{8,10},{10,8},{12,14},{14,12},{16,18},{18,... | collective-permute-start | bytes 3538952 | tf_op jit(solution)/shard_map/ppermute | solution.py:78
  334.0 56.4 %collective-permute-start.57 = (bf16[2,2,2,2,1,64,768]{6,5,4,3,2,1,0:T(8,128)(2,1)}, bf16[2,2,2,2,1,64,768]{6,5,4,3,2,1,0:T(8,128)(2,1)}, u32[]{:S(2)}, u32[]{:S(2)}) collective-permute-start(bf16[2,2,2,2,1,64,768]{6,5,4,3,2,1,0:T(8,128)(2,1)} %constant_dynamic-slice_fusion.5), channel_id=1, source_target_pairs={{0,2},{2,0},{4,6},{6,4},{8,10},{10,8},{12,14},{14,12},{16,18},{18,... | collective-permute-start | bytes 4718600 | tf_op jit(solution)/shard_map/ppermute | solution.py:78
  367.6 48.1 %collective-permute-start.43 = (bf16[2,2,2,1,1,24,1536]{6,5,4,3,2,1,0:T(8,128)(2,1)}, bf16[2,2,2,1,1,24,1536]{6,5,4,3,2,1,0:T(8,128)(2,1)}, u32[]{:S(2)}, u32[]{:S(2)}) collective-permute-start(bf16[2,2,2,1,1,24,1536]{6,5,4,3,2,1,0:T(8,128)(2,1)} %constant_dynamic-slice_fusion.19), channel_id=1, source_target_pairs={{0,1},{1,0},{2,3},{3,2},{4,5},{5,4},{6,7},{7,6},{8,9},{9,8},{10,11... | collective-permute-start | bytes 1769480 | tf_op jit(solution)/shard_map/ppermute | solution.py:78
  370.9 47.3 %collective-permute-start.53 = (bf16[2,2,2,1,1,24,1536]{6,5,4,3,2,1,0:T(8,128)(2,1)}, bf16[2,2,2,1,1,24,1536]{6,5,4,3,2,1,0:T(8,128)(2,1)}, u32[]{:S(2)}, u32[]{:S(2)}) collective-permute-start(bf16[2,2,2,1,1,24,1536]{6,5,4,3,2,1,0:T(8,128)(2,1)} %constant_dynamic-slice_fusion.9), channel_id=1, source_target_pairs={{0,1},{1,0},{2,3},{3,2},{4,5},{5,4},{6,7},{7,6},{8,9},{9,8},{10,11... | collective-permute-start | bytes 1769480 | tf_op jit(solution)/shard_map/ppermute | solution.py:78
  382.3 180.5 %collective-permute-start.36 = (bf16[512,768]{1,0:T(8,128)(2,1)}, bf16[512,768]{1,0:T(8,128)(2,1)}, u32[]{:S(2)}, u32[]{:S(2)}) collective-permute-start(bf16[512,768]{1,0:T(8,128)(2,1)} %add_convert_fusion.6), channel_id=1, source_target_pairs={{0,0},{1,2},{2,1},{3,3},{4,4},{5,6},{6,5},{7,7},{8,8},{9,10},{10,9... | collective-permute-start | bytes 2359304 | tf_op jit(solution)/shard_map/ppermute | solution.py:143
  390.4 14.9 %collective-permute-start.38 = (f32[1,1,1,1,4608]{4,3,2,1,0:T(1,128)}, f32[1,1,1,1,4608]{4,3,2,1,0:T(1,128)}, u32[]{:S(2)}, u32[]{:S(2)}) collective-permute-start(f32[1,1,1,1,4608]{4,3,2,1,0:T(1,128)} %add_bitcast_fusion.3), channel_id=1, source_target_pairs={{0,16},{2,18},{4,20},{6,22},{8,24},{10,26},{12,28},{14,30},{16,0},... | collective-permute-start | bytes 55304 | tf_op jit(solution)/shard_map/ppermute | solution.py:78
  415.4 83.5 %collective-permute-start.47 = (bf16[2,2,2,1,2,24,1536]{6,5,4,3,2,1,0:T(8,128)(2,1)}, bf16[2,2,2,1,2,24,1536]{6,5,4,3,2,1,0:T(8,128)(2,1)}, u32[]{:S(2)}, u32[]{:S(2)}) collective-permute-start(bf16[2,2,2,1,2,24,1536]{6,5,4,3,2,1,0:T(8,128)(2,1)} %constant_dynamic-slice_fusion.15), channel_id=1, source_target_pairs={{0,2},{2,0},{4,6},{6,4},{8,10},{10,8},{12,14},{14,12},{16,18},{18,... | collective-permute-start | bytes 3538952 | tf_op jit(solution)/shard_map/ppermute | solution.py:78
  415.7 81.7 %collective-permute-start.58 = (bf16[2,2,2,1,1,64,768]{6,5,4,3,2,1,0:T(8,128)(2,1)}, bf16[2,2,2,1,1,64,768]{6,5,4,3,2,1,0:T(8,128)(2,1)}, u32[]{:S(2)}, u32[]{:S(2)}) collective-permute-start(bf16[2,2,2,1,1,64,768]{6,5,4,3,2,1,0:T(8,128)(2,1)} %constant_dynamic-slice_fusion.4), channel_id=1, source_target_pairs={{0,4},{2,6},{4,0},{6,2},{8,12},{10,14},{12,8},{14,10},{16,20},{18,... | collective-permute-start | bytes 2359304 | tf_op jit(solution)/shard_map/ppermute | solution.py:78
  418.2 9.6 %collective-permute-start.41 = (f32[2,2,2,1,4608]{4,3,2,1,0:T(1,128)S(1)}, f32[2,2,2,1,4608]{4,3,2,1,0:T(1,128)S(1)}, u32[]{:S(2)}, u32[]{:S(2)}) collective-permute-start(f32[2,2,2,1,4608]{4,3,2,1,0:T(1,128)S(1)} %pad_maximum_fusion.25), channel_id=1, source_target_pairs={{0,1},{1,0},{2,3},{3,2},{4,5},{5,4},{6,7},{7,6},{8,9},{9,8},{10,11... | collective-permute-start | bytes 442376 | tf_op jit(solution)/shard_map/ppermute | solution.py:78
  427.7 27.1 %collective-permute-start.44 = (bf16[2,2,1,1,1,24,1536]{6,5,4,3,2,1,0:T(8,128)(2,1)}, bf16[2,2,1,1,1,24,1536]{6,5,4,3,2,1,0:T(8,128)(2,1)}, u32[]{:S(2)}, u32[]{:S(2)}) collective-permute-start(bf16[2,2,1,1,1,24,1536]{6,5,4,3,2,1,0:T(8,128)(2,1)} %constant_dynamic-slice_fusion.18), channel_id=1, source_target_pairs={{0,4},{2,6},{4,0},{6,2},{8,12},{10,14},{12,8},{14,10},{16,20},{18,... | collective-permute-start | bytes 884744 | tf_op jit(solution)/shard_map/ppermute | solution.py:78
  454.8 10.6 %collective-permute-start.54 = (bf16[2,2,1,1,1,24,1536]{6,5,4,3,2,1,0:T(8,128)(2,1)}, bf16[2,2,1,1,1,24,1536]{6,5,4,3,2,1,0:T(8,128)(2,1)S(1)}, u32[]{:S(2)}, u32[]{:S(2)}) collective-permute-start(bf16[2,2,1,1,1,24,1536]{6,5,4,3,2,1,0:T(8,128)(2,1)} %constant_dynamic-slice_fusion.8), channel_id=1, source_target_pairs={{0,4},{2,6},{4,0},{6,2},{8,12},{10,14},{12,8},{14,10},{16,20},{18,... | collective-permute-start | bytes 884744 | tf_op jit(solution)/shard_map/ppermute | solution.py:78
  465.4 9.6 %collective-permute-start.45 = (bf16[1,2,1,1,1,24,1536]{6,5,4,3,2,1,0:T(8,128)(2,1)S(1)}, bf16[1,2,1,1,1,24,1536]{6,5,4,3,2,1,0:T(8,128)(2,1)S(1)}, u32[]{:S(2)}, u32[]{:S(2)}) collective-permute-start(bf16[1,2,1,1,1,24,1536]{6,5,4,3,2,1,0:T(8,128)(2,1)S(1)} %constant_dynamic-slice_fusion.17), channel_id=1, source_target_pairs={{0,16},{2,18},{4,20},{6,22},{8,24},{10,26},{12,28},{14,30},{16,0},... | collective-permute-start | bytes 442376 | tf_op jit(solution)/shard_map/ppermute | solution.py:78
  475.0 16.7 %collective-permute-start.55 = (bf16[1,2,1,1,1,24,1536]{6,5,4,3,2,1,0:T(8,128)(2,1)S(1)}, bf16[1,2,1,1,1,24,1536]{6,5,4,3,2,1,0:T(8,128)(2,1)S(1)}, u32[]{:S(2)}, u32[]{:S(2)}) collective-permute-start(bf16[1,2,1,1,1,24,1536]{6,5,4,3,2,1,0:T(8,128)(2,1)S(1)} %constant_dynamic-slice_fusion.7), channel_id=1, source_target_pairs={{0,16},{2,18},{4,20},{6,22},{8,24},{10,26},{12,28},{14,30},{16,0},... | collective-permute-start | bytes 442376 | tf_op jit(solution)/shard_map/ppermute | solution.py:78
  498.8 12.5 %collective-permute-start.59 = (bf16[1,2,2,1,1,64,768]{6,5,4,3,2,1,0:T(8,128)(2,1)S(1)}, bf16[1,2,2,1,1,64,768]{6,5,4,3,2,1,0:T(8,128)(2,1)S(1)}, u32[]{:S(2)}, u32[]{:S(2)}) collective-permute-start(bf16[1,2,2,1,1,64,768]{6,5,4,3,2,1,0:T(8,128)(2,1)S(1)} %constant_dynamic-slice_fusion.3), channel_id=1, source_target_pairs={{0,1},{1,0},{2,3},{3,2},{4,5},{5,4},{6,7},{7,6},{8,9},{9,8},{10,11... | collective-permute-start | bytes 1179656 | tf_op jit(solution)/shard_map/ppermute | solution.py:78
  500.6 16.7 %collective-permute-start.48 = (bf16[2,2,1,1,2,24,1536]{6,5,4,3,2,1,0:T(8,128)(2,1)S(1)}, bf16[2,2,1,1,2,24,1536]{6,5,4,3,2,1,0:T(8,128)(2,1)S(1)}, u32[]{:S(2)}, u32[]{:S(2)}) collective-permute-start(bf16[2,2,1,1,2,24,1536]{6,5,4,3,2,1,0:T(8,128)(2,1)S(1)} %constant_dynamic-slice_fusion.14), channel_id=1, source_target_pairs={{0,4},{2,6},{4,0},{6,2},{8,12},{10,14},{12,8},{14,10},{16,20},{18,... | collective-permute-start | bytes 1769480 | tf_op jit(solution)/shard_map/ppermute | solution.py:78
  511.4 11.6 %collective-permute-start.60 = (bf16[1,1,2,1,1,64,768]{6,5,4,3,2,1,0:T(8,128)(2,1)S(1)}, bf16[1,1,2,1,1,64,768]{6,5,4,3,2,1,0:T(8,128)(2,1)S(1)}, u32[]{:S(2)}, u32[]{:S(2)}) collective-permute-start(bf16[1,1,2,1,1,64,768]{6,5,4,3,2,1,0:T(8,128)(2,1)S(1)} %constant_dynamic-slice_fusion.2), channel_id=1, source_target_pairs={{0,16},{2,18},{4,20},{6,22},{8,24},{10,26},{12,28},{14,30},{16,0},... | collective-permute-start | bytes 589832 | tf_op jit(solution)/shard_map/ppermute | solution.py:78
  517.5 8.5 %collective-permute-start.49 = (bf16[2,2,1,1,1,24,1536]{6,5,4,3,2,1,0:T(8,128)(2,1)S(1)}, bf16[2,2,1,1,1,24,1536]{6,5,4,3,2,1,0:T(8,128)(2,1)S(1)}, u32[]{:S(2)}, u32[]{:S(2)}) collective-permute-start(bf16[2,2,1,1,1,24,1536]{6,5,4,3,2,1,0:T(8,128)(2,1)S(1)} %constant_dynamic-slice_fusion.13), channel_id=1, source_target_pairs={{0,1},{1,0},{2,3},{3,2},{4,5},{5,4},{6,7},{7,6},{8,9},{9,8},{10,11... | collective-permute-start | bytes 884744 | tf_op jit(solution)/shard_map/ppermute | solution.py:78
  526.1 8.6 %collective-permute-start.50 = (bf16[1,2,1,1,1,24,1536]{6,5,4,3,2,1,0:T(8,128)(2,1)S(1)}, bf16[1,2,1,1,1,24,1536]{6,5,4,3,2,1,0:T(8,128)(2,1)S(1)}, u32[]{:S(2)}, u32[]{:S(2)}) collective-permute-start(bf16[1,2,1,1,1,24,1536]{6,5,4,3,2,1,0:T(8,128)(2,1)S(1)} %constant_dynamic-slice_fusion.12), channel_id=1, source_target_pairs={{0,16},{2,18},{4,20},{6,22},{8,24},{10,26},{12,28},{14,30},{16,0},... | collective-permute-start | bytes 442376 | tf_op jit(solution)/shard_map/ppermute | solution.py:78
  (125 other events, 1435.0 us)
Sparse Core Ops, SparseCore 0:
  29.8 103.7 all-gather.2
  364.7 156.1 reduce-scatter.1

commit v2 on v1

v2 whole, which is shorter than its diff:
```python
import functools

import jax
import jax.numpy as jnp
from jax import lax
from jax.experimental import pallas as pl
from jax.experimental.pallas import tpu as pltpu
from jax.sharding import PartitionSpec as P

D = 768
FF = 3072
DT = 1024
HD = 64
HALF = FF // 2

PRECISE = lax.Precision.HIGHEST
FLOAT = jnp.float32
BFLOAT = jnp.bfloat16
EPS_NORM = 1e-06
EPS_FACTOR = 1e-30
CLIP_NORM = 1.0
CLIP_UPDATE = 0.25
DECAY_RATE = 0.5
RELATIVE_RATE = 4.0
SCALE_FLOOR = 0.001
SCORE_SCALE = 0.125
MASKED_SCORE = -1e30
ALL = ("dp", "head")
PAIR = 2 * HD
PAIRS = D // PAIR


def embed_part(steps, first, count):
    halfway = D // 2
    place = first + jnp.arange(count)
    freqs = jnp.exp(-jnp.log(10000.0) * (place % halfway).astype(FLOAT) / halfway)
    angles = steps.astype(FLOAT)[:, None] * freqs
    waves = jnp.where(place < halfway, jnp.cos(angles), jnp.sin(angles))
    return jax.nn.silu(waves).astype(BFLOAT)


def layer_norm(values):
    centered = values - jnp.mean(values, axis=-1, keepdims=True)
    variance = jnp.mean(centered * centered, axis=-1, keepdims=True)
    return centered * lax.rsqrt(variance + EPS_NORM)


def modulate(values, shift, scale):
    return layer_norm(values) * (1.0 + scale) + shift


def core_link():
    return ("dp", 1)


def row_link():
    return ("head", 1)


def far_links():
    masks, mask = [], 2
    while mask < lax.axis_size("dp"):
        masks.append(mask)
        mask = mask * 2
    return [("dp", mask) for mask in masks]


def dp_bits():
    return lax.axis_size("dp").bit_length() - 1


def bit_of(link):
    return (lax.axis_index(link[0]) // link[1]) % 2


def cross(values, link):
    pairs = [(place, place ^ link[1]) for place in range(lax.axis_size(link[0]))]
    return lax.ppermute(values, link[0], pairs)


def dim_of(link, head):
    if link[0] == "head":
        return {"first": 0, "last": dp_bits(), "columns": dp_bits() + 1}[head]
    return (1 if head == "first" else 0) + dp_bits() - link[1].bit_length()


def leading(head):
    return dp_bits() + (0 if head == "columns" else 1)


def grow(block, link, head):
    other = cross(block, link)
    upper = bit_of(link) == 1
    low = jnp.where(upper, other, block)
    high = jnp.where(upper, block, other)
    return jnp.concatenate([low, high], axis=dim_of(link, head))


def shrink(block, link, head, kind=BFLOAT):
    dim, bit = dim_of(link, head), bit_of(link)
    half = block.shape[dim] // 2
    kept = lax.dynamic_slice_in_dim(block, bit * half, half, axis=dim)
    sent = lax.dynamic_slice_in_dim(block, (1 - bit) * half, half, axis=dim)
    return (kept.astype(FLOAT) + cross(sent.astype(BFLOAT), link).astype(FLOAT)).astype(kind)


class Chain:
    def __init__(self, state, steps):
        self.state, self.steps = state, list(steps)

    def advance(self, count=1):
        for _ in range(min(count, len(self.steps))):
            self.state = self.steps.pop(0)(self.state)
        return self

    def finish(self):
        return self.advance(len(self.steps)).state


def tie(chains, *values):
    states, values = lax.optimization_barrier(([chain.state for chain in chains], values))
    for chain, state in zip(chains, states):
        chain.state = state
    return values


def gather_chain(shard, head, row_early):
    block = shard.reshape((1,) * leading(head) + shard.shape)
    far = far_links()
    plane = [row_link(), far[0]] if row_early else [far[0], row_link()]
    links = far[1:] + plane + [core_link()]
    return Chain(block, [lambda state, link=link: grow(state, link, head) for link in links])


def scatter_chain(matrix, head, row_early):
    bits = leading(head)
    rows, columns = matrix.shape[-2:]
    split = dp_bits() if head == "first" else bits
    block = matrix.reshape((2,) * bits + (rows // 2**split, columns))
    far = far_links()
    plane = [far[0], row_link()] if row_early else [row_link(), far[0]]
    order = [core_link()] + plane + far[:0:-1]
    kinds = [BFLOAT] * (len(order) - 1) + [FLOAT]
    steps = [
        lambda state, link=link, kind=kind: shrink(state, link, head, kind)
        for link, kind in zip(order, kinds)
    ]
    return Chain(block, steps + [lambda state: state.reshape(state.shape[bits:])])


def sum_all(values):
    for link in [core_link(), row_link()] + far_links():
        values = values + cross(values, link)
    return values


def on_own_chip():
    return bit_of(core_link()) == bit_of(row_link())


def swap_place(values):
    pairs = []
    for place in range(lax.axis_size("dp")):
        for head in range(2):
            if place & 1 != head:
                pairs.append((place * 2 + head, ((place & ~1) | head) * 2 + (place & 1)))
    return jnp.where(on_own_chip(), values, lax.ppermute(values, ALL, pairs))


def from_clip_core(values):
    pairs = []
    for place in range(0, lax.axis_size("dp"), 2):
        for head in range(2):
            pairs.append(((place + head) * 2 + head, (place + 1 - head) * 2 + head))
    return jnp.where(on_own_chip(), values, lax.ppermute(values, ALL, pairs))


def nt(left, right):
    return lax.dot_general(left, right, (((1,), (1,)), ((), ())), preferred_element_type=FLOAT)


def nn(left, right):
    return lax.dot_general(left, right, (((1,), (0,)), ((), ())), preferred_element_type=FLOAT)


def lanes_of(length):
    return lax.broadcasted_iota(jnp.int32, (length, PAIR), 1)


def with_spare(pair, head, spare):
    lane = lanes_of(pair.shape[0])
    rest = jnp.where(lane == HD * (1 - head), spare, jnp.zeros_like(pair))
    return jnp.where(lane // HD == head, pair, rest)


def attend_kernel(blocks, *refs):
    query_ref = refs[0]
    key_refs, value_refs, bias_refs = refs[1 : 1 + 3 * blocks : 3], refs[2 : 2 + 3 * blocks : 3], refs[3 : 3 + 3 * blocks : 3]
    out_ref, log_ref = refs[1 + 3 * blocks :]
    queries = query_ref[...] * jnp.asarray(SCORE_SCALE, BFLOAT)
    one = jnp.ones((1, 1), BFLOAT)
    values_t = [ref[...].T for ref in value_refs]
    results, logs = [], []
    for head in range(2):
        query = with_spare(queries, head, one)
        scores = [
            nt(with_spare(key_ref[...], head, bias_ref[...]), query)
            for key_ref, bias_ref in zip(key_refs, bias_refs)
        ]
        peak = functools.reduce(
            jnp.maximum, [jnp.max(score, axis=0, keepdims=True) for score in scores]
        )
        total = None
        for score, value_t in zip(scores, values_t):
            probs = jnp.exp(score - peak).astype(BFLOAT)
            row = lax.broadcasted_iota(jnp.int32, value_t.shape, 0)
            term = nn(jnp.where(row // HD == head, value_t, one), probs)
            total = term if total is None else total + term
        weight = total[HD * (1 - head) : HD * (1 - head) + 1, :]
        results.append(total[HD * head : HD * (head + 1), :] / weight)
        logs.append(peak + jnp.log(weight))
    out_ref[...] = jnp.concatenate(results, axis=0).T.astype(BFLOAT)
    log_ref[0] = jnp.concatenate(logs, axis=0)


def back_kernel(blocks, places, *refs):
    query_ref, out_ref, grad_ref, log_ref = refs[:4]
    ins = refs[4 : 4 + 3 * blocks]
    key_refs, value_refs, bias_refs = ins[0::3], ins[1::3], ins[2::3]
    query_grad_ref = refs[4 + 3 * blocks]
    pair_grad_refs = refs[5 + 3 * blocks :]
    queries = query_ref[...] * jnp.asarray(SCORE_SCALE, BFLOAT)
    out_grad = grad_ref[...]
    zero = jnp.zeros((1, 1), BFLOAT)
    one = jnp.ones((1, 1), BFLOAT)
    product = out_ref[...].astype(FLOAT) * out_grad.astype(FLOAT)
    chooser = (
        lax.broadcasted_iota(jnp.int32, (8, PAIR), 1) // HD
        == lax.broadcasted_iota(jnp.int32, (8, PAIR), 0)
    ).astype(FLOAT)
    inner = lax.dot_general(
        chooser, product, (((1,), (1,)), ((), ())), precision=PRECISE, preferred_element_type=FLOAT
    )
    keys_t = [ref[...].T for ref in key_refs]
    query_parts = [None, None]
    for block in range(blocks):
        key_grad, value_grad = None, None
        for head in range(2):
            grad_here = with_spare(out_grad, head, zero)
            score = nt(
                with_spare(key_refs[block][...], head, bias_refs[block][...]),
                with_spare(queries, head, one),
            )
            probs = jnp.exp(score - log_ref[0, head : head + 1, :])
            prob_grad = nt(value_refs[block][...], grad_here)
            score_grad = (probs * (prob_grad - inner[head : head + 1, :])).astype(BFLOAT)
            value_term = nn(probs.astype(BFLOAT), grad_here)
            key_term = nn(score_grad, with_spare(queries, head, zero))
            query_term = nn(keys_t[block][HD * head : HD * (head + 1), :], score_grad)
            value_grad = value_term if value_grad is None else value_grad + value_term
            key_grad = key_term if key_grad is None else key_grad + key_term
            query_parts[head] = (
                query_term if query_parts[head] is None else query_parts[head] + query_term
            )
        key_at, value_at = places(pl.program_id(0))
        key_at = pl.multiple_of(key_at * PAIR, PAIR)
        value_at = pl.multiple_of(value_at * PAIR, PAIR)
        pair_grad_refs[block][:, pl.ds(key_at, PAIR)] = key_grad.astype(BFLOAT)
        pair_grad_refs[block][:, pl.ds(value_at, PAIR)] = value_grad.astype(BFLOAT)
    joined = jnp.concatenate(query_parts, axis=0) * SCORE_SCALE
    query_grad_ref[...] = joined.T.astype(BFLOAT)


def column_block(length):
    return pl.BlockSpec((length, PAIR), lambda pair: (0, pair))


def plain_places(pair):
    return pair, pair + PAIRS


def half_places(pair):
    half, part = pair // (PAIRS // 2), pair % (PAIRS // 2)
    return half * PAIRS + part, half * PAIRS + PAIRS // 2 + part


def whole_block(shape):
    return pl.BlockSpec(shape, lambda pair: (0,) * len(shape))


def log_block(frames):
    return pl.BlockSpec((1, 2, frames), lambda pair: (pair, 0, 0))


def key_specs(key_values, places):
    specs, operands = [], []
    for joint, bias in key_values:
        length = joint.shape[0]
        specs += [
            pl.BlockSpec((length, PAIR), lambda pair: (0, places(pair)[0])),
            pl.BlockSpec((length, PAIR), lambda pair: (0, places(pair)[1])),
            whole_block((length, PAIR)),
        ]
        operands += [joint, joint, bias]
    return specs, operands


KERNEL = pltpu.CompilerParams(vmem_limit_bytes=48 * 1024 * 1024)
LIGHT = pl.CostEstimate(flops=1000, bytes_accessed=1000, transcendentals=0)


def attend(queries, key_values, places):
    frames, blocks = queries.shape[0], len(key_values)
    specs, operands = key_specs(key_values, places)
    return pl.pallas_call(
        functools.partial(attend_kernel, blocks),
        grid=(PAIRS,),
        in_specs=[column_block(frames)] + specs,
        out_specs=[column_block(frames), log_block(frames)],
        out_shape=[
            jax.ShapeDtypeStruct((frames, D), BFLOAT),
            jax.ShapeDtypeStruct((PAIRS, 2, frames), FLOAT),
        ],
        compiler_params=KERNEL,
        cost_estimate=LIGHT,
    )(queries, *operands)


def attend_back(queries, out, out_grad, logs, key_values, places):
    frames, blocks = queries.shape[0], len(key_values)
    specs, operands = key_specs(key_values, places)
    return pl.pallas_call(
        functools.partial(back_kernel, blocks, places),
        grid=(PAIRS,),
        in_specs=[column_block(frames)] * 3 + [log_block(frames)] + specs,
        out_specs=[column_block(frames)] + [whole_block(joint.shape) for joint, _ in key_values],
        out_shape=[jax.ShapeDtypeStruct((frames, D), BFLOAT)]
        + [jax.ShapeDtypeStruct(joint.shape, BFLOAT) for joint, _ in key_values],
        compiler_params=KERNEL,
        cost_estimate=LIGHT,
    )(queries, out, out_grad, logs, *operands)


def outer_kernel(*refs):
    out_ref, count = refs[-1], len(refs) // 2
    at = 0
    for place in range(count):
        left, right = refs[2 * place], refs[2 * place + 1]
        width = right.shape[1]
        product = lax.dot_general(
            left[...], right[...], (((0,), (0,)), ((), ())), preferred_element_type=FLOAT
        )
        out_ref[:, at : at + width] = product.astype(BFLOAT)
        at += width


def outer(*pairs):
    operands = [matrix for pair in pairs for matrix in pair]
    shape = (pairs[0][0].shape[1], sum(right.shape[1] for _, right in pairs))
    return pl.pallas_call(
        outer_kernel,
        out_shape=jax.ShapeDtypeStruct(shape, BFLOAT),
        compiler_params=KERNEL,
        cost_estimate=LIGHT,
    )(*operands)


def bias_of(allowed):
    column = jnp.where(allowed > 0, 0.0, MASKED_SCORE).astype(BFLOAT)
    return jnp.broadcast_to(column[:, None], (allowed.shape[0], PAIR))


LINE = 128
ROW_SIZES = [D, D, D, D, D, DT, D, FF]
COL_SIZES = [6 * D, 3 * D, D, D, D, 2 * D, FF, D]
ROW_LINES = sum(ROW_SIZES) // LINE
COL_LINES = sum(COL_SIZES) // LINE
STAT_LINES = ROW_LINES + COL_LINES + 2


def starts_of(sizes, first):
    starts = []
    for size in sizes:
        starts.append(first)
        first += size // LINE
    return starts


ROW_STARTS = starts_of(ROW_SIZES, 0)
COL_STARTS = starts_of(COL_SIZES, ROW_LINES)


def lines_at(line, shape):
    return lax.broadcasted_iota(jnp.int32, shape, 1) + line * LINE


def down_lines(column, offset, lines):
    shape = (column.shape[0], LINE)
    wanted = lax.broadcasted_iota(jnp.int32, shape, 0) + offset
    return [
        jnp.sum(jnp.where(lines_at(line, shape) == wanted, column, 0.0), axis=0, keepdims=True)
        for line in range(lines)
    ]


def from_lines(lines, offset, count):
    shape = (count, LINE)
    wanted = lax.broadcasted_iota(jnp.int32, shape, 0) + offset
    total = jnp.zeros(shape, FLOAT)
    for line in range(lines.shape[0]):
        here = jnp.where(lines_at(line, shape) == wanted, lines[line : line + 1, :], 0.0)
        total = total + here
    return jnp.sum(total, axis=1, keepdims=True)


def pieces_of(grad_refs):
    ada, query_out, key_value, cross_pair, text_pair, mlp = grad_refs
    return [
        [(ada, 0, 6 * D)],
        [(query_out, 0, D), (key_value, 0, 2 * D)],
        [(query_out, D, D)],
        [(cross_pair, 0, D)],
        [(cross_pair, D, D)],
        [(text_pair, 0, D)],
        [(mlp, 0, HALF)],
        [(mlp, HALF, HALF)],
    ]


def statistics_kernel(place_ref, weight_ref, *refs):
    grad_refs, out_ref = refs[:6], refs[6]
    data_at, head_at = place_ref[0], place_ref[1]
    flat_at = data_at * 2 + head_at
    out_ref[STAT_LINES - 2 : STAT_LINES - 1, :] = weight_ref[...]
    out_ref[STAT_LINES - 1 : STAT_LINES, :] = jnp.zeros((1, LINE), FLOAT)
    for place, parts in enumerate(pieces_of(grad_refs)):
        across, down = 0.0, []
        for ref, first, columns in parts:
            rows = ref.shape[0]
            wide = jnp.zeros((rows, LINE), FLOAT)
            for line in range(columns // LINE):
                piece = ref[:, first + line * LINE : first + (line + 1) * LINE]
                square = piece * piece
                wide = wide + square
                down.append(jnp.sum(square, axis=0, keepdims=True))
            across = across + jnp.sum(wide, axis=1, keepdims=True)
        offset = (flat_at if place < 5 else data_at) * rows
        row_start, col_start = ROW_STARTS[place], COL_STARTS[place]
        if place == 7:
            row_start, col_start = col_start, row_start
        row_lines = (COL_SIZES if place == 7 else ROW_SIZES)[place] // LINE
        for line, entry in enumerate(down_lines(across, offset, row_lines)):
            out_ref[row_start + line : row_start + line + 1, :] = entry
        groups = {5: 2}.get(place, 1)
        size = len(down) // groups
        for line, entry in enumerate(down):
            if place < 5:
                out_ref[col_start + line : col_start + line + 1, :] = entry
            else:
                for half in range(2):
                    at = col_start + (line // size * 2 + half) * size + line % size
                    out_ref[at : at + 1, :] = jnp.where(head_at == half, entry, 0.0)


def lane_of(lines, lane):
    shape = (1, LINE)
    here = lax.broadcasted_iota(jnp.int32, shape, 1) == lane
    return jnp.sum(jnp.where(here, lines, 0.0), axis=1, keepdims=True)


def update_kernel(place_ref, sums_ref, row_ref, col_ref, *refs):
    grad_refs, outs = refs[:6], refs[6:]
    row_out, col_out, norm_out, total_out = outs[:4]
    clipped_refs, update_refs = outs[4:12], outs[12:20]
    data_at, head_at = place_ref[0], place_ref[1]
    flat_at = data_at * 2 + head_at
    row_sums = sums_ref[0:ROW_LINES, :]
    square_total = jnp.sum(jnp.sum(row_sums, axis=0, keepdims=True), axis=1, keepdims=True)
    norm = jnp.sqrt(square_total)
    factor = 1.0 / jnp.maximum(1.0, norm / CLIP_NORM)
    norm_out[...] = jnp.broadcast_to(norm, (1, LINE))
    square_factor = factor * factor
    lane = lax.broadcasted_iota(jnp.int32, (1, LINE), 1)
    totals = jnp.zeros((1, LINE), FLOAT)
    for place, parts in enumerate(pieces_of(grad_refs)):
        rows_len, cols_len = ROW_SIZES[place], COL_SIZES[place]
        row_from, row_to = ROW_STARTS[place], ROW_STARTS[place] + rows_len // LINE
        col_from, col_to = COL_STARTS[place], COL_STARTS[place] + cols_len // LINE
        new_row = DECAY_RATE * row_ref[row_from:row_to, :] + (1.0 - DECAY_RATE) * (
            square_factor * sums_ref[row_from:row_to, :] / float(cols_len) + EPS_FACTOR
        )
        col_from, col_to = col_from - ROW_LINES, col_to - ROW_LINES
        new_col = DECAY_RATE * col_ref[col_from:col_to, :] + (1.0 - DECAY_RATE) * (
            square_factor
            * sums_ref[ROW_LINES + col_from : ROW_LINES + col_to, :]
            / float(rows_len)
            + EPS_FACTOR
        )
        row_out[row_from:row_to, :] = new_row
        col_out[col_from:col_to, :] = new_col
        row_mean = (
            jnp.sum(jnp.sum(new_row, axis=0, keepdims=True), axis=1, keepdims=True) / rows_len
        )
        rows = parts[0][0].shape[0]
        offset = (flat_at if place < 5 else data_at) * rows
        if place == 7:
            down = lax.rsqrt(from_lines(new_col, offset, rows))
            across = jnp.where(head_at == 0, new_row[:12], new_row[12:])
            across = lax.rsqrt(across / row_mean)
        else:
            down = lax.rsqrt(from_lines(new_row, offset, rows) / row_mean)
            if place == 5:
                keys = jnp.where(head_at == 0, new_col[0:3], new_col[3:6])
                values = jnp.where(head_at == 0, new_col[6:9], new_col[9:12])
                across = lax.rsqrt(jnp.concatenate([keys, values], axis=0))
            elif place == 6:
                across = lax.rsqrt(jnp.where(head_at == 0, new_col[:12], new_col[12:]))
            else:
                across = lax.rsqrt(new_col)
        square = jnp.zeros((rows, LINE), FLOAT)
        line_at = 0
        for ref, first, columns in parts:
            for line in range(columns // LINE):
                piece = ref[:, first + line * LINE : first + (line + 1) * LINE] * factor
                update = piece * (down * across[line_at : line_at + 1, :])
                clipped_refs[place][:, line_at * LINE : (line_at + 1) * LINE] = piece
                update_refs[place][:, line_at * LINE : (line_at + 1) * LINE] = update
                square = square + update * update
                line_at += 1
        total = jnp.sum(jnp.sum(square, axis=0, keepdims=True), axis=1, keepdims=True)
        totals = jnp.where(lane == place, total, totals)
    total_out[...] = totals


def apply_kernel(total_ref, weight_ref, *refs):
    for place in range(8):
        entries = float(ROW_SIZES[place] * COL_SIZES[place])
        total = lane_of(total_ref[...], place)
        weight = lane_of(weight_ref[...], place)
        limit = jnp.maximum(1.0, jnp.sqrt(total / entries) / CLIP_UPDATE)
        rate = RELATIVE_RATE * jnp.maximum(SCALE_FLOOR, jnp.sqrt(weight / entries))
        scale = rate / limit
        refs[16 + place][...] = refs[place][...] - scale * refs[8 + place][...]


def weight_kernel(*refs):
    lane = lax.broadcasted_iota(jnp.int32, (1, LINE), 1)
    totals = jnp.zeros((1, LINE), FLOAT)
    for place in range(8):
        matrix = refs[place][...]
        total = jnp.sum(jnp.sum(matrix * matrix, axis=0, keepdims=True), axis=1, keepdims=True)
        totals = jnp.where(lane == place, total, totals)
    refs[8][...] = totals


def whole_call(kernel, shapes, *operands, places=0):
    memory = [pl.BlockSpec(memory_space=pltpu.SMEM)] * places
    memory += [pl.BlockSpec(memory_space=pltpu.VMEM)] * (len(operands) - places)
    return pl.pallas_call(
        kernel,
        in_specs=memory,
        out_specs=[pl.BlockSpec(memory_space=pltpu.VMEM)] * len(shapes),
        out_shape=[jax.ShapeDtypeStruct(shape, FLOAT) for shape in shapes],
        compiler_params=KERNEL,
        cost_estimate=LIGHT,
    )(*operands)


def mlp_outer_kernel(input_ref, grad_ref, pre_ref, act_ref, out_ref):
    turn = (((0,), (0,)), ((), ()))
    width = pre_ref.shape[2]
    for at in range(0, width, D):
        first = lax.dot_general(
            input_ref[...], pre_ref[0, :, at : at + D], turn, preferred_element_type=FLOAT
        )
        out_ref[0, :, at : at + D] = first.astype(BFLOAT)
        second = lax.dot_general(
            grad_ref[...], act_ref[0, :, at : at + D], turn, preferred_element_type=FLOAT
        )
        out_ref[0, :, width + at : width + at + D] = second.astype(BFLOAT)


def mlp_outer(mlp_input, mlp_grad, pre_grad, hidden_act):
    frames, width = mlp_input.shape[0], pre_grad.shape[2]
    whole = pl.BlockSpec((frames, D), lambda half: (0, 0))
    hidden = pl.BlockSpec((1, frames, width), lambda half: (half, 0, 0))
    return pl.pallas_call(
        mlp_outer_kernel,
        grid=(2,),
        in_specs=[whole, whole, hidden, hidden],
        out_specs=pl.BlockSpec((1, D, 2 * width), lambda half: (half, 0, 0)),
        out_shape=jax.ShapeDtypeStruct((2, D, 2 * width), BFLOAT),
        compiler_params=KERNEL,
        cost_estimate=LIGHT,
    )(mlp_input, mlp_grad, pre_grad, hidden_act)


def per_device(
    block_in,
    text,
    timesteps,
    frame_mask,
    text_mask,
    cotangent,
    w_ada,
    w_qkv,
    w_out,
    w_cq,
    w_cout,
    w_ckv,
    w_fc1,
    w_fc2,
    row_state,
    col_state,
):
    clips = lax.axis_size("dp")
    devices = clips * 2
    data_at = lax.axis_index("dp")
    head_at = lax.axis_index("head")
    flat_at = data_at * 2 + head_at
    frames = block_in.shape[1]
    rows = w_qkv.shape[0]

    first = [
        gather_chain(
            jnp.concatenate([w_qkv[:, :D], w_out], axis=1).astype(BFLOAT), "last", False
        ),
        gather_chain(w_qkv[:, D:].astype(BFLOAT), "last", True),
    ]
    second = [
        gather_chain(jnp.concatenate([w_cq, w_cout], axis=1).astype(BFLOAT), "last", False),
        gather_chain(w_ckv.astype(BFLOAT).reshape(w_ckv.shape[0], D), "columns", True),
    ]
    masters = [
        w_ada,
        w_qkv,
        w_out,
        w_cq,
        w_cout,
        w_ckv.reshape(w_ckv.shape[0], D),
        w_fc1,
        w_fc2.T,
    ]
    mlp_shard = jnp.concatenate([w_fc1.astype(BFLOAT), w_fc2.T.astype(BFLOAT)], axis=1)
    mlp_all = lax.all_gather(mlp_shard, ("head", "dp"), axis=0, tiled=True)

    def add_step(link):
        return lambda state: state + cross(state, link)

    def project(steps):
        condition = embed_part(steps, flat_at * rows, rows)
        product = jnp.dot(condition, w_ada.astype(BFLOAT), preferred_element_type=FLOAT)
        return condition, product.reshape(clips // 2, 2, 6 * D)

    def keep_step(link):
        def step(state):
            condition, product = state
            bit = bit_of(link)
            product = product.reshape(-1, 2, 6 * D)
            kept = lax.dynamic_slice_in_dim(product, bit, 1, axis=1)
            sent = lax.dynamic_slice_in_dim(product, 1 - bit, 1, axis=1)
            return condition, (kept + cross(sent, link)).reshape(-1, 6 * D)

        return step

    def last_step(state):
        condition, product = state
        return condition, product + cross(product, core_link())

    steps = lax.dynamic_update_slice(jnp.zeros((clips,), jnp.int32), timesteps, (data_at,))
    timing = Chain(
        steps,
        [add_step(link) for link in [core_link()] + far_links()[1:] + far_links()[:1]]
        + [lambda steps: keep_step(row_link())(project(steps))]
        + [keep_step(link) for link in far_links()]
        + [last_step],
    )
    slots, far_count = len(first[0].steps), len(far_links()) - 1
    for slot in range(slots):
        timing.advance({0: 1 + far_count, 1: 3, 2: far_count, 3: 1}.get(slot, 0))
        for chain in first:
            chain.advance()
        if slot >= 2:
            for chain in second:
                chain.advance()
        if slot == 0:
            block_in, joint_mask, text = tie(
                [timing] + first,
                block_in,
                jnp.concatenate([frame_mask[0], text_mask[0]]),
                text,
            )
            inputs = swap_place(block_in[0])
            masks = from_clip_core(joint_mask)
            clip_text = from_clip_core(text[0])
        elif slot == 1:
            tie([timing] + first)
        elif slot < slots - 1:
            tie([timing] + first + second)
        else:
            masters = tie([timing] + first, *masters)
            (weight_squares,) = whole_call(weight_kernel, [(1, LINE)], *masters)
    condition, modulation = timing.finish()
    query_out, w_key_value = [chain.finish().reshape(D, 2 * D) for chain in first]
    w_query, w_project = query_out[:, :D], query_out[:, D:]

    inputs = inputs.astype(FLOAT)
    core_at = data_at % 2
    own_allowed = lax.dynamic_slice_in_dim(masks, core_at * frames, frames)
    other_allowed = lax.dynamic_slice_in_dim(masks, (1 - core_at) * frames, frames)
    own_bias, other_bias = bias_of(own_allowed), bias_of(other_allowed)
    text_bias = bias_of(masks[2 * frames :])
    shift_self, scale_self, gate_self, shift_mlp, scale_mlp, gate_mlp = jnp.split(
        modulation, 6, axis=-1
    )

    out_grad = swap_place(cotangent[0])
    self_input = modulate(inputs, shift_self, scale_self).astype(BFLOAT)
    key_value = nn(self_input, w_key_value).astype(BFLOAT)
    query = nn(self_input, w_query).astype(BFLOAT)
    other_key_value = cross(key_value, core_link())
    for chain in second:
        chain.advance()
    query, other_key_value = tie(second, query, other_key_value)
    cross_pair, w_text = [chain.finish() for chain in second]
    cross_pair, w_text = cross_pair.reshape(D, 2 * D), w_text.reshape(DT, 2 * D)
    w_cross_query, w_cross_project = cross_pair[:, :D], cross_pair[:, D:]

    self_keys = [(key_value, own_bias), (other_key_value, other_bias)]
    self_attn, self_logs = attend(query, self_keys, plain_places)
    self_branch = nn(self_attn, w_project)
    after_self = inputs + gate_self * self_branch

    text_pair = nn(clip_text, w_text).astype(BFLOAT)
    cross_input = layer_norm(after_self).astype(BFLOAT)
    cross_query = nn(cross_input, w_cross_query).astype(BFLOAT)
    text_keys = [(text_pair, text_bias)]
    cross_attn, cross_logs = attend(cross_query, text_keys, half_places)
    after_cross = after_self + nn(cross_attn, w_cross_project)

    mlp_input = modulate(after_cross, shift_mlp, scale_mlp).astype(BFLOAT)
    mlp_input, out_grad = tie([], mlp_input, out_grad)
    out_grad = out_grad.astype(FLOAT)
    mlp_all = mlp_all.reshape(2, D, 2 * HALF)
    fc1_halves, fc2_halves = mlp_all[:, :, :HALF], mlp_all[:, :, HALF:]
    hidden_pre = jnp.einsum("fd,hdk->hfk", mlp_input, fc1_halves, preferred_element_type=FLOAT)
    hidden_act = jax.nn.gelu(hidden_pre).astype(BFLOAT)
    mlp_grad = (gate_mlp * out_grad).astype(BFLOAT)
    act_grad = jnp.einsum("fd,hdk->hfk", mlp_grad, fc2_halves, preferred_element_type=FLOAT)
    gelu_back = jax.vjp(jax.nn.gelu, hidden_pre)[1]
    pre_grad = gelu_back(act_grad)[0].astype(BFLOAT)
    mlp_part = mlp_outer(mlp_input, mlp_grad, pre_grad, hidden_act)
    mlp_part, hidden_act, pre_grad = tie([], mlp_part, hidden_act, pre_grad)
    mlp_raw = lax.psum_scatter(
        mlp_part.reshape(2 * D, 2 * HALF), ("head", "dp"), scatter_dimension=0, tiled=True
    ).astype(FLOAT)

    mlp_branch = jnp.einsum("hfk,hdk->fd", hidden_act, fc2_halves, preferred_element_type=FLOAT)
    block_out = (after_cross + gate_mlp * mlp_branch).astype(BFLOAT)
    gate_mlp_grad = jnp.sum(out_grad * mlp_branch, axis=0, keepdims=True)
    mlp_in_grad = jnp.einsum("hfk,hdk->fd", pre_grad, fc1_halves, preferred_element_type=FLOAT)
    mlp_back = jax.vjp(modulate, after_cross, shift_mlp, scale_mlp)[1]
    cross_res_grad, shift_mlp_grad, scale_mlp_grad = mlp_back(mlp_in_grad)
    cross_res_grad = out_grad + cross_res_grad
    cross_res_grad, block_out, gate_mlp_grad = tie([], cross_res_grad, block_out, gate_mlp_grad)

    cross_out_grad = cross_res_grad.astype(BFLOAT)
    cross_attn_grad = nt(cross_out_grad, w_cross_project).astype(BFLOAT)
    cross_query_grad, text_pair_grad = attend_back(
        cross_query, cross_attn, cross_attn_grad, cross_logs, text_keys, half_places
    )
    cross_chains = [
        scatter_chain(
            outer((cross_input, cross_query_grad), (cross_attn, cross_out_grad)), "last", False
        ),
        scatter_chain(outer((clip_text, text_pair_grad)), "columns", True),
    ]
    (cross_query_grad,) = tie(cross_chains, cross_query_grad)
    for chain in cross_chains:
        chain.advance()
    cross_in_grad = nt(cross_query_grad, w_cross_query)
    norm_back = jax.vjp(layer_norm, after_self)[1]
    self_res_grad = cross_res_grad + norm_back(cross_in_grad)[0]

    gate_self_grad = jnp.sum(self_res_grad * self_branch, axis=0, keepdims=True)
    self_out_grad = (gate_self * self_res_grad).astype(BFLOAT)
    self_attn_grad = nt(self_out_grad, w_project).astype(BFLOAT)
    self_attn_grad, self_out_grad = tie(cross_chains, self_attn_grad, self_out_grad)
    for chain in cross_chains:
        chain.advance()
    query_grad, own_pair_grad, other_pair_grad = attend_back(
        query, self_attn, self_attn_grad, self_logs, self_keys, plain_places
    )
    query_grad, own_pair_grad, other_pair_grad = tie(
        cross_chains, query_grad, own_pair_grad, other_pair_grad
    )
    for chain in cross_chains:
        chain.advance()
    pair_grad = (
        own_pair_grad.astype(FLOAT) + cross(other_pair_grad, core_link()).astype(FLOAT)
    ).astype(BFLOAT)
    last_chains = [
        scatter_chain(
            outer((self_input, query_grad), (self_attn, self_out_grad)), "last", False
        ),
        scatter_chain(outer((self_input, pair_grad)), "last", True),
    ]
    query_grad, pair_grad = tie(cross_chains + last_chains, query_grad, pair_grad)
    for chain in cross_chains + last_chains:
        chain.advance()
    in_grad_normed = nt(query_grad, w_query) + nt(pair_grad, w_key_value)
    self_back = jax.vjp(modulate, inputs, shift_self, scale_self)[1]
    input_res_grad, shift_self_grad, scale_self_grad = self_back(in_grad_normed)
    input_grad = (self_res_grad + input_res_grad).astype(BFLOAT)
    input_grad, shift_self_grad, scale_self_grad = tie(
        cross_chains + last_chains, input_grad, shift_self_grad, scale_self_grad
    )
    for chain in cross_chains + last_chains:
        chain.advance()

    modulation_grad = jnp.concatenate(
        [
            shift_self_grad,
            scale_self_grad,
            gate_self_grad,
            shift_mlp_grad,
            scale_mlp_grad,
            gate_mlp_grad,
        ],
        axis=-1,
    )
    modulation_grad = modulation_grad + cross(modulation_grad, core_link())
    modulation_grad, block_out, input_grad = tie(
        cross_chains + last_chains, modulation_grad, block_out, input_grad
    )
    block_out, input_grad = swap_place(jnp.stack([block_out, input_grad]))
    modulation_grad = modulation_grad.reshape((1,) * dp_bits() + (6 * D,))
    for link in far_links()[::-1] + [row_link()]:
        other = cross(modulation_grad, link)
        upper = bit_of(link) == 1
        dim = dp_bits() - 1 if link[0] == "head" else dp_bits() - link[1].bit_length()
        modulation_grad = jnp.concatenate(
            [
                jnp.where(upper, other, modulation_grad),
                jnp.where(upper, modulation_grad, other),
            ],
            axis=dim,
        )
    ada_raw = jnp.einsum(
        "cr,cx->rx",
        condition.astype(FLOAT),
        modulation_grad.reshape(clips, 6 * D),
        precision=PRECISE,
    )

    cross_raw, ckv_raw = [chain.finish() for chain in cross_chains]
    query_out_raw, pair_raw = [chain.finish() for chain in last_chains]

    place = jnp.stack([data_at, head_at]).astype(jnp.int32)
    raw_grads = [ada_raw, query_out_raw, pair_raw, cross_raw, ckv_raw, mlp_raw]
    (statistics,) = whole_call(
        statistics_kernel, [(STAT_LINES, LINE)], place, weight_squares, *raw_grads, places=1
    )
    sums = sum_all(statistics)
    shapes = [master.shape for master in masters]
    line = (1, LINE)
    row_new, col_new, norm, update_squares, *rest = whole_call(
        update_kernel,
        [(ROW_LINES, LINE), (COL_LINES, LINE), line, line] + shapes + shapes,
        place,
        sums,
        row_state.reshape(ROW_LINES, LINE),
        col_state.reshape(COL_LINES, LINE),
        *raw_grads,
        places=1,
    )
    clipped, updates = list(rest[:8]), rest[8:]
    updated = whole_call(
        apply_kernel,
        shapes,
        sum_all(update_squares),
        sums[STAT_LINES - 2 : STAT_LINES - 1],
        *masters,
        *updates,
    )
    updated = list(updated)
    clipped[5] = clipped[5].reshape(w_ckv.shape)
    updated[5] = updated[5].reshape(w_ckv.shape)
    clipped[7] = clipped[7].T
    updated[7] = updated[7].T
    return (
        block_out[None],
        input_grad[None],
        norm[0, 0],
        row_new.reshape(-1),
        col_new.reshape(-1),
        *clipped,
        *updated,
    )


def solution(mesh):
    return jax.shard_map(
        per_device,
        mesh=mesh,
        in_specs=(
            P("dp", "head", None),
            P("dp", None, None),
            P("dp"),
            P("dp", None),
            P("dp", None),
            P("dp", "head", None),
            P(("dp", "head"), None),
            P(("dp", "head"), None),
            P(("dp", "head"), None),
            P(("dp", "head"), None),
            P(("dp", "head"), None),
            P("dp", None, "head"),
            P("dp", "head"),
            P("head", "dp"),
            P(),
            P(),
        ),
        out_specs=(
            P("dp", "head", None),
            P("dp", "head", None),
            P(),
            P(),
            P(),
            P(("dp", "head"), None),
            P(("dp", "head"), None),
            P(("dp", "head"), None),
            P(("dp", "head"), None),
            P(("dp", "head"), None),
            P("dp", None, "head"),
            P("dp", "head"),
            P("head", "dp"),
            P(("dp", "head"), None),
            P(("dp", "head"), None),
            P(("dp", "head"), None),
            P(("dp", "head"), None),
            P(("dp", "head"), None),
            P("dp", None, "head"),
            P("dp", "head"),
            P("head", "dp"),
        ),
        check_vma=False,
    )
```

time: 647 us -> 486 us (0.75)
  local copies, waits for them, and re-layouts: 91.3 us -> 21.4 us
  other arithmetic: 85.7 us -> 38.8 us
  matrix products: 69.8 us -> 37.7 us
  Pallas kernels: 48.6 us -> 67.7 us
  starting transfers between devices: 90.2 us -> 74.1 us
  between operations: 24.6 us -> 17.5 us
  waiting for transfers between devices: 226 us -> 219 us
    ppermute x66, waiting for transfers between devices: 226 us -> 179 us  [cross(): return lax.ppermute(values, link[0], pairs)]
    reduce_scatter x1, waiting for transfers between devices: 0.01 us -> 39.8 us  [per_device(): lax.psum_scatter(mlp_part.reshape(2 * D, 2 * HALF), ('head', 'dp'), scatt...]
    dot_general x11 -> x1, matrix products: 31.6 us -> 0.3 us  [project(): jnp.dot(condition, w_ada.astype(BFLOAT), preferred_element_type=FLOAT)]
    another operation x19 -> x4, local copies, waits for them, and re-layouts: 27.1 us -> 2.95 us  [the longest x1 1.24 us: per_device(): block_out, input_grad = swap_place(jnp.stack([block_out, input_grad]))]
    pallas_call x2 -> x11, Pallas kernels: 29.2 us -> 49.1 us  [the longest x2 29.9 us: attend_back(): pl.pallas_call(functools.partial(back_kernel, blocks, places), grid=(PAIR...]
    ppermute x6 -> x5, starting transfers between devices: 28.2 us -> 10.9 us  [the longest x2 6.53 us: from_clip_core(): return jnp.where(on_own_chip(), values, lax.ppermute(values, ALL, pairs))]
    reduce_sum x21 -> x0, other arithmetic: 15.9 us -> none  [the longest x8 9.43 us: per_device(): weight_local = jnp.stack([jnp.sum(master * master) for master in masters])]
    sub x7 -> x0, other arithmetic: 14.8 us -> none  [per_device(): master - rates[place] * (update / limits[place])]
  transfers between devices with their start and end apart: 74 -> 73, of which waited for: 44 -> 44; matrix products, arithmetic and copies ran while one was open for 27% -> 12% of each run, Pallas kernels for 6% -> 10%
where the time goes in v2:
time: 486 us; the launch traced here: 476 us
  waiting for transfers between devices  219 us (45%)
  starting transfers between devices  74.1 us (15%)
  Pallas kernels  67.7 us (14%)
  other arithmetic  38.8 us (8%)
  matrix products  37.7 us (8%)
  local copies, waits for them, and re-layouts  21.4 us (4%)
  between operations  17.5 us (4%)
    ppermute x66, waiting for transfers between devices, cross(): return lax.ppermute(values, link[0], pairs)  179 us
    ppermute x66, starting transfers between devices, cross(): return lax.ppermute(values, link[0], pairs)  63.2 us
    reduce_scatter x1, waiting for transfers between devices, per_device(): lax.psum_scatter(mlp_part.reshape(2 * D, 2 * HALF), ('head', 'dp'), scatt...  39.8 us
    pallas_call x2, Pallas kernels, attend_back(): pl.pallas_call(functools.partial(back_kernel, blocks, places), grid=(PAIR...  29.9 us
    pallas_call x2, Pallas kernels, attend(): pl.pallas_call(functools.partial(attend_kernel, blocks), grid=(PAIRS,), i...  18.6 us
    unnamed x221, local copies, waits for them, and re-layouts  11.7 us
  transfers between devices with their start and end apart: 73, of which 44 were waited for; matrix products, arithmetic and copies ran while one was open for 12% of the time, Pallas kernels for 10%

profile of v2, /device:TPU:0, one launch (start us, length us, event | category | flops | bytes accessed | tf_op | source)
XLA Modules:
  0.0 476.5 jit_solution(408239570851420841)
XLA Ops:
  9.5 2.7 collective-permute-start.15
  25.1 2.9 collective-permute-start.2
  33.9 4.4 collective-permute-start.29
  38.3 2.7 collective-permute-start.9
  47.1 5.4 %collective-permute-done.9 = bf16[1,2,1,1,1,24,1536]{6,5,4,3,2,1,0:T(8,128)(2,1)} collective-permute-done((bf16[1,2,1,1,1,24,1536]{6,5,4,3,2,1,0:T(8,128)(2,1)}, bf16[1,2,1,1,1,24,1536]{6,5,4,3,2,1,0:T(8,128)(2,1)}, u32[]{:S(2)}, u32[]{:S(2)}) %collective-permute-start.9) | collective-permute-done | bytes 147488 | tf_op jit(solution)/shard_map/ppermute | solution.py:78
  58.4 14.1 %collective-permute-done.7 = f32[8,1,4608]{2,1,0:T(1,128)S(1)} collective-permute-done((f32[8,1,4608]{2,1,0:T(1,128)S(1)}, f32[8,1,4608]{2,1,0:T(1,128)S(1)}, u32[]{:S(2)}, u32[]{:S(2)}) %collective-permute-start.7) | collective-permute-done | bytes 147488 | tf_op jit(solution)/shard_map/ppermute | solution.py:78
  80.9 4.7 collective-permute-done.11
  88.4 4.4 collective-permute-done.12
  93.0 8.5 %collective-permute-done.13 = bf16[2,2,1,1,1,24,1536]{6,5,4,3,2,1,0:T(8,128)(2,1)S(1)} collective-permute-done((bf16[2,2,1,1,1,24,1536]{6,5,4,3,2,1,0:T(8,128)(2,1)S(1)}, bf16[2,2,1,1,1,24,1536]{6,5,4,3,2,1,0:T(8,128)(2,1)S(1)}, u32[]{:S(2)}, u32[]{:S(2)}) %collective-permute-start.13) | collective-permute-done | bytes 294944 | tf_op jit(solution)/shard_map/ppermute | solution.py:78
  103.6 2.5 collective-permute-start.20
  108.1 17.3 %collective-permute-done.20 = bf16[1,2,1,1,1,24,1536]{6,5,4,3,2,1,0:T(8,128)(2,1)S(1)} collective-permute-done((bf16[1,2,1,1,1,24,1536]{6,5,4,3,2,1,0:T(8,128)(2,1)S(1)}, bf16[1,2,1,1,1,24,1536]{6,5,4,3,2,1,0:T(8,128)(2,1)S(1)}, u32[]{:S(2)}, u32[]{:S(2)}) %collective-permute-start.20) | collective-permute-done | bytes 147488 | tf_op jit(solution)/shard_map/ppermute | solution.py:78
  126.5 3.6 collective-permute-done.21
  130.8 9.9 %collective-permute-done.19 = bf16[2,2,1,1,2,24,1536]{6,5,4,3,2,1,0:T(8,128)(2,1)S(1)} collective-permute-done((bf16[2,2,1,1,2,24,1536]{6,5,4,3,2,1,0:T(8,128)(2,1)S(1)}, bf16[2,2,1,1,2,24,1536]{6,5,4,3,2,1,0:T(8,128)(2,1)S(1)}, u32[]{:S(2)}, u32[]{:S(2)}) %collective-permute-start.19) | collective-permute-done | bytes 589856 | tf_op jit(solution)/shard_map/ppermute | solution.py:78
  144.0 5.3 %collective-permute-done.24 = bf16[2,2,1,1,1,24,1536]{6,5,4,3,2,1,0:T(8,128)(2,1)S(1)} collective-permute-done((bf16[2,2,1,1,1,24,1536]{6,5,4,3,2,1,0:T(8,128)(2,1)S(1)}, bf16[2,2,1,1,1,24,1536]{6,5,4,3,2,1,0:T(8,128)(2,1)S(1)}, u32[]{:S(2)}, u32[]{:S(2)}) %collective-permute-start.24) | collective-permute-done | bytes 294944 | tf_op jit(solution)/shard_map/ppermute | solution.py:78
  149.7 4.9 %collective-permute-done.26 = bf16[2,2,1,1,64,768]{5,4,3,2,1,0:T(8,128)(2,1)S(1)} collective-permute-done((bf16[2,2,1,1,64,768]{5,4,3,2,1,0:T(8,128)(2,1)S(1)}, bf16[2,2,1,1,64,768]{5,4,3,2,1,0:T(8,128)(2,1)S(1)}, u32[]{:S(2)}, u32[]{:S(2)}) %collective-permute-start.26) | collective-permute-done | bytes 393248 | tf_op jit(solution)/shard_map/ppermute | solution.py:78
  159.8 5.6 %collective-permute-done.25 = bf16[2,2,2,1,1,24,1536]{6,5,4,3,2,1,0:T(8,128)(2,1)S(1)} collective-permute-done((bf16[2,2,2,1,1,24,1536]{6,5,4,3,2,1,0:T(8,128)(2,1)S(1)}, bf16[2,2,2,1,1,24,1536]{6,5,4,3,2,1,0:T(8,128)(2,1)S(1)}, u32[]{:S(2)}, u32[]{:S(2)}) %collective-permute-start.25) | collective-permute-done | bytes 589856 | tf_op jit(solution)/shard_map/ppermute | solution.py:78
  165.5 5.0 %collective-permute-done.27 = bf16[2,2,1,1,64,1536]{5,4,3,2,1,0:T(8,128)(2,1)S(1)} collective-permute-done((bf16[2,2,1,1,64,1536]{5,4,3,2,1,0:T(8,128)(2,1)S(1)}, bf16[2,2,1,1,64,1536]{5,4,3,2,1,0:T(8,128)(2,1)S(1)}, u32[]{:S(2)}, u32[]{:S(2)}) %collective-permute-start.27) | collective-permute-done | bytes 786464 | tf_op jit(solution)/shard_map/ppermute | solution.py:78
  172.7 12.7 %shard_map.319 = (bf16[512,768]{1,0:T(8,128)(2,1)S(1)}, f32[6,2,512]{2,1,0:T(2,128)S(1)}) custom-call(bf16[512,768]{1,0:T(8,128)(2,1)S(1)} %convolution_convert_fusion.5.refs_0_, bf16[512,1536]{1,0:T(8,128)(2,1)S(1)} %convolution_convert_fusion.refs_1_.refs_2_.refs_4_.refs_5_, bf16[512,1536]{1,0:T(8,128)(2,1)S(1)} %convolution_convert_fusion.refs_1_.refs_2_.refs_4_.refs_5_, ...), custom_call_target="tpu_custom_call" | custom-call | flops 1000 | bytes 1000 | tf_op jit(solution)/shard_map/pallas_call | solution.py:315
  191.9 5.9 %shard_map.320 = (bf16[512,768]{1,0:T(8,128)(2,1)S(1)}, f32[6,2,512]{2,1,0:T(2,128)S(1)}) custom-call(bf16[512,768]{1,0:T(8,128)(2,1)S(1)} %convolution_convert_fusion.4.refs_0_, bf16[256,1536]{1,0:T(8,128)(2,1)S(1)} %convolution_convert_fusion.1.refs_1_.refs_2_.refs_4_.refs_5_, ...), custom_call_target="tpu_custom_call" | custom-call | flops 1000 | bytes 1000 | tf_op jit(solution)/shard_map/pallas_call | solution.py:315
  200.0 7.7 %fusion.7 = (bf16[2,512,1536]{2,1,0:T(8,128)(2,1)}, f32[2,1536,512]{1,2,0:T(8,128)S(1)}) fusion(bf16[2,768,3072]{2,1,0:T(8,128)(2,1)} %bitcast.175, bf16[512,768]{1,0:T(8,128)(2,1)S(1)} %add_convert_fusion.7.input_ref), kind=kOutput, calls=%fused_computation.11 | convolution fusion | flops 2430074880 | bytes 14942208 | tf_op jit(solution)/shard_map/fd,hdk->hfk/dot_general | solution.py:746
  207.7 6.2 %fusion.6.pre_ref = bf16[2,512,1536]{2,1,0:T(8,128)(2,1)S(1)} fusion(f32[2,1536,512]{1,2,0:T(8,128)S(1)} %get-tuple-element.333, bf16[2,768,3072]{2,1,0:T(8,128)(2,1)S(1)} %bitcast.178, bf16[512,768]{1,0:T(8,128)(2,1)S(1)} %fusion.29.grad_ref), kind=kOutput, calls=%fused_computation.8 | convolution fusion | flops 2447376384 | bytes 14942208 | tf_op jit(solution)/shard_map/fd,hdk->hfk/dot_general | solution.py:749
  213.9 9.3 %shard_map.321 = bf16[2,768,3072]{2,1,0:T(8,128)(2,1)} custom-call(bf16[512,768]{1,0:T(8,128)(2,1)S(1)} %add_convert_fusion.7.input_ref, bf16[512,768]{1,0:T(8,128)(2,1)S(1)} %fusion.29.grad_ref, bf16[2,512,1536]{2,1,0:T(8,128)(2,1)S(1)} %fusion.6.pre_ref, bf16[2,512,1536]{2,1,0:T(8,128)(2,1)} %get-tuple-element.170.act_ref), custom_call_target="tpu_custom_call" | custom-call | flops 1000 | bytes 1000 | tf_op jit(solution)/shard_map/pallas_call | solution.py:587
  223.2 5.4 %fusion.33 = (f32[768]{0:T(1024)S(1)}, f32[512]{0:T(512)S(1)}, f32[768]{0:T(1024)S(1)}, f32[512,768,1]{1,0,2:T(8,128)S(1)}) fusion(f32[512,768]{1,0:T(8,128)S(1)} %copy-done.47, f32[512]{0:T(512)S(1)} %copy-done.100, f32[512]{0:T(512)S(1)} %copy-done.87, f32[768]{0:T(1024)S(1)} %copy-done.98, bf16[2,512,1536]{2,1,0:T(8,128)(2,1)S(1)} %fusion.6.pre_ref, ...), kind=kOutput, calls=%fused_computation.64 | convolution fusion | flops 2419062784 | bytes 11025408 | tf_op jit(solution)/shard_map/hfk,hdk->fd/dot_general | solution.py:761
  228.7 6.2 %fusion.30 = (f32[768]{0:T(1024)S(1)}, bf16[512,768]{1,0:T(8,128)(2,1)}, f32[512]{0:T(512)S(1)}, f32[512,768]{1,0:T(8,128)S(1)}) fusion(bf16[512,768]{1,0:T(8,128)(2,1)S(1)} %copy-done.56, f32[512,768]{1,0:T(8,128)S(1)} %copy-done.47, f32[768]{0:T(1024)S(1)} %copy-done.96, f32[512]{0:T(512)S(1)} %multiply_multiply_fusion.4, f32[512]{0:T(512)S(1)} %copy-done.87, ...), kind=kOutput, calls=%fused_computation.55 | convolution fusion | flops 2421029632 | bytes 14173184 | tf_op jit(solution)/shard_map/hfk,hdk->fd/dot_general | solution.py:758
  237.9 8.2 %shard_map.322 = (bf16[512,768]{1,0:T(8,128)(2,1)S(1)}, bf16[256,1536]{1,0:T(8,128)(2,1)S(1)}) custom-call(bf16[512,768]{1,0:T(8,128)(2,1)S(1)} %copy-done.13, bf16[512,768]{1,0:T(8,128)(2,1)S(1)} %get-tuple-element.166.refs_1_.refs_2_, bf16[512,768]{1,0:T(8,128)(2,1)S(1)} %convolution_convert_fusion.3.refs_2_, f32[6,2,512]{2,1,0:T(2,128)S(1)} %get-tuple-element.172.refs_3_, ...), custom_call_target="tpu_custom_call" | custom-call | flops 1000 | bytes 1000 | tf_op jit(solution)/shard_map/pallas_call | solution.py:332
  257.8 21.8 %shard_map.325 = (bf16[512,768]{1,0:T(8,128)(2,1)S(1)}, bf16[512,1536]{1,0:T(8,128)(2,1)S(1)}, bf16[512,1536]{1,0:T(8,128)(2,1)}) custom-call(bf16[512,768]{1,0:T(8,128)(2,1)S(1)} %copy-done.9, bf16[512,768]{1,0:T(8,128)(2,1)S(1)} %copy-done.3, bf16[512,768]{1,0:T(8,128)(2,1)S(1)} %convolution_convert_fusion.2.refs_2_, ...), custom_call_target="tpu_custom_call" | custom-call | flops 1000 | bytes 1000 | tf_op jit(solution)/shard_map/pallas_call | solution.py:332
  287.4 4.2 collective-permute-done.38
  301.9 3.0 collective-permute-start.42
  306.3 7.5 %collective-permute-done.41 = bf16[1,2,1,1,1,24,1536]{6,5,4,3,2,1,0:T(8,128)(2,1)S(1)} collective-permute-done((bf16[1,2,1,1,1,24,1536]{6,5,4,3,2,1,0:T(8,128)(2,1)S(1)}, bf16[1,2,1,1,1,24,1536]{6,5,4,3,2,1,0:T(8,128)(2,1)S(1)}, u32[]{:S(2)}, u32[]{:S(2)}) %collective-permute-start.41) | collective-permute-done | bytes 147488 | tf_op jit(solution)/shard_map/ppermute | solution.py:78
  313.9 4.1 collective-permute-done.42
  325.9 10.5 %collective-permute-done.48 = bf16[2,2,1,1,2,24,1536]{6,5,4,3,2,1,0:T(8,128)(2,1)S(1)} collective-permute-done((bf16[2,2,1,1,2,24,1536]{6,5,4,3,2,1,0:T(8,128)(2,1)S(1)}, bf16[2,2,1,1,2,24,1536]{6,5,4,3,2,1,0:T(8,128)(2,1)S(1)}, u32[]{:S(2)}, u32[]{:S(2)}) %collective-permute-start.48) | collective-permute-done | bytes 589856 | tf_op jit(solution)/shard_map/ppermute | solution.py:78
  336.6 2.1 collective-permute-done.47
  339.3 5.5 %collective-permute-done.51 = f32[1,1,1,1,4608]{4,3,2,1,0:T(1,128)S(1)} collective-permute-done((f32[1,1,1,1,4608]{4,3,2,1,0:T(1,128)S(1)}, f32[1,1,1,1,4608]{4,3,2,1,0:T(1,128)S(1)}, u32[]{:S(2)}, u32[]{:S(2)}) %collective-permute-start.51) | collective-permute-done | bytes 18464 | tf_op jit(solution)/shard_map/ppermute | solution.py:78
  345.7 5.3 %collective-permute-done.52 = f32[2,1,1,1,4608]{4,3,2,1,0:T(1,128)S(1)} collective-permute-done((f32[2,1,1,1,4608]{4,3,2,1,0:T(1,128)S(1)}, f32[2,1,1,1,4608]{4,3,2,1,0:T(1,128)S(1)}, u32[]{:S(2)}, u32[]{:S(2)}) %collective-permute-start.52) | collective-permute-done | bytes 36896 | tf_op jit(solution)/shard_map/ppermute | solution.py:78
  352.0 2.1 collective-permute-start.58
  359.4 2.1 collective-permute-start.50
  361.5 2.5 collective-permute-done.54
  367.6 3.0 collective-permute-start.56
  370.5 5.8 %collective-permute-done.59 = bf16[1,2,1,1,1,24,1536]{6,5,4,3,2,1,0:T(8,128)(2,1)S(1)} collective-permute-done((bf16[1,2,1,1,1,24,1536]{6,5,4,3,2,1,0:T(8,128)(2,1)S(1)}, bf16[1,2,1,1,1,24,1536]{6,5,4,3,2,1,0:T(8,128)(2,1)S(1)}, u32[]{:S(2)}, u32[]{:S(2)}) %collective-permute-start.59) | collective-permute-done | bytes 147488 | tf_op jit(solution)/shard_map/ppermute | solution.py:78
  376.5 2.9 collective-permute-done.56
  381.0 2.9 collective-permute-done.57
  383.9 39.8 %reduce-scatter.2.cloned.1.call-done = bf16[48,3072]{1,0:T(8,128)(2,1)} async-done(((bf16[1536,3072]{1,0:T(8,128)(2,1)}), bf16[48,3072]{1,0:T(8,128)(2,1)}) %reduce-scatter.2.cloned.1.call-update) | async-done | bytes 294928 | tf_op jit(solution)/shard_map/reduce_scatter | solution.py:754
  428.8 3.1 collective-permute-done.62
  433.7 2.8 collective-permute-done.63
  437.8 3.4 collective-permute-done.64
  442.7 5.1 %collective-permute-done.65 = f32[184,128]{1,0:T(8,128)S(1)} collective-permute-done((f32[184,128]{1,0:T(8,128)S(1)}, f32[184,128]{1,0:T(8,128)S(1)}, u32[]{:S(2)}, u32[]{:S(2)}) %collective-permute-start.65) | collective-permute-done | bytes 94240 | tf_op jit(solution)/shard_map/ppermute | solution.py:78
  447.8 2.2 shard_map.330
  458.9 3.0 collective-permute-done.69
  (533 shorter events, 149.0 us)
Async XLA Ops:
  7.2 192.8 %all-gather.2.cloned.1.call-start = ((), (), s32[]{:S(2)}) async-start(), calls=%async_computation.1 | async-start | bytes 9732096 | tf_op jit(solution)/shard_map/all_gather | solution.py:645
  8.1 13.3 %collective-permute-start = (s32[16]{0:T(128)S(1)}, s32[16]{0:T(128)S(1)}, u32[]{:S(2)}, u32[]{:S(2)}) collective-permute-start(s32[16]{0:T(128)S(1)} %dynamic_update_slice.5), channel_id=1, source_target_pairs={{0,2},{2,0},{4,6},{6,4},{8,10},{10,8},{12,14},{14,12},{16,18},{18,... | collective-permute-start | bytes 200 | tf_op jit(solution)/shard_map/ppermute | solution.py:78
  9.5 28.8 %collective-permute-start.15 = (bf16[1,1,1,1,1,24,1536]{6,5,4,3,2,1,0:T(8,128)(2,1)S(1)}, bf16[1,1,1,1,1,24,1536]{6,5,4,3,2,1,0:T(8,128)(2,1)}, u32[]{:S(2)}, u32[]{:S(2)}) collective-permute-start(bf16[1,1,1,1,1,24,1536]{6,5,4,3,2,1,0:T(8,128)(2,1)S(1)} %pad_maximum_fusion.25), channel_id=1, source_target_pairs={{0,8},{2,10},{4,12},{6,14},{8,0},{10,2},{12,4},{14,6},{16,24},{18,... | collective-permute-start | bytes 221192 | tf_op jit(solution)/shard_map/ppermute | solution.py:78
  13.9 66.1 %collective-permute-start.16 = (bf16[1,1,1,1,64,768]{5,4,3,2,1,0:T(8,128)(2,1)}, bf16[1,1,1,1,64,768]{5,4,3,2,1,0:T(8,128)(2,1)}, u32[]{:S(2)}, u32[]{:S(2)}) collective-permute-start(bf16[1,1,1,1,64,768]{5,4,3,2,1,0:T(8,128)(2,1)} %reshape_reshape.8), channel_id=1, source_target_pairs={{0,8},{2,10},{4,12},{6,14},{8,0},{10,2},{12,4},{14,6},{16,24},{18,... | collective-permute-start | bytes 294920 | tf_op jit(solution)/shard_map/ppermute | solution.py:78
  14.9 15.3 %collective-permute-start.4 = (bf16[1,1,1,1,1,24,1536]{6,5,4,3,2,1,0:T(8,128)(2,1)S(1)}, bf16[1,1,1,1,1,24,1536]{6,5,4,3,2,1,0:T(8,128)(2,1)S(1)}, u32[]{:S(2)}, u32[]{:S(2)}) collective-permute-start(bf16[1,1,1,1,1,24,1536]{6,5,4,3,2,1,0:T(8,128)(2,1)S(1)} %slice_bitcast_fusion), channel_id=1, source_target_pairs={{0,8},{2,10},{4,12},{6,14},{8,0},{10,2},{12,4},{14,6},{16,24},{18,... | collective-permute-start | bytes 221192 | tf_op jit(solution)/shard_map/ppermute | solution.py:78
  18.5 11.8 %collective-permute-start.3 = (bf16[1,1,1,1,1,24,1536]{6,5,4,3,2,1,0:T(8,128)(2,1)}, bf16[1,1,1,1,1,24,1536]{6,5,4,3,2,1,0:T(8,128)(2,1)}, u32[]{:S(2)}, u32[]{:S(2)}) collective-permute-start(bf16[1,1,1,1,1,24,1536]{6,5,4,3,2,1,0:T(8,128)(2,1)} %pad_maximum_fusion.24), channel_id=1, source_target_pairs={{0,8},{2,10},{4,12},{6,14},{8,0},{10,2},{12,4},{14,6},{16,24},{18,... | collective-permute-start | bytes 221192 | tf_op jit(solution)/shard_map/ppermute | solution.py:78
  19.4 404.4 %reduce-scatter.2.cloned.1.call-start = ((), (), s32[]{:S(2)}) async-start(), calls=%async_computation.2 | async-start | bytes 9732096 | tf_op jit(solution)/shard_map/reduce_scatter | solution.py:754
  29.5 96.9 %collective-permute-start.33 = (bf16[512,768]{1,0:T(8,128)(2,1)S(1)}, bf16[512,768]{1,0:T(8,128)(2,1)S(1)}, u32[]{:S(2)}, u32[]{:S(2)}) collective-permute-start(bf16[512,768]{1,0:T(8,128)(2,1)S(1)} %bitcast.167), channel_id=1, source_target_pairs={{1,2},{2,1},{5,6},{6,5},{9,10},{10,9},{13,14},{14,13},{17,18},{18,... | collective-permute-start | bytes 2359304 | tf_op jit(solution)/shard_map/ppermute | solution.py:167
  32.0 9.9 %collective-permute-start.6 = (s32[16]{0:T(128)S(1)}, s32[16]{0:T(128)S(1)}, u32[]{:S(2)}, u32[]{:S(2)}) collective-permute-start(s32[16]{0:T(128)S(1)} %add.410), channel_id=1, source_target_pairs={{0,4},{2,6},{4,0},{6,2},{8,12},{10,14},{12,8},{14,10},{16,20},{18,... | collective-permute-start | bytes 200 | tf_op jit(solution)/shard_map/ppermute | solution.py:78
  33.9 11.0 %collective-permute-start.29 = (s32[1280]{0:T(1024)S(1)}, s32[1280]{0:T(1024)S(1)}, u32[]{:S(2)}, u32[]{:S(2)}) collective-permute-start(s32[1280]{0:T(1024)S(1)} %pad_add_fusion), channel_id=1, source_target_pairs={{0,2},{3,1},{4,6},{7,5},{8,10},{11,9},{12,14},{15,13},{16,18},{19,... | collective-permute-start | bytes 15368 | tf_op jit(solution)/shard_map/ppermute | solution.py:175
  38.3 14.2 %collective-permute-start.9 = (bf16[1,2,1,1,1,24,1536]{6,5,4,3,2,1,0:T(8,128)(2,1)}, bf16[1,2,1,1,1,24,1536]{6,5,4,3,2,1,0:T(8,128)(2,1)}, u32[]{:S(2)}, u32[]{:S(2)}) collective-permute-start(bf16[1,2,1,1,1,24,1536]{6,5,4,3,2,1,0:T(8,128)(2,1)} %get-tuple-element.138), channel_id=1, source_target_pairs={{0,16},{2,18},{4,20},{6,22},{8,24},{10,26},{12,28},{14,30},{16,0},... | collective-permute-start | bytes 442376 | tf_op jit(solution)/shard_map/ppermute | solution.py:78
  41.9 13.4 %collective-permute-start.10 = (bf16[1,2,1,1,1,24,1536]{6,5,4,3,2,1,0:T(8,128)(2,1)}, bf16[1,2,1,1,1,24,1536]{6,5,4,3,2,1,0:T(8,128)(2,1)}, u32[]{:S(2)}, u32[]{:S(2)}) collective-permute-start(bf16[1,2,1,1,1,24,1536]{6,5,4,3,2,1,0:T(8,128)(2,1)} %get-tuple-element.139), channel_id=1, source_target_pairs={{0,16},{2,18},{4,20},{6,22},{8,24},{10,26},{12,28},{14,30},{16,0},... | collective-permute-start | bytes 442376 | tf_op jit(solution)/shard_map/ppermute | solution.py:78
  44.9 61.2 %collective-permute-start.31 = (bf16[256,1024]{1,0:T(8,128)(2,1)}, bf16[256,1024]{1,0:T(8,128)(2,1)}, u32[]{:S(2)}, u32[]{:S(2)}) collective-permute-start(bf16[256,1024]{1,0:T(8,128)(2,1)} %bitcast.170), channel_id=1, source_target_pairs={{0,2},{3,1},{4,6},{7,5},{8,10},{11,9},{12,14},{15,13},{16,18},{19,... | collective-permute-start | bytes 1572872 | tf_op jit(solution)/shard_map/ppermute | solution.py:175
  52.5 77.8 %collective-permute-start.5 = (bf16[512,768]{1,0:T(8,128)(2,1)S(1)}, bf16[512,768]{1,0:T(8,128)(2,1)}, u32[]{:S(2)}, u32[]{:S(2)}) collective-permute-start(bf16[512,768]{1,0:T(8,128)(2,1)S(1)} %bitcast.169), channel_id=1, source_target_pairs={{1,2},{2,1},{5,6},{6,5},{9,10},{10,9},{13,14},{14,13},{17,18},{18,... | collective-permute-start | bytes 2359304 | tf_op jit(solution)/shard_map/ppermute | solution.py:167
  55.3 17.2 %collective-permute-start.7 = (f32[8,1,4608]{2,1,0:T(1,128)S(1)}, f32[8,1,4608]{2,1,0:T(1,128)S(1)}, u32[]{:S(2)}, u32[]{:S(2)}) collective-permute-start(f32[8,1,4608]{2,1,0:T(1,128)S(1)} %constant_dynamic-slice_fusion.23), channel_id=1, source_target_pairs={{0,1},{1,0},{2,3},{3,2},{4,5},{5,4},{6,7},{7,6},{8,9},{9,8},{10,11... | collective-permute-start | bytes 442376 | tf_op jit(solution)/shard_map/ppermute | solution.py:78
  87.3 14.2 %collective-permute-start.13 = (bf16[2,2,1,1,1,24,1536]{6,5,4,3,2,1,0:T(8,128)(2,1)S(1)}, bf16[2,2,1,1,1,24,1536]{6,5,4,3,2,1,0:T(8,128)(2,1)S(1)}, u32[]{:S(2)}, u32[]{:S(2)}) collective-permute-start(bf16[2,2,1,1,1,24,1536]{6,5,4,3,2,1,0:T(8,128)(2,1)S(1)} %pad_maximum_fusion.14), channel_id=1, source_target_pairs={{0,4},{2,6},{4,0},{6,2},{8,12},{10,14},{12,8},{14,10},{16,20},{18,... | collective-permute-start | bytes 884744 | tf_op jit(solution)/shard_map/ppermute | solution.py:78
  92.8 10.6 %collective-permute-start.14 = (bf16[2,2,1,1,1,24,1536]{6,5,4,3,2,1,0:T(8,128)(2,1)S(1)}, bf16[2,2,1,1,1,24,1536]{6,5,4,3,2,1,0:T(8,128)(2,1)S(1)}, u32[]{:S(2)}, u32[]{:S(2)}) collective-permute-start(bf16[2,2,1,1,1,24,1536]{6,5,4,3,2,1,0:T(8,128)(2,1)S(1)} %pad_maximum_fusion.15), channel_id=1, source_target_pairs={{0,1},{1,0},{2,3},{3,2},{4,5},{5,4},{6,7},{7,6},{8,9},{9,8},{10,11... | collective-permute-start | bytes 884744 | tf_op jit(solution)/shard_map/ppermute | solution.py:78
  103.6 21.8 %collective-permute-start.20 = (bf16[1,2,1,1,1,24,1536]{6,5,4,3,2,1,0:T(8,128)(2,1)S(1)}, bf16[1,2,1,1,1,24,1536]{6,5,4,3,2,1,0:T(8,128)(2,1)S(1)}, u32[]{:S(2)}, u32[]{:S(2)}) collective-permute-start(bf16[1,2,1,1,1,24,1536]{6,5,4,3,2,1,0:T(8,128)(2,1)S(1)} %pad_maximum_fusion.22), channel_id=1, source_target_pairs={{0,16},{2,18},{4,20},{6,22},{8,24},{10,26},{12,28},{14,30},{16,0},... | collective-permute-start | bytes 442376 | tf_op jit(solution)/shard_map/ppermute | solution.py:78
  106.1 24.1 %collective-permute-start.21 = (bf16[1,2,1,1,64,768]{5,4,3,2,1,0:T(8,128)(2,1)S(1)}, bf16[1,2,1,1,64,768]{5,4,3,2,1,0:T(8,128)(2,1)S(1)}, u32[]{:S(2)}, u32[]{:S(2)}) collective-permute-start(bf16[1,2,1,1,64,768]{5,4,3,2,1,0:T(8,128)(2,1)S(1)} %pad_maximum_fusion.19), channel_id=1, source_target_pairs={{0,16},{2,18},{4,20},{6,22},{8,24},{10,26},{12,28},{14,30},{16,0},... | collective-permute-start | bytes 589832 | tf_op jit(solution)/shard_map/ppermute | solution.py:78
  106.7 23.9 %collective-permute-start.18 = (bf16[2,2,2,1,1,24,1536]{6,5,4,3,2,1,0:T(8,128)(2,1)S(1)}, bf16[2,2,2,1,1,24,1536]{6,5,4,3,2,1,0:T(8,128)(2,1)S(1)}, u32[]{:S(2)}, u32[]{:S(2)}) collective-permute-start(bf16[2,2,2,1,1,24,1536]{6,5,4,3,2,1,0:T(8,128)(2,1)S(1)} %pad_maximum_fusion.10), channel_id=1, source_target_pairs={{0,1},{1,0},{2,3},{3,2},{4,5},{5,4},{6,7},{7,6},{8,9},{9,8},{10,11... | collective-permute-start | bytes 1769480 | tf_op jit(solution)/shard_map/ppermute | solution.py:78
  125.4 15.4 %collective-permute-start.19 = (bf16[2,2,1,1,2,24,1536]{6,5,4,3,2,1,0:T(8,128)(2,1)S(1)}, bf16[2,2,1,1,2,24,1536]{6,5,4,3,2,1,0:T(8,128)(2,1)S(1)}, u32[]{:S(2)}, u32[]{:S(2)}) collective-permute-start(bf16[2,2,1,1,2,24,1536]{6,5,4,3,2,1,0:T(8,128)(2,1)S(1)} %pad_maximum_fusion.11), channel_id=1, source_target_pairs={{0,4},{2,6},{4,0},{6,2},{8,12},{10,14},{12,8},{14,10},{16,20},{18,... | collective-permute-start | bytes 1769480 | tf_op jit(solution)/shard_map/ppermute | solution.py:78
  141.0 8.3 %collective-permute-start.24 = (bf16[2,2,1,1,1,24,1536]{6,5,4,3,2,1,0:T(8,128)(2,1)S(1)}, bf16[2,2,1,1,1,24,1536]{6,5,4,3,2,1,0:T(8,128)(2,1)S(1)}, u32[]{:S(2)}, u32[]{:S(2)}) collective-permute-start(bf16[2,2,1,1,1,24,1536]{6,5,4,3,2,1,0:T(8,128)(2,1)S(1)} %pad_maximum_fusion.16), channel_id=1, source_target_pairs={{0,4},{2,6},{4,0},{6,2},{8,12},{10,14},{12,8},{14,10},{16,20},{18,... | collective-permute-start | bytes 884744 | tf_op jit(solution)/shard_map/ppermute | solution.py:78
  142.5 12.1 %collective-permute-start.26 = (bf16[2,2,1,1,64,768]{5,4,3,2,1,0:T(8,128)(2,1)S(1)}, bf16[2,2,1,1,64,768]{5,4,3,2,1,0:T(8,128)(2,1)S(1)}, u32[]{:S(2)}, u32[]{:S(2)}) collective-permute-start(bf16[2,2,1,1,64,768]{5,4,3,2,1,0:T(8,128)(2,1)S(1)} %pad_maximum_fusion.13), channel_id=1, source_target_pairs={{0,1},{1,0},{2,3},{3,2},{4,5},{5,4},{6,7},{7,6},{8,9},{9,8},{10,11... | collective-permute-start | bytes 1179656 | tf_op jit(solution)/shard_map/ppermute | solution.py:78
  143.5 12.2 %collective-permute-start.22 = (bf16[2,2,2,1,2,24,1536]{6,5,4,3,2,1,0:T(8,128)(2,1)S(1)}, bf16[2,2,2,1,2,24,1536]{6,5,4,3,2,1,0:T(8,128)(2,1)S(1)}, u32[]{:S(2)}, u32[]{:S(2)}) collective-permute-start(bf16[2,2,2,1,2,24,1536]{6,5,4,3,2,1,0:T(8,128)(2,1)S(1)} %pad_maximum_fusion.6), channel_id=1, source_target_pairs={{0,2},{2,0},{4,6},{6,4},{8,10},{10,8},{12,14},{14,12},{16,18},{18,... | collective-permute-start | bytes 3538952 | tf_op jit(solution)/shard_map/ppermute | solution.py:78
  143.5 12.7 %collective-permute-start.23 = (bf16[2,2,2,1,2,24,1536]{6,5,4,3,2,1,0:T(8,128)(2,1)S(1)}, bf16[2,2,2,1,2,24,1536]{6,5,4,3,2,1,0:T(8,128)(2,1)S(1)}, u32[]{:S(2)}, u32[]{:S(2)}) collective-permute-start(bf16[2,2,2,1,2,24,1536]{6,5,4,3,2,1,0:T(8,128)(2,1)S(1)} %pad_maximum_fusion.7), channel_id=1, source_target_pairs={{0,2},{2,0},{4,6},{6,4},{8,10},{10,8},{12,14},{14,12},{16,18},{18,... | collective-permute-start | bytes 3538952 | tf_op jit(solution)/shard_map/ppermute | solution.py:78
  149.4 15.9 %collective-permute-start.25 = (bf16[2,2,2,1,1,24,1536]{6,5,4,3,2,1,0:T(8,128)(2,1)S(1)}, bf16[2,2,2,1,1,24,1536]{6,5,4,3,2,1,0:T(8,128)(2,1)S(1)}, u32[]{:S(2)}, u32[]{:S(2)}) collective-permute-start(bf16[2,2,2,1,1,24,1536]{6,5,4,3,2,1,0:T(8,128)(2,1)S(1)} %pad_maximum_fusion.12), channel_id=1, source_target_pairs={{0,1},{1,0},{2,3},{3,2},{4,5},{5,4},{6,7},{7,6},{8,9},{9,8},{10,11... | collective-permute-start | bytes 1769480 | tf_op jit(solution)/shard_map/ppermute | solution.py:78
  154.7 15.8 %collective-permute-start.27 = (bf16[2,2,1,1,64,1536]{5,4,3,2,1,0:T(8,128)(2,1)S(1)}, bf16[2,2,1,1,64,1536]{5,4,3,2,1,0:T(8,128)(2,1)S(1)}, u32[]{:S(2)}, u32[]{:S(2)}) collective-permute-start(bf16[2,2,1,1,64,1536]{5,4,3,2,1,0:T(8,128)(2,1)S(1)} %pad_maximum_fusion.9), channel_id=1, source_target_pairs={{0,4},{2,6},{4,0},{6,2},{8,12},{10,14},{12,8},{14,10},{16,20},{18,... | collective-permute-start | bytes 2359304 | tf_op jit(solution)/shard_map/ppermute | solution.py:78
  159.7 12.1 %collective-permute-start.28 = (bf16[512,1536]{1,0:T(8,128)(2,1)S(1)}, bf16[512,1536]{1,0:T(8,128)(2,1)S(1)}, u32[]{:S(2)}, u32[]{:S(2)}) collective-permute-start(bf16[512,1536]{1,0:T(8,128)(2,1)S(1)} %convolution_convert_fusion.refs_1_.refs_2_.refs_4_.refs_5_), channel_id=1, source_target_pairs={{0,2},{2,0},{4,6},{6,4},{8,10},{10,8},{12,14},{14,12},{16,18},{18,... | collective-permute-start | bytes 4718600 | tf_op jit(solution)/shard_map/ppermute | solution.py:78
  171.8 16.7 %collective-permute-start.30 = (bf16[2,2,2,1,2,24,1536]{6,5,4,3,2,1,0:T(8,128)(2,1)S(1)}, bf16[2,2,2,1,2,24,1536]{6,5,4,3,2,1,0:T(8,128)(2,1)S(1)}, u32[]{:S(2)}, u32[]{:S(2)}) collective-permute-start(bf16[2,2,2,1,2,24,1536]{6,5,4,3,2,1,0:T(8,128)(2,1)S(1)} %pad_maximum_fusion.8), channel_id=1, source_target_pairs={{0,2},{2,0},{4,6},{6,4},{8,10},{10,8},{12,14},{14,12},{16,18},{18,... | collective-permute-start | bytes 3538952 | tf_op jit(solution)/shard_map/ppermute | solution.py:78
  171.9 18.3 %collective-permute-start.32 = (bf16[2,2,2,1,64,1536]{5,4,3,2,1,0:T(8,128)(2,1)S(1)}, bf16[2,2,2,1,64,1536]{5,4,3,2,1,0:T(8,128)(2,1)S(1)}, u32[]{:S(2)}, u32[]{:S(2)}) collective-permute-start(bf16[2,2,2,1,64,1536]{5,4,3,2,1,0:T(8,128)(2,1)S(1)} %pad_maximum_fusion.4), channel_id=1, source_target_pairs={{0,2},{2,0},{4,6},{6,4},{8,10},{10,8},{12,14},{14,12},{16,18},{18,... | collective-permute-start | bytes 4718600 | tf_op jit(solution)/shard_map/ppermute | solution.py:78
  256.4 23.1 %collective-permute-start.36 = (bf16[2,2,2,1,1,24,1536]{6,5,4,3,2,1,0:T(8,128)(2,1)S(1)}, bf16[2,2,2,1,1,24,1536]{6,5,4,3,2,1,0:T(8,128)(2,1)S(1)}, u32[]{:S(2)}, u32[]{:S(2)}) collective-permute-start(bf16[2,2,2,1,1,24,1536]{6,5,4,3,2,1,0:T(8,128)(2,1)S(1)} %constant_dynamic-slice_fusion.17), channel_id=1, source_target_pairs={{0,1},{1,0},{2,3},{3,2},{4,5},{5,4},{6,7},{7,6},{8,9},{9,8},{10,11... | collective-permute-start | bytes 1769480 | tf_op jit(solution)/shard_map/ppermute | solution.py:78
  257.3 22.4 %collective-permute-start.37 = (bf16[2,2,1,1,64,1536]{5,4,3,2,1,0:T(8,128)(2,1)S(1)}, bf16[2,2,1,1,64,1536]{5,4,3,2,1,0:T(8,128)(2,1)S(1)}, u32[]{:S(2)}, u32[]{:S(2)}) collective-permute-start(bf16[2,2,1,1,64,1536]{5,4,3,2,1,0:T(8,128)(2,1)S(1)} %constant_dynamic-slice_fusion.16), channel_id=1, source_target_pairs={{0,4},{2,6},{4,0},{6,2},{8,12},{10,14},{12,8},{14,10},{16,20},{18,... | collective-permute-start | bytes 2359304 | tf_op jit(solution)/shard_map/ppermute | solution.py:78
  281.1 11.5 %collective-permute-start.40 = (bf16[512,1536]{1,0:T(8,128)(2,1)}, bf16[512,1536]{1,0:T(8,128)(2,1)}, u32[]{:S(2)}, u32[]{:S(2)}) collective-permute-start(bf16[512,1536]{1,0:T(8,128)(2,1)} %get-tuple-element.190), channel_id=1, source_target_pairs={{0,2},{2,0},{4,6},{6,4},{8,10},{10,8},{12,14},{14,12},{16,18},{18,... | collective-permute-start | bytes 4718600 | tf_op jit(solution)/shard_map/ppermute | solution.py:78
  281.9 9.7 %collective-permute-start.38 = (bf16[2,2,1,1,1,24,1536]{6,5,4,3,2,1,0:T(8,128)(2,1)}, bf16[2,2,1,1,1,24,1536]{6,5,4,3,2,1,0:T(8,128)(2,1)}, u32[]{:S(2)}, u32[]{:S(2)}) collective-permute-start(bf16[2,2,1,1,1,24,1536]{6,5,4,3,2,1,0:T(8,128)(2,1)} %constant_dynamic-slice_fusion.15), channel_id=1, source_target_pairs={{0,4},{2,6},{4,0},{6,2},{8,12},{10,14},{12,8},{14,10},{16,20},{18,... | collective-permute-start | bytes 884744 | tf_op jit(solution)/shard_map/ppermute | solution.py:78
  284.6 11.3 %collective-permute-start.39 = (bf16[2,2,1,1,64,768]{5,4,3,2,1,0:T(8,128)(2,1)S(1)}, bf16[2,2,1,1,64,768]{5,4,3,2,1,0:T(8,128)(2,1)S(1)}, u32[]{:S(2)}, u32[]{:S(2)}) collective-permute-start(bf16[2,2,1,1,64,768]{5,4,3,2,1,0:T(8,128)(2,1)S(1)} %constant_dynamic-slice_fusion.14), channel_id=1, source_target_pairs={{0,1},{1,0},{2,3},{3,2},{4,5},{5,4},{6,7},{7,6},{8,9},{9,8},{10,11... | collective-permute-start | bytes 1179656 | tf_op jit(solution)/shard_map/ppermute | solution.py:78
  301.8 12.1 %collective-permute-start.41 = (bf16[1,2,1,1,1,24,1536]{6,5,4,3,2,1,0:T(8,128)(2,1)S(1)}, bf16[1,2,1,1,1,24,1536]{6,5,4,3,2,1,0:T(8,128)(2,1)S(1)}, u32[]{:S(2)}, u32[]{:S(2)}) collective-permute-start(bf16[1,2,1,1,1,24,1536]{6,5,4,3,2,1,0:T(8,128)(2,1)S(1)} %constant_dynamic-slice_fusion.13), channel_id=1, source_target_pairs={{0,16},{2,18},{4,20},{6,22},{8,24},{10,26},{12,28},{14,30},{16,0},... | collective-permute-start | bytes 442376 | tf_op jit(solution)/shard_map/ppermute | solution.py:78
  301.9 16.1 %collective-permute-start.42 = (bf16[1,2,1,1,64,768]{5,4,3,2,1,0:T(8,128)(2,1)S(1)}, bf16[1,2,1,1,64,768]{5,4,3,2,1,0:T(8,128)(2,1)S(1)}, u32[]{:S(2)}, u32[]{:S(2)}) collective-permute-start(bf16[1,2,1,1,64,768]{5,4,3,2,1,0:T(8,128)(2,1)S(1)} %constant_dynamic-slice_fusion.12), channel_id=1, source_target_pairs={{0,16},{2,18},{4,20},{6,22},{8,24},{10,26},{12,28},{14,30},{16,0},... | collective-permute-start | bytes 589832 | tf_op jit(solution)/shard_map/ppermute | solution.py:78
  305.0 13.1 %collective-permute-start.44 = (bf16[2,2,2,1,2,24,1536]{6,5,4,3,2,1,0:T(8,128)(2,1)S(1)}, bf16[2,2,2,1,2,24,1536]{6,5,4,3,2,1,0:T(8,128)(2,1)S(1)}, u32[]{:S(2)}, u32[]{:S(2)}) collective-permute-start(bf16[2,2,2,1,2,24,1536]{6,5,4,3,2,1,0:T(8,128)(2,1)S(1)} %constant_dynamic-slice_fusion.10), channel_id=1, source_target_pairs={{0,2},{2,0},{4,6},{6,4},{8,10},{10,8},{12,14},{14,12},{16,18},{18,... | collective-permute-start | bytes 3538952 | tf_op jit(solution)/shard_map/ppermute | solution.py:78
  305.8 12.6 %collective-permute-start.43 = (bf16[2,2,2,1,2,24,1536]{6,5,4,3,2,1,0:T(8,128)(2,1)S(1)}, bf16[2,2,2,1,2,24,1536]{6,5,4,3,2,1,0:T(8,128)(2,1)S(1)}, u32[]{:S(2)}, u32[]{:S(2)}) collective-permute-start(bf16[2,2,2,1,2,24,1536]{6,5,4,3,2,1,0:T(8,128)(2,1)S(1)} %constant_dynamic-slice_fusion.11), channel_id=1, source_target_pairs={{0,2},{2,0},{4,6},{6,4},{8,10},{10,8},{12,14},{14,12},{16,18},{18,... | collective-permute-start | bytes 3538952 | tf_op jit(solution)/shard_map/ppermute | solution.py:78
  319.1 6.7 %collective-permute-start.46 = (bf16[1,1,1,1,64,768]{5,4,3,2,1,0:T(8,128)(2,1)S(1)}, bf16[1,1,1,1,64,768]{5,4,3,2,1,0:T(8,128)(2,1)S(1)}, u32[]{:S(2)}, u32[]{:S(2)}) collective-permute-start(bf16[1,1,1,1,64,768]{5,4,3,2,1,0:T(8,128)(2,1)S(1)} %constant_dynamic-slice_fusion.8), channel_id=1, source_target_pairs={{0,8},{2,10},{4,12},{6,14},{8,0},{10,2},{12,4},{14,6},{16,24},{18,... | collective-permute-start | bytes 294920 | tf_op jit(solution)/shard_map/ppermute | solution.py:78
  321.2 15.2 %collective-permute-start.48 = (bf16[2,2,1,1,2,24,1536]{6,5,4,3,2,1,0:T(8,128)(2,1)S(1)}, bf16[2,2,1,1,2,24,1536]{6,5,4,3,2,1,0:T(8,128)(2,1)S(1)}, u32[]{:S(2)}, u32[]{:S(2)}) collective-permute-start(bf16[2,2,1,1,2,24,1536]{6,5,4,3,2,1,0:T(8,128)(2,1)S(1)} %constant_dynamic-slice_fusion.6), channel_id=1, source_target_pairs={{0,4},{2,6},{4,0},{6,2},{8,12},{10,14},{12,8},{14,10},{16,20},{18,... | collective-permute-start | bytes 1769480 | tf_op jit(solution)/shard_map/ppermute | solution.py:78
  322.3 16.3 %collective-permute-start.47 = (bf16[2,2,2,1,1,24,1536]{6,5,4,3,2,1,0:T(8,128)(2,1)S(1)}, bf16[2,2,2,1,1,24,1536]{6,5,4,3,2,1,0:T(8,128)(2,1)S(1)}, u32[]{:S(2)}, u32[]{:S(2)}) collective-permute-start(bf16[2,2,2,1,1,24,1536]{6,5,4,3,2,1,0:T(8,128)(2,1)S(1)} %constant_dynamic-slice_fusion.7), channel_id=1, source_target_pairs={{0,1},{1,0},{2,3},{3,2},{4,5},{5,4},{6,7},{7,6},{8,9},{9,8},{10,11... | collective-permute-start | bytes 1769480 | tf_op jit(solution)/shard_map/ppermute | solution.py:78
  352.0 13.2 %collective-permute-start.58 = (bf16[2,2,1,1,1,24,1536]{6,5,4,3,2,1,0:T(8,128)(2,1)}, bf16[2,2,1,1,1,24,1536]{6,5,4,3,2,1,0:T(8,128)(2,1)}, u32[]{:S(2)}, u32[]{:S(2)}) collective-permute-start(bf16[2,2,1,1,1,24,1536]{6,5,4,3,2,1,0:T(8,128)(2,1)} %constant_dynamic-slice_fusion.2), channel_id=1, source_target_pairs={{0,1},{1,0},{2,3},{3,2},{4,5},{5,4},{6,7},{7,6},{8,9},{9,8},{10,11... | collective-permute-start | bytes 884744 | tf_op jit(solution)/shard_map/ppermute | solution.py:78
  354.1 12.3 %collective-permute-start.55 = (bf16[2,2,1,1,1,24,1536]{6,5,4,3,2,1,0:T(8,128)(2,1)}, bf16[2,2,1,1,1,24,1536]{6,5,4,3,2,1,0:T(8,128)(2,1)}, u32[]{:S(2)}, u32[]{:S(2)}) collective-permute-start(bf16[2,2,1,1,1,24,1536]{6,5,4,3,2,1,0:T(8,128)(2,1)} %constant_dynamic-slice_fusion.5), channel_id=1, source_target_pairs={{0,4},{2,6},{4,0},{6,2},{8,12},{10,14},{12,8},{14,10},{16,20},{18,... | collective-permute-start | bytes 884744 | tf_op jit(solution)/shard_map/ppermute | solution.py:78
  356.7 7.4 %collective-permute-start.54 = (f32[2,2,2,1,4608]{4,3,2,1,0:T(1,128)S(1)}, f32[2,2,2,1,4608]{4,3,2,1,0:T(1,128)S(1)}, u32[]{:S(2)}, u32[]{:S(2)}) collective-permute-start(f32[2,2,2,1,4608]{4,3,2,1,0:T(1,128)S(1)} %pad_maximum_fusion.23), channel_id=1, source_target_pairs={{0,1},{1,0},{2,3},{3,2},{4,5},{5,4},{6,7},{7,6},{8,9},{9,8},{10,11... | collective-permute-start | bytes 442376 | tf_op jit(solution)/shard_map/ppermute | solution.py:78
  359.4 99.2 %collective-permute-start.50 = (bf16[2,512,768]{2,1,0:T(8,128)(2,1)}, bf16[2,512,768]{2,1,0:T(8,128)(2,1)}, u32[]{:S(2)}, u32[]{:S(2)}) collective-permute-start(bf16[2,512,768]{2,1,0:T(8,128)(2,1)} %pad_maximum_fusion.5), channel_id=1, source_target_pairs={{1,2},{2,1},{5,6},{6,5},{9,10},{10,9},{13,14},{14,13},{17,18},{18,... | collective-permute-start | bytes 4718600 | tf_op jit(solution)/shard_map/ppermute | solution.py:167
  366.4 9.9 %collective-permute-start.59 = (bf16[1,2,1,1,1,24,1536]{6,5,4,3,2,1,0:T(8,128)(2,1)S(1)}, bf16[1,2,1,1,1,24,1536]{6,5,4,3,2,1,0:T(8,128)(2,1)S(1)}, u32[]{:S(2)}, u32[]{:S(2)}) collective-permute-start(bf16[1,2,1,1,1,24,1536]{6,5,4,3,2,1,0:T(8,128)(2,1)S(1)} %constant_dynamic-slice_fusion.1), channel_id=1, source_target_pairs={{0,16},{2,18},{4,20},{6,22},{8,24},{10,26},{12,28},{14,30},{16,0},... | collective-permute-start | bytes 442376 | tf_op jit(solution)/shard_map/ppermute | solution.py:78
  367.6 11.8 %collective-permute-start.56 = (bf16[1,2,1,1,1,24,1536]{6,5,4,3,2,1,0:T(8,128)(2,1)S(1)}, bf16[1,2,1,1,1,24,1536]{6,5,4,3,2,1,0:T(8,128)(2,1)S(1)}, u32[]{:S(2)}, u32[]{:S(2)}) collective-permute-start(bf16[1,2,1,1,1,24,1536]{6,5,4,3,2,1,0:T(8,128)(2,1)S(1)} %constant_dynamic-slice_fusion.4), channel_id=1, source_target_pairs={{0,16},{2,18},{4,20},{6,22},{8,24},{10,26},{12,28},{14,30},{16,0},... | collective-permute-start | bytes 442376 | tf_op jit(solution)/shard_map/ppermute | solution.py:78
  (132 other events, 1261.6 us)
Sparse Core Ops, SparseCore 0:
  19.5 109.6 all-gather.1
  283.6 140.0 reduce-scatter.1

commit v3 on v2

--- a/solution.py
+++ b/solution.py
@@ -25,7 +25,9 @@
 SCALE_FLOOR = 0.001
 SCORE_SCALE = 0.125
 MASKED_SCORE = -1e30
-ALL = ("dp", "head")
+DP = ("far", "near", "core")
+ALL = DP + ("head",)
+HEAD = ("head",)
 PAIR = 2 * HD
 PAIRS = D // PAIR
 
@@ -50,23 +52,23 @@
 
 
 def core_link():
-    return ("dp", 1)
+    return (DP, 1)
 
 
 def row_link():
-    return ("head", 1)
+    return (HEAD, 1)
 
 
 def far_links():
     masks, mask = [], 2
-    while mask < lax.axis_size("dp"):
+    while mask < lax.axis_size(DP):
         masks.append(mask)
         mask = mask * 2
-    return [("dp", mask) for mask in masks]
+    return [(DP, mask) for mask in masks]
 
 
 def dp_bits():
-    return lax.axis_size("dp").bit_length() - 1
+    return lax.axis_size(DP).bit_length() - 1
 
 
 def bit_of(link):
@@ -79,7 +81,7 @@
 
 
 def dim_of(link, head):
-    if link[0] == "head":
+    if link[0] == HEAD:
         return {"first": 0, "last": dp_bits(), "columns": dp_bits() + 1}[head]
     return (1 if head == "first" else 0) + dp_bits() - link[1].bit_length()
 
@@ -124,12 +126,12 @@
     return values
 
 
-def gather_chain(shard, head, row_early):
-    block = shard.reshape((1,) * leading(head) + shard.shape)
-    far = far_links()
-    plane = [row_link(), far[0]] if row_early else [far[0], row_link()]
-    links = far[1:] + plane + [core_link()]
+def gather_chain(block, head, links):
     return Chain(block, [lambda state, link=link: grow(state, link, head) for link in links])
+
+
+def with_bits(shard, head):
+    return shard.reshape((1,) * leading(head) + shard.shape)
 
 
 def scatter_chain(matrix, head, row_early):
@@ -158,18 +160,22 @@
     return bit_of(core_link()) == bit_of(row_link())
 
 
-def swap_place(values):
+def swap_only(values):
     pairs = []
-    for place in range(lax.axis_size("dp")):
+    for place in range(lax.axis_size(DP)):
         for head in range(2):
             if place & 1 != head:
                 pairs.append((place * 2 + head, ((place & ~1) | head) * 2 + (place & 1)))
-    return jnp.where(on_own_chip(), values, lax.ppermute(values, ALL, pairs))
+    return lax.ppermute(values, ALL, pairs)
+
+
+def swap_place(values):
+    return jnp.where(on_own_chip(), values, swap_only(values))
 
 
 def from_clip_core(values):
     pairs = []
-    for place in range(0, lax.axis_size("dp"), 2):
+    for place in range(0, lax.axis_size(DP), 2):
         for head in range(2):
             pairs.append(((place + head) * 2 + head, (place + 1 - head) * 2 + head))
     return jnp.where(on_own_chip(), values, lax.ppermute(values, ALL, pairs))
@@ -422,9 +428,18 @@
         [(cross_pair, 0, D)],
         [(cross_pair, D, D)],
         [(text_pair, 0, D)],
-        [(mlp, 0, HALF)],
-        [(mlp, HALF, HALF)],
+        [(mlp.at[0], 0, HALF)],
+        [(mlp.at[1], 0, HALF)],
     ]
+
+
+def joined_pieces(refs):
+    square, text_pair, mlp = refs
+    parts, at = [], 0
+    for place in range(5):
+        parts.append((square, at, COL_SIZES[place]))
+        at += COL_SIZES[place]
+    return parts + [(text_pair, 0, D), (mlp, 0, HALF), (mlp, HALF, HALF)]
 
 
 def statistics_kernel(place_ref, weight_ref, *refs):
@@ -471,7 +486,7 @@
 def update_kernel(place_ref, sums_ref, row_ref, col_ref, *refs):
     grad_refs, outs = refs[:6], refs[6:]
     row_out, col_out, norm_out, total_out = outs[:4]
-    clipped_refs, update_refs = outs[4:12], outs[12:20]
+    clipped_refs, update_refs = outs[4:12], joined_pieces(outs[12:15])
     data_at, head_at = place_ref[0], place_ref[1]
     flat_at = data_at * 2 + head_at
     row_sums = sums_ref[0:ROW_LINES, :]
@@ -524,7 +539,9 @@
                 piece = ref[:, first + line * LINE : first + (line + 1) * LINE] * factor
                 update = piece * (down * across[line_at : line_at + 1, :])
                 clipped_refs[place][:, line_at * LINE : (line_at + 1) * LINE] = piece
-                update_refs[place][:, line_at * LINE : (line_at + 1) * LINE] = update
+                update_ref, update_at, _ = update_refs[place]
+                update_at += line_at * LINE
+                update_ref[:, update_at : update_at + LINE] = update
                 square = square + update * update
                 line_at += 1
         total = jnp.sum(jnp.sum(square, axis=0, keepdims=True), axis=1, keepdims=True)
@@ -533,6 +550,7 @@
 
 
 def apply_kernel(total_ref, weight_ref, *refs):
+    master_refs, update_refs = joined_pieces(refs[:3]), joined_pieces(refs[3:6])
     for place in range(8):
         entries = float(ROW_SIZES[place] * COL_SIZES[place])
         total = lane_of(total_ref[...], place)
@@ -540,17 +558,20 @@
         limit = jnp.maximum(1.0, jnp.sqrt(total / entries) / CLIP_UPDATE)
         rate = RELATIVE_RATE * jnp.maximum(SCALE_FLOOR, jnp.sqrt(weight / entries))
         scale = rate / limit
-        refs[16 + place][...] = refs[place][...] - scale * refs[8 + place][...]
+        ref, at, columns = master_refs[place]
+        update = update_refs[place][0][:, at : at + columns]
+        refs[6 + place][...] = ref[:, at : at + columns] - scale * update
 
 
 def weight_kernel(*refs):
     lane = lax.broadcasted_iota(jnp.int32, (1, LINE), 1)
     totals = jnp.zeros((1, LINE), FLOAT)
     for place in range(8):
-        matrix = refs[place][...]
+        ref, at, columns = joined_pieces(refs[:3])[place]
+        matrix = ref[:, at : at + columns]
         total = jnp.sum(jnp.sum(matrix * matrix, axis=0, keepdims=True), axis=1, keepdims=True)
         totals = jnp.where(lane == place, total, totals)
-    refs[8][...] = totals
+    refs[3][...] = totals
 
 
 def whole_call(kernel, shapes, *operands, places=0):
@@ -566,33 +587,85 @@
     )(*operands)
 
 
-def mlp_outer_kernel(input_ref, grad_ref, pre_ref, act_ref, out_ref):
-    turn = (((0,), (0,)), ((), ()))
-    width = pre_ref.shape[2]
-    for at in range(0, width, D):
-        first = lax.dot_general(
-            input_ref[...], pre_ref[0, :, at : at + D], turn, preferred_element_type=FLOAT
-        )
-        out_ref[0, :, at : at + D] = first.astype(BFLOAT)
-        second = lax.dot_general(
-            grad_ref[...], act_ref[0, :, at : at + D], turn, preferred_element_type=FLOAT
-        )
-        out_ref[0, :, width + at : width + at + D] = second.astype(BFLOAT)
-
-
-def mlp_outer(mlp_input, mlp_grad, pre_grad, hidden_act):
-    frames, width = mlp_input.shape[0], pre_grad.shape[2]
-    whole = pl.BlockSpec((frames, D), lambda half: (0, 0))
-    hidden = pl.BlockSpec((1, frames, width), lambda half: (half, 0, 0))
+GELU_WIDTH = 0.7978845608028654
+GELU_CUBE = 0.044715
+
+
+def gelu_parts(values):
+    square = values * values
+    bend = jnp.tanh(values * (GELU_WIDTH + GELU_WIDTH * GELU_CUBE * square))
+    half = 0.5 + 0.5 * bend
+    slope = GELU_WIDTH + 3.0 * GELU_WIDTH * GELU_CUBE * square
+    return values * half, half + (0.5 * values) * (1.0 - bend * bend) * slope
+
+
+def mlp_kernel(
+    input_ref, grad_ref, fc1_ref, fc2_ref, branch_ref, in_grad_ref, part_ref, input_t, grad_t
+):
+    step = pl.program_id(0) * pl.num_programs(1) + pl.program_id(1)
+
+    @pl.when(step == 0)
+    def _():
+        input_t[...] = input_ref[...].T
+        grad_t[...] = grad_ref[...].T
+
+    fc1, fc2 = fc1_ref[0], fc2_ref[0]
+    act, slope = gelu_parts(nn(input_ref[...], fc1))
+    act = act.astype(BFLOAT)
+    pre_grad = (nn(grad_ref[...], fc2) * slope).astype(BFLOAT)
+    branch, in_grad = nt(act, fc2), nt(pre_grad, fc1)
+
+    @pl.when(step == 0)
+    def _():
+        branch_ref[...] = branch
+        in_grad_ref[...] = in_grad
+
+    @pl.when(step > 0)
+    def _():
+        branch_ref[...] += branch
+        in_grad_ref[...] += in_grad
+
+    far, rows = part_ref.shape[2], part_ref.shape[4]
+    for kind, product in enumerate((nn(input_t[...], pre_grad), nn(grad_t[...], act))):
+        product = product.astype(BFLOAT)
+        for place in range(4 * far):
+            part_ref[0, place % 4, place // 4, kind] = product[place * rows : (place + 1) * rows]
+
+
+MLP_TILE = 512
+
+
+def mlp_both(mlp_input, mlp_grad, weights):
+    frames = mlp_input.shape[0]
+    far = lax.axis_size("far")
+    rows = D // (4 * far)
+    tiles = HALF // MLP_TILE
+    whole = pl.BlockSpec((frames, D), lambda half, tile: (0, 0))
     return pl.pallas_call(
-        mlp_outer_kernel,
-        grid=(2,),
-        in_specs=[whole, whole, hidden, hidden],
-        out_specs=pl.BlockSpec((1, D, 2 * width), lambda half: (half, 0, 0)),
-        out_shape=jax.ShapeDtypeStruct((2, D, 2 * width), BFLOAT),
+        mlp_kernel,
+        grid=(2, tiles),
+        in_specs=[
+            whole,
+            whole,
+            pl.BlockSpec((1, D, MLP_TILE), lambda half, tile: (half, 0, tile)),
+            pl.BlockSpec((1, D, MLP_TILE), lambda half, tile: (half, 0, tile + tiles)),
+        ],
+        out_specs=[
+            whole,
+            whole,
+            pl.BlockSpec(
+                (1, 4, far, 2, rows, MLP_TILE), lambda half, tile: (half, 0, 0, 0, 0, tile)
+            ),
+        ],
+        out_shape=[
+            jax.ShapeDtypeStruct((frames, D), FLOAT),
+            jax.ShapeDtypeStruct((frames, D), FLOAT),
+            jax.ShapeDtypeStruct((2, 4, far, 2, rows, HALF), BFLOAT),
+        ],
+        scratch_shapes=[pltpu.VMEM((D, frames), BFLOAT), pltpu.VMEM((D, frames), BFLOAT)],
         compiler_params=KERNEL,
         cost_estimate=LIGHT,
-    )(mlp_input, mlp_grad, pre_grad, hidden_act)
+    )(mlp_input, mlp_grad, weights, weights)
 
 
 def per_device(
@@ -613,36 +686,46 @@
     row_state,
     col_state,
 ):
-    clips = lax.axis_size("dp")
+    clips = lax.axis_size(DP)
     devices = clips * 2
-    data_at = lax.axis_index("dp")
+    data_at = lax.axis_index(DP)
     head_at = lax.axis_index("head")
     flat_at = data_at * 2 + head_at
     frames = block_in.shape[1]
     rows = w_qkv.shape[0]
 
+    far = far_links()
+    x_first = [far[0], row_link(), core_link()]
+    y_first = [row_link(), far[0], core_link()]
     first = [
         gather_chain(
-            jnp.concatenate([w_qkv[:, :D], w_out], axis=1).astype(BFLOAT), "last", False
-        ),
-        gather_chain(w_qkv[:, D:].astype(BFLOAT), "last", True),
+            with_bits(
+                jnp.concatenate([w_qkv[:, :D], w_out, w_qkv[:, D:]], axis=1).astype(BFLOAT), "last"
+            ),
+            "last",
+            far[1:],
+        )
     ]
     second = [
-        gather_chain(jnp.concatenate([w_cq, w_cout], axis=1).astype(BFLOAT), "last", False),
-        gather_chain(w_ckv.astype(BFLOAT).reshape(w_ckv.shape[0], D), "columns", True),
+        gather_chain(
+            with_bits(jnp.concatenate([w_cq, w_cout], axis=1).astype(BFLOAT), "last"),
+            "last",
+            far[1:] + x_first,
+        ),
+        gather_chain(
+            with_bits(w_ckv.astype(BFLOAT).reshape(w_ckv.shape[0], D), "columns"),
+            "columns",
+            far[1:] + y_first,
+        ),
     ]
     masters = [
-        w_ada,
-        w_qkv,
-        w_out,
-        w_cq,
-        w_cout,
+        jnp.concatenate([w_ada, w_qkv, w_out, w_cq, w_cout], axis=1),
         w_ckv.reshape(w_ckv.shape[0], D),
-        w_fc1,
-        w_fc2.T,
+        jnp.concatenate([w_fc1, w_fc2.T], axis=1),
     ]
     mlp_shard = jnp.concatenate([w_fc1.astype(BFLOAT), w_fc2.T.astype(BFLOAT)], axis=1)
-    mlp_all = lax.all_gather(mlp_shard, ("head", "dp"), axis=0, tiled=True)
+    inputs = swap_place(block_in[0])
+    joint_mask = jnp.concatenate([frame_mask[0], text_mask[0]])
 
     def add_step(link):
         return lambda state: state + cross(state, link)
@@ -675,26 +758,28 @@
         + [keep_step(link) for link in far_links()]
         + [last_step],
     )
-    slots, far_count = len(first[0].steps), len(far_links()) - 1
+    far_count = len(far) - 1
+    slots = far_count + 3
     for slot in range(slots):
         timing.advance({0: 1 + far_count, 1: 3, 2: far_count, 3: 1}.get(slot, 0))
+        if slot == far_count:
+            joint = first[0].state
+            first = [
+                gather_chain(joint[..., : 2 * D], "last", x_first),
+                gather_chain(joint[..., 2 * D :], "last", y_first),
+            ]
         for chain in first:
             chain.advance()
         if slot >= 2:
             for chain in second:
                 chain.advance()
-        if slot == 0:
-            block_in, joint_mask, text = tie(
-                [timing] + first,
-                block_in,
-                jnp.concatenate([frame_mask[0], text_mask[0]]),
-                text,
+        if slot == far_count - 1:
+            inputs, mlp_shard, joint_mask, text = tie(
+                [timing] + first + second, inputs, mlp_shard, joint_mask, text
             )
-            inputs = swap_place(block_in[0])
+            mlp_all = lax.all_gather(mlp_shard, HEAD + DP, axis=0, tiled=True)
             masks = from_clip_core(joint_mask)
             clip_text = from_clip_core(text[0])
-        elif slot == 1:
-            tie([timing] + first)
         elif slot < slots - 1:
             tie([timing] + first + second)
         else:
@@ -714,20 +799,21 @@
         modulation, 6, axis=-1
     )
 
-    out_grad = swap_place(cotangent[0])
     self_input = modulate(inputs, shift_self, scale_self).astype(BFLOAT)
     key_value = nn(self_input, w_key_value).astype(BFLOAT)
     query = nn(self_input, w_query).astype(BFLOAT)
     other_key_value = cross(key_value, core_link())
+    query, other_key_value = tie(second, query, other_key_value)
     for chain in second:
         chain.advance()
-    query, other_key_value = tie(second, query, other_key_value)
+
+    self_keys = [(key_value, own_bias), (other_key_value, other_bias)]
+    self_attn, self_logs = attend(query, self_keys, plain_places)
+    self_attn, cotangent = tie(second, self_attn, cotangent)
+    out_grad = swap_place(cotangent[0])
     cross_pair, w_text = [chain.finish() for chain in second]
     cross_pair, w_text = cross_pair.reshape(D, 2 * D), w_text.reshape(DT, 2 * D)
     w_cross_query, w_cross_project = cross_pair[:, :D], cross_pair[:, D:]
-
-    self_keys = [(key_value, own_bias), (other_key_value, other_bias)]
-    self_attn, self_logs = attend(query, self_keys, plain_places)
     self_branch = nn(self_attn, w_project)
     after_self = inputs + gate_self * self_branch
 
@@ -741,24 +827,18 @@
     mlp_input = modulate(after_cross, shift_mlp, scale_mlp).astype(BFLOAT)
     mlp_input, out_grad = tie([], mlp_input, out_grad)
     out_grad = out_grad.astype(FLOAT)
-    mlp_all = mlp_all.reshape(2, D, 2 * HALF)
-    fc1_halves, fc2_halves = mlp_all[:, :, :HALF], mlp_all[:, :, HALF:]
-    hidden_pre = jnp.einsum("fd,hdk->hfk", mlp_input, fc1_halves, preferred_element_type=FLOAT)
-    hidden_act = jax.nn.gelu(hidden_pre).astype(BFLOAT)
     mlp_grad = (gate_mlp * out_grad).astype(BFLOAT)
-    act_grad = jnp.einsum("fd,hdk->hfk", mlp_grad, fc2_halves, preferred_element_type=FLOAT)
-    gelu_back = jax.vjp(jax.nn.gelu, hidden_pre)[1]
-    pre_grad = gelu_back(act_grad)[0].astype(BFLOAT)
-    mlp_part = mlp_outer(mlp_input, mlp_grad, pre_grad, hidden_act)
-    mlp_part, hidden_act, pre_grad = tie([], mlp_part, hidden_act, pre_grad)
-    mlp_raw = lax.psum_scatter(
-        mlp_part.reshape(2 * D, 2 * HALF), ("head", "dp"), scatter_dimension=0, tiled=True
-    ).astype(FLOAT)
-
-    mlp_branch = jnp.einsum("hfk,hdk->fd", hidden_act, fc2_halves, preferred_element_type=FLOAT)
+    mlp_branch, mlp_in_grad, mlp_part = mlp_both(
+        mlp_input, mlp_grad, mlp_all.reshape(2, D, 2 * HALF)
+    )
+    mlp_part = lax.psum_scatter(
+        mlp_part.reshape((8,) + mlp_part.shape[2:]),
+        HEAD + ("near", "core"),
+        scatter_dimension=0,
+        tiled=False,
+    )
     block_out = (after_cross + gate_mlp * mlp_branch).astype(BFLOAT)
     gate_mlp_grad = jnp.sum(out_grad * mlp_branch, axis=0, keepdims=True)
-    mlp_in_grad = jnp.einsum("hfk,hdk->fd", pre_grad, fc1_halves, preferred_element_type=FLOAT)
     mlp_back = jax.vjp(modulate, after_cross, shift_mlp, scale_mlp)[1]
     cross_res_grad, shift_mlp_grad, scale_mlp_grad = mlp_back(mlp_in_grad)
     cross_res_grad = out_grad + cross_res_grad
@@ -812,12 +892,6 @@
     self_back = jax.vjp(modulate, inputs, shift_self, scale_self)[1]
     input_res_grad, shift_self_grad, scale_self_grad = self_back(in_grad_normed)
     input_grad = (self_res_grad + input_res_grad).astype(BFLOAT)
-    input_grad, shift_self_grad, scale_self_grad = tie(
-        cross_chains + last_chains, input_grad, shift_self_grad, scale_self_grad
-    )
-    for chain in cross_chains + last_chains:
-        chain.advance()
-
     modulation_grad = jnp.concatenate(
         [
             shift_self_grad,
@@ -829,23 +903,40 @@
         ],
         axis=-1,
     )
-    modulation_grad = modulation_grad + cross(modulation_grad, core_link())
-    modulation_grad, block_out, input_grad = tie(
-        cross_chains + last_chains, modulation_grad, block_out, input_grad
-    )
-    block_out, input_grad = swap_place(jnp.stack([block_out, input_grad]))
-    modulation_grad = modulation_grad.reshape((1,) * dp_bits() + (6 * D,))
-    for link in far_links()[::-1] + [row_link()]:
-        other = cross(modulation_grad, link)
-        upper = bit_of(link) == 1
-        dim = dp_bits() - 1 if link[0] == "head" else dp_bits() - link[1].bit_length()
-        modulation_grad = jnp.concatenate(
-            [
-                jnp.where(upper, other, modulation_grad),
-                jnp.where(upper, modulation_grad, other),
-            ],
-            axis=dim,
+
+    def join_step(link):
+        def step(state):
+            other = cross(state, link)
+            upper = bit_of(link) == 1
+            dim = dp_bits() - 1 if link[0] == HEAD else dp_bits() - link[1].bit_length()
+            low, high = jnp.where(upper, other, state), jnp.where(upper, state, other)
+            return jnp.concatenate([low, high], axis=dim)
+
+        return step
+
+    far = far_links()
+    shape = (1,) * dp_bits() + (6 * D,)
+    joining = Chain(
+        modulation_grad,
+        [lambda state: (state + cross(state, core_link())).reshape(shape)]
+        + [join_step(link) for link in far[::-1] + [row_link()]],
+    )
+    joining.advance(2)
+    block_out, input_grad, mlp_part = tie(
+        [joining] + cross_chains + last_chains, block_out, input_grad, mlp_part
+    )
+    mlp_raw = lax.psum_scatter(mlp_part, "far", scatter_dimension=0, tiled=False).astype(FLOAT)
+    for count in (len(far) - 2, 2):
+        for chain in cross_chains + last_chains:
+            chain.advance()
+        joining.advance(count)
+        block_out, input_grad = tie(
+            [joining] + cross_chains + last_chains, block_out, input_grad
         )
+    mlp_raw, block_out, input_grad = tie(last_chains, mlp_raw, block_out, input_grad)
+    own_results = jnp.stack([block_out, input_grad])
+    swapped_results = swap_only(own_results)
+    modulation_grad = joining.finish()
     ada_raw = jnp.einsum(
         "cr,cx->rx",
         condition.astype(FLOAT),
@@ -862,11 +953,14 @@
         statistics_kernel, [(STAT_LINES, LINE)], place, weight_squares, *raw_grads, places=1
     )
     sums = sum_all(statistics)
-    shapes = [master.shape for master in masters]
+    shapes = [(rows, columns) for columns in COL_SIZES[:5]]
+    shapes += [masters[1].shape] + [(rows * 2, HALF)] * 2
     line = (1, LINE)
     row_new, col_new, norm, update_squares, *rest = whole_call(
         update_kernel,
-        [(ROW_LINES, LINE), (COL_LINES, LINE), line, line] + shapes + shapes,
+        [(ROW_LINES, LINE), (COL_LINES, LINE), line, line]
+        + shapes
+        + [master.shape for master in masters],
         place,
         sums,
         row_state.reshape(ROW_LINES, LINE),
@@ -884,6 +978,9 @@
         *updates,
     )
     updated = list(updated)
+    (own,) = tie([], own_results)
+    late, _ = tie([], on_own_chip(), update_squares)
+    block_out, input_grad = jnp.where(late, own, swapped_results)
     clipped[5] = clipped[5].reshape(w_ckv.shape)
     updated[5] = updated[5].reshape(w_ckv.shape)
     clipped[7] = clipped[7].T
@@ -900,49 +997,51 @@
 
 
 def solution(mesh):
+    devices = mesh.devices
+    refined = jax.sharding.Mesh(devices.reshape(devices.shape[0] // 4, 2, 2, 2), ALL)
     return jax.shard_map(
         per_device,
-        mesh=mesh,
+        mesh=refined,
         in_specs=(
-            P("dp", "head", None),
-            P("dp", None, None),
-            P("dp"),
-            P("dp", None),
-            P("dp", None),
-            P("dp", "head", None),
-            P(("dp", "head"), None),
-            P(("dp", "head"), None),
-            P(("dp", "head"), None),
-            P(("dp", "head"), None),
-            P(("dp", "head"), None),
-            P("dp", None, "head"),
-            P("dp", "head"),
-            P("head", "dp"),
+            P(DP, "head", None),
+            P(DP, None, None),
+            P(DP),
+            P(DP, None),
+            P(DP, None),
+            P(DP, "head", None),
+            P(ALL, None),
+            P(ALL, None),
+            P(ALL, None),
+            P(ALL, None),
+            P(ALL, None),
+            P(DP, None, "head"),
+            P(DP, "head"),
+            P("head", DP),
             P(),
             P(),
         ),
         out_specs=(
-            P("dp", "head", None),
-            P("dp", "head", None),
+            P(DP, "head", None),
+            P(DP, "head", None),
             P(),
             P(),
             P(),
-            P(("dp", "head"), None),
-            P(("dp", "head"), None),
-            P(("dp", "head"), None),
-            P(("dp", "head"), None),
-            P(("dp", "head"), None),
-            P("dp", None, "head"),
-            P("dp", "head"),
-            P("head", "dp"),
-            P(("dp", "head"), None),
-            P(("dp", "head"), None),
-            P(("dp", "head"), None),
-            P(("dp", "head"), None),
-            P(("dp", "head"), None),
-            P("dp", None, "head"),
-            P("dp", "head"),
-            P("head", "dp"),
+            P(ALL, None),
+            P(ALL, None),
+            P(ALL, None),
+            P(ALL, None),
+            P(ALL, None),
+            P(DP, None, "head"),
+            P(DP, "head"),
+            P("head", DP),
+            P(ALL, None),
+            P(ALL, None),
+            P(ALL, None),
+            P(ALL, None),
+            P(ALL, None),
+            P(DP, None, "head"),
+            P(DP, "head"),
+            P("head", DP),
         ),
         check_vma=False,
     )

time: 486 us -> 431 us (0.89)
  waiting for transfers between devices: 219 us -> 166 us
  matrix products: 37.7 us -> 13.3 us
  Pallas kernels: 67.7 us -> 80.1 us
  local copies, waits for them, and re-layouts: 21.4 us -> 30.5 us
    reduce_scatter x1 -> x2, waiting for transfers between devices: 39.8 us -> 0.02 us  [the longest x1 0.02 us: per_device(): lax.psum_scatter(mlp_part, 'far', scatter_dimension=0, tiled=False)]
    dot_general x4 -> x0, matrix products: 25.4 us -> none  [the longest x1 7.68 us: per_device(): jnp.einsum('fd,hdk->hfk', mlp_input, fc1_halves, preferred_element_type=F...]
    ppermute x66 -> x64, waiting for transfers between devices: 179 us -> 166 us  [cross(): return lax.ppermute(values, link[0], pairs)]
    pallas_call x1, Pallas kernels: 9.26 us -> 22.2 us  [mlp_both(): pl.pallas_call(mlp_kernel, grid=(2, tiles), in_specs=[whole, whole, pl.Bl...]
    unnamed x221 -> x218, local copies, waits for them, and re-layouts: 11.7 us -> 19.8 us
    ppermute x66 -> x64, starting transfers between devices: 63.2 us -> 66.3 us  [cross(): return lax.ppermute(values, link[0], pairs)]
  transfers between devices with their start and end apart: 73 -> 72, of which waited for: 44 -> 40; matrix products, arithmetic and copies ran while one was open for 12% -> 15% of each run, Pallas kernels for 10% -> 14%
where the time goes in v3:
time: 431 us; the launch traced here: 425 us
  waiting for transfers between devices  166 us (39%)
  Pallas kernels  80.1 us (19%)
  starting transfers between devices  74.6 us (17%)
  other arithmetic  43.2 us (10%)
  local copies, waits for them, and re-layouts  30.5 us (7%)
  between operations  17 us (4%)
  matrix products  13.3 us (3%)
    ppermute x64, waiting for transfers between devices, cross(): return lax.ppermute(values, link[0], pairs)  166 us
    ppermute x64, starting transfers between devices, cross(): return lax.ppermute(values, link[0], pairs)  66.3 us
    pallas_call x2, Pallas kernels, attend_back(): pl.pallas_call(functools.partial(back_kernel, blocks, places), grid=(PAIR...  29.7 us
    pallas_call x1, Pallas kernels, mlp_both(): pl.pallas_call(mlp_kernel, grid=(2, tiles), in_specs=[whole, whole, pl.Bl...  22.2 us
    unnamed x218, local copies, waits for them, and re-layouts  19.8 us
    pallas_call x2, Pallas kernels, attend(): pl.pallas_call(functools.partial(attend_kernel, blocks), grid=(PAIRS,), i...  18.4 us
  transfers between devices with their start and end apart: 72, of which 40 were waited for; matrix products, arithmetic and copies ran while one was open for 15% of the time, Pallas kernels for 14%

profile of v3, /device:TPU:0, one launch (start us, length us, event | category | flops | bytes accessed | tf_op | source)
XLA Modules:
  0.0 425.0 jit_solution(1653198582577122779)
XLA Ops:
  11.6 2.7 collective-permute-start.3
  18.1 2.8 collective-permute-done.1
  20.9 2.6 collective-permute-start.2
  27.0 2.0 collective-permute-done.4
  29.7 3.4 collective-permute-start.5
  34.4 2.6 collective-permute-start.7
  39.9 2.1 collective-permute-done.6
  42.8 3.4 collective-permute-done.7
  56.5 4.7 %collective-permute-done.12 = bf16[2,2,1,1,1,24,1536]{6,5,4,3,2,1,0:T(8,128)(2,1)S(1)} collective-permute-done((bf16[2,2,1,1,1,24,1536]{6,5,4,3,2,1,0:T(8,128)(2,1)S(1)}, bf16[2,2,1,1,1,24,1536]{6,5,4,3,2,1,0:T(8,128)(2,1)S(1)}, u32[]{:S(2)}, u32[]{:S(2)}) %collective-permute-start.12) | collective-permute-done | bytes 294944 | tf_op jit(solution)/shard_map/ppermute | solution.py:80
  61.2 2.5 collective-permute-done.11
  69.3 9.9 %collective-permute-done.18 = bf16[1,2,1,1,1,24,1536]{6,5,4,3,2,1,0:T(8,128)(2,1)S(1)} collective-permute-done((bf16[1,2,1,1,1,24,1536]{6,5,4,3,2,1,0:T(8,128)(2,1)S(1)}, bf16[1,2,1,1,1,24,1536]{6,5,4,3,2,1,0:T(8,128)(2,1)S(1)}, u32[]{:S(2)}, u32[]{:S(2)}) %collective-permute-start.18) | collective-permute-done | bytes 147488 | tf_op jit(solution)/shard_map/ppermute | solution.py:80
  80.0 2.1 collective-permute-done.19
  86.7 2.4 collective-permute-start.27
  99.4 9.1 %collective-permute-done.23 = bf16[2,2,1,1,64,768]{5,4,3,2,1,0:T(8,128)(2,1)S(1)} collective-permute-done((bf16[2,2,1,1,64,768]{5,4,3,2,1,0:T(8,128)(2,1)S(1)}, bf16[2,2,1,1,64,768]{5,4,3,2,1,0:T(8,128)(2,1)S(1)}, u32[]{:S(2)}, u32[]{:S(2)}) %collective-permute-start.23) | collective-permute-done | bytes 393248 | tf_op jit(solution)/shard_map/ppermute | solution.py:80
  112.0 12.5 %shard_map.320 = (bf16[512,768]{1,0:T(8,128)(2,1)S(1)}, f32[6,2,512]{2,1,0:T(2,128)S(1)}) custom-call(bf16[512,768]{1,0:T(8,128)(2,1)S(1)} %convolution_convert_fusion.5.refs_0_, bf16[512,1536]{1,0:T(8,128)(2,1)S(1)} %convolution_convert_fusion.refs_1_.refs_2_.refs_4_.refs_5_, bf16[512,1536]{1,0:T(8,128)(2,1)S(1)} %convolution_convert_fusion.refs_1_.refs_2_.refs_4_.refs_5_, ...), custom_call_target="tpu_custom_call" | custom-call | flops 1000 | bytes 1000 | tf_op jit(solution)/shard_map/pallas_call | solution.py:321
  124.6 13.2 %collective-permute-done.25 = bf16[2,2,2,1,1,24,1536]{6,5,4,3,2,1,0:T(8,128)(2,1)S(1)} collective-permute-done((bf16[2,2,2,1,1,24,1536]{6,5,4,3,2,1,0:T(8,128)(2,1)S(1)}, bf16[2,2,2,1,1,24,1536]{6,5,4,3,2,1,0:T(8,128)(2,1)S(1)}, u32[]{:S(2)}, u32[]{:S(2)}) %collective-permute-start.25) | collective-permute-done | bytes 589856 | tf_op jit(solution)/shard_map/ppermute | solution.py:80
  138.1 3.9 collective-permute-done.26
  144.2 2.9 collective-permute-start.28
  154.9 5.9 %shard_map.321 = (bf16[512,768]{1,0:T(8,128)(2,1)S(1)}, f32[6,2,512]{2,1,0:T(2,128)S(1)}) custom-call(bf16[512,768]{1,0:T(8,128)(2,1)S(1)} %convolution_convert_fusion.4.refs_0_, bf16[256,1536]{1,0:T(8,128)(2,1)S(1)} %convolution_convert_fusion.1.refs_1_.refs_2_.refs_4_.refs_5_, ...), custom_call_target="tpu_custom_call" | custom-call | flops 1000 | bytes 1000 | tf_op jit(solution)/shard_map/pallas_call | solution.py:321
  166.5 22.2 %shard_map.322 = (f32[512,768]{1,0:T(8,128)S(1)}, f32[512,768]{1,0:T(8,128)S(1)}, bf16[2,4,4,2,48,1536]{5,4,3,2,1,0:T(8,128)(2,1)}) custom-call(bf16[512,768]{1,0:T(8,128)(2,1)S(1)} %copy-done.10, bf16[512,768]{1,0:T(8,128)(2,1)S(1)} %copy-done.9, bf16[2,768,3072]{2,1,0:T(8,128)(2,1)} %bitcast.93, bf16[2,768,3072]{2,1,0:T(8,128)(2,1)} %bitcast.94), custom_call_target="tpu_custom_call" | custom-call | flops 1000 | bytes 1000 | tf_op jit(solution)/shard_map/pallas_call | solution.py:644
  190.6 2.8 multiply_reduce_fusion
  193.4 2.9 fusion.12
  199.9 7.8 %shard_map.323 = (bf16[512,768]{1,0:T(8,128)(2,1)S(1)}, bf16[256,1536]{1,0:T(8,128)(2,1)S(1)}) custom-call(bf16[512,768]{1,0:T(8,128)(2,1)S(1)} %copy-done.18, bf16[512,768]{1,0:T(8,128)(2,1)S(1)} %get-tuple-element.186.refs_1_.refs_2_, bf16[512,768]{1,0:T(8,128)(2,1)S(1)} %convolution_convert_fusion.3.refs_2_, f32[6,2,512]{2,1,0:T(2,128)S(1)} %copy-done.36, ...), custom_call_target="tpu_custom_call" | custom-call | flops 1000 | bytes 1000 | tf_op jit(solution)/shard_map/pallas_call | solution.py:338
  212.9 4.6 %collective-permute-start.32 = (bf16[2,2,2,1,2,24,1536]{6,5,4,3,2,1,0:T(8,128)(2,1)S(1)}, bf16[2,2,2,1,2,24,1536]{6,5,4,3,2,1,0:T(8,128)(2,1)S(1)}, u32[]{:S(2)}, u32[]{:S(2)}) collective-permute-start(bf16[2,2,2,1,2,24,1536]{6,5,4,3,2,1,0:T(8,128)(2,1)S(1)} %constant_dynamic-slice_fusion.19), channel_id=1, source_target_pairs={{0,2},{2,0},{4,6},{6,4},{8,10},{10,8},{12,14},{14,12},{16,18},{18,... | collective-permute-start | bytes 3538952 | tf_op jit(solution)/shard_map/ppermute | solution.py:80
  220.1 2.4 copy-done.49
  226.9 21.9 %shard_map.326 = (bf16[512,768]{1,0:T(8,128)(2,1)S(1)}, bf16[512,1536]{1,0:T(8,128)(2,1)S(1)}, bf16[512,1536]{1,0:T(8,128)(2,1)}) custom-call(bf16[512,768]{1,0:T(8,128)(2,1)S(1)} %copy-done.12, bf16[512,768]{1,0:T(8,128)(2,1)S(1)} %copy-done.3, bf16[512,768]{1,0:T(8,128)(2,1)S(1)} %convolution_convert_fusion.2.refs_2_, f32[6,2,512]{2,1,0:T(2,128)S(1)} %copy-done.34, ...), custom_call_target="tpu_custom_call" | custom-call | flops 1000 | bytes 1000 | tf_op jit(solution)/shard_map/pallas_call | solution.py:338
  250.0 2.9 collective-permute-done.34
  253.1 10.1 %collective-permute-done.35 = bf16[2,2,1,1,64,1536]{5,4,3,2,1,0:T(8,128)(2,1)S(1)} collective-permute-done((bf16[2,2,1,1,64,1536]{5,4,3,2,1,0:T(8,128)(2,1)S(1)}, bf16[2,2,1,1,64,1536]{5,4,3,2,1,0:T(8,128)(2,1)S(1)}, u32[]{:S(2)}, u32[]{:S(2)}) %collective-permute-start.35) | collective-permute-done | bytes 786464 | tf_op jit(solution)/shard_map/ppermute | solution.py:80
  268.8 7.2 %collective-permute-done.36 = bf16[2,2,1,1,1,24,1536]{6,5,4,3,2,1,0:T(8,128)(2,1)S(1)} collective-permute-done((bf16[2,2,1,1,1,24,1536]{6,5,4,3,2,1,0:T(8,128)(2,1)}, bf16[2,2,1,1,1,24,1536]{6,5,4,3,2,1,0:T(8,128)(2,1)S(1)}, u32[]{:S(2)}, u32[]{:S(2)}) %collective-permute-start.36) | collective-permute-done | bytes 294944 | tf_op jit(solution)/shard_map/ppermute | solution.py:80
  278.0 5.7 %collective-permute-done.37 = bf16[2,2,1,1,64,768]{5,4,3,2,1,0:T(8,128)(2,1)S(1)} collective-permute-done((bf16[2,2,1,1,64,768]{5,4,3,2,1,0:T(8,128)(2,1)S(1)}, bf16[2,2,1,1,64,768]{5,4,3,2,1,0:T(8,128)(2,1)S(1)}, u32[]{:S(2)}, u32[]{:S(2)}) %collective-permute-start.37) | collective-permute-done | bytes 393248 | tf_op jit(solution)/shard_map/ppermute | solution.py:80
  289.6 2.5 collective-permute-start.41
  294.3 2.5 collective-permute-start.40
  297.4 11.8 %collective-permute-done.40 = f32[1,1,1,1,4608]{4,3,2,1,0:T(1,128)S(1)} collective-permute-done((f32[1,1,1,1,4608]{4,3,2,1,0:T(1,128)S(1)}, f32[1,1,1,1,4608]{4,3,2,1,0:T(1,128)S(1)}, u32[]{:S(2)}, u32[]{:S(2)}) %collective-permute-start.40) | collective-permute-done | bytes 18464 | tf_op jit(solution)/shard_map/ppermute | solution.py:80
  318.9 11.3 %collective-permute-done.49 = bf16[2,2,1,1,2,24,1536]{6,5,4,3,2,1,0:T(8,128)(2,1)S(1)} collective-permute-done((bf16[2,2,1,1,2,24,1536]{6,5,4,3,2,1,0:T(8,128)(2,1)S(1)}, bf16[2,2,1,1,2,24,1536]{6,5,4,3,2,1,0:T(8,128)(2,1)S(1)}, u32[]{:S(2)}, u32[]{:S(2)}) %collective-permute-start.49) | collective-permute-done | bytes 589856 | tf_op jit(solution)/shard_map/ppermute | solution.py:80
  332.6 3.5 collective-permute-done.50
  337.2 5.3 %collective-permute-done.51 = f32[2,2,2,1,4608]{4,3,2,1,0:T(1,128)S(1)} collective-permute-done((f32[2,2,2,1,4608]{4,3,2,1,0:T(1,128)S(1)}, f32[2,2,2,1,4608]{4,3,2,1,0:T(1,128)S(1)}, u32[]{:S(2)}, u32[]{:S(2)}) %collective-permute-start.51) | collective-permute-done | bytes 147488 | tf_op jit(solution)/shard_map/ppermute | solution.py:80
  348.3 3.5 collective-permute-start.56
  355.1 5.6 %collective-permute-done.56 = bf16[1,2,1,1,1,24,1536]{6,5,4,3,2,1,0:T(8,128)(2,1)S(1)} collective-permute-done((bf16[1,2,1,1,1,24,1536]{6,5,4,3,2,1,0:T(8,128)(2,1)S(1)}, bf16[1,2,1,1,1,24,1536]{6,5,4,3,2,1,0:T(8,128)(2,1)S(1)}, u32[]{:S(2)}, u32[]{:S(2)}) %collective-permute-start.56) | collective-permute-done | bytes 147488 | tf_op jit(solution)/shard_map/ppermute | solution.py:80
  363.0 2.5 collective-permute-done.57
  369.9 7.1 %collective-permute-done.59 = f32[184,128]{1,0:T(8,128)S(1)} collective-permute-done((f32[184,128]{1,0:T(8,128)S(1)}, f32[184,128]{1,0:T(8,128)S(1)}, u32[]{:S(2)}, u32[]{:S(2)}) %collective-permute-start.59) | collective-permute-done | bytes 94240 | tf_op jit(solution)/shard_map/ppermute | solution.py:80
  377.6 4.1 collective-permute-done.60
  382.4 3.9 collective-permute-done.61
  386.3 3.1 collective-permute-start.62
  389.4 3.6 collective-permute-done.62
  393.0 2.1 shard_map.330
  398.3 2.3 collective-permute-done.65
  401.2 3.0 collective-permute-done.66
  404.2 3.5 collective-permute-done.67
  (524 shorter events, 145.5 us)
Async XLA Ops:
  7.2 157.0 %all-gather.2.cloned.1.call-start = ((), (), s32[]{:S(2)}) async-start(), calls=%async_computation.2 | async-start | bytes 9732096 | tf_op jit(solution)/shard_map/all_gather | solution.py:780
  8.1 9.1 %collective-permute-start = (s32[16]{0:T(128)S(1)}, s32[16]{0:T(128)S(1)}, u32[]{:S(2)}, u32[]{:S(2)}) collective-permute-start(s32[16]{0:T(128)S(1)} %dynamic_update_slice.5), channel_id=1, source_target_pairs={{0,2},{2,0},{4,6},{6,4},{8,10},{10,8},{12,14},{14,12},{16,18},{18,... | collective-permute-start | bytes 200 | tf_op jit(solution)/shard_map/ppermute | solution.py:80
  8.5 37.9 %collective-permute-start.8 = (bf16[512,768]{1,0:T(8,128)(2,1)}, bf16[512,768]{1,0:T(8,128)(2,1)S(1)}, u32[]{:S(2)}, u32[]{:S(2)}) collective-permute-start(bf16[512,768]{1,0:T(8,128)(2,1)} %bitcast.111), channel_id=1, source_target_pairs={{1,2},{2,1},{5,6},{6,5},{9,10},{10,9},{13,14},{14,13},{17,18},{18,... | collective-permute-start | bytes 2359304 | tf_op jit(solution)/shard_map/ppermute | solution.py:169
  11.6 13.7 %collective-permute-start.3 = (bf16[1,1,1,1,1,24,3072]{6,5,4,3,2,1,0:T(8,128)(2,1)S(1)}, bf16[1,1,1,1,1,24,3072]{6,5,4,3,2,1,0:T(8,128)(2,1)S(1)}, u32[]{:S(2)}, u32[]{:S(2)}) collective-permute-start(bf16[1,1,1,1,1,24,3072]{6,5,4,3,2,1,0:T(8,128)(2,1)S(1)} %pad_maximum_fusion.21), channel_id=1, source_target_pairs={{0,8},{2,10},{4,12},{6,14},{8,0},{10,2},{12,4},{14,6},{16,24},{18,... | collective-permute-start | bytes 442376 | tf_op jit(solution)/shard_map/ppermute | solution.py:80
  29.7 7.3 %collective-permute-start.5 = (f32[8,1,4608]{2,1,0:T(1,128)S(1)}, f32[8,1,4608]{2,1,0:T(1,128)S(1)}, u32[]{:S(2)}, u32[]{:S(2)}) collective-permute-start(f32[8,1,4608]{2,1,0:T(1,128)S(1)} %constant_dynamic-slice_fusion.23), channel_id=1, source_target_pairs={{0,1},{1,0},{2,3},{3,2},{4,5},{5,4},{6,7},{7,6},{8,9},{9,8},{10,11... | collective-permute-start | bytes 442376 | tf_op jit(solution)/shard_map/ppermute | solution.py:80
  34.4 11.8 %collective-permute-start.7 = (bf16[1,2,1,1,1,24,3072]{6,5,4,3,2,1,0:T(8,128)(2,1)S(1)}, bf16[1,2,1,1,1,24,3072]{6,5,4,3,2,1,0:T(8,128)(2,1)S(1)}, u32[]{:S(2)}, u32[]{:S(2)}) collective-permute-start(bf16[1,2,1,1,1,24,3072]{6,5,4,3,2,1,0:T(8,128)(2,1)S(1)} %pad_maximum_fusion.16), channel_id=1, source_target_pairs={{0,16},{2,18},{4,20},{6,22},{8,24},{10,26},{12,28},{14,30},{16,0},... | collective-permute-start | bytes 884744 | tf_op jit(solution)/shard_map/ppermute | solution.py:80
  47.4 264.4 %reduce-scatter.3.cloned.1.call-start = ((), (), s32[]{:S(2)}) async-start(), calls=%async_computation.3 | async-start | bytes 10616832 | tf_op jit(solution)/shard_map/reduce_scatter | solution.py:834
  47.5 8.9 %collective-permute-start.13 = (bf16[1,1,1,1,1,24,1536]{6,5,4,3,2,1,0:T(8,128)(2,1)S(1)}, bf16[1,1,1,1,1,24,1536]{6,5,4,3,2,1,0:T(8,128)(2,1)S(1)}, u32[]{:S(2)}, u32[]{:S(2)}) collective-permute-start(bf16[1,1,1,1,1,24,1536]{6,5,4,3,2,1,0:T(8,128)(2,1)S(1)} %copy-done.76), channel_id=1, source_target_pairs={{0,8},{2,10},{4,12},{6,14},{8,0},{10,2},{12,4},{14,6},{16,24},{18,... | collective-permute-start | bytes 221192 | tf_op jit(solution)/shard_map/ppermute | solution.py:80
  49.5 6.9 %collective-permute-start.14 = (bf16[1,1,1,1,64,768]{5,4,3,2,1,0:T(8,128)(2,1)S(1)}, bf16[1,1,1,1,64,768]{5,4,3,2,1,0:T(8,128)(2,1)S(1)}, u32[]{:S(2)}, u32[]{:S(2)}) collective-permute-start(bf16[1,1,1,1,64,768]{5,4,3,2,1,0:T(8,128)(2,1)S(1)} %copy-done.74), channel_id=1, source_target_pairs={{0,8},{2,10},{4,12},{6,14},{8,0},{10,2},{12,4},{14,6},{16,24},{18,... | collective-permute-start | bytes 294920 | tf_op jit(solution)/shard_map/ppermute | solution.py:80
  53.0 8.1 %collective-permute-start.12 = (bf16[2,2,1,1,1,24,1536]{6,5,4,3,2,1,0:T(8,128)(2,1)S(1)}, bf16[2,2,1,1,1,24,1536]{6,5,4,3,2,1,0:T(8,128)(2,1)S(1)}, u32[]{:S(2)}, u32[]{:S(2)}) collective-permute-start(bf16[2,2,1,1,1,24,1536]{6,5,4,3,2,1,0:T(8,128)(2,1)S(1)} %get-tuple-element.325), channel_id=1, source_target_pairs={{0,1},{1,0},{2,3},{3,2},{4,5},{5,4},{6,7},{7,6},{8,9},{9,8},{10,11... | collective-permute-start | bytes 884744 | tf_op jit(solution)/shard_map/ppermute | solution.py:80
  54.8 8.8 %collective-permute-start.11 = (bf16[2,2,1,1,1,24,1536]{6,5,4,3,2,1,0:T(8,128)(2,1)S(1)}, bf16[2,2,1,1,1,24,1536]{6,5,4,3,2,1,0:T(8,128)(2,1)S(1)}, u32[]{:S(2)}, u32[]{:S(2)}) collective-permute-start(bf16[2,2,1,1,1,24,1536]{6,5,4,3,2,1,0:T(8,128)(2,1)S(1)} %get-tuple-element.326), channel_id=1, source_target_pairs={{0,4},{2,6},{4,0},{6,2},{8,12},{10,14},{12,8},{14,10},{16,20},{18,... | collective-permute-start | bytes 884744 | tf_op jit(solution)/shard_map/ppermute | solution.py:80
  63.9 15.3 %collective-permute-start.18 = (bf16[1,2,1,1,1,24,1536]{6,5,4,3,2,1,0:T(8,128)(2,1)S(1)}, bf16[1,2,1,1,1,24,1536]{6,5,4,3,2,1,0:T(8,128)(2,1)S(1)}, u32[]{:S(2)}, u32[]{:S(2)}) collective-permute-start(bf16[1,2,1,1,1,24,1536]{6,5,4,3,2,1,0:T(8,128)(2,1)S(1)} %pad_maximum_fusion.22), channel_id=1, source_target_pairs={{0,16},{2,18},{4,20},{6,22},{8,24},{10,26},{12,28},{14,30},{16,0},... | collective-permute-start | bytes 442376 | tf_op jit(solution)/shard_map/ppermute | solution.py:80
  65.8 16.3 %collective-permute-start.19 = (bf16[1,2,1,1,64,768]{5,4,3,2,1,0:T(8,128)(2,1)S(1)}, bf16[1,2,1,1,64,768]{5,4,3,2,1,0:T(8,128)(2,1)S(1)}, u32[]{:S(2)}, u32[]{:S(2)}) collective-permute-start(bf16[1,2,1,1,64,768]{5,4,3,2,1,0:T(8,128)(2,1)S(1)} %pad_maximum_fusion.20), channel_id=1, source_target_pairs={{0,16},{2,18},{4,20},{6,22},{8,24},{10,26},{12,28},{14,30},{16,0},... | collective-permute-start | bytes 589832 | tf_op jit(solution)/shard_map/ppermute | solution.py:80
  66.9 16.1 %collective-permute-start.16 = (bf16[2,2,2,1,1,24,1536]{6,5,4,3,2,1,0:T(8,128)(2,1)S(1)}, bf16[2,2,2,1,1,24,1536]{6,5,4,3,2,1,0:T(8,128)(2,1)S(1)}, u32[]{:S(2)}, u32[]{:S(2)}) collective-permute-start(bf16[2,2,2,1,1,24,1536]{6,5,4,3,2,1,0:T(8,128)(2,1)S(1)} %pad_maximum_fusion.11), channel_id=1, source_target_pairs={{0,1},{1,0},{2,3},{3,2},{4,5},{5,4},{6,7},{7,6},{8,9},{9,8},{10,11... | collective-permute-start | bytes 1769480 | tf_op jit(solution)/shard_map/ppermute | solution.py:80
  66.9 16.1 %collective-permute-start.17 = (bf16[2,2,1,1,2,24,1536]{6,5,4,3,2,1,0:T(8,128)(2,1)S(1)}, bf16[2,2,1,1,2,24,1536]{6,5,4,3,2,1,0:T(8,128)(2,1)S(1)}, u32[]{:S(2)}, u32[]{:S(2)}) collective-permute-start(bf16[2,2,1,1,2,24,1536]{6,5,4,3,2,1,0:T(8,128)(2,1)S(1)} %pad_maximum_fusion.12), channel_id=1, source_target_pairs={{0,4},{2,6},{4,0},{6,2},{8,12},{10,14},{12,8},{14,10},{16,20},{18,... | collective-permute-start | bytes 1769480 | tf_op jit(solution)/shard_map/ppermute | solution.py:80
  83.3 8.9 %collective-permute-start.20 = (bf16[2,2,2,1,2,24,1536]{6,5,4,3,2,1,0:T(8,128)(2,1)S(1)}, bf16[2,2,2,1,2,24,1536]{6,5,4,3,2,1,0:T(8,128)(2,1)}, u32[]{:S(2)}, u32[]{:S(2)}) collective-permute-start(bf16[2,2,2,1,2,24,1536]{6,5,4,3,2,1,0:T(8,128)(2,1)S(1)} %get-tuple-element.164), channel_id=1, source_target_pairs={{0,2},{2,0},{4,6},{6,4},{8,10},{10,8},{12,14},{14,12},{16,18},{18,... | collective-permute-start | bytes 3538952 | tf_op jit(solution)/shard_map/ppermute | solution.py:80
  86.3 7.7 %collective-permute-start.21 = (bf16[2,2,2,1,2,24,1536]{6,5,4,3,2,1,0:T(8,128)(2,1)S(1)}, bf16[2,2,2,1,2,24,1536]{6,5,4,3,2,1,0:T(8,128)(2,1)S(1)}, u32[]{:S(2)}, u32[]{:S(2)}) collective-permute-start(bf16[2,2,2,1,2,24,1536]{6,5,4,3,2,1,0:T(8,128)(2,1)S(1)} %get-tuple-element.165), channel_id=1, source_target_pairs={{0,2},{2,0},{4,6},{6,4},{8,10},{10,8},{12,14},{14,12},{16,18},{18,... | collective-permute-start | bytes 3538952 | tf_op jit(solution)/shard_map/ppermute | solution.py:80
  86.7 10.1 %collective-permute-start.27 = (s32[1280]{0:T(1024)}, s32[1280]{0:T(1024)S(1)}, u32[]{:S(2)}, u32[]{:S(2)}) collective-permute-start(s32[1280]{0:T(1024)} %pad_add_fusion), channel_id=1, source_target_pairs={{0,2},{3,1},{4,6},{7,5},{8,10},{11,9},{12,14},{15,13},{16,18},{19,... | collective-permute-start | bytes 15368 | tf_op jit(solution)/shard_map/ppermute | solution.py:181
  89.1 22.5 %collective-permute-start.29 = (bf16[256,1024]{1,0:T(8,128)(2,1)S(1)}, bf16[256,1024]{1,0:T(8,128)(2,1)S(1)}, u32[]{:S(2)}, u32[]{:S(2)}) collective-permute-start(bf16[256,1024]{1,0:T(8,128)(2,1)S(1)} %bitcast.114), channel_id=1, source_target_pairs={{0,2},{3,1},{4,6},{7,5},{8,10},{11,9},{12,14},{15,13},{16,18},{19,... | collective-permute-start | bytes 1572872 | tf_op jit(solution)/shard_map/ppermute | solution.py:181
  90.7 8.6 %collective-permute-start.22 = (bf16[2,2,1,1,1,24,1536]{6,5,4,3,2,1,0:T(8,128)(2,1)S(1)}, bf16[2,2,1,1,1,24,1536]{6,5,4,3,2,1,0:T(8,128)(2,1)S(1)}, u32[]{:S(2)}, u32[]{:S(2)}) collective-permute-start(bf16[2,2,1,1,1,24,1536]{6,5,4,3,2,1,0:T(8,128)(2,1)S(1)} %copy-done.68), channel_id=1, source_target_pairs={{0,4},{2,6},{4,0},{6,2},{8,12},{10,14},{12,8},{14,10},{16,20},{18,... | collective-permute-start | bytes 884744 | tf_op jit(solution)/shard_map/ppermute | solution.py:80
  96.8 12.7 %collective-permute-start.24 = (bf16[512,1536]{1,0:T(8,128)(2,1)S(1)}, bf16[512,1536]{1,0:T(8,128)(2,1)S(1)}, u32[]{:S(2)}, u32[]{:S(2)}) collective-permute-start(bf16[512,1536]{1,0:T(8,128)(2,1)S(1)} %convolution_convert_fusion.refs_1_.refs_2_.refs_4_.refs_5_), channel_id=1, source_target_pairs={{0,2},{2,0},{4,6},{6,4},{8,10},{10,8},{12,14},{14,12},{16,18},{18,... | collective-permute-start | bytes 4718600 | tf_op jit(solution)/shard_map/ppermute | solution.py:80
  97.6 10.9 %collective-permute-start.23 = (bf16[2,2,1,1,64,768]{5,4,3,2,1,0:T(8,128)(2,1)S(1)}, bf16[2,2,1,1,64,768]{5,4,3,2,1,0:T(8,128)(2,1)S(1)}, u32[]{:S(2)}, u32[]{:S(2)}) collective-permute-start(bf16[2,2,1,1,64,768]{5,4,3,2,1,0:T(8,128)(2,1)S(1)} %copy-done.64), channel_id=1, source_target_pairs={{0,1},{1,0},{2,3},{3,2},{4,5},{5,4},{6,7},{7,6},{8,9},{9,8},{10,11... | collective-permute-start | bytes 1179656 | tf_op jit(solution)/shard_map/ppermute | solution.py:80
  109.5 28.4 %collective-permute-start.25 = (bf16[2,2,2,1,1,24,1536]{6,5,4,3,2,1,0:T(8,128)(2,1)S(1)}, bf16[2,2,2,1,1,24,1536]{6,5,4,3,2,1,0:T(8,128)(2,1)S(1)}, u32[]{:S(2)}, u32[]{:S(2)}) collective-permute-start(bf16[2,2,2,1,1,24,1536]{6,5,4,3,2,1,0:T(8,128)(2,1)S(1)} %pad_maximum_fusion.14), channel_id=1, source_target_pairs={{0,1},{1,0},{2,3},{3,2},{4,5},{5,4},{6,7},{7,6},{8,9},{9,8},{10,11... | collective-permute-start | bytes 1769480 | tf_op jit(solution)/shard_map/ppermute | solution.py:80
  111.7 30.3 %collective-permute-start.26 = (bf16[2,2,1,1,64,1536]{5,4,3,2,1,0:T(8,128)(2,1)S(1)}, bf16[2,2,1,1,64,1536]{5,4,3,2,1,0:T(8,128)(2,1)S(1)}, u32[]{:S(2)}, u32[]{:S(2)}) collective-permute-start(bf16[2,2,1,1,64,1536]{5,4,3,2,1,0:T(8,128)(2,1)S(1)} %pad_maximum_fusion.9), channel_id=1, source_target_pairs={{0,4},{2,6},{4,0},{6,2},{8,12},{10,14},{12,8},{14,10},{16,20},{18,... | collective-permute-start | bytes 2359304 | tf_op jit(solution)/shard_map/ppermute | solution.py:80
  143.2 6.5 %collective-permute-start.31 = (bf16[512,768]{1,0:T(8,128)(2,1)S(1)}, bf16[512,768]{1,0:T(8,128)(2,1)S(1)}, u32[]{:S(2)}, u32[]{:S(2)}) collective-permute-start(bf16[512,768]{1,0:T(8,128)(2,1)S(1)} %bitcast.112), channel_id=1, source_target_pairs={{1,2},{2,1},{5,6},{6,5},{9,10},{10,9},{13,14},{14,13},{17,18},{18,... | collective-permute-start | bytes 2359304 | tf_op jit(solution)/shard_map/ppermute | solution.py:169
  147.1 6.2 %collective-permute-start.30 = (bf16[2,2,2,1,64,1536]{5,4,3,2,1,0:T(8,128)(2,1)S(1)}, bf16[2,2,2,1,64,1536]{5,4,3,2,1,0:T(8,128)(2,1)S(1)}, u32[]{:S(2)}, u32[]{:S(2)}) collective-permute-start(bf16[2,2,2,1,64,1536]{5,4,3,2,1,0:T(8,128)(2,1)S(1)} %pad_maximum_fusion.4), channel_id=1, source_target_pairs={{0,2},{2,0},{4,6},{6,4},{8,10},{10,8},{12,14},{14,12},{16,18},{18,... | collective-permute-start | bytes 4718600 | tf_op jit(solution)/shard_map/ppermute | solution.py:80
  190.0 156.3 %reduce-scatter.5.cloned.1.call-start = ((), (), s32[]{:S(2)}) async-start(), calls=%async_computation.4 | async-start | bytes 1474560 | tf_op jit(solution)/shard_map/reduce_scatter | solution.py:928
  212.9 10.5 %collective-permute-start.32 = (bf16[2,2,2,1,2,24,1536]{6,5,4,3,2,1,0:T(8,128)(2,1)S(1)}, bf16[2,2,2,1,2,24,1536]{6,5,4,3,2,1,0:T(8,128)(2,1)S(1)}, u32[]{:S(2)}, u32[]{:S(2)}) collective-permute-start(bf16[2,2,2,1,2,24,1536]{6,5,4,3,2,1,0:T(8,128)(2,1)S(1)} %constant_dynamic-slice_fusion.19), channel_id=1, source_target_pairs={{0,2},{2,0},{4,6},{6,4},{8,10},{10,8},{12,14},{14,12},{16,18},{18,... | collective-permute-start | bytes 3538952 | tf_op jit(solution)/shard_map/ppermute | solution.py:80
  217.6 6.2 %collective-permute-start.33 = (bf16[2,2,2,1,64,1536]{5,4,3,2,1,0:T(8,128)(2,1)S(1)}, bf16[2,2,2,1,64,1536]{5,4,3,2,1,0:T(8,128)(2,1)S(1)}, u32[]{:S(2)}, u32[]{:S(2)}) collective-permute-start(bf16[2,2,2,1,64,1536]{5,4,3,2,1,0:T(8,128)(2,1)S(1)} %constant_dynamic-slice_fusion.18), channel_id=1, source_target_pairs={{0,2},{2,0},{4,6},{6,4},{8,10},{10,8},{12,14},{14,12},{16,18},{18,... | collective-permute-start | bytes 4718600 | tf_op jit(solution)/shard_map/ppermute | solution.py:80
  224.3 28.7 %collective-permute-start.34 = (bf16[2,2,2,1,1,24,1536]{6,5,4,3,2,1,0:T(8,128)(2,1)S(1)}, bf16[2,2,2,1,1,24,1536]{6,5,4,3,2,1,0:T(8,128)(2,1)S(1)}, u32[]{:S(2)}, u32[]{:S(2)}) collective-permute-start(bf16[2,2,2,1,1,24,1536]{6,5,4,3,2,1,0:T(8,128)(2,1)S(1)} %constant_dynamic-slice_fusion.17), channel_id=1, source_target_pairs={{0,1},{1,0},{2,3},{3,2},{4,5},{5,4},{6,7},{7,6},{8,9},{9,8},{10,11... | collective-permute-start | bytes 1769480 | tf_op jit(solution)/shard_map/ppermute | solution.py:80
  226.3 36.9 %collective-permute-start.35 = (bf16[2,2,1,1,64,1536]{5,4,3,2,1,0:T(8,128)(2,1)S(1)}, bf16[2,2,1,1,64,1536]{5,4,3,2,1,0:T(8,128)(2,1)S(1)}, u32[]{:S(2)}, u32[]{:S(2)}) collective-permute-start(bf16[2,2,1,1,64,1536]{5,4,3,2,1,0:T(8,128)(2,1)S(1)} %constant_dynamic-slice_fusion.16), channel_id=1, source_target_pairs={{0,4},{2,6},{4,0},{6,2},{8,12},{10,14},{12,8},{14,10},{16,20},{18,... | collective-permute-start | bytes 2359304 | tf_op jit(solution)/shard_map/ppermute | solution.py:80
  264.4 11.8 %collective-permute-start.38 = (bf16[512,1536]{1,0:T(8,128)(2,1)}, bf16[512,1536]{1,0:T(8,128)(2,1)}, u32[]{:S(2)}, u32[]{:S(2)}) collective-permute-start(bf16[512,1536]{1,0:T(8,128)(2,1)} %get-tuple-element.212), channel_id=1, source_target_pairs={{0,2},{2,0},{4,6},{6,4},{8,10},{10,8},{12,14},{14,12},{16,18},{18,... | collective-permute-start | bytes 4718600 | tf_op jit(solution)/shard_map/ppermute | solution.py:80
  265.1 10.9 %collective-permute-start.36 = (bf16[2,2,1,1,1,24,1536]{6,5,4,3,2,1,0:T(8,128)(2,1)}, bf16[2,2,1,1,1,24,1536]{6,5,4,3,2,1,0:T(8,128)(2,1)S(1)}, u32[]{:S(2)}, u32[]{:S(2)}) collective-permute-start(bf16[2,2,1,1,1,24,1536]{6,5,4,3,2,1,0:T(8,128)(2,1)} %constant_dynamic-slice_fusion.15), channel_id=1, source_target_pairs={{0,4},{2,6},{4,0},{6,2},{8,12},{10,14},{12,8},{14,10},{16,20},{18,... | collective-permute-start | bytes 884744 | tf_op jit(solution)/shard_map/ppermute | solution.py:80
  267.1 16.6 %collective-permute-start.37 = (bf16[2,2,1,1,64,768]{5,4,3,2,1,0:T(8,128)(2,1)S(1)}, bf16[2,2,1,1,64,768]{5,4,3,2,1,0:T(8,128)(2,1)S(1)}, u32[]{:S(2)}, u32[]{:S(2)}) collective-permute-start(bf16[2,2,1,1,64,768]{5,4,3,2,1,0:T(8,128)(2,1)S(1)} %constant_dynamic-slice_fusion.14), channel_id=1, source_target_pairs={{0,1},{1,0},{2,3},{3,2},{4,5},{5,4},{6,7},{7,6},{8,9},{9,8},{10,11... | collective-permute-start | bytes 1179656 | tf_op jit(solution)/shard_map/ppermute | solution.py:80
  289.6 20.3 %collective-permute-start.41 = (bf16[1,2,1,1,1,24,1536]{6,5,4,3,2,1,0:T(8,128)(2,1)S(1)}, bf16[1,2,1,1,1,24,1536]{6,5,4,3,2,1,0:T(8,128)(2,1)S(1)}, u32[]{:S(2)}, u32[]{:S(2)}) collective-permute-start(bf16[1,2,1,1,1,24,1536]{6,5,4,3,2,1,0:T(8,128)(2,1)S(1)} %constant_dynamic-slice_fusion.13), channel_id=1, source_target_pairs={{0,16},{2,18},{4,20},{6,22},{8,24},{10,26},{12,28},{14,30},{16,0},... | collective-permute-start | bytes 442376 | tf_op jit(solution)/shard_map/ppermute | solution.py:80
  292.1 17.8 %collective-permute-start.42 = (bf16[1,2,1,1,64,768]{5,4,3,2,1,0:T(8,128)(2,1)S(1)}, bf16[1,2,1,1,64,768]{5,4,3,2,1,0:T(8,128)(2,1)S(1)}, u32[]{:S(2)}, u32[]{:S(2)}) collective-permute-start(bf16[1,2,1,1,64,768]{5,4,3,2,1,0:T(8,128)(2,1)S(1)} %constant_dynamic-slice_fusion.12), channel_id=1, source_target_pairs={{0,16},{2,18},{4,20},{6,22},{8,24},{10,26},{12,28},{14,30},{16,0},... | collective-permute-start | bytes 589832 | tf_op jit(solution)/shard_map/ppermute | solution.py:80
  294.3 14.9 %collective-permute-start.40 = (f32[1,1,1,1,4608]{4,3,2,1,0:T(1,128)S(1)}, f32[1,1,1,1,4608]{4,3,2,1,0:T(1,128)S(1)}, u32[]{:S(2)}, u32[]{:S(2)}) collective-permute-start(f32[1,1,1,1,4608]{4,3,2,1,0:T(1,128)S(1)} %add_bitcast_fusion.2), channel_id=1, source_target_pairs={{0,16},{2,18},{4,20},{6,22},{8,24},{10,26},{12,28},{14,30},{16,0},... | collective-permute-start | bytes 55304 | tf_op jit(solution)/shard_map/ppermute | solution.py:80
  296.8 13.1 %collective-permute-start.44 = (bf16[2,2,2,1,2,24,1536]{6,5,4,3,2,1,0:T(8,128)(2,1)S(1)}, bf16[2,2,2,1,2,24,1536]{6,5,4,3,2,1,0:T(8,128)(2,1)S(1)}, u32[]{:S(2)}, u32[]{:S(2)}) collective-permute-start(bf16[2,2,2,1,2,24,1536]{6,5,4,3,2,1,0:T(8,128)(2,1)S(1)} %constant_dynamic-slice_fusion.10), channel_id=1, source_target_pairs={{0,2},{2,0},{4,6},{6,4},{8,10},{10,8},{12,14},{14,12},{16,18},{18,... | collective-permute-start | bytes 3538952 | tf_op jit(solution)/shard_map/ppermute | solution.py:80
  296.9 13.4 %collective-permute-start.43 = (bf16[2,2,2,1,2,24,1536]{6,5,4,3,2,1,0:T(8,128)(2,1)S(1)}, bf16[2,2,2,1,2,24,1536]{6,5,4,3,2,1,0:T(8,128)(2,1)S(1)}, u32[]{:S(2)}, u32[]{:S(2)}) collective-permute-start(bf16[2,2,2,1,2,24,1536]{6,5,4,3,2,1,0:T(8,128)(2,1)S(1)} %constant_dynamic-slice_fusion.11), channel_id=1, source_target_pairs={{0,2},{2,0},{4,6},{6,4},{8,10},{10,8},{12,14},{14,12},{16,18},{18,... | collective-permute-start | bytes 3538952 | tf_op jit(solution)/shard_map/ppermute | solution.py:80
  315.7 14.5 %collective-permute-start.49 = (bf16[2,2,1,1,2,24,1536]{6,5,4,3,2,1,0:T(8,128)(2,1)S(1)}, bf16[2,2,1,1,2,24,1536]{6,5,4,3,2,1,0:T(8,128)(2,1)S(1)}, u32[]{:S(2)}, u32[]{:S(2)}) collective-permute-start(bf16[2,2,1,1,2,24,1536]{6,5,4,3,2,1,0:T(8,128)(2,1)S(1)} %constant_dynamic-slice_fusion.6), channel_id=1, source_target_pairs={{0,4},{2,6},{4,0},{6,2},{8,12},{10,14},{12,8},{14,10},{16,20},{18,... | collective-permute-start | bytes 1769480 | tf_op jit(solution)/shard_map/ppermute | solution.py:80
  317.4 14.2 %collective-permute-start.48 = (bf16[2,2,2,1,1,24,1536]{6,5,4,3,2,1,0:T(8,128)(2,1)S(1)}, bf16[2,2,2,1,1,24,1536]{6,5,4,3,2,1,0:T(8,128)(2,1)S(1)}, u32[]{:S(2)}, u32[]{:S(2)}) collective-permute-start(bf16[2,2,2,1,1,24,1536]{6,5,4,3,2,1,0:T(8,128)(2,1)S(1)} %constant_dynamic-slice_fusion.7), channel_id=1, source_target_pairs={{0,1},{1,0},{2,3},{3,2},{4,5},{5,4},{6,7},{7,6},{8,9},{9,8},{10,11... | collective-permute-start | bytes 1769480 | tf_op jit(solution)/shard_map/ppermute | solution.py:80
  332.2 10.8 %collective-permute-start.53 = (bf16[2,2,1,1,1,24,1536]{6,5,4,3,2,1,0:T(8,128)(2,1)S(1)}, bf16[2,2,1,1,1,24,1536]{6,5,4,3,2,1,0:T(8,128)(2,1)S(1)}, u32[]{:S(2)}, u32[]{:S(2)}) collective-permute-start(bf16[2,2,1,1,1,24,1536]{6,5,4,3,2,1,0:T(8,128)(2,1)S(1)} %constant_dynamic-slice_fusion.4), channel_id=1, source_target_pairs={{0,1},{1,0},{2,3},{3,2},{4,5},{5,4},{6,7},{7,6},{8,9},{9,8},{10,11... | collective-permute-start | bytes 884744 | tf_op jit(solution)/shard_map/ppermute | solution.py:80
  336.7 7.1 %collective-permute-start.52 = (bf16[2,2,1,1,1,24,1536]{6,5,4,3,2,1,0:T(8,128)(2,1)S(1)}, bf16[2,2,1,1,1,24,1536]{6,5,4,3,2,1,0:T(8,128)(2,1)S(1)}, u32[]{:S(2)}, u32[]{:S(2)}) collective-permute-start(bf16[2,2,1,1,1,24,1536]{6,5,4,3,2,1,0:T(8,128)(2,1)S(1)} %constant_dynamic-slice_fusion.5), channel_id=1, source_target_pairs={{0,4},{2,6},{4,0},{6,2},{8,12},{10,14},{12,8},{14,10},{16,20},{18,... | collective-permute-start | bytes 884744 | tf_op jit(solution)/shard_map/ppermute | solution.py:80
  348.3 12.4 %collective-permute-start.56 = (bf16[1,2,1,1,1,24,1536]{6,5,4,3,2,1,0:T(8,128)(2,1)S(1)}, bf16[1,2,1,1,1,24,1536]{6,5,4,3,2,1,0:T(8,128)(2,1)S(1)}, u32[]{:S(2)}, u32[]{:S(2)}) collective-permute-start(bf16[1,2,1,1,1,24,1536]{6,5,4,3,2,1,0:T(8,128)(2,1)S(1)} %constant_dynamic-slice_fusion.1), channel_id=1, source_target_pairs={{0,16},{2,18},{4,20},{6,22},{8,24},{10,26},{12,28},{14,30},{16,0},... | collective-permute-start | bytes 442376 | tf_op jit(solution)/shard_map/ppermute | solution.py:80
  351.8 10.8 %collective-permute-start.54 = (bf16[1,2,1,1,1,24,1536]{6,5,4,3,2,1,0:T(8,128)(2,1)S(1)}, bf16[1,2,1,1,1,24,1536]{6,5,4,3,2,1,0:T(8,128)(2,1)S(1)}, u32[]{:S(2)}, u32[]{:S(2)}) collective-permute-start(bf16[1,2,1,1,1,24,1536]{6,5,4,3,2,1,0:T(8,128)(2,1)S(1)} %constant_dynamic-slice_fusion.3), channel_id=1, source_target_pairs={{0,16},{2,18},{4,20},{6,22},{8,24},{10,26},{12,28},{14,30},{16,0},... | collective-permute-start | bytes 442376 | tf_op jit(solution)/shard_map/ppermute | solution.py:80
  353.1 62.3 %collective-permute-start.63 = (bf16[2,512,768]{2,1,0:T(8,128)(2,1)}, bf16[2,512,768]{2,1,0:T(8,128)(2,1)}, u32[]{:S(2)}, u32[]{:S(2)}) collective-permute-start(bf16[2,512,768]{2,1,0:T(8,128)(2,1)} %pad_maximum_fusion.5), channel_id=1, source_target_pairs={{1,2},{2,1},{5,6},{6,5},{9,10},{10,9},{13,14},{14,13},{17,18},{18,... | collective-permute-start | bytes 4718600 | tf_op jit(solution)/shard_map/ppermute | solution.py:169
  369.4 7.6 %collective-permute-start.59 = (f32[184,128]{1,0:T(8,128)S(1)}, f32[184,128]{1,0:T(8,128)S(1)}, u32[]{:S(2)}, u32[]{:S(2)}) collective-permute-start(f32[184,128]{1,0:T(8,128)S(1)} %add.560), channel_id=1, source_target_pairs={{0,1},{1,0},{2,3},{3,2},{4,5},{5,4},{6,7},{7,6},{8,9},{9,8},{10,11... | collective-permute-start | bytes 282632 | tf_op jit(solution)/shard_map/ppermute | solution.py:80
  386.3 6.6 %collective-permute-start.62 = (f32[184,128]{1,0:T(8,128)S(1)}, f32[184,128]{1,0:T(8,128)S(1)}, u32[]{:S(2)}, u32[]{:S(2)}) collective-permute-start(f32[184,128]{1,0:T(8,128)S(1)} %add.563), channel_id=1, source_target_pairs={{0,16},{2,18},{4,20},{6,22},{8,24},{10,26},{12,28},{14,30},{16,0},... | collective-permute-start | bytes 282632 | tf_op jit(solution)/shard_map/ppermute | solution.py:80
  (129 other events, 909.2 us)
Sparse Core Ops, SparseCore 0:
  47.5 104.9 all-gather.1
  190.1 102.4 reduce-scatter.2
  311.9 29.2 reduce-scatter.4

commit v4 on v3

--- a/solution.py
+++ b/solution.py
@@ -41,16 +41,6 @@
     return jax.nn.silu(waves).astype(BFLOAT)
 
 
-def layer_norm(values):
-    centered = values - jnp.mean(values, axis=-1, keepdims=True)
-    variance = jnp.mean(centered * centered, axis=-1, keepdims=True)
-    return centered * lax.rsqrt(variance + EPS_NORM)
-
-
-def modulate(values, shift, scale):
-    return layer_norm(values) * (1.0 + scale) + shift
-
-
 def core_link():
     return (DP, 1)
 
@@ -141,7 +131,7 @@
     block = matrix.reshape((2,) * bits + (rows // 2**split, columns))
     far = far_links()
     plane = [far[0], row_link()] if row_early else [row_link(), far[0]]
-    order = [core_link()] + plane + far[:0:-1]
+    order = [core_link()] + plane + far[1:]
     kinds = [BFLOAT] * (len(order) - 1) + [FLOAT]
     steps = [
         lambda state, link=link, kind=kind: shrink(state, link, head, kind)
@@ -311,7 +301,10 @@
     return specs, operands
 
 
-KERNEL = pltpu.CompilerParams(vmem_limit_bytes=48 * 1024 * 1024)
+def room(mebibytes):
+    return pltpu.CompilerParams(vmem_limit_bytes=mebibytes * 1024 * 1024)
+
+
 LIGHT = pl.CostEstimate(flops=1000, bytes_accessed=1000, transcendentals=0)
 
 
@@ -327,7 +320,7 @@
             jax.ShapeDtypeStruct((frames, D), BFLOAT),
             jax.ShapeDtypeStruct((PAIRS, 2, frames), FLOAT),
         ],
-        compiler_params=KERNEL,
+        compiler_params=room(48),
         cost_estimate=LIGHT,
     )(queries, *operands)
 
@@ -342,7 +335,7 @@
         out_specs=[column_block(frames)] + [whole_block(joint.shape) for joint, _ in key_values],
         out_shape=[jax.ShapeDtypeStruct((frames, D), BFLOAT)]
         + [jax.ShapeDtypeStruct(joint.shape, BFLOAT) for joint, _ in key_values],
-        compiler_params=KERNEL,
+        compiler_params=room(48),
         cost_estimate=LIGHT,
     )(queries, out, out_grad, logs, *operands)
 
@@ -366,7 +359,7 @@
     return pl.pallas_call(
         outer_kernel,
         out_shape=jax.ShapeDtypeStruct(shape, BFLOAT),
-        compiler_params=KERNEL,
+        compiler_params=room(48),
         cost_estimate=LIGHT,
     )(*operands)
 
@@ -582,7 +575,7 @@
         in_specs=memory,
         out_specs=[pl.BlockSpec(memory_space=pltpu.VMEM)] * len(shapes),
         out_shape=[jax.ShapeDtypeStruct(shape, FLOAT) for shape in shapes],
-        compiler_params=KERNEL,
+        compiler_params=room(48),
         cost_estimate=LIGHT,
     )(*operands)
 
@@ -599,13 +592,121 @@
     return values * half, half + (0.5 * values) * (1.0 - bend * bend) * slope
 
 
+ROWS = 512
+SHIFT_SELF, SCALE_SELF, GATE_SELF, SHIFT_MLP, SCALE_MLP, GATE_MLP = range(6)
+
+
+def block_of(modulation_ref, place):
+    return modulation_ref[:, place * D : (place + 1) * D]
+
+
+def over_rows(frames, body, start=None):
+    def step(place, carry):
+        return body(pl.ds(pl.multiple_of(place * ROWS, ROWS), ROWS), carry)
+
+    return lax.fori_loop(0, frames // ROWS, step, start)
+
+
+def normed(values):
+    centered = values - jnp.mean(values, axis=-1, keepdims=True)
+    rate = lax.rsqrt(jnp.mean(centered * centered, axis=-1, keepdims=True) + EPS_NORM)
+    return centered * rate, rate
+
+
+def normed_back(grad, norm, rate):
+    inner = jnp.mean(grad * norm, axis=-1, keepdims=True)
+    return rate * (grad - jnp.mean(grad, axis=-1, keepdims=True) - norm * inner)
+
+
+def down(values):
+    return jnp.sum(values, axis=0, keepdims=True)
+
+
+def no_sums(count):
+    return (jnp.zeros((1, D), FLOAT),) * count
+
+
+def first_kernel(
+    in_ref, modulation_ref, query_weight_ref, pair_weight_ref, self_input_ref, query_ref, pair_ref
+):
+    shift = block_of(modulation_ref, SHIFT_SELF)
+    scale = 1.0 + block_of(modulation_ref, SCALE_SELF)
+
+    def some(rows, carry):
+        norm, _ = normed(in_ref[rows, :].astype(FLOAT))
+        self_input_ref[rows, :] = (norm * scale + shift).astype(BFLOAT)
+        return carry
+
+    over_rows(in_ref.shape[0], some)
+    pair_ref[...] = nn(self_input_ref[...], pair_weight_ref[...]).astype(BFLOAT)
+    query_ref[...] = nn(self_input_ref[...], query_weight_ref[...]).astype(BFLOAT)
+
+
+def between_kernel(
+    attn_ref,
+    project_ref,
+    in_ref,
+    modulation_ref,
+    query_weight_ref,
+    branch_ref,
+    after_ref,
+    cross_input_ref,
+    query_ref,
+):
+    branch_ref[...] = nn(attn_ref[...], project_ref[...])
+    gate = block_of(modulation_ref, GATE_SELF)
+
+    def some(rows, carry):
+        after = in_ref[rows, :].astype(FLOAT) + gate * branch_ref[rows, :]
+        after_ref[rows, :] = after
+        norm, _ = normed(after)
+        cross_input_ref[rows, :] = norm.astype(BFLOAT)
+        return carry
+
+    over_rows(in_ref.shape[0], some)
+    query_ref[...] = nn(cross_input_ref[...], query_weight_ref[...]).astype(BFLOAT)
+
+
 def mlp_kernel(
-    input_ref, grad_ref, fc1_ref, fc2_ref, branch_ref, in_grad_ref, part_ref, input_t, grad_t
+    attn_ref,
+    project_ref,
+    after_ref,
+    modulation_ref,
+    out_grad_ref,
+    fc1_ref,
+    fc2_ref,
+    out_ref,
+    res_grad_ref,
+    cross_out_grad_ref,
+    attn_grad_ref,
+    sums_ref,
+    part_ref,
+    input_ref,
+    grad_ref,
+    input_t,
+    grad_t,
+    joined_ref,
+    branch_ref,
+    in_grad_ref,
 ):
     step = pl.program_id(0) * pl.num_programs(1) + pl.program_id(1)
+    last = pl.num_programs(0) * pl.num_programs(1) - 1
+    frames = attn_ref.shape[0]
+    gate = block_of(modulation_ref, GATE_MLP)
+    scale = 1.0 + block_of(modulation_ref, SCALE_MLP)
 
     @pl.when(step == 0)
     def _():
+        shift = block_of(modulation_ref, SHIFT_MLP)
+        joined_ref[...] = after_ref[...] + nn(attn_ref[...], project_ref[...])
+
+        def some(rows, carry):
+            norm, _ = normed(joined_ref[rows, :])
+            input_ref[rows, :] = (norm * scale + shift).astype(BFLOAT)
+            grad_ref[rows, :] = (gate * out_grad_ref[rows, :].astype(FLOAT)).astype(BFLOAT)
+            return carry
+
+        over_rows(frames, some)
         input_t[...] = input_ref[...].T
         grad_t[...] = grad_ref[...].T
 
@@ -625,47 +726,172 @@
         branch_ref[...] += branch
         in_grad_ref[...] += in_grad
 
-    far, rows = part_ref.shape[2], part_ref.shape[4]
+    far, size = part_ref.shape[2], part_ref.shape[4]
     for kind, product in enumerate((nn(input_t[...], pre_grad), nn(grad_t[...], act))):
         product = product.astype(BFLOAT)
         for place in range(4 * far):
-            part_ref[0, place % 4, place // 4, kind] = product[place * rows : (place + 1) * rows]
+            part_ref[0, place % 4, place // 4, kind] = product[place * size : (place + 1) * size]
+
+    @pl.when(step == last)
+    def _():
+        def some(rows, carry):
+            gate_sum, shift_sum, scale_sum = carry
+            joined, branch_here = joined_ref[rows, :], branch_ref[rows, :]
+            out_grad, in_grad_here = out_grad_ref[rows, :].astype(FLOAT), in_grad_ref[rows, :]
+            out_ref[rows, :] = (joined + gate * branch_here).astype(BFLOAT)
+            norm, rate = normed(joined)
+            res_grad = out_grad + normed_back(in_grad_here * scale, norm, rate)
+            res_grad_ref[rows, :] = res_grad
+            cross_out_grad_ref[rows, :] = res_grad.astype(BFLOAT)
+            return (
+                gate_sum + down(out_grad * branch_here),
+                shift_sum + down(in_grad_here),
+                scale_sum + down(in_grad_here * norm),
+            )
+
+        gate_sum, shift_sum, scale_sum = over_rows(frames, some, no_sums(3))
+        sums_ref[:, :D] = shift_sum
+        sums_ref[:, D : 2 * D] = scale_sum
+        sums_ref[:, 2 * D :] = gate_sum
+        attn_grad_ref[...] = nt(cross_out_grad_ref[...], project_ref[...]).astype(BFLOAT)
+
+
+def between_back_kernel(
+    query_grad_ref,
+    query_weight_ref,
+    after_ref,
+    res_grad_ref,
+    branch_ref,
+    modulation_ref,
+    project_ref,
+    self_res_ref,
+    out_grad_ref,
+    attn_grad_ref,
+    sums_ref,
+    in_grad_ref,
+):
+    in_grad_ref[...] = nt(query_grad_ref[...], query_weight_ref[...])
+    gate = block_of(modulation_ref, GATE_SELF)
+
+    def some(rows, carry):
+        norm, rate = normed(after_ref[rows, :])
+        res_grad = res_grad_ref[rows, :] + normed_back(in_grad_ref[rows, :], norm, rate)
+        self_res_ref[rows, :] = res_grad
+        out_grad_ref[rows, :] = (gate * res_grad).astype(BFLOAT)
+        return (carry[0] + down(res_grad * branch_ref[rows, :]),)
+
+    (sums_ref[...],) = over_rows(after_ref.shape[0], some, no_sums(1))
+    attn_grad_ref[...] = nt(out_grad_ref[...], project_ref[...]).astype(BFLOAT)
+
+
+def first_back_kernel(
+    query_grad_ref,
+    pair_grad_ref,
+    query_weight_ref,
+    pair_weight_ref,
+    in_ref,
+    modulation_ref,
+    self_res_ref,
+    out_ref,
+    sums_ref,
+    in_grad_ref,
+):
+    in_grad_ref[...] = nt(query_grad_ref[...], query_weight_ref[...]) + nt(
+        pair_grad_ref[...], pair_weight_ref[...]
+    )
+    scale = 1.0 + block_of(modulation_ref, SCALE_SELF)
+
+    def some(rows, carry):
+        norm, rate = normed(in_ref[rows, :].astype(FLOAT))
+        grad = in_grad_ref[rows, :]
+        res_grad = self_res_ref[rows, :] + normed_back(grad * scale, norm, rate)
+        out_ref[rows, :] = res_grad.astype(BFLOAT)
+        return carry[0] + down(grad), carry[1] + down(grad * norm)
+
+    shift_sum, scale_sum = over_rows(in_ref.shape[0], some, no_sums(2))
+    sums_ref[:, :D] = shift_sum
+    sums_ref[:, D:] = scale_sum
+
+
+def left_half(weights):
+    return weights, pl.BlockSpec((D, D), lambda step: (0, 0))
+
+
+def right_half(weights):
+    return weights, pl.BlockSpec((D, D), lambda step: (0, 1))
+
+
+def frame_call(kernel, results, *operands, scratch=()):
+    specs, arrays = [], []
+    for operand in operands:
+        if isinstance(operand, tuple):
+            arrays.append(operand[0])
+            specs.append(operand[1])
+        else:
+            arrays.append(operand)
+            specs.append(whole_block(operand.shape))
+    return pl.pallas_call(
+        kernel,
+        grid=(1,),
+        in_specs=specs,
+        out_specs=[whole_block(shape) for shape, _ in results],
+        out_shape=[jax.ShapeDtypeStruct(shape, kind) for shape, kind in results],
+        scratch_shapes=[pltpu.VMEM(shape, kind) for shape, kind in scratch],
+        compiler_params=room(48),
+        cost_estimate=LIGHT,
+    )(*arrays)
 
 
 MLP_TILE = 512
 
 
-def mlp_both(mlp_input, mlp_grad, weights):
-    frames = mlp_input.shape[0]
+def mlp_both(cross_attn, project, after_self, modulation, out_grad, weights):
+    frames = cross_attn.shape[0]
     far = lax.axis_size("far")
     rows = D // (4 * far)
     tiles = HALF // MLP_TILE
-    whole = pl.BlockSpec((frames, D), lambda half, tile: (0, 0))
+    once = dict(pipeline_mode=pl.Buffered(1))
+    whole = pl.BlockSpec((frames, D), lambda half, tile: (0, 0), **once)
+    square = (frames, D)
     return pl.pallas_call(
         mlp_kernel,
         grid=(2, tiles),
         in_specs=[
             whole,
+            pl.BlockSpec((D, D), lambda half, tile: (0, 1), **once),
+            whole,
+            pl.BlockSpec((1, 6 * D), lambda half, tile: (0, 0)),
             whole,
             pl.BlockSpec((1, D, MLP_TILE), lambda half, tile: (half, 0, tile)),
             pl.BlockSpec((1, D, MLP_TILE), lambda half, tile: (half, 0, tile + tiles)),
         ],
-        out_specs=[
-            whole,
-            whole,
+        out_specs=[whole] * 4
+        + [
+            pl.BlockSpec((1, 3 * D), lambda half, tile: (0, 0)),
             pl.BlockSpec(
                 (1, 4, far, 2, rows, MLP_TILE), lambda half, tile: (half, 0, 0, 0, 0, tile)
             ),
         ],
         out_shape=[
-            jax.ShapeDtypeStruct((frames, D), FLOAT),
-            jax.ShapeDtypeStruct((frames, D), FLOAT),
+            jax.ShapeDtypeStruct(square, BFLOAT),
+            jax.ShapeDtypeStruct(square, FLOAT),
+            jax.ShapeDtypeStruct(square, BFLOAT),
+            jax.ShapeDtypeStruct(square, BFLOAT),
+            jax.ShapeDtypeStruct((1, 3 * D), FLOAT),
             jax.ShapeDtypeStruct((2, 4, far, 2, rows, HALF), BFLOAT),
         ],
-        scratch_shapes=[pltpu.VMEM((D, frames), BFLOAT), pltpu.VMEM((D, frames), BFLOAT)],
-        compiler_params=KERNEL,
+        scratch_shapes=[
+            pltpu.VMEM(square, BFLOAT),
+            pltpu.VMEM(square, BFLOAT),
+            pltpu.VMEM((D, frames), BFLOAT),
+            pltpu.VMEM((D, frames), BFLOAT),
+            pltpu.VMEM(square, FLOAT),
+            pltpu.VMEM(square, FLOAT),
+            pltpu.VMEM(square, FLOAT),
+        ],
+        compiler_params=room(48),
         cost_estimate=LIGHT,
-    )(mlp_input, mlp_grad, weights, weights)
+    )(cross_attn, project, after_self, modulation, out_grad, weights, weights)
 
 
 def per_device(
@@ -703,25 +929,20 @@
                 jnp.concatenate([w_qkv[:, :D], w_out, w_qkv[:, D:]], axis=1).astype(BFLOAT), "last"
             ),
             "last",
-            far[1:],
+            far[:0:-1],
         )
     ]
     second = [
         gather_chain(
             with_bits(jnp.concatenate([w_cq, w_cout], axis=1).astype(BFLOAT), "last"),
             "last",
-            far[1:] + x_first,
+            far[:0:-1] + x_first,
         ),
         gather_chain(
             with_bits(w_ckv.astype(BFLOAT).reshape(w_ckv.shape[0], D), "columns"),
             "columns",
-            far[1:] + y_first,
+            far[:0:-1] + y_first,
         ),
-    ]
-    masters = [
-        jnp.concatenate([w_ada, w_qkv, w_out, w_cq, w_cout], axis=1),
-        w_ckv.reshape(w_ckv.shape[0], D),
-        jnp.concatenate([w_fc1, w_fc2.T], axis=1),
     ]
     mlp_shard = jnp.concatenate([w_fc1.astype(BFLOAT), w_fc2.T.astype(BFLOAT)], axis=1)
     inputs = swap_place(block_in[0])
@@ -739,29 +960,35 @@
         def step(state):
             condition, product = state
             bit = bit_of(link)
-            product = product.reshape(-1, 2, 6 * D)
-            kept = lax.dynamic_slice_in_dim(product, bit, 1, axis=1)
-            sent = lax.dynamic_slice_in_dim(product, 1 - bit, 1, axis=1)
-            return condition, (kept + cross(sent, link)).reshape(-1, 6 * D)
+            dim = 1 if link == row_link() else dp_bits() - link[1].bit_length()
+            kept = lax.dynamic_slice_in_dim(product, bit, 1, axis=dim)
+            sent = lax.dynamic_slice_in_dim(product, 1 - bit, 1, axis=dim)
+            product = kept + cross(sent, link)
+            if link == row_link():
+                product = product.reshape((2,) * (dp_bits() - 1) + (6 * D,))
+            return condition, product
 
         return step
 
     def last_step(state):
         condition, product = state
-        return condition, product + cross(product, core_link())
+        return condition, (product + cross(product, core_link())).reshape(1, 6 * D)
 
     steps = lax.dynamic_update_slice(jnp.zeros((clips,), jnp.int32), timesteps, (data_at,))
     timing = Chain(
         steps,
         [add_step(link) for link in [core_link()] + far_links()[1:] + far_links()[:1]]
         + [lambda steps: keep_step(row_link())(project(steps))]
-        + [keep_step(link) for link in far_links()]
+        + [keep_step(link) for link in far_links()[1:] + far_links()[:1]]
         + [last_step],
     )
     far_count = len(far) - 1
     slots = far_count + 3
     for slot in range(slots):
-        timing.advance({0: 1 + far_count, 1: 3, 2: far_count, 3: 1}.get(slot, 0))
+        if slot < far_count:
+            timing.advance(1 + (slot == 0) + (slot == far_count - 1))
+        else:
+            timing.advance((1, far_count, 2)[slot - far_count])
         if slot == far_count:
             joint = first[0].state
             first = [
@@ -783,25 +1010,30 @@
         elif slot < slots - 1:
             tie([timing] + first + second)
         else:
-            masters = tie([timing] + first, *masters)
+            wide = tie([timing] + first, w_ada, w_qkv, w_out, w_cq, w_cout, w_fc1, w_fc2)
+            masters = [
+                jnp.concatenate(wide[:5], axis=1),
+                w_ckv.reshape(w_ckv.shape[0], D),
+                jnp.concatenate([wide[5], wide[6].T], axis=1),
+            ]
             (weight_squares,) = whole_call(weight_kernel, [(1, LINE)], *masters)
     condition, modulation = timing.finish()
     query_out, w_key_value = [chain.finish().reshape(D, 2 * D) for chain in first]
-    w_query, w_project = query_out[:, :D], query_out[:, D:]
-
-    inputs = inputs.astype(FLOAT)
+    square = (frames, D)
     core_at = data_at % 2
     own_allowed = lax.dynamic_slice_in_dim(masks, core_at * frames, frames)
     other_allowed = lax.dynamic_slice_in_dim(masks, (1 - core_at) * frames, frames)
     own_bias, other_bias = bias_of(own_allowed), bias_of(other_allowed)
     text_bias = bias_of(masks[2 * frames :])
-    shift_self, scale_self, gate_self, shift_mlp, scale_mlp, gate_mlp = jnp.split(
-        modulation, 6, axis=-1
-    )
-
-    self_input = modulate(inputs, shift_self, scale_self).astype(BFLOAT)
-    key_value = nn(self_input, w_key_value).astype(BFLOAT)
-    query = nn(self_input, w_query).astype(BFLOAT)
+
+    self_input, query, key_value = frame_call(
+        first_kernel,
+        [(square, BFLOAT), (square, BFLOAT), ((frames, 2 * D), BFLOAT)],
+        inputs,
+        modulation,
+        left_half(query_out),
+        w_key_value,
+    )
     other_key_value = cross(key_value, core_link())
     query, other_key_value = tie(second, query, other_key_value)
     for chain in second:
@@ -810,26 +1042,32 @@
     self_keys = [(key_value, own_bias), (other_key_value, other_bias)]
     self_attn, self_logs = attend(query, self_keys, plain_places)
     self_attn, cotangent = tie(second, self_attn, cotangent)
-    out_grad = swap_place(cotangent[0])
+    swapped_cotangent = swap_only(cotangent[0])
     cross_pair, w_text = [chain.finish() for chain in second]
     cross_pair, w_text = cross_pair.reshape(D, 2 * D), w_text.reshape(DT, 2 * D)
-    w_cross_query, w_cross_project = cross_pair[:, :D], cross_pair[:, D:]
-    self_branch = nn(self_attn, w_project)
-    after_self = inputs + gate_self * self_branch
+    self_branch, after_self, cross_input, cross_query = frame_call(
+        between_kernel,
+        [(square, FLOAT), (square, FLOAT), (square, BFLOAT), (square, BFLOAT)],
+        self_attn,
+        right_half(query_out),
+        inputs,
+        modulation,
+        left_half(cross_pair),
+    )
 
     text_pair = nn(clip_text, w_text).astype(BFLOAT)
-    cross_input = layer_norm(after_self).astype(BFLOAT)
-    cross_query = nn(cross_input, w_cross_query).astype(BFLOAT)
     text_keys = [(text_pair, text_bias)]
     cross_attn, cross_logs = attend(cross_query, text_keys, half_places)
-    after_cross = after_self + nn(cross_attn, w_cross_project)
-
-    mlp_input = modulate(after_cross, shift_mlp, scale_mlp).astype(BFLOAT)
-    mlp_input, out_grad = tie([], mlp_input, out_grad)
-    out_grad = out_grad.astype(FLOAT)
-    mlp_grad = (gate_mlp * out_grad).astype(BFLOAT)
-    mlp_branch, mlp_in_grad, mlp_part = mlp_both(
-        mlp_input, mlp_grad, mlp_all.reshape(2, D, 2 * HALF)
+
+    cross_attn, own, cotangent = tie([], cross_attn, on_own_chip(), cotangent)
+    out_grad = jnp.where(own, cotangent[0], swapped_cotangent)
+    block_out, cross_res_grad, cross_out_grad, cross_attn_grad, mlp_sums, mlp_part = mlp_both(
+        cross_attn,
+        cross_pair,
+        after_self,
+        modulation,
+        out_grad,
+        mlp_all.reshape(2, D, 2 * HALF),
     )
     mlp_part = lax.psum_scatter(
         mlp_part.reshape((8,) + mlp_part.shape[2:]),
@@ -837,45 +1075,26 @@
         scatter_dimension=0,
         tiled=False,
     )
-    block_out = (after_cross + gate_mlp * mlp_branch).astype(BFLOAT)
-    gate_mlp_grad = jnp.sum(out_grad * mlp_branch, axis=0, keepdims=True)
-    mlp_back = jax.vjp(modulate, after_cross, shift_mlp, scale_mlp)[1]
-    cross_res_grad, shift_mlp_grad, scale_mlp_grad = mlp_back(mlp_in_grad)
-    cross_res_grad = out_grad + cross_res_grad
-    cross_res_grad, block_out, gate_mlp_grad = tie([], cross_res_grad, block_out, gate_mlp_grad)
-
-    cross_out_grad = cross_res_grad.astype(BFLOAT)
-    cross_attn_grad = nt(cross_out_grad, w_cross_project).astype(BFLOAT)
+
     cross_query_grad, text_pair_grad = attend_back(
         cross_query, cross_attn, cross_attn_grad, cross_logs, text_keys, half_places
     )
-    cross_chains = [
-        scatter_chain(
-            outer((cross_input, cross_query_grad), (cross_attn, cross_out_grad)), "last", False
-        ),
-        scatter_chain(outer((clip_text, text_pair_grad)), "columns", True),
-    ]
-    (cross_query_grad,) = tie(cross_chains, cross_query_grad)
-    for chain in cross_chains:
-        chain.advance()
-    cross_in_grad = nt(cross_query_grad, w_cross_query)
-    norm_back = jax.vjp(layer_norm, after_self)[1]
-    self_res_grad = cross_res_grad + norm_back(cross_in_grad)[0]
-
-    gate_self_grad = jnp.sum(self_res_grad * self_branch, axis=0, keepdims=True)
-    self_out_grad = (gate_self * self_res_grad).astype(BFLOAT)
-    self_attn_grad = nt(self_out_grad, w_project).astype(BFLOAT)
-    self_attn_grad, self_out_grad = tie(cross_chains, self_attn_grad, self_out_grad)
-    for chain in cross_chains:
-        chain.advance()
+    self_res_grad, self_out_grad, self_attn_grad, gate_self_grad = frame_call(
+        between_back_kernel,
+        [(square, FLOAT), (square, BFLOAT), (square, BFLOAT), ((1, D), FLOAT)],
+        cross_query_grad,
+        left_half(cross_pair),
+        after_self,
+        cross_res_grad,
+        self_branch,
+        modulation,
+        right_half(query_out),
+        scratch=[(square, FLOAT)],
+    )
+
     query_grad, own_pair_grad, other_pair_grad = attend_back(
         query, self_attn, self_attn_grad, self_logs, self_keys, plain_places
     )
-    query_grad, own_pair_grad, other_pair_grad = tie(
-        cross_chains, query_grad, own_pair_grad, other_pair_grad
-    )
-    for chain in cross_chains:
-        chain.advance()
     pair_grad = (
         own_pair_grad.astype(FLOAT) + cross(other_pair_grad, core_link()).astype(FLOAT)
     ).astype(BFLOAT)
@@ -885,24 +1104,31 @@
         ),
         scatter_chain(outer((self_input, pair_grad)), "last", True),
     ]
+    cross_query_grad, text_pair_grad = tie(last_chains, cross_query_grad, text_pair_grad)
+    for chain in last_chains:
+        chain.advance()
+    cross_chains = [
+        scatter_chain(
+            outer((cross_input, cross_query_grad), (cross_attn, cross_out_grad)), "last", False
+        ),
+        scatter_chain(outer((clip_text, text_pair_grad)), "columns", True),
+    ]
     query_grad, pair_grad = tie(cross_chains + last_chains, query_grad, pair_grad)
-    for chain in cross_chains + last_chains:
+    for chain in last_chains + cross_chains:
         chain.advance()
-    in_grad_normed = nt(query_grad, w_query) + nt(pair_grad, w_key_value)
-    self_back = jax.vjp(modulate, inputs, shift_self, scale_self)[1]
-    input_res_grad, shift_self_grad, scale_self_grad = self_back(in_grad_normed)
-    input_grad = (self_res_grad + input_res_grad).astype(BFLOAT)
-    modulation_grad = jnp.concatenate(
-        [
-            shift_self_grad,
-            scale_self_grad,
-            gate_self_grad,
-            shift_mlp_grad,
-            scale_mlp_grad,
-            gate_mlp_grad,
-        ],
-        axis=-1,
-    )
+    input_grad, self_sums = frame_call(
+        first_back_kernel,
+        [(square, BFLOAT), ((1, 2 * D), FLOAT)],
+        query_grad,
+        pair_grad,
+        left_half(query_out),
+        w_key_value,
+        inputs,
+        modulation,
+        self_res_grad,
+        scratch=[(square, FLOAT)],
+    )
+    modulation_grad = jnp.concatenate([self_sums, gate_self_grad, mlp_sums], axis=-1)
 
     def join_step(link):
         def step(state):
@@ -919,23 +1145,29 @@
     joining = Chain(
         modulation_grad,
         [lambda state: (state + cross(state, core_link())).reshape(shape)]
-        + [join_step(link) for link in far[::-1] + [row_link()]],
-    )
+        + [join_step(link) for link in far[:0:-1] + [far[0], row_link()]],
+    )
+
+    chains = last_chains + cross_chains
+    joining.advance()
+    block_out, input_grad, mlp_part = tie([joining] + chains, block_out, input_grad, mlp_part)
+    mlp_raw = lax.psum_scatter(mlp_part, "far", scatter_dimension=0, tiled=False).astype(FLOAT)
+    for chain in chains:
+        chain.advance()
+    joining.advance(len(far) - 1)
+    block_out, input_grad = tie([joining] + chains, block_out, input_grad)
+    for chain in chains:
+        chain.advance()
     joining.advance(2)
-    block_out, input_grad, mlp_part = tie(
-        [joining] + cross_chains + last_chains, block_out, input_grad, mlp_part
-    )
-    mlp_raw = lax.psum_scatter(mlp_part, "far", scatter_dimension=0, tiled=False).astype(FLOAT)
-    for count in (len(far) - 2, 2):
-        for chain in cross_chains + last_chains:
-            chain.advance()
-        joining.advance(count)
-        block_out, input_grad = tie(
-            [joining] + cross_chains + last_chains, block_out, input_grad
-        )
-    mlp_raw, block_out, input_grad = tie(last_chains, mlp_raw, block_out, input_grad)
+    block_out, input_grad, mlp_raw = tie([joining] + chains, block_out, input_grad, mlp_raw)
+    for chain in chains:
+        chain.advance()
+    block_out, input_grad = tie(chains, block_out, input_grad)
     own_results = jnp.stack([block_out, input_grad])
     swapped_results = swap_only(own_results)
+    for chain in cross_chains:
+        chain.advance()
+    (swapped_results,) = tie(cross_chains, swapped_results)
     modulation_grad = joining.finish()
     ada_raw = jnp.einsum(
         "cr,cx->rx",

time: 431 us -> 424 us (0.984)
  waiting for transfers between devices: 166 us -> 126 us
  Pallas kernels: 80.1 us -> 112 us
  matrix products: 13.3 us -> 1.66 us
  starting transfers between devices: 74.6 us -> 85.2 us
    ppermute x64, waiting for transfers between devices: 166 us -> 124 us  [cross(): return lax.ppermute(values, link[0], pairs)]
    pallas_call x1 -> x5, Pallas kernels: 22.2 us -> 45.8 us  [the longest x1 26.1 us: mlp_both(): pl.pallas_call(mlp_kernel, grid=(2, tiles), in_specs=[whole, pl.BlockSpec...]
    ppermute x64, starting transfers between devices: 66.3 us -> 77.7 us  [cross(): return lax.ppermute(values, link[0], pairs)]
    convert_element_type x16, other arithmetic: 5.33 us -> 14.8 us  [shrink(): (kept.astype(FLOAT) + cross(sent.astype(BFLOAT), link).astype(FLOAT)).ast...]
    reduce_sum x9 -> x0, other arithmetic: 9.1 us -> none  [the longest x1 2.9 us: per_device(): gate_mlp_grad = jnp.sum(out_grad * mlp_branch, axis=0, keepdims=True)]
    pallas_call x2, Pallas kernels: 29.7 us -> 37.9 us  [attend_back(): pl.pallas_call(functools.partial(back_kernel, blocks, places), grid=(PAIR...]
    concatenate x17 -> x18, other arithmetic: 3.31 us -> 10.3 us  [grow(): return jnp.concatenate([low, high], axis=dim_of(link, head))]
    dot_general x6 -> x1, matrix products: 6.75 us -> 0.99 us  [nn(): lax.dot_general(left, right, (((1,), (0,)), ((), ())), preferred_element_...]
  transfers between devices with their start and end apart: 72 -> 72, of which waited for: 40 -> 40; matrix products, arithmetic and copies ran while one was open for 15% -> 14% of each run, Pallas kernels for 14% -> 19%
where the time goes in v4:
time: 424 us; the launch traced here: 419 us
  waiting for transfers between devices  126 us (30%)
  Pallas kernels  112 us (26%)
  starting transfers between devices  85.2 us (20%)
  other arithmetic  47.2 us (11%)
  local copies, waits for them, and re-layouts  29.9 us (7%)
  between operations  16.5 us (4%)
    ppermute x64, waiting for transfers between devices, cross(): return lax.ppermute(values, link[0], pairs)  124 us
    ppermute x64, starting transfers between devices, cross(): return lax.ppermute(values, link[0], pairs)  77.7 us
    pallas_call x2, Pallas kernels, attend_back(): pl.pallas_call(functools.partial(back_kernel, blocks, places), grid=(PAIR...  37.9 us
    pallas_call x1, Pallas kernels, mlp_both(): pl.pallas_call(mlp_kernel, grid=(2, tiles), in_specs=[whole, pl.BlockSpec...  26.1 us
    pallas_call x4, Pallas kernels, frame_call(): pl.pallas_call(kernel, grid=(1,), in_specs=specs, out_specs=[whole_block(...  19.6 us
    pallas_call x2, Pallas kernels, attend(): pl.pallas_call(functools.partial(attend_kernel, blocks), grid=(PAIRS,), i...  18.4 us
    unnamed x149, local copies, waits for them, and re-layouts  18 us
    convert_element_type x16, other arithmetic, shrink(): (kept.astype(FLOAT) + cross(sent.astype(BFLOAT), link).astype(FLOAT)).ast...  14.8 us
  transfers between devices with their start and end apart: 72, of which 40 were waited for; matrix products, arithmetic and copies ran while one was open for 14% of the time, Pallas kernels for 19%

profile of v4, /device:TPU:0, one launch (start us, length us, event | category | flops | bytes accessed | tf_op | source)
XLA Modules:
  0.0 418.7 jit_solution(6542334935303436889)
XLA Ops:
  10.5 3.7 collective-permute-start.2
  19.8 2.0 collective-permute-done.1
  24.2 2.6 collective-permute-start.3
  26.8 4.0 collective-permute-done.3
  32.3 2.0 collective-permute-done.4
  37.5 3.3 collective-permute-start.10
  43.9 5.8 %collective-permute-done.11 = bf16[1,1,1,1,64,768]{5,4,3,2,1,0:T(8,128)(2,1)S(1)} collective-permute-done((bf16[1,1,1,1,64,768]{5,4,3,2,1,0:T(8,128)(2,1)S(1)}, bf16[1,1,1,1,64,768]{5,4,3,2,1,0:T(8,128)(2,1)S(1)}, u32[]{:S(2)}, u32[]{:S(2)}) %collective-permute-start.11) | collective-permute-done | bytes 98336 | tf_op jit(solution)/shard_map/ppermute | solution.py:70
  52.5 5.6 %collective-permute-done.12 = f32[2,1,2,4608]{3,2,1,0:T(2,128)S(1)} collective-permute-done((f32[2,1,2,4608]{3,2,1,0:T(2,128)S(1)}, f32[2,1,2,4608]{3,2,1,0:T(2,128)S(1)}, u32[]{:S(2)}, u32[]{:S(2)}) %collective-permute-start.12) | collective-permute-done | bytes 73760 | tf_op jit(solution)/shard_map/ppermute | solution.py:70
  62.4 2.3 collective-permute-start.16
  64.7 4.3 %collective-permute-done.16 = bf16[2,1,1,1,1,24,1536]{6,5,4,3,2,1,0:T(8,128)(2,1)S(1)} collective-permute-done((bf16[2,1,1,1,1,24,1536]{6,5,4,3,2,1,0:T(8,128)(2,1)S(1)}, bf16[2,1,1,1,1,24,1536]{6,5,4,3,2,1,0:T(8,128)(2,1)S(1)}, u32[]{:S(2)}, u32[]{:S(2)}) %collective-permute-start.16) | collective-permute-done | bytes 147488 | tf_op jit(solution)/shard_map/ppermute | solution.py:70
  74.4 3.2 collective-permute-done.18
  85.1 4.5 %shard_map.320 = (bf16[512,768]{1,0:T(8,128)(2,1)S(1)}, bf16[512,768]{1,0:T(8,128)(2,1)S(1)}, bf16[512,1536]{1,0:T(8,128)(2,1)S(1)}) custom-call(bf16[512,768]{1,0:T(8,128)(2,1)S(1)} %broadcast_select_fusion.11.in_ref, f32[1,4608]{1,0:T(1,128)S(1)} %add_bitcast_fusion.1.modulation_ref, bf16[768,1536]{1,0:T(8,128)(2,1)} %bitcast.84, bf16[768,1536]{1,0:T(8,128)(2,1)} %bitcast.93), custom_call_target="tpu_custom_call" | custom-call | flops 1000 | bytes 1000 | tf_op jit(solution)/shard_map/pallas_call | solution.py:833
  92.4 9.2 %collective-permute-done.22 = bf16[2,2,1,1,1,24,1536]{6,5,4,3,2,1,0:T(8,128)(2,1)S(1)} collective-permute-done((bf16[2,2,1,1,1,24,1536]{6,5,4,3,2,1,0:T(8,128)(2,1)S(1)}, bf16[2,2,1,1,1,24,1536]{6,5,4,3,2,1,0:T(8,128)(2,1)S(1)}, u32[]{:S(2)}, u32[]{:S(2)}) %collective-permute-start.22) | collective-permute-done | bytes 294944 | tf_op jit(solution)/shard_map/ppermute | solution.py:70
  102.5 5.4 %collective-permute-done.23 = bf16[2,2,1,1,64,768]{5,4,3,2,1,0:T(8,128)(2,1)S(1)} collective-permute-done((bf16[2,2,1,1,64,768]{5,4,3,2,1,0:T(8,128)(2,1)S(1)}, bf16[2,2,1,1,64,768]{5,4,3,2,1,0:T(8,128)(2,1)S(1)}, u32[]{:S(2)}, u32[]{:S(2)}) %collective-permute-start.23) | collective-permute-done | bytes 393248 | tf_op jit(solution)/shard_map/ppermute | solution.py:70
  109.0 2.5 collective-permute-start.25
  115.2 12.5 %shard_map.321 = (bf16[512,768]{1,0:T(8,128)(2,1)S(1)}, f32[6,2,512]{2,1,0:T(2,128)S(1)}) custom-call(bf16[512,768]{1,0:T(8,128)(2,1)S(1)} %copy-done.12, bf16[512,1536]{1,0:T(8,128)(2,1)S(1)} %get-tuple-element.194.refs_1_.refs_2_.refs_4_.refs_5_, bf16[512,1536]{1,0:T(8,128)(2,1)S(1)} %get-tuple-element.194.refs_1_.refs_2_.refs_4_.refs_5_, ...), custom_call_target="tpu_custom_call" | custom-call | flops 1000 | bytes 1000 | tf_op jit(solution)/shard_map/pallas_call | solution.py:314
  127.7 3.8 collective-permute-done.25
  141.6 3.9 shard_map.322
  148.4 5.9 %shard_map.323 = (bf16[512,768]{1,0:T(8,128)(2,1)S(1)}, f32[6,2,512]{2,1,0:T(2,128)S(1)}) custom-call(bf16[512,768]{1,0:T(8,128)(2,1)S(1)} %get-tuple-element.205.refs_0_, bf16[256,1536]{1,0:T(8,128)(2,1)S(1)} %convolution_convert_fusion.refs_1_.refs_2_.refs_4_.refs_5_, bf16[256,1536]{1,0:T(8,128)(2,1)S(1)} %convolution_convert_fusion.refs_1_.refs_2_.refs_4_.refs_5_, ...), custom_call_target="tpu_custom_call" | custom-call | flops 1000 | bytes 1000 | tf_op jit(solution)/shard_map/pallas_call | solution.py:314
  154.4 26.1 %shard_map.324 = (bf16[512,768]{1,0:T(8,128)(2,1)S(1)}, f32[512,768]{1,0:T(8,128)S(1)}, bf16[512,768]{1,0:T(8,128)(2,1)S(1)}, bf16[512,768]{1,0:T(8,128)(2,1)S(1...) custom-call(bf16[512,768]{1,0:T(8,128)(2,1)S(1)} %get-tuple-element.210.attn_ref.refs_1_.refs_2_, ...), custom_call_target="tpu_custom_call" | custom-call | flops 1000 | bytes 1000 | tf_op jit(solution)/shard_map/pallas_call | solution.py:856
  186.7 7.8 %shard_map.325 = (bf16[512,768]{1,0:T(8,128)(2,1)S(1)}, bf16[256,1536]{1,0:T(8,128)(2,1)S(1)}) custom-call(bf16[512,768]{1,0:T(8,128)(2,1)S(1)} %copy-done.19, bf16[512,768]{1,0:T(8,128)(2,1)S(1)} %get-tuple-element.210.attn_ref.refs_1_.refs_2_, bf16[512,768]{1,0:T(8,128)(2,1)S(1)} %copy-done.42, f32[6,2,512]{2,1,0:T(2,128)S(1)} %get-tuple-element.216.refs_3_, ...), custom_call_target="tpu_custom_call" | custom-call | flops 1000 | bytes 1000 | tf_op jit(solution)/shard_map/pallas_call | solution.py:331
  195.4 6.5 %shard_map.326 = (f32[512,768]{1,0:T(8,128)S(1)}, bf16[512,768]{1,0:T(8,128)(2,1)S(1)}, bf16[512,768]{1,0:T(8,128)(2,1)S(1)}, f32[1,768]{1,0:T(1,128)S(1)}) custom-call(bf16[512,768]{1,0:T(8,128)(2,1)S(1)} %get-tuple-element.227.query_grad_ref.refs_1_, bf16[768,1536]{1,0:T(8,128)(2,1)} %bitcast.90, f32[512,768]{1,0:T(8,128)S(1)} %copy-done.8, ...), custom_call_target="tpu_custom_call" | custom-call | flops 1000 | bytes 1000 | tf_op jit(solution)/shard_map/pallas_call | solution.py:833
  203.1 30.1 %shard_map.327 = (bf16[512,768]{1,0:T(8,128)(2,1)S(1)}, bf16[512,1536]{1,0:T(8,128)(2,1)S(1)}, bf16[512,1536]{1,0:T(8,128)(2,1)}) custom-call(bf16[512,768]{1,0:T(8,128)(2,1)S(1)} %copy-done.13, bf16[512,768]{1,0:T(8,128)(2,1)S(1)} %copy-done.7, bf16[512,768]{1,0:T(8,128)(2,1)S(1)} %get-tuple-element.220.refs_2_, ...), custom_call_target="tpu_custom_call" | custom-call | flops 1000 | bytes 1000 | tf_op jit(solution)/shard_map/pallas_call | solution.py:331
  234.4 2.9 collective-permute-start.32
  238.4 2.3 collective-permute-done.32
  240.7 2.3 add_convert_fusion.1.refs_1_.pair_grad_ref
  254.9 2.7 add_convert_fusion.4
  259.7 4.8 %shard_map.332 = (bf16[512,768]{1,0:T(8,128)(2,1)S(1)}, f32[1,1536]{1,0:T(1,128)S(1)}) custom-call(bf16[512,768]{1,0:T(8,128)(2,1)S(1)} %copy-done.21, bf16[512,1536]{1,0:T(8,128)(2,1)S(1)} %add_convert_fusion.1.refs_1_.pair_grad_ref, bf16[768,1536]{1,0:T(8,128)(2,1)} %bitcast.87, bf16[768,1536]{1,0:T(8,128)(2,1)} %bitcast.94, ...), custom_call_target="tpu_custom_call" | custom-call | flops 1000 | bytes 1000 | tf_op jit(solution)/shard_map/pallas_call | solution.py:833
  267.2 13.3 %collective-permute-done.36 = bf16[2,2,2,1,1,24,1536]{6,5,4,3,2,1,0:T(8,128)(2,1)S(1)} collective-permute-done((bf16[2,2,2,1,1,24,1536]{6,5,4,3,2,1,0:T(8,128)(2,1)S(1)}, bf16[2,2,2,1,1,24,1536]{6,5,4,3,2,1,0:T(8,128)(2,1)S(1)}, u32[]{:S(2)}, u32[]{:S(2)}) %collective-permute-start.36) | collective-permute-done | bytes 589856 | tf_op jit(solution)/shard_map/ppermute | solution.py:70
  298.1 2.0 collective-permute-done.43
  301.3 9.2 %collective-permute-done.44 = bf16[2,2,2,1,1,24,1536]{6,5,4,3,2,1,0:T(8,128)(2,1)} collective-permute-done((bf16[2,2,2,1,1,24,1536]{6,5,4,3,2,1,0:T(8,128)(2,1)}, bf16[2,2,2,1,1,24,1536]{6,5,4,3,2,1,0:T(8,128)(2,1)}, u32[]{:S(2)}, u32[]{:S(2)}) %collective-permute-start.44) | collective-permute-done | bytes 589856 | tf_op jit(solution)/shard_map/ppermute | solution.py:70
  320.9 3.5 collective-permute-done.48
  324.4 3.1 collective-permute-done.49
  331.1 2.8 collective-permute-start.52
  336.3 2.3 collective-permute-done.52
  340.1 2.4 collective-permute-done.54
  346.5 2.0 collective-permute-start.58
  352.7 4.1 collective-permute-done.56
  356.8 4.2 %collective-permute-done.57 = bf16[1,1,1,1,64,768]{5,4,3,2,1,0:T(8,128)(2,1)S(1)} collective-permute-done((bf16[1,1,1,1,64,768]{5,4,3,2,1,0:T(8,128)(2,1)S(1)}, bf16[1,1,1,1,64,768]{5,4,3,2,1,0:T(8,128)(2,1)S(1)}, u32[]{:S(2)}, u32[]{:S(2)}) %collective-permute-start.57) | collective-permute-done | bytes 98336 | tf_op jit(solution)/shard_map/ppermute | solution.py:70
  362.0 7.6 %collective-permute-start.59 = (f32[184,128]{1,0:T(8,128)S(1)}, f32[184,128]{1,0:T(8,128)S(1)}, u32[]{:S(2)}, u32[]{:S(2)}) collective-permute-start(f32[184,128]{1,0:T(8,128)S(1)} %shard_map.333), channel_id=1, source_target_pairs={{0,2},{2,0},{4,6},{6,4},{8,10},{10,8},{12,14},{14,12},{16,18},{18,... | collective-permute-start | bytes 282632 | tf_op jit(solution)/shard_map/ppermute | solution.py:70
  370.5 2.0 collective-permute-start.60
  372.5 3.0 collective-permute-done.60
  377.0 3.2 collective-permute-done.61
  380.6 4.3 %collective-permute-done.62 = f32[184,128]{1,0:T(8,128)S(1)} collective-permute-done((f32[184,128]{1,0:T(8,128)S(1)}, f32[184,128]{1,0:T(8,128)S(1)}, u32[]{:S(2)}, u32[]{:S(2)}) %collective-permute-start.62) | collective-permute-done | bytes 94240 | tf_op jit(solution)/shard_map/ppermute | solution.py:70
  384.9 2.0 collective-permute-start.63
  386.9 4.5 %collective-permute-done.63 = f32[184,128]{1,0:T(8,128)S(1)} collective-permute-done((f32[184,128]{1,0:T(8,128)S(1)}, f32[184,128]{1,0:T(8,128)S(1)}, u32[]{:S(2)}, u32[]{:S(2)}) %collective-permute-start.63) | collective-permute-done | bytes 94240 | tf_op jit(solution)/shard_map/ppermute | solution.py:70
  391.5 2.1 shard_map.334
  399.6 2.2 collective-permute-done.66
  (419 shorter events, 150.4 us)
Async XLA Ops:
  7.2 147.2 %all-gather.2.cloned.1.call-start = ((), (), s32[]{:S(2)}) async-start(), calls=%async_computation.2 | async-start | bytes 9732096 | tf_op jit(solution)/shard_map/all_gather | solution.py:1007
  8.1 9.9 %collective-permute-start = (s32[16]{0:T(128)S(1)}, s32[16]{0:T(128)S(1)}, u32[]{:S(2)}, u32[]{:S(2)}) collective-permute-start(s32[16]{0:T(128)S(1)} %dynamic_update_slice.5), channel_id=1, source_target_pairs={{0,2},{2,0},{4,6},{6,4},{8,10},{10,8},{12,14},{14,12},{16,18},{18,... | collective-permute-start | bytes 200 | tf_op jit(solution)/shard_map/ppermute | solution.py:70
  10.5 11.3 %collective-permute-start.2 = (bf16[1,1,1,1,1,24,3072]{6,5,4,3,2,1,0:T(8,128)(2,1)S(1)}, bf16[1,1,1,1,1,24,3072]{6,5,4,3,2,1,0:T(8,128)(2,1)S(1)}, u32[]{:S(2)}, u32[]{:S(2)}) collective-permute-start(bf16[1,1,1,1,1,24,3072]{6,5,4,3,2,1,0:T(8,128)(2,1)S(1)} %pad_maximum_fusion.21), channel_id=1, source_target_pairs={{0,16},{2,18},{4,20},{6,22},{8,24},{10,26},{12,28},{14,30},{16,0},... | collective-permute-start | bytes 442376 | tf_op jit(solution)/shard_map/ppermute | solution.py:70
  14.1 20.4 %collective-permute-start.6 = (bf16[512,768]{1,0:T(8,128)(2,1)}, bf16[512,768]{1,0:T(8,128)(2,1)}, u32[]{:S(2)}, u32[]{:S(2)}) collective-permute-start(bf16[512,768]{1,0:T(8,128)(2,1)} %bitcast.99), channel_id=1, source_target_pairs={{1,2},{2,1},{5,6},{6,5},{9,10},{10,9},{13,14},{14,13},{17,18},{18,... | collective-permute-start | bytes 2359304 | tf_op jit(solution)/shard_map/ppermute | solution.py:159
  21.9 12.5 %collective-permute-start.5 = (bf16[2,1,1,1,1,24,3072]{6,5,4,3,2,1,0:T(8,128)(2,1)S(1)}, bf16[2,1,1,1,1,24,3072]{6,5,4,3,2,1,0:T(8,128)(2,1)S(1)}, u32[]{:S(2)}, u32[]{:S(2)}) collective-permute-start(bf16[2,1,1,1,1,24,3072]{6,5,4,3,2,1,0:T(8,128)(2,1)S(1)} %pad_maximum_fusion.16), channel_id=1, source_target_pairs={{0,8},{2,10},{4,12},{6,14},{8,0},{10,2},{12,4},{14,6},{16,24},{18,... | collective-permute-start | bytes 884744 | tf_op jit(solution)/shard_map/ppermute | solution.py:70
  24.2 6.6 %collective-permute-start.3 = (s32[16]{0:T(128)S(1)}, s32[16]{0:T(128)S(1)}, u32[]{:S(2)}, u32[]{:S(2)}) collective-permute-start(s32[16]{0:T(128)S(1)} %add.411), channel_id=1, source_target_pairs={{0,16},{2,18},{4,20},{6,22},{8,24},{10,26},{12,28},{14,30},{16,0},... | collective-permute-start | bytes 200 | tf_op jit(solution)/shard_map/ppermute | solution.py:70
  36.1 13.6 %collective-permute-start.7 = (f32[8,1,4608]{2,1,0:T(1,128)S(1)}, f32[8,1,4608]{2,1,0:T(1,128)}, u32[]{:S(2)}, u32[]{:S(2)}) collective-permute-start(f32[8,1,4608]{2,1,0:T(1,128)S(1)} %constant_dynamic-slice_fusion.23), channel_id=1, source_target_pairs={{0,1},{1,0},{2,3},{3,2},{4,5},{5,4},{6,7},{7,6},{8,9},{9,8},{10,11... | collective-permute-start | bytes 442376 | tf_op jit(solution)/shard_map/ppermute | solution.py:70
  37.5 6.4 %collective-permute-start.10 = (bf16[1,1,1,1,1,24,1536]{6,5,4,3,2,1,0:T(8,128)(2,1)S(1)}, bf16[1,1,1,1,1,24,1536]{6,5,4,3,2,1,0:T(8,128)(2,1)S(1)}, u32[]{:S(2)}, u32[]{:S(2)}) collective-permute-start(bf16[1,1,1,1,1,24,1536]{6,5,4,3,2,1,0:T(8,128)(2,1)S(1)} %pad_maximum_fusion.24), channel_id=1, source_target_pairs={{0,16},{2,18},{4,20},{6,22},{8,24},{10,26},{12,28},{14,30},{16,0},... | collective-permute-start | bytes 221192 | tf_op jit(solution)/shard_map/ppermute | solution.py:70
  41.5 9.7 %collective-permute-start.9 = (bf16[2,2,1,1,1,24,1536]{6,5,4,3,2,1,0:T(8,128)(2,1)}, bf16[2,2,1,1,1,24,1536]{6,5,4,3,2,1,0:T(8,128)(2,1)S(1)}, u32[]{:S(2)}, u32[]{:S(2)}) collective-permute-start(bf16[2,2,1,1,1,24,1536]{6,5,4,3,2,1,0:T(8,128)(2,1)} %get-tuple-element.329), channel_id=1, source_target_pairs={{0,1},{1,0},{2,3},{3,2},{4,5},{5,4},{6,7},{7,6},{8,9},{9,8},{10,11... | collective-permute-start | bytes 884744 | tf_op jit(solution)/shard_map/ppermute | solution.py:70
  42.3 8.9 %collective-permute-start.8 = (bf16[2,2,1,1,1,24,1536]{6,5,4,3,2,1,0:T(8,128)(2,1)S(1)}, bf16[2,2,1,1,1,24,1536]{6,5,4,3,2,1,0:T(8,128)(2,1)}, u32[]{:S(2)}, u32[]{:S(2)}) collective-permute-start(bf16[2,2,1,1,1,24,1536]{6,5,4,3,2,1,0:T(8,128)(2,1)S(1)} %get-tuple-element.330), channel_id=1, source_target_pairs={{0,4},{2,6},{4,0},{6,2},{8,12},{10,14},{12,8},{14,10},{16,20},{18,... | collective-permute-start | bytes 884744 | tf_op jit(solution)/shard_map/ppermute | solution.py:70
  43.8 240.5 %reduce-scatter.3.cloned.1.call-start = ((), (), s32[]{:S(2)}) async-start(), calls=%async_computation.3 | async-start | bytes 10616832 | tf_op jit(solution)/shard_map/reduce_scatter | solution.py:1072
  58.2 6.4 %collective-permute-start.13 = (f32[1,1,2,4608]{3,2,1,0:T(2,128)S(1)}, f32[1,1,2,4608]{3,2,1,0:T(2,128)S(1)}, u32[]{:S(2)}, u32[]{:S(2)}) collective-permute-start(f32[1,1,2,4608]{3,2,1,0:T(2,128)S(1)} %constant_dynamic-slice_fusion.21), channel_id=1, source_target_pairs={{0,16},{2,18},{4,20},{6,22},{8,24},{10,26},{12,28},{14,30},{16,0},... | collective-permute-start | bytes 110600 | tf_op jit(solution)/shard_map/ppermute | solution.py:70
  59.7 12.2 %collective-permute-start.14 = (bf16[2,2,2,1,1,24,1536]{6,5,4,3,2,1,0:T(8,128)(2,1)S(1)}, bf16[2,2,2,1,1,24,1536]{6,5,4,3,2,1,0:T(8,128)(2,1)S(1)}, u32[]{:S(2)}, u32[]{:S(2)}) collective-permute-start(bf16[2,2,2,1,1,24,1536]{6,5,4,3,2,1,0:T(8,128)(2,1)S(1)} %pad_maximum_fusion.11), channel_id=1, source_target_pairs={{0,1},{1,0},{2,3},{3,2},{4,5},{5,4},{6,7},{7,6},{8,9},{9,8},{10,11... | collective-permute-start | bytes 1769480 | tf_op jit(solution)/shard_map/ppermute | solution.py:70
  61.3 10.8 %collective-permute-start.15 = (bf16[2,2,1,1,2,24,1536]{6,5,4,3,2,1,0:T(8,128)(2,1)S(1)}, bf16[2,2,1,1,2,24,1536]{6,5,4,3,2,1,0:T(8,128)(2,1)S(1)}, u32[]{:S(2)}, u32[]{:S(2)}) collective-permute-start(bf16[2,2,1,1,2,24,1536]{6,5,4,3,2,1,0:T(8,128)(2,1)S(1)} %pad_maximum_fusion.12), channel_id=1, source_target_pairs={{0,4},{2,6},{4,0},{6,2},{8,12},{10,14},{12,8},{14,10},{16,20},{18,... | collective-permute-start | bytes 1769480 | tf_op jit(solution)/shard_map/ppermute | solution.py:70
  62.4 6.6 %collective-permute-start.16 = (bf16[2,1,1,1,1,24,1536]{6,5,4,3,2,1,0:T(8,128)(2,1)S(1)}, bf16[2,1,1,1,1,24,1536]{6,5,4,3,2,1,0:T(8,128)(2,1)S(1)}, u32[]{:S(2)}, u32[]{:S(2)}) collective-permute-start(bf16[2,1,1,1,1,24,1536]{6,5,4,3,2,1,0:T(8,128)(2,1)S(1)} %pad_maximum_fusion.22), channel_id=1, source_target_pairs={{0,8},{2,10},{4,12},{6,14},{8,0},{10,2},{12,4},{14,6},{16,24},{18,... | collective-permute-start | bytes 442376 | tf_op jit(solution)/shard_map/ppermute | solution.py:70
  64.6 6.4 %collective-permute-start.17 = (bf16[2,1,1,1,64,768]{5,4,3,2,1,0:T(8,128)(2,1)S(1)}, bf16[2,1,1,1,64,768]{5,4,3,2,1,0:T(8,128)(2,1)S(1)}, u32[]{:S(2)}, u32[]{:S(2)}) collective-permute-start(bf16[2,1,1,1,64,768]{5,4,3,2,1,0:T(8,128)(2,1)S(1)} %pad_maximum_fusion.20), channel_id=1, source_target_pairs={{0,8},{2,10},{4,12},{6,14},{8,0},{10,2},{12,4},{14,6},{16,24},{18,... | collective-permute-start | bytes 589832 | tf_op jit(solution)/shard_map/ppermute | solution.py:70
  89.6 19.3 %collective-permute-start.24 = (bf16[512,1536]{1,0:T(8,128)(2,1)S(1)}, bf16[512,1536]{1,0:T(8,128)(2,1)S(1)}, u32[]{:S(2)}, u32[]{:S(2)}) collective-permute-start(bf16[512,1536]{1,0:T(8,128)(2,1)S(1)} %get-tuple-element.194.refs_1_.refs_2_.refs_4_.refs_5_), channel_id=1, source_target_pairs={{0,2},{2,0},{4,6},{6,4},{8,10},{10,8},{12,14},{14,12},{16,18},{18,... | collective-permute-start | bytes 4718600 | tf_op jit(solution)/shard_map/ppermute | solution.py:70
  89.9 11.8 %collective-permute-start.22 = (bf16[2,2,1,1,1,24,1536]{6,5,4,3,2,1,0:T(8,128)(2,1)S(1)}, bf16[2,2,1,1,1,24,1536]{6,5,4,3,2,1,0:T(8,128)(2,1)S(1)}, u32[]{:S(2)}, u32[]{:S(2)}) collective-permute-start(bf16[2,2,1,1,1,24,1536]{6,5,4,3,2,1,0:T(8,128)(2,1)S(1)} %copy-done.57), channel_id=1, source_target_pairs={{0,4},{2,6},{4,0},{6,2},{8,12},{10,14},{12,8},{14,10},{16,20},{18,... | collective-permute-start | bytes 884744 | tf_op jit(solution)/shard_map/ppermute | solution.py:70
  90.8 17.1 %collective-permute-start.23 = (bf16[2,2,1,1,64,768]{5,4,3,2,1,0:T(8,128)(2,1)S(1)}, bf16[2,2,1,1,64,768]{5,4,3,2,1,0:T(8,128)(2,1)S(1)}, u32[]{:S(2)}, u32[]{:S(2)}) collective-permute-start(bf16[2,2,1,1,64,768]{5,4,3,2,1,0:T(8,128)(2,1)S(1)} %copy-done.52), channel_id=1, source_target_pairs={{0,1},{1,0},{2,3},{3,2},{4,5},{5,4},{6,7},{7,6},{8,9},{9,8},{10,11... | collective-permute-start | bytes 1179656 | tf_op jit(solution)/shard_map/ppermute | solution.py:70
  109.0 22.5 %collective-permute-start.25 = (bf16[2,2,2,1,1,24,1536]{6,5,4,3,2,1,0:T(8,128)(2,1)}, bf16[2,2,2,1,1,24,1536]{6,5,4,3,2,1,0:T(8,128)(2,1)}, u32[]{:S(2)}, u32[]{:S(2)}) collective-permute-start(bf16[2,2,2,1,1,24,1536]{6,5,4,3,2,1,0:T(8,128)(2,1)} %pad_maximum_fusion.14), channel_id=1, source_target_pairs={{0,1},{1,0},{2,3},{3,2},{4,5},{5,4},{6,7},{7,6},{8,9},{9,8},{10,11... | collective-permute-start | bytes 1769480 | tf_op jit(solution)/shard_map/ppermute | solution.py:70
  113.6 20.0 %collective-permute-start.26 = (bf16[2,2,1,1,64,1536]{5,4,3,2,1,0:T(8,128)(2,1)}, bf16[2,2,1,1,64,1536]{5,4,3,2,1,0:T(8,128)(2,1)S(1)}, u32[]{:S(2)}, u32[]{:S(2)}) collective-permute-start(bf16[2,2,1,1,64,1536]{5,4,3,2,1,0:T(8,128)(2,1)} %pad_maximum_fusion.9), channel_id=1, source_target_pairs={{0,4},{2,6},{4,0},{6,2},{8,12},{10,14},{12,8},{14,10},{16,20},{18,... | collective-permute-start | bytes 2359304 | tf_op jit(solution)/shard_map/ppermute | solution.py:70
  137.1 8.4 %collective-permute-start.30 = (bf16[2,2,2,1,64,1536]{5,4,3,2,1,0:T(8,128)(2,1)S(1)}, bf16[2,2,2,1,64,1536]{5,4,3,2,1,0:T(8,128)(2,1)S(1)}, u32[]{:S(2)}, u32[]{:S(2)}) collective-permute-start(bf16[2,2,2,1,64,1536]{5,4,3,2,1,0:T(8,128)(2,1)S(1)} %pad_maximum_fusion.4), channel_id=1, source_target_pairs={{0,2},{2,0},{4,6},{6,4},{8,10},{10,8},{12,14},{14,12},{16,18},{18,... | collective-permute-start | bytes 4718600 | tf_op jit(solution)/shard_map/ppermute | solution.py:70
  139.1 15.2 %collective-permute-start.31 = (bf16[512,768]{1,0:T(8,128)(2,1)S(1)}, bf16[512,768]{1,0:T(8,128)(2,1)S(1)}, u32[]{:S(2)}, u32[]{:S(2)}) collective-permute-start(bf16[512,768]{1,0:T(8,128)(2,1)S(1)} %bitcast.100), channel_id=1, source_target_pairs={{1,2},{2,1},{5,6},{6,5},{9,10},{10,9},{13,14},{14,13},{17,18},{18,... | collective-permute-start | bytes 2359304 | tf_op jit(solution)/shard_map/ppermute | solution.py:159
  184.5 145.4 %reduce-scatter.5.cloned.1.call-start = ((), (), s32[]{:S(2)}) async-start(), calls=%async_computation.4 | async-start | bytes 1474560 | tf_op jit(solution)/shard_map/reduce_scatter | solution.py:1154
  247.0 7.9 %collective-permute-start.33 = (bf16[2,2,2,1,2,24,1536]{6,5,4,3,2,1,0:T(8,128)(2,1)}, bf16[2,2,2,1,2,24,1536]{6,5,4,3,2,1,0:T(8,128)(2,1)}, u32[]{:S(2)}, u32[]{:S(2)}) collective-permute-start(bf16[2,2,2,1,2,24,1536]{6,5,4,3,2,1,0:T(8,128)(2,1)} %constant_dynamic-slice_fusion.19), channel_id=1, source_target_pairs={{0,2},{2,0},{4,6},{6,4},{8,10},{10,8},{12,14},{14,12},{16,18},{18,... | collective-permute-start | bytes 3538952 | tf_op jit(solution)/shard_map/ppermute | solution.py:70
  248.6 9.0 %collective-permute-start.34 = (bf16[2,2,2,1,2,24,1536]{6,5,4,3,2,1,0:T(8,128)(2,1)}, bf16[2,2,2,1,2,24,1536]{6,5,4,3,2,1,0:T(8,128)(2,1)}, u32[]{:S(2)}, u32[]{:S(2)}) collective-permute-start(bf16[2,2,2,1,2,24,1536]{6,5,4,3,2,1,0:T(8,128)(2,1)} %constant_dynamic-slice_fusion.18), channel_id=1, source_target_pairs={{0,2},{2,0},{4,6},{6,4},{8,10},{10,8},{12,14},{14,12},{16,18},{18,... | collective-permute-start | bytes 3538952 | tf_op jit(solution)/shard_map/ppermute | solution.py:70
  265.1 15.4 %collective-permute-start.36 = (bf16[2,2,2,1,1,24,1536]{6,5,4,3,2,1,0:T(8,128)(2,1)S(1)}, bf16[2,2,2,1,1,24,1536]{6,5,4,3,2,1,0:T(8,128)(2,1)S(1)}, u32[]{:S(2)}, u32[]{:S(2)}) collective-permute-start(bf16[2,2,2,1,1,24,1536]{6,5,4,3,2,1,0:T(8,128)(2,1)S(1)} %constant_dynamic-slice_fusion.17), channel_id=1, source_target_pairs={{0,1},{1,0},{2,3},{3,2},{4,5},{5,4},{6,7},{7,6},{8,9},{9,8},{10,11... | collective-permute-start | bytes 1769480 | tf_op jit(solution)/shard_map/ppermute | solution.py:70
  265.5 16.0 %collective-permute-start.37 = (bf16[2,2,1,1,2,24,1536]{6,5,4,3,2,1,0:T(8,128)(2,1)S(1)}, bf16[2,2,1,1,2,24,1536]{6,5,4,3,2,1,0:T(8,128)(2,1)S(1)}, u32[]{:S(2)}, u32[]{:S(2)}) collective-permute-start(bf16[2,2,1,1,2,24,1536]{6,5,4,3,2,1,0:T(8,128)(2,1)S(1)} %constant_dynamic-slice_fusion.16), channel_id=1, source_target_pairs={{0,4},{2,6},{4,0},{6,2},{8,12},{10,14},{12,8},{14,10},{16,20},{18,... | collective-permute-start | bytes 1769480 | tf_op jit(solution)/shard_map/ppermute | solution.py:70
  266.4 16.1 %collective-permute-start.38 = (bf16[2,2,2,1,2,24,1536]{6,5,4,3,2,1,0:T(8,128)(2,1)S(1)}, bf16[2,2,2,1,2,24,1536]{6,5,4,3,2,1,0:T(8,128)(2,1)S(1)}, u32[]{:S(2)}, u32[]{:S(2)}) collective-permute-start(bf16[2,2,2,1,2,24,1536]{6,5,4,3,2,1,0:T(8,128)(2,1)S(1)} %constant_dynamic-slice_fusion.15), channel_id=1, source_target_pairs={{0,2},{2,0},{4,6},{6,4},{8,10},{10,8},{12,14},{14,12},{16,18},{18,... | collective-permute-start | bytes 3538952 | tf_op jit(solution)/shard_map/ppermute | solution.py:70
  266.6 17.3 %collective-permute-start.39 = (bf16[2,2,2,1,64,1536]{5,4,3,2,1,0:T(8,128)(2,1)S(1)}, bf16[2,2,2,1,64,1536]{5,4,3,2,1,0:T(8,128)(2,1)S(1)}, u32[]{:S(2)}, u32[]{:S(2)}) collective-permute-start(bf16[2,2,2,1,64,1536]{5,4,3,2,1,0:T(8,128)(2,1)S(1)} %constant_dynamic-slice_fusion.14), channel_id=1, source_target_pairs={{0,2},{2,0},{4,6},{6,4},{8,10},{10,8},{12,14},{14,12},{16,18},{18,... | collective-permute-start | bytes 4718600 | tf_op jit(solution)/shard_map/ppermute | solution.py:70
  284.3 8.4 %collective-permute-start.40 = (f32[1,1,1,1,4608]{4,3,2,1,0:T(1,128)S(1)}, f32[1,1,1,1,4608]{4,3,2,1,0:T(1,128)S(1)}, u32[]{:S(2)}, u32[]{:S(2)}) collective-permute-start(f32[1,1,1,1,4608]{4,3,2,1,0:T(1,128)S(1)} %add_bitcast_fusion), channel_id=1, source_target_pairs={{0,16},{2,18},{4,20},{6,22},{8,24},{10,26},{12,28},{14,30},{16,0},... | collective-permute-start | bytes 55304 | tf_op jit(solution)/shard_map/ppermute | solution.py:70
  286.8 10.2 %collective-permute-start.42 = (bf16[2,2,1,1,1,24,1536]{6,5,4,3,2,1,0:T(8,128)(2,1)S(1)}, bf16[2,2,1,1,1,24,1536]{6,5,4,3,2,1,0:T(8,128)(2,1)}, u32[]{:S(2)}, u32[]{:S(2)}) collective-permute-start(bf16[2,2,1,1,1,24,1536]{6,5,4,3,2,1,0:T(8,128)(2,1)S(1)} %constant_dynamic-slice_fusion.13), channel_id=1, source_target_pairs={{0,4},{2,6},{4,0},{6,2},{8,12},{10,14},{12,8},{14,10},{16,20},{18,... | collective-permute-start | bytes 884744 | tf_op jit(solution)/shard_map/ppermute | solution.py:70
  289.8 10.3 %collective-permute-start.43 = (bf16[2,2,1,1,1,24,1536]{6,5,4,3,2,1,0:T(8,128)(2,1)}, bf16[2,2,1,1,1,24,1536]{6,5,4,3,2,1,0:T(8,128)(2,1)}, u32[]{:S(2)}, u32[]{:S(2)}) collective-permute-start(bf16[2,2,1,1,1,24,1536]{6,5,4,3,2,1,0:T(8,128)(2,1)} %constant_dynamic-slice_fusion.12), channel_id=1, source_target_pairs={{0,1},{1,0},{2,3},{3,2},{4,5},{5,4},{6,7},{7,6},{8,9},{9,8},{10,11... | collective-permute-start | bytes 884744 | tf_op jit(solution)/shard_map/ppermute | solution.py:70
  291.6 18.9 %collective-permute-start.44 = (bf16[2,2,2,1,1,24,1536]{6,5,4,3,2,1,0:T(8,128)(2,1)}, bf16[2,2,2,1,1,24,1536]{6,5,4,3,2,1,0:T(8,128)(2,1)}, u32[]{:S(2)}, u32[]{:S(2)}) collective-permute-start(bf16[2,2,2,1,1,24,1536]{6,5,4,3,2,1,0:T(8,128)(2,1)} %constant_dynamic-slice_fusion.11), channel_id=1, source_target_pairs={{0,1},{1,0},{2,3},{3,2},{4,5},{5,4},{6,7},{7,6},{8,9},{9,8},{10,11... | collective-permute-start | bytes 1769480 | tf_op jit(solution)/shard_map/ppermute | solution.py:70
  294.8 17.7 %collective-permute-start.45 = (bf16[2,2,1,1,64,1536]{5,4,3,2,1,0:T(8,128)(2,1)}, bf16[2,2,1,1,64,1536]{5,4,3,2,1,0:T(8,128)(2,1)}, u32[]{:S(2)}, u32[]{:S(2)}) collective-permute-start(bf16[2,2,1,1,64,1536]{5,4,3,2,1,0:T(8,128)(2,1)} %constant_dynamic-slice_fusion.10), channel_id=1, source_target_pairs={{0,4},{2,6},{4,0},{6,2},{8,12},{10,14},{12,8},{14,10},{16,20},{18,... | collective-permute-start | bytes 2359304 | tf_op jit(solution)/shard_map/ppermute | solution.py:70
  314.9 9.5 %collective-permute-start.48 = (bf16[2,1,1,1,1,24,1536]{6,5,4,3,2,1,0:T(8,128)(2,1)S(1)}, bf16[2,1,1,1,1,24,1536]{6,5,4,3,2,1,0:T(8,128)(2,1)S(1)}, u32[]{:S(2)}, u32[]{:S(2)}) collective-permute-start(bf16[2,1,1,1,1,24,1536]{6,5,4,3,2,1,0:T(8,128)(2,1)S(1)} %constant_dynamic-slice_fusion.9), channel_id=1, source_target_pairs={{0,8},{2,10},{4,12},{6,14},{8,0},{10,2},{12,4},{14,6},{16,24},{18,... | collective-permute-start | bytes 442376 | tf_op jit(solution)/shard_map/ppermute | solution.py:70
  315.8 11.8 %collective-permute-start.49 = (bf16[2,1,1,1,1,24,1536]{6,5,4,3,2,1,0:T(8,128)(2,1)S(1)}, bf16[2,1,1,1,1,24,1536]{6,5,4,3,2,1,0:T(8,128)(2,1)S(1)}, u32[]{:S(2)}, u32[]{:S(2)}) collective-permute-start(bf16[2,1,1,1,1,24,1536]{6,5,4,3,2,1,0:T(8,128)(2,1)S(1)} %constant_dynamic-slice_fusion.8), channel_id=1, source_target_pairs={{0,8},{2,10},{4,12},{6,14},{8,0},{10,2},{12,4},{14,6},{16,24},{18,... | collective-permute-start | bytes 442376 | tf_op jit(solution)/shard_map/ppermute | solution.py:70
  317.1 12.6 %collective-permute-start.50 = (bf16[2,2,1,1,1,24,1536]{6,5,4,3,2,1,0:T(8,128)(2,1)S(1)}, bf16[2,2,1,1,1,24,1536]{6,5,4,3,2,1,0:T(8,128)(2,1)S(1)}, u32[]{:S(2)}, u32[]{:S(2)}) collective-permute-start(bf16[2,2,1,1,1,24,1536]{6,5,4,3,2,1,0:T(8,128)(2,1)S(1)} %constant_dynamic-slice_fusion.7), channel_id=1, source_target_pairs={{0,4},{2,6},{4,0},{6,2},{8,12},{10,14},{12,8},{14,10},{16,20},{18,... | collective-permute-start | bytes 884744 | tf_op jit(solution)/shard_map/ppermute | solution.py:70
  318.3 11.5 %collective-permute-start.51 = (bf16[2,2,1,1,64,768]{5,4,3,2,1,0:T(8,128)(2,1)S(1)}, bf16[2,2,1,1,64,768]{5,4,3,2,1,0:T(8,128)(2,1)S(1)}, u32[]{:S(2)}, u32[]{:S(2)}) collective-permute-start(bf16[2,2,1,1,64,768]{5,4,3,2,1,0:T(8,128)(2,1)S(1)} %constant_dynamic-slice_fusion.6), channel_id=1, source_target_pairs={{0,1},{1,0},{2,3},{3,2},{4,5},{5,4},{6,7},{7,6},{8,9},{9,8},{10,11... | collective-permute-start | bytes 1179656 | tf_op jit(solution)/shard_map/ppermute | solution.py:70
  319.4 9.0 %collective-permute-start.47 = (f32[2,2,2,1,4608]{4,3,2,1,0:T(1,128)S(1)}, f32[2,2,2,1,4608]{4,3,2,1,0:T(1,128)S(1)}, u32[]{:S(2)}, u32[]{:S(2)}) collective-permute-start(f32[2,2,2,1,4608]{4,3,2,1,0:T(1,128)S(1)} %pad_maximum_fusion.23), channel_id=1, source_target_pairs={{0,1},{1,0},{2,3},{3,2},{4,5},{5,4},{6,7},{7,6},{8,9},{9,8},{10,11... | collective-permute-start | bytes 442376 | tf_op jit(solution)/shard_map/ppermute | solution.py:70
  331.1 7.5 %collective-permute-start.52 = (bf16[1,1,1,1,1,24,1536]{6,5,4,3,2,1,0:T(8,128)(2,1)S(1)}, bf16[1,1,1,1,1,24,1536]{6,5,4,3,2,1,0:T(8,128)(2,1)S(1)}, u32[]{:S(2)}, u32[]{:S(2)}) collective-permute-start(bf16[1,1,1,1,1,24,1536]{6,5,4,3,2,1,0:T(8,128)(2,1)S(1)} %constant_dynamic-slice_fusion.5), channel_id=1, source_target_pairs={{0,16},{2,18},{4,20},{6,22},{8,24},{10,26},{12,28},{14,30},{16,0},... | collective-permute-start | bytes 221192 | tf_op jit(solution)/shard_map/ppermute | solution.py:70
  334.2 8.4 %collective-permute-start.54 = (bf16[2,1,1,1,1,24,1536]{6,5,4,3,2,1,0:T(8,128)(2,1)S(1)}, bf16[2,1,1,1,1,24,1536]{6,5,4,3,2,1,0:T(8,128)(2,1)S(1)}, u32[]{:S(2)}, u32[]{:S(2)}) collective-permute-start(bf16[2,1,1,1,1,24,1536]{6,5,4,3,2,1,0:T(8,128)(2,1)S(1)} %constant_dynamic-slice_fusion.3), channel_id=1, source_target_pairs={{0,8},{2,10},{4,12},{6,14},{8,0},{10,2},{12,4},{14,6},{16,24},{18,... | collective-permute-start | bytes 442376 | tf_op jit(solution)/shard_map/ppermute | solution.py:70
  335.3 9.8 %collective-permute-start.55 = (bf16[2,1,1,1,64,768]{5,4,3,2,1,0:T(8,128)(2,1)S(1)}, bf16[2,1,1,1,64,768]{5,4,3,2,1,0:T(8,128)(2,1)S(1)}, u32[]{:S(2)}, u32[]{:S(2)}) collective-permute-start(bf16[2,1,1,1,64,768]{5,4,3,2,1,0:T(8,128)(2,1)S(1)} %constant_dynamic-slice_fusion.2), channel_id=1, source_target_pairs={{0,8},{2,10},{4,12},{6,14},{8,0},{10,2},{12,4},{14,6},{16,24},{18,... | collective-permute-start | bytes 589832 | tf_op jit(solution)/shard_map/ppermute | solution.py:70
  346.5 14.5 %collective-permute-start.58 = (bf16[2,512,768]{2,1,0:T(8,128)(2,1)}, bf16[2,512,768]{2,1,0:T(8,128)(2,1)}, u32[]{:S(2)}, u32[]{:S(2)}) collective-permute-start(bf16[2,512,768]{2,1,0:T(8,128)(2,1)} %pad_maximum_fusion.5), channel_id=1, source_target_pairs={{1,2},{2,1},{5,6},{6,5},{9,10},{10,9},{13,14},{14,13},{17,18},{18,... | collective-permute-start | bytes 4718600 | tf_op jit(solution)/shard_map/ppermute | solution.py:159
  349.6 7.1 %collective-permute-start.56 = (bf16[1,1,1,1,1,24,1536]{6,5,4,3,2,1,0:T(8,128)(2,1)S(1)}, bf16[1,1,1,1,1,24,1536]{6,5,4,3,2,1,0:T(8,128)(2,1)S(1)}, u32[]{:S(2)}, u32[]{:S(2)}) collective-permute-start(bf16[1,1,1,1,1,24,1536]{6,5,4,3,2,1,0:T(8,128)(2,1)S(1)} %constant_dynamic-slice_fusion.1), channel_id=1, source_target_pairs={{0,16},{2,18},{4,20},{6,22},{8,24},{10,26},{12,28},{14,30},{16,0},... | collective-permute-start | bytes 221192 | tf_op jit(solution)/shard_map/ppermute | solution.py:70
  351.2 9.8 %collective-permute-start.57 = (bf16[1,1,1,1,64,768]{5,4,3,2,1,0:T(8,128)(2,1)S(1)}, bf16[1,1,1,1,64,768]{5,4,3,2,1,0:T(8,128)(2,1)S(1)}, u32[]{:S(2)}, u32[]{:S(2)}) collective-permute-start(bf16[1,1,1,1,64,768]{5,4,3,2,1,0:T(8,128)(2,1)S(1)} %constant_dynamic-slice_fusion), channel_id=1, source_target_pairs={{0,16},{2,18},{4,20},{6,22},{8,24},{10,26},{12,28},{14,30},{16,0},... | collective-permute-start | bytes 294920 | tf_op jit(solution)/shard_map/ppermute | solution.py:70
  362.0 8.5 %collective-permute-start.59 = (f32[184,128]{1,0:T(8,128)S(1)}, f32[184,128]{1,0:T(8,128)S(1)}, u32[]{:S(2)}, u32[]{:S(2)}) collective-permute-start(f32[184,128]{1,0:T(8,128)S(1)} %shard_map.333), channel_id=1, source_target_pairs={{0,2},{2,0},{4,6},{6,4},{8,10},{10,8},{12,14},{14,12},{16,18},{18,... | collective-permute-start | bytes 282632 | tf_op jit(solution)/shard_map/ppermute | solution.py:70
  384.9 6.5 %collective-permute-start.63 = (f32[184,128]{1,0:T(8,128)S(1)}, f32[184,128]{1,0:T(8,128)S(1)}, u32[]{:S(2)}, u32[]{:S(2)}) collective-permute-start(f32[184,128]{1,0:T(8,128)S(1)} %add.463), channel_id=1, source_target_pairs={{0,16},{2,18},{4,20},{6,22},{8,24},{10,26},{12,28},{14,30},{16,0},... | collective-permute-start | bytes 282632 | tf_op jit(solution)/shard_map/ppermute | solution.py:70
  (95 other events, 589.3 us)
Sparse Core Ops, SparseCore 0:
  43.9 98.9 all-gather.1
  184.6 77.5 reduce-scatter.2
  295.8 33.7 reduce-scatter.4

commit v5 on v4

--- a/solution.py
+++ b/solution.py
@@ -842,7 +842,7 @@
     )(*arrays)
 
 
-MLP_TILE = 512
+MLP_TILE = 768
 
 
 def mlp_both(cross_attn, project, after_self, modulation, out_grad, weights):

time: 424 us -> 423 us (level)
  transfers between devices with their start and end apart: 72 -> 72, of which waited for: 40 -> 40; matrix products, arithmetic and copies ran while one was open for 14% -> 14% of each run, Pallas kernels for 19% -> 20%
where the time goes in v5:
time: 423 us; the launch traced here: 418 us
  waiting for transfers between devices  126 us (30%)
  Pallas kernels  111 us (26%)
  starting transfers between devices  85.2 us (20%)
  other arithmetic  47.2 us (11%)
  local copies, waits for them, and re-layouts  29.9 us (7%)
  between operations  16.5 us (4%)
    ppermute x64, waiting for transfers between devices, cross(): return lax.ppermute(values, link[0], pairs)  124 us
    ppermute x64, starting transfers between devices, cross(): return lax.ppermute(values, link[0], pairs)  77.7 us
    pallas_call x2, Pallas kernels, attend_back(): pl.pallas_call(functools.partial(back_kernel, blocks, places), grid=(PAIR...  37.9 us
    pallas_call x1, Pallas kernels, mlp_both(): pl.pallas_call(mlp_kernel, grid=(2, tiles), in_specs=[whole, pl.BlockSpec...  25.1 us
    pallas_call x4, Pallas kernels, frame_call(): pl.pallas_call(kernel, grid=(1,), in_specs=specs, out_specs=[whole_block(...  19.6 us
    pallas_call x2, Pallas kernels, attend(): pl.pallas_call(functools.partial(attend_kernel, blocks), grid=(PAIRS,), i...  18.4 us
    unnamed x149, local copies, waits for them, and re-layouts  18 us
    convert_element_type x16, other arithmetic, shrink(): (kept.astype(FLOAT) + cross(sent.astype(BFLOAT), link).astype(FLOAT)).ast...  14.8 us
  transfers between devices with their start and end apart: 72, of which 40 were waited for; matrix products, arithmetic and copies ran while one was open for 14% of the time, Pallas kernels for 20%

profile of v5, /device:TPU:0, one launch (start us, length us, event | category | flops | bytes accessed | tf_op | source)
XLA Modules:
  0.0 417.7 jit_solution(13667396445745750257)
XLA Ops:
  10.5 3.7 collective-permute-start.2
  19.8 2.0 collective-permute-done.1
  24.2 2.6 collective-permute-start.3
  26.8 4.0 collective-permute-done.3
  32.3 2.0 collective-permute-done.4
  37.5 3.3 collective-permute-start.10
  43.9 5.8 %collective-permute-done.11 = bf16[1,1,1,1,64,768]{5,4,3,2,1,0:T(8,128)(2,1)S(1)} collective-permute-done((bf16[1,1,1,1,64,768]{5,4,3,2,1,0:T(8,128)(2,1)S(1)}, bf16[1,1,1,1,64,768]{5,4,3,2,1,0:T(8,128)(2,1)S(1)}, u32[]{:S(2)}, u32[]{:S(2)}) %collective-permute-start.11) | collective-permute-done | bytes 98336 | tf_op jit(solution)/shard_map/ppermute | solution.py:70
  52.5 5.6 %collective-permute-done.12 = f32[2,1,2,4608]{3,2,1,0:T(2,128)S(1)} collective-permute-done((f32[2,1,2,4608]{3,2,1,0:T(2,128)S(1)}, f32[2,1,2,4608]{3,2,1,0:T(2,128)S(1)}, u32[]{:S(2)}, u32[]{:S(2)}) %collective-permute-start.12) | collective-permute-done | bytes 73760 | tf_op jit(solution)/shard_map/ppermute | solution.py:70
  62.4 2.3 collective-permute-start.16
  64.7 4.3 %collective-permute-done.16 = bf16[2,1,1,1,1,24,1536]{6,5,4,3,2,1,0:T(8,128)(2,1)S(1)} collective-permute-done((bf16[2,1,1,1,1,24,1536]{6,5,4,3,2,1,0:T(8,128)(2,1)S(1)}, bf16[2,1,1,1,1,24,1536]{6,5,4,3,2,1,0:T(8,128)(2,1)S(1)}, u32[]{:S(2)}, u32[]{:S(2)}) %collective-permute-start.16) | collective-permute-done | bytes 147488 | tf_op jit(solution)/shard_map/ppermute | solution.py:70
  74.4 3.2 collective-permute-done.18
  85.1 4.5 %shard_map.320 = (bf16[512,768]{1,0:T(8,128)(2,1)S(1)}, bf16[512,768]{1,0:T(8,128)(2,1)S(1)}, bf16[512,1536]{1,0:T(8,128)(2,1)S(1)}) custom-call(bf16[512,768]{1,0:T(8,128)(2,1)S(1)} %broadcast_select_fusion.11.in_ref, f32[1,4608]{1,0:T(1,128)S(1)} %add_bitcast_fusion.1.modulation_ref, bf16[768,1536]{1,0:T(8,128)(2,1)} %bitcast.84, bf16[768,1536]{1,0:T(8,128)(2,1)} %bitcast.93), custom_call_target="tpu_custom_call" | custom-call | flops 1000 | bytes 1000 | tf_op jit(solution)/shard_map/pallas_call | solution.py:833
  92.4 9.2 %collective-permute-done.22 = bf16[2,2,1,1,1,24,1536]{6,5,4,3,2,1,0:T(8,128)(2,1)S(1)} collective-permute-done((bf16[2,2,1,1,1,24,1536]{6,5,4,3,2,1,0:T(8,128)(2,1)S(1)}, bf16[2,2,1,1,1,24,1536]{6,5,4,3,2,1,0:T(8,128)(2,1)S(1)}, u32[]{:S(2)}, u32[]{:S(2)}) %collective-permute-start.22) | collective-permute-done | bytes 294944 | tf_op jit(solution)/shard_map/ppermute | solution.py:70
  102.5 5.4 %collective-permute-done.23 = bf16[2,2,1,1,64,768]{5,4,3,2,1,0:T(8,128)(2,1)S(1)} collective-permute-done((bf16[2,2,1,1,64,768]{5,4,3,2,1,0:T(8,128)(2,1)S(1)}, bf16[2,2,1,1,64,768]{5,4,3,2,1,0:T(8,128)(2,1)S(1)}, u32[]{:S(2)}, u32[]{:S(2)}) %collective-permute-start.23) | collective-permute-done | bytes 393248 | tf_op jit(solution)/shard_map/ppermute | solution.py:70
  109.0 2.5 collective-permute-start.25
  115.2 12.5 %shard_map.321 = (bf16[512,768]{1,0:T(8,128)(2,1)S(1)}, f32[6,2,512]{2,1,0:T(2,128)S(1)}) custom-call(bf16[512,768]{1,0:T(8,128)(2,1)S(1)} %copy-done.12, bf16[512,1536]{1,0:T(8,128)(2,1)S(1)} %get-tuple-element.194.refs_1_.refs_2_.refs_4_.refs_5_, bf16[512,1536]{1,0:T(8,128)(2,1)S(1)} %get-tuple-element.194.refs_1_.refs_2_.refs_4_.refs_5_, ...), custom_call_target="tpu_custom_call" | custom-call | flops 1000 | bytes 1000 | tf_op jit(solution)/shard_map/pallas_call | solution.py:314
  127.7 3.8 collective-permute-done.25
  141.6 3.9 shard_map.322
  148.4 5.9 %shard_map.323 = (bf16[512,768]{1,0:T(8,128)(2,1)S(1)}, f32[6,2,512]{2,1,0:T(2,128)S(1)}) custom-call(bf16[512,768]{1,0:T(8,128)(2,1)S(1)} %get-tuple-element.205.refs_0_, bf16[256,1536]{1,0:T(8,128)(2,1)S(1)} %convolution_convert_fusion.refs_1_.refs_2_.refs_4_.refs_5_, bf16[256,1536]{1,0:T(8,128)(2,1)S(1)} %convolution_convert_fusion.refs_1_.refs_2_.refs_4_.refs_5_, ...), custom_call_target="tpu_custom_call" | custom-call | flops 1000 | bytes 1000 | tf_op jit(solution)/shard_map/pallas_call | solution.py:314
  154.4 25.1 %shard_map.324 = (bf16[512,768]{1,0:T(8,128)(2,1)S(1)}, f32[512,768]{1,0:T(8,128)S(1)}, bf16[512,768]{1,0:T(8,128)(2,1)S(1)}, bf16[512,768]{1,0:T(8,128)(2,1)S(1...) custom-call(bf16[512,768]{1,0:T(8,128)(2,1)S(1)} %get-tuple-element.210.attn_ref.refs_1_.refs_2_, ...), custom_call_target="tpu_custom_call" | custom-call | flops 1000 | bytes 1000 | tf_op jit(solution)/shard_map/pallas_call | solution.py:856
  185.7 7.8 %shard_map.325 = (bf16[512,768]{1,0:T(8,128)(2,1)S(1)}, bf16[256,1536]{1,0:T(8,128)(2,1)S(1)}) custom-call(bf16[512,768]{1,0:T(8,128)(2,1)S(1)} %copy-done.19, bf16[512,768]{1,0:T(8,128)(2,1)S(1)} %get-tuple-element.210.attn_ref.refs_1_.refs_2_, bf16[512,768]{1,0:T(8,128)(2,1)S(1)} %copy-done.42, f32[6,2,512]{2,1,0:T(2,128)S(1)} %get-tuple-element.216.refs_3_, ...), custom_call_target="tpu_custom_call" | custom-call | flops 1000 | bytes 1000 | tf_op jit(solution)/shard_map/pallas_call | solution.py:331
  194.4 6.5 %shard_map.326 = (f32[512,768]{1,0:T(8,128)S(1)}, bf16[512,768]{1,0:T(8,128)(2,1)S(1)}, bf16[512,768]{1,0:T(8,128)(2,1)S(1)}, f32[1,768]{1,0:T(1,128)S(1)}) custom-call(bf16[512,768]{1,0:T(8,128)(2,1)S(1)} %get-tuple-element.227.query_grad_ref.refs_1_, bf16[768,1536]{1,0:T(8,128)(2,1)} %bitcast.90, f32[512,768]{1,0:T(8,128)S(1)} %copy-done.8, ...), custom_call_target="tpu_custom_call" | custom-call | flops 1000 | bytes 1000 | tf_op jit(solution)/shard_map/pallas_call | solution.py:833
  202.1 30.1 %shard_map.327 = (bf16[512,768]{1,0:T(8,128)(2,1)S(1)}, bf16[512,1536]{1,0:T(8,128)(2,1)S(1)}, bf16[512,1536]{1,0:T(8,128)(2,1)}) custom-call(bf16[512,768]{1,0:T(8,128)(2,1)S(1)} %copy-done.13, bf16[512,768]{1,0:T(8,128)(2,1)S(1)} %copy-done.7, bf16[512,768]{1,0:T(8,128)(2,1)S(1)} %get-tuple-element.220.refs_2_, ...), custom_call_target="tpu_custom_call" | custom-call | flops 1000 | bytes 1000 | tf_op jit(solution)/shard_map/pallas_call | solution.py:331
  233.4 2.9 collective-permute-start.32
  237.3 2.3 collective-permute-done.32
  239.7 2.3 add_convert_fusion.1.refs_1_.pair_grad_ref
  253.9 2.7 add_convert_fusion.4
  258.7 4.8 %shard_map.332 = (bf16[512,768]{1,0:T(8,128)(2,1)S(1)}, f32[1,1536]{1,0:T(1,128)S(1)}) custom-call(bf16[512,768]{1,0:T(8,128)(2,1)S(1)} %copy-done.21, bf16[512,1536]{1,0:T(8,128)(2,1)S(1)} %add_convert_fusion.1.refs_1_.pair_grad_ref, bf16[768,1536]{1,0:T(8,128)(2,1)} %bitcast.87, bf16[768,1536]{1,0:T(8,128)(2,1)} %bitcast.94, ...), custom_call_target="tpu_custom_call" | custom-call | flops 1000 | bytes 1000 | tf_op jit(solution)/shard_map/pallas_call | solution.py:833
  266.2 13.3 %collective-permute-done.36 = bf16[2,2,2,1,1,24,1536]{6,5,4,3,2,1,0:T(8,128)(2,1)S(1)} collective-permute-done((bf16[2,2,2,1,1,24,1536]{6,5,4,3,2,1,0:T(8,128)(2,1)S(1)}, bf16[2,2,2,1,1,24,1536]{6,5,4,3,2,1,0:T(8,128)(2,1)S(1)}, u32[]{:S(2)}, u32[]{:S(2)}) %collective-permute-start.36) | collective-permute-done | bytes 589856 | tf_op jit(solution)/shard_map/ppermute | solution.py:70
  297.1 2.0 collective-permute-done.43
  300.3 9.2 %collective-permute-done.44 = bf16[2,2,2,1,1,24,1536]{6,5,4,3,2,1,0:T(8,128)(2,1)} collective-permute-done((bf16[2,2,2,1,1,24,1536]{6,5,4,3,2,1,0:T(8,128)(2,1)}, bf16[2,2,2,1,1,24,1536]{6,5,4,3,2,1,0:T(8,128)(2,1)}, u32[]{:S(2)}, u32[]{:S(2)}) %collective-permute-start.44) | collective-permute-done | bytes 589856 | tf_op jit(solution)/shard_map/ppermute | solution.py:70
  319.9 3.5 collective-permute-done.48
  323.4 3.1 collective-permute-done.49
  330.1 2.8 collective-permute-start.52
  335.4 2.2 collective-permute-done.52
  339.1 2.5 collective-permute-done.54
  345.5 2.0 collective-permute-start.58
  351.7 4.1 collective-permute-done.56
  355.8 4.2 %collective-permute-done.57 = bf16[1,1,1,1,64,768]{5,4,3,2,1,0:T(8,128)(2,1)S(1)} collective-permute-done((bf16[1,1,1,1,64,768]{5,4,3,2,1,0:T(8,128)(2,1)S(1)}, bf16[1,1,1,1,64,768]{5,4,3,2,1,0:T(8,128)(2,1)S(1)}, u32[]{:S(2)}, u32[]{:S(2)}) %collective-permute-start.57) | collective-permute-done | bytes 98336 | tf_op jit(solution)/shard_map/ppermute | solution.py:70
  360.9 7.6 %collective-permute-start.59 = (f32[184,128]{1,0:T(8,128)S(1)}, f32[184,128]{1,0:T(8,128)S(1)}, u32[]{:S(2)}, u32[]{:S(2)}) collective-permute-start(f32[184,128]{1,0:T(8,128)S(1)} %shard_map.333), channel_id=1, source_target_pairs={{0,2},{2,0},{4,6},{6,4},{8,10},{10,8},{12,14},{14,12},{16,18},{18,... | collective-permute-start | bytes 282632 | tf_op jit(solution)/shard_map/ppermute | solution.py:70
  369.5 2.0 collective-permute-start.60
  371.5 3.0 collective-permute-done.60
  376.0 3.2 collective-permute-done.61
  379.5 4.3 %collective-permute-done.62 = f32[184,128]{1,0:T(8,128)S(1)} collective-permute-done((f32[184,128]{1,0:T(8,128)S(1)}, f32[184,128]{1,0:T(8,128)S(1)}, u32[]{:S(2)}, u32[]{:S(2)}) %collective-permute-start.62) | collective-permute-done | bytes 94240 | tf_op jit(solution)/shard_map/ppermute | solution.py:70
  383.9 2.0 collective-permute-start.63
  385.9 4.5 %collective-permute-done.63 = f32[184,128]{1,0:T(8,128)S(1)} collective-permute-done((f32[184,128]{1,0:T(8,128)S(1)}, f32[184,128]{1,0:T(8,128)S(1)}, u32[]{:S(2)}, u32[]{:S(2)}) %collective-permute-start.63) | collective-permute-done | bytes 94240 | tf_op jit(solution)/shard_map/ppermute | solution.py:70
  390.5 2.1 shard_map.334
  398.6 2.2 collective-permute-done.66
  (419 shorter events, 150.4 us)
Async XLA Ops:
  7.2 147.2 %all-gather.2.cloned.1.call-start = ((), (), s32[]{:S(2)}) async-start(), calls=%async_computation.2 | async-start | bytes 9732096 | tf_op jit(solution)/shard_map/all_gather | solution.py:1007
  8.1 9.9 %collective-permute-start = (s32[16]{0:T(128)S(1)}, s32[16]{0:T(128)S(1)}, u32[]{:S(2)}, u32[]{:S(2)}) collective-permute-start(s32[16]{0:T(128)S(1)} %dynamic_update_slice.5), channel_id=1, source_target_pairs={{0,2},{2,0},{4,6},{6,4},{8,10},{10,8},{12,14},{14,12},{16,18},{18,... | collective-permute-start | bytes 200 | tf_op jit(solution)/shard_map/ppermute | solution.py:70
  10.5 11.3 %collective-permute-start.2 = (bf16[1,1,1,1,1,24,3072]{6,5,4,3,2,1,0:T(8,128)(2,1)S(1)}, bf16[1,1,1,1,1,24,3072]{6,5,4,3,2,1,0:T(8,128)(2,1)S(1)}, u32[]{:S(2)}, u32[]{:S(2)}) collective-permute-start(bf16[1,1,1,1,1,24,3072]{6,5,4,3,2,1,0:T(8,128)(2,1)S(1)} %pad_maximum_fusion.21), channel_id=1, source_target_pairs={{0,16},{2,18},{4,20},{6,22},{8,24},{10,26},{12,28},{14,30},{16,0},... | collective-permute-start | bytes 442376 | tf_op jit(solution)/shard_map/ppermute | solution.py:70
  14.1 20.4 %collective-permute-start.6 = (bf16[512,768]{1,0:T(8,128)(2,1)}, bf16[512,768]{1,0:T(8,128)(2,1)}, u32[]{:S(2)}, u32[]{:S(2)}) collective-permute-start(bf16[512,768]{1,0:T(8,128)(2,1)} %bitcast.99), channel_id=1, source_target_pairs={{1,2},{2,1},{5,6},{6,5},{9,10},{10,9},{13,14},{14,13},{17,18},{18,... | collective-permute-start | bytes 2359304 | tf_op jit(solution)/shard_map/ppermute | solution.py:159
  21.9 12.5 %collective-permute-start.5 = (bf16[2,1,1,1,1,24,3072]{6,5,4,3,2,1,0:T(8,128)(2,1)S(1)}, bf16[2,1,1,1,1,24,3072]{6,5,4,3,2,1,0:T(8,128)(2,1)S(1)}, u32[]{:S(2)}, u32[]{:S(2)}) collective-permute-start(bf16[2,1,1,1,1,24,3072]{6,5,4,3,2,1,0:T(8,128)(2,1)S(1)} %pad_maximum_fusion.16), channel_id=1, source_target_pairs={{0,8},{2,10},{4,12},{6,14},{8,0},{10,2},{12,4},{14,6},{16,24},{18,... | collective-permute-start | bytes 884744 | tf_op jit(solution)/shard_map/ppermute | solution.py:70
  24.2 6.6 %collective-permute-start.3 = (s32[16]{0:T(128)S(1)}, s32[16]{0:T(128)S(1)}, u32[]{:S(2)}, u32[]{:S(2)}) collective-permute-start(s32[16]{0:T(128)S(1)} %add.411), channel_id=1, source_target_pairs={{0,16},{2,18},{4,20},{6,22},{8,24},{10,26},{12,28},{14,30},{16,0},... | collective-permute-start | bytes 200 | tf_op jit(solution)/shard_map/ppermute | solution.py:70
  36.1 13.6 %collective-permute-start.7 = (f32[8,1,4608]{2,1,0:T(1,128)S(1)}, f32[8,1,4608]{2,1,0:T(1,128)}, u32[]{:S(2)}, u32[]{:S(2)}) collective-permute-start(f32[8,1,4608]{2,1,0:T(1,128)S(1)} %constant_dynamic-slice_fusion.23), channel_id=1, source_target_pairs={{0,1},{1,0},{2,3},{3,2},{4,5},{5,4},{6,7},{7,6},{8,9},{9,8},{10,11... | collective-permute-start | bytes 442376 | tf_op jit(solution)/shard_map/ppermute | solution.py:70
  37.5 6.4 %collective-permute-start.10 = (bf16[1,1,1,1,1,24,1536]{6,5,4,3,2,1,0:T(8,128)(2,1)S(1)}, bf16[1,1,1,1,1,24,1536]{6,5,4,3,2,1,0:T(8,128)(2,1)S(1)}, u32[]{:S(2)}, u32[]{:S(2)}) collective-permute-start(bf16[1,1,1,1,1,24,1536]{6,5,4,3,2,1,0:T(8,128)(2,1)S(1)} %pad_maximum_fusion.24), channel_id=1, source_target_pairs={{0,16},{2,18},{4,20},{6,22},{8,24},{10,26},{12,28},{14,30},{16,0},... | collective-permute-start | bytes 221192 | tf_op jit(solution)/shard_map/ppermute | solution.py:70
  41.5 9.7 %collective-permute-start.9 = (bf16[2,2,1,1,1,24,1536]{6,5,4,3,2,1,0:T(8,128)(2,1)}, bf16[2,2,1,1,1,24,1536]{6,5,4,3,2,1,0:T(8,128)(2,1)S(1)}, u32[]{:S(2)}, u32[]{:S(2)}) collective-permute-start(bf16[2,2,1,1,1,24,1536]{6,5,4,3,2,1,0:T(8,128)(2,1)} %get-tuple-element.329), channel_id=1, source_target_pairs={{0,1},{1,0},{2,3},{3,2},{4,5},{5,4},{6,7},{7,6},{8,9},{9,8},{10,11... | collective-permute-start | bytes 884744 | tf_op jit(solution)/shard_map/ppermute | solution.py:70
  42.3 8.9 %collective-permute-start.8 = (bf16[2,2,1,1,1,24,1536]{6,5,4,3,2,1,0:T(8,128)(2,1)S(1)}, bf16[2,2,1,1,1,24,1536]{6,5,4,3,2,1,0:T(8,128)(2,1)}, u32[]{:S(2)}, u32[]{:S(2)}) collective-permute-start(bf16[2,2,1,1,1,24,1536]{6,5,4,3,2,1,0:T(8,128)(2,1)S(1)} %get-tuple-element.330), channel_id=1, source_target_pairs={{0,4},{2,6},{4,0},{6,2},{8,12},{10,14},{12,8},{14,10},{16,20},{18,... | collective-permute-start | bytes 884744 | tf_op jit(solution)/shard_map/ppermute | solution.py:70
  43.8 239.5 %reduce-scatter.3.cloned.1.call-start = ((), (), s32[]{:S(2)}) async-start(), calls=%async_computation.3 | async-start | bytes 10616832 | tf_op jit(solution)/shard_map/reduce_scatter | solution.py:1072
  58.2 6.4 %collective-permute-start.13 = (f32[1,1,2,4608]{3,2,1,0:T(2,128)S(1)}, f32[1,1,2,4608]{3,2,1,0:T(2,128)S(1)}, u32[]{:S(2)}, u32[]{:S(2)}) collective-permute-start(f32[1,1,2,4608]{3,2,1,0:T(2,128)S(1)} %constant_dynamic-slice_fusion.21), channel_id=1, source_target_pairs={{0,16},{2,18},{4,20},{6,22},{8,24},{10,26},{12,28},{14,30},{16,0},... | collective-permute-start | bytes 110600 | tf_op jit(solution)/shard_map/ppermute | solution.py:70
  59.7 12.2 %collective-permute-start.14 = (bf16[2,2,2,1,1,24,1536]{6,5,4,3,2,1,0:T(8,128)(2,1)S(1)}, bf16[2,2,2,1,1,24,1536]{6,5,4,3,2,1,0:T(8,128)(2,1)S(1)}, u32[]{:S(2)}, u32[]{:S(2)}) collective-permute-start(bf16[2,2,2,1,1,24,1536]{6,5,4,3,2,1,0:T(8,128)(2,1)S(1)} %pad_maximum_fusion.11), channel_id=1, source_target_pairs={{0,1},{1,0},{2,3},{3,2},{4,5},{5,4},{6,7},{7,6},{8,9},{9,8},{10,11... | collective-permute-start | bytes 1769480 | tf_op jit(solution)/shard_map/ppermute | solution.py:70
  61.3 10.8 %collective-permute-start.15 = (bf16[2,2,1,1,2,24,1536]{6,5,4,3,2,1,0:T(8,128)(2,1)S(1)}, bf16[2,2,1,1,2,24,1536]{6,5,4,3,2,1,0:T(8,128)(2,1)S(1)}, u32[]{:S(2)}, u32[]{:S(2)}) collective-permute-start(bf16[2,2,1,1,2,24,1536]{6,5,4,3,2,1,0:T(8,128)(2,1)S(1)} %pad_maximum_fusion.12), channel_id=1, source_target_pairs={{0,4},{2,6},{4,0},{6,2},{8,12},{10,14},{12,8},{14,10},{16,20},{18,... | collective-permute-start | bytes 1769480 | tf_op jit(solution)/shard_map/ppermute | solution.py:70
  62.4 6.6 %collective-permute-start.16 = (bf16[2,1,1,1,1,24,1536]{6,5,4,3,2,1,0:T(8,128)(2,1)S(1)}, bf16[2,1,1,1,1,24,1536]{6,5,4,3,2,1,0:T(8,128)(2,1)S(1)}, u32[]{:S(2)}, u32[]{:S(2)}) collective-permute-start(bf16[2,1,1,1,1,24,1536]{6,5,4,3,2,1,0:T(8,128)(2,1)S(1)} %pad_maximum_fusion.22), channel_id=1, source_target_pairs={{0,8},{2,10},{4,12},{6,14},{8,0},{10,2},{12,4},{14,6},{16,24},{18,... | collective-permute-start | bytes 442376 | tf_op jit(solution)/shard_map/ppermute | solution.py:70
  64.6 6.4 %collective-permute-start.17 = (bf16[2,1,1,1,64,768]{5,4,3,2,1,0:T(8,128)(2,1)S(1)}, bf16[2,1,1,1,64,768]{5,4,3,2,1,0:T(8,128)(2,1)S(1)}, u32[]{:S(2)}, u32[]{:S(2)}) collective-permute-start(bf16[2,1,1,1,64,768]{5,4,3,2,1,0:T(8,128)(2,1)S(1)} %pad_maximum_fusion.20), channel_id=1, source_target_pairs={{0,8},{2,10},{4,12},{6,14},{8,0},{10,2},{12,4},{14,6},{16,24},{18,... | collective-permute-start | bytes 589832 | tf_op jit(solution)/shard_map/ppermute | solution.py:70
  89.6 19.3 %collective-permute-start.24 = (bf16[512,1536]{1,0:T(8,128)(2,1)S(1)}, bf16[512,1536]{1,0:T(8,128)(2,1)S(1)}, u32[]{:S(2)}, u32[]{:S(2)}) collective-permute-start(bf16[512,1536]{1,0:T(8,128)(2,1)S(1)} %get-tuple-element.194.refs_1_.refs_2_.refs_4_.refs_5_), channel_id=1, source_target_pairs={{0,2},{2,0},{4,6},{6,4},{8,10},{10,8},{12,14},{14,12},{16,18},{18,... | collective-permute-start | bytes 4718600 | tf_op jit(solution)/shard_map/ppermute | solution.py:70
  89.9 11.8 %collective-permute-start.22 = (bf16[2,2,1,1,1,24,1536]{6,5,4,3,2,1,0:T(8,128)(2,1)S(1)}, bf16[2,2,1,1,1,24,1536]{6,5,4,3,2,1,0:T(8,128)(2,1)S(1)}, u32[]{:S(2)}, u32[]{:S(2)}) collective-permute-start(bf16[2,2,1,1,1,24,1536]{6,5,4,3,2,1,0:T(8,128)(2,1)S(1)} %copy-done.57), channel_id=1, source_target_pairs={{0,4},{2,6},{4,0},{6,2},{8,12},{10,14},{12,8},{14,10},{16,20},{18,... | collective-permute-start | bytes 884744 | tf_op jit(solution)/shard_map/ppermute | solution.py:70
  90.8 17.1 %collective-permute-start.23 = (bf16[2,2,1,1,64,768]{5,4,3,2,1,0:T(8,128)(2,1)S(1)}, bf16[2,2,1,1,64,768]{5,4,3,2,1,0:T(8,128)(2,1)S(1)}, u32[]{:S(2)}, u32[]{:S(2)}) collective-permute-start(bf16[2,2,1,1,64,768]{5,4,3,2,1,0:T(8,128)(2,1)S(1)} %copy-done.52), channel_id=1, source_target_pairs={{0,1},{1,0},{2,3},{3,2},{4,5},{5,4},{6,7},{7,6},{8,9},{9,8},{10,11... | collective-permute-start | bytes 1179656 | tf_op jit(solution)/shard_map/ppermute | solution.py:70
  109.0 22.5 %collective-permute-start.25 = (bf16[2,2,2,1,1,24,1536]{6,5,4,3,2,1,0:T(8,128)(2,1)}, bf16[2,2,2,1,1,24,1536]{6,5,4,3,2,1,0:T(8,128)(2,1)}, u32[]{:S(2)}, u32[]{:S(2)}) collective-permute-start(bf16[2,2,2,1,1,24,1536]{6,5,4,3,2,1,0:T(8,128)(2,1)} %pad_maximum_fusion.14), channel_id=1, source_target_pairs={{0,1},{1,0},{2,3},{3,2},{4,5},{5,4},{6,7},{7,6},{8,9},{9,8},{10,11... | collective-permute-start | bytes 1769480 | tf_op jit(solution)/shard_map/ppermute | solution.py:70
  113.6 20.0 %collective-permute-start.26 = (bf16[2,2,1,1,64,1536]{5,4,3,2,1,0:T(8,128)(2,1)}, bf16[2,2,1,1,64,1536]{5,4,3,2,1,0:T(8,128)(2,1)S(1)}, u32[]{:S(2)}, u32[]{:S(2)}) collective-permute-start(bf16[2,2,1,1,64,1536]{5,4,3,2,1,0:T(8,128)(2,1)} %pad_maximum_fusion.9), channel_id=1, source_target_pairs={{0,4},{2,6},{4,0},{6,2},{8,12},{10,14},{12,8},{14,10},{16,20},{18,... | collective-permute-start | bytes 2359304 | tf_op jit(solution)/shard_map/ppermute | solution.py:70
  137.1 8.4 %collective-permute-start.30 = (bf16[2,2,2,1,64,1536]{5,4,3,2,1,0:T(8,128)(2,1)S(1)}, bf16[2,2,2,1,64,1536]{5,4,3,2,1,0:T(8,128)(2,1)S(1)}, u32[]{:S(2)}, u32[]{:S(2)}) collective-permute-start(bf16[2,2,2,1,64,1536]{5,4,3,2,1,0:T(8,128)(2,1)S(1)} %pad_maximum_fusion.4), channel_id=1, source_target_pairs={{0,2},{2,0},{4,6},{6,4},{8,10},{10,8},{12,14},{14,12},{16,18},{18,... | collective-permute-start | bytes 4718600 | tf_op jit(solution)/shard_map/ppermute | solution.py:70
  139.1 15.2 %collective-permute-start.31 = (bf16[512,768]{1,0:T(8,128)(2,1)S(1)}, bf16[512,768]{1,0:T(8,128)(2,1)S(1)}, u32[]{:S(2)}, u32[]{:S(2)}) collective-permute-start(bf16[512,768]{1,0:T(8,128)(2,1)S(1)} %bitcast.100), channel_id=1, source_target_pairs={{1,2},{2,1},{5,6},{6,5},{9,10},{10,9},{13,14},{14,13},{17,18},{18,... | collective-permute-start | bytes 2359304 | tf_op jit(solution)/shard_map/ppermute | solution.py:159
  183.5 145.5 %reduce-scatter.5.cloned.1.call-start = ((), (), s32[]{:S(2)}) async-start(), calls=%async_computation.4 | async-start | bytes 1474560 | tf_op jit(solution)/shard_map/reduce_scatter | solution.py:1154
  246.0 7.9 %collective-permute-start.33 = (bf16[2,2,2,1,2,24,1536]{6,5,4,3,2,1,0:T(8,128)(2,1)}, bf16[2,2,2,1,2,24,1536]{6,5,4,3,2,1,0:T(8,128)(2,1)}, u32[]{:S(2)}, u32[]{:S(2)}) collective-permute-start(bf16[2,2,2,1,2,24,1536]{6,5,4,3,2,1,0:T(8,128)(2,1)} %constant_dynamic-slice_fusion.19), channel_id=1, source_target_pairs={{0,2},{2,0},{4,6},{6,4},{8,10},{10,8},{12,14},{14,12},{16,18},{18,... | collective-permute-start | bytes 3538952 | tf_op jit(solution)/shard_map/ppermute | solution.py:70
  247.6 9.0 %collective-permute-start.34 = (bf16[2,2,2,1,2,24,1536]{6,5,4,3,2,1,0:T(8,128)(2,1)}, bf16[2,2,2,1,2,24,1536]{6,5,4,3,2,1,0:T(8,128)(2,1)}, u32[]{:S(2)}, u32[]{:S(2)}) collective-permute-start(bf16[2,2,2,1,2,24,1536]{6,5,4,3,2,1,0:T(8,128)(2,1)} %constant_dynamic-slice_fusion.18), channel_id=1, source_target_pairs={{0,2},{2,0},{4,6},{6,4},{8,10},{10,8},{12,14},{14,12},{16,18},{18,... | collective-permute-start | bytes 3538952 | tf_op jit(solution)/shard_map/ppermute | solution.py:70
  264.1 15.4 %collective-permute-start.36 = (bf16[2,2,2,1,1,24,1536]{6,5,4,3,2,1,0:T(8,128)(2,1)S(1)}, bf16[2,2,2,1,1,24,1536]{6,5,4,3,2,1,0:T(8,128)(2,1)S(1)}, u32[]{:S(2)}, u32[]{:S(2)}) collective-permute-start(bf16[2,2,2,1,1,24,1536]{6,5,4,3,2,1,0:T(8,128)(2,1)S(1)} %constant_dynamic-slice_fusion.17), channel_id=1, source_target_pairs={{0,1},{1,0},{2,3},{3,2},{4,5},{5,4},{6,7},{7,6},{8,9},{9,8},{10,11... | collective-permute-start | bytes 1769480 | tf_op jit(solution)/shard_map/ppermute | solution.py:70
  264.5 16.0 %collective-permute-start.37 = (bf16[2,2,1,1,2,24,1536]{6,5,4,3,2,1,0:T(8,128)(2,1)S(1)}, bf16[2,2,1,1,2,24,1536]{6,5,4,3,2,1,0:T(8,128)(2,1)S(1)}, u32[]{:S(2)}, u32[]{:S(2)}) collective-permute-start(bf16[2,2,1,1,2,24,1536]{6,5,4,3,2,1,0:T(8,128)(2,1)S(1)} %constant_dynamic-slice_fusion.16), channel_id=1, source_target_pairs={{0,4},{2,6},{4,0},{6,2},{8,12},{10,14},{12,8},{14,10},{16,20},{18,... | collective-permute-start | bytes 1769480 | tf_op jit(solution)/shard_map/ppermute | solution.py:70
  265.4 16.0 %collective-permute-start.38 = (bf16[2,2,2,1,2,24,1536]{6,5,4,3,2,1,0:T(8,128)(2,1)S(1)}, bf16[2,2,2,1,2,24,1536]{6,5,4,3,2,1,0:T(8,128)(2,1)S(1)}, u32[]{:S(2)}, u32[]{:S(2)}) collective-permute-start(bf16[2,2,2,1,2,24,1536]{6,5,4,3,2,1,0:T(8,128)(2,1)S(1)} %constant_dynamic-slice_fusion.15), channel_id=1, source_target_pairs={{0,2},{2,0},{4,6},{6,4},{8,10},{10,8},{12,14},{14,12},{16,18},{18,... | collective-permute-start | bytes 3538952 | tf_op jit(solution)/shard_map/ppermute | solution.py:70
  265.6 17.2 %collective-permute-start.39 = (bf16[2,2,2,1,64,1536]{5,4,3,2,1,0:T(8,128)(2,1)S(1)}, bf16[2,2,2,1,64,1536]{5,4,3,2,1,0:T(8,128)(2,1)S(1)}, u32[]{:S(2)}, u32[]{:S(2)}) collective-permute-start(bf16[2,2,2,1,64,1536]{5,4,3,2,1,0:T(8,128)(2,1)S(1)} %constant_dynamic-slice_fusion.14), channel_id=1, source_target_pairs={{0,2},{2,0},{4,6},{6,4},{8,10},{10,8},{12,14},{14,12},{16,18},{18,... | collective-permute-start | bytes 4718600 | tf_op jit(solution)/shard_map/ppermute | solution.py:70
  283.3 8.4 %collective-permute-start.40 = (f32[1,1,1,1,4608]{4,3,2,1,0:T(1,128)S(1)}, f32[1,1,1,1,4608]{4,3,2,1,0:T(1,128)S(1)}, u32[]{:S(2)}, u32[]{:S(2)}) collective-permute-start(f32[1,1,1,1,4608]{4,3,2,1,0:T(1,128)S(1)} %add_bitcast_fusion), channel_id=1, source_target_pairs={{0,16},{2,18},{4,20},{6,22},{8,24},{10,26},{12,28},{14,30},{16,0},... | collective-permute-start | bytes 55304 | tf_op jit(solution)/shard_map/ppermute | solution.py:70
  285.8 10.2 %collective-permute-start.42 = (bf16[2,2,1,1,1,24,1536]{6,5,4,3,2,1,0:T(8,128)(2,1)S(1)}, bf16[2,2,1,1,1,24,1536]{6,5,4,3,2,1,0:T(8,128)(2,1)}, u32[]{:S(2)}, u32[]{:S(2)}) collective-permute-start(bf16[2,2,1,1,1,24,1536]{6,5,4,3,2,1,0:T(8,128)(2,1)S(1)} %constant_dynamic-slice_fusion.13), channel_id=1, source_target_pairs={{0,4},{2,6},{4,0},{6,2},{8,12},{10,14},{12,8},{14,10},{16,20},{18,... | collective-permute-start | bytes 884744 | tf_op jit(solution)/shard_map/ppermute | solution.py:70
  288.8 10.3 %collective-permute-start.43 = (bf16[2,2,1,1,1,24,1536]{6,5,4,3,2,1,0:T(8,128)(2,1)}, bf16[2,2,1,1,1,24,1536]{6,5,4,3,2,1,0:T(8,128)(2,1)}, u32[]{:S(2)}, u32[]{:S(2)}) collective-permute-start(bf16[2,2,1,1,1,24,1536]{6,5,4,3,2,1,0:T(8,128)(2,1)} %constant_dynamic-slice_fusion.12), channel_id=1, source_target_pairs={{0,1},{1,0},{2,3},{3,2},{4,5},{5,4},{6,7},{7,6},{8,9},{9,8},{10,11... | collective-permute-start | bytes 884744 | tf_op jit(solution)/shard_map/ppermute | solution.py:70
  290.6 18.9 %collective-permute-start.44 = (bf16[2,2,2,1,1,24,1536]{6,5,4,3,2,1,0:T(8,128)(2,1)}, bf16[2,2,2,1,1,24,1536]{6,5,4,3,2,1,0:T(8,128)(2,1)}, u32[]{:S(2)}, u32[]{:S(2)}) collective-permute-start(bf16[2,2,2,1,1,24,1536]{6,5,4,3,2,1,0:T(8,128)(2,1)} %constant_dynamic-slice_fusion.11), channel_id=1, source_target_pairs={{0,1},{1,0},{2,3},{3,2},{4,5},{5,4},{6,7},{7,6},{8,9},{9,8},{10,11... | collective-permute-start | bytes 1769480 | tf_op jit(solution)/shard_map/ppermute | solution.py:70
  293.8 17.7 %collective-permute-start.45 = (bf16[2,2,1,1,64,1536]{5,4,3,2,1,0:T(8,128)(2,1)}, bf16[2,2,1,1,64,1536]{5,4,3,2,1,0:T(8,128)(2,1)}, u32[]{:S(2)}, u32[]{:S(2)}) collective-permute-start(bf16[2,2,1,1,64,1536]{5,4,3,2,1,0:T(8,128)(2,1)} %constant_dynamic-slice_fusion.10), channel_id=1, source_target_pairs={{0,4},{2,6},{4,0},{6,2},{8,12},{10,14},{12,8},{14,10},{16,20},{18,... | collective-permute-start | bytes 2359304 | tf_op jit(solution)/shard_map/ppermute | solution.py:70
  313.9 9.5 %collective-permute-start.48 = (bf16[2,1,1,1,1,24,1536]{6,5,4,3,2,1,0:T(8,128)(2,1)S(1)}, bf16[2,1,1,1,1,24,1536]{6,5,4,3,2,1,0:T(8,128)(2,1)S(1)}, u32[]{:S(2)}, u32[]{:S(2)}) collective-permute-start(bf16[2,1,1,1,1,24,1536]{6,5,4,3,2,1,0:T(8,128)(2,1)S(1)} %constant_dynamic-slice_fusion.9), channel_id=1, source_target_pairs={{0,8},{2,10},{4,12},{6,14},{8,0},{10,2},{12,4},{14,6},{16,24},{18,... | collective-permute-start | bytes 442376 | tf_op jit(solution)/shard_map/ppermute | solution.py:70
  314.8 11.8 %collective-permute-start.49 = (bf16[2,1,1,1,1,24,1536]{6,5,4,3,2,1,0:T(8,128)(2,1)S(1)}, bf16[2,1,1,1,1,24,1536]{6,5,4,3,2,1,0:T(8,128)(2,1)S(1)}, u32[]{:S(2)}, u32[]{:S(2)}) collective-permute-start(bf16[2,1,1,1,1,24,1536]{6,5,4,3,2,1,0:T(8,128)(2,1)S(1)} %constant_dynamic-slice_fusion.8), channel_id=1, source_target_pairs={{0,8},{2,10},{4,12},{6,14},{8,0},{10,2},{12,4},{14,6},{16,24},{18,... | collective-permute-start | bytes 442376 | tf_op jit(solution)/shard_map/ppermute | solution.py:70
  316.1 12.7 %collective-permute-start.50 = (bf16[2,2,1,1,1,24,1536]{6,5,4,3,2,1,0:T(8,128)(2,1)S(1)}, bf16[2,2,1,1,1,24,1536]{6,5,4,3,2,1,0:T(8,128)(2,1)S(1)}, u32[]{:S(2)}, u32[]{:S(2)}) collective-permute-start(bf16[2,2,1,1,1,24,1536]{6,5,4,3,2,1,0:T(8,128)(2,1)S(1)} %constant_dynamic-slice_fusion.7), channel_id=1, source_target_pairs={{0,4},{2,6},{4,0},{6,2},{8,12},{10,14},{12,8},{14,10},{16,20},{18,... | collective-permute-start | bytes 884744 | tf_op jit(solution)/shard_map/ppermute | solution.py:70
  317.3 11.5 %collective-permute-start.51 = (bf16[2,2,1,1,64,768]{5,4,3,2,1,0:T(8,128)(2,1)S(1)}, bf16[2,2,1,1,64,768]{5,4,3,2,1,0:T(8,128)(2,1)S(1)}, u32[]{:S(2)}, u32[]{:S(2)}) collective-permute-start(bf16[2,2,1,1,64,768]{5,4,3,2,1,0:T(8,128)(2,1)S(1)} %constant_dynamic-slice_fusion.6), channel_id=1, source_target_pairs={{0,1},{1,0},{2,3},{3,2},{4,5},{5,4},{6,7},{7,6},{8,9},{9,8},{10,11... | collective-permute-start | bytes 1179656 | tf_op jit(solution)/shard_map/ppermute | solution.py:70
  318.4 9.1 %collective-permute-start.47 = (f32[2,2,2,1,4608]{4,3,2,1,0:T(1,128)S(1)}, f32[2,2,2,1,4608]{4,3,2,1,0:T(1,128)S(1)}, u32[]{:S(2)}, u32[]{:S(2)}) collective-permute-start(f32[2,2,2,1,4608]{4,3,2,1,0:T(1,128)S(1)} %pad_maximum_fusion.23), channel_id=1, source_target_pairs={{0,1},{1,0},{2,3},{3,2},{4,5},{5,4},{6,7},{7,6},{8,9},{9,8},{10,11... | collective-permute-start | bytes 442376 | tf_op jit(solution)/shard_map/ppermute | solution.py:70
  330.1 7.5 %collective-permute-start.52 = (bf16[1,1,1,1,1,24,1536]{6,5,4,3,2,1,0:T(8,128)(2,1)S(1)}, bf16[1,1,1,1,1,24,1536]{6,5,4,3,2,1,0:T(8,128)(2,1)S(1)}, u32[]{:S(2)}, u32[]{:S(2)}) collective-permute-start(bf16[1,1,1,1,1,24,1536]{6,5,4,3,2,1,0:T(8,128)(2,1)S(1)} %constant_dynamic-slice_fusion.5), channel_id=1, source_target_pairs={{0,16},{2,18},{4,20},{6,22},{8,24},{10,26},{12,28},{14,30},{16,0},... | collective-permute-start | bytes 221192 | tf_op jit(solution)/shard_map/ppermute | solution.py:70
  333.2 8.4 %collective-permute-start.54 = (bf16[2,1,1,1,1,24,1536]{6,5,4,3,2,1,0:T(8,128)(2,1)S(1)}, bf16[2,1,1,1,1,24,1536]{6,5,4,3,2,1,0:T(8,128)(2,1)S(1)}, u32[]{:S(2)}, u32[]{:S(2)}) collective-permute-start(bf16[2,1,1,1,1,24,1536]{6,5,4,3,2,1,0:T(8,128)(2,1)S(1)} %constant_dynamic-slice_fusion.3), channel_id=1, source_target_pairs={{0,8},{2,10},{4,12},{6,14},{8,0},{10,2},{12,4},{14,6},{16,24},{18,... | collective-permute-start | bytes 442376 | tf_op jit(solution)/shard_map/ppermute | solution.py:70
  334.3 9.8 %collective-permute-start.55 = (bf16[2,1,1,1,64,768]{5,4,3,2,1,0:T(8,128)(2,1)S(1)}, bf16[2,1,1,1,64,768]{5,4,3,2,1,0:T(8,128)(2,1)S(1)}, u32[]{:S(2)}, u32[]{:S(2)}) collective-permute-start(bf16[2,1,1,1,64,768]{5,4,3,2,1,0:T(8,128)(2,1)S(1)} %constant_dynamic-slice_fusion.2), channel_id=1, source_target_pairs={{0,8},{2,10},{4,12},{6,14},{8,0},{10,2},{12,4},{14,6},{16,24},{18,... | collective-permute-start | bytes 589832 | tf_op jit(solution)/shard_map/ppermute | solution.py:70
  345.5 14.5 %collective-permute-start.58 = (bf16[2,512,768]{2,1,0:T(8,128)(2,1)}, bf16[2,512,768]{2,1,0:T(8,128)(2,1)}, u32[]{:S(2)}, u32[]{:S(2)}) collective-permute-start(bf16[2,512,768]{2,1,0:T(8,128)(2,1)} %pad_maximum_fusion.5), channel_id=1, source_target_pairs={{1,2},{2,1},{5,6},{6,5},{9,10},{10,9},{13,14},{14,13},{17,18},{18,... | collective-permute-start | bytes 4718600 | tf_op jit(solution)/shard_map/ppermute | solution.py:159
  348.6 7.1 %collective-permute-start.56 = (bf16[1,1,1,1,1,24,1536]{6,5,4,3,2,1,0:T(8,128)(2,1)S(1)}, bf16[1,1,1,1,1,24,1536]{6,5,4,3,2,1,0:T(8,128)(2,1)S(1)}, u32[]{:S(2)}, u32[]{:S(2)}) collective-permute-start(bf16[1,1,1,1,1,24,1536]{6,5,4,3,2,1,0:T(8,128)(2,1)S(1)} %constant_dynamic-slice_fusion.1), channel_id=1, source_target_pairs={{0,16},{2,18},{4,20},{6,22},{8,24},{10,26},{12,28},{14,30},{16,0},... | collective-permute-start | bytes 221192 | tf_op jit(solution)/shard_map/ppermute | solution.py:70
  350.2 9.8 %collective-permute-start.57 = (bf16[1,1,1,1,64,768]{5,4,3,2,1,0:T(8,128)(2,1)S(1)}, bf16[1,1,1,1,64,768]{5,4,3,2,1,0:T(8,128)(2,1)S(1)}, u32[]{:S(2)}, u32[]{:S(2)}) collective-permute-start(bf16[1,1,1,1,64,768]{5,4,3,2,1,0:T(8,128)(2,1)S(1)} %constant_dynamic-slice_fusion), channel_id=1, source_target_pairs={{0,16},{2,18},{4,20},{6,22},{8,24},{10,26},{12,28},{14,30},{16,0},... | collective-permute-start | bytes 294920 | tf_op jit(solution)/shard_map/ppermute | solution.py:70
  360.9 8.5 %collective-permute-start.59 = (f32[184,128]{1,0:T(8,128)S(1)}, f32[184,128]{1,0:T(8,128)S(1)}, u32[]{:S(2)}, u32[]{:S(2)}) collective-permute-start(f32[184,128]{1,0:T(8,128)S(1)} %shard_map.333), channel_id=1, source_target_pairs={{0,2},{2,0},{4,6},{6,4},{8,10},{10,8},{12,14},{14,12},{16,18},{18,... | collective-permute-start | bytes 282632 | tf_op jit(solution)/shard_map/ppermute | solution.py:70
  383.9 6.5 %collective-permute-start.63 = (f32[184,128]{1,0:T(8,128)S(1)}, f32[184,128]{1,0:T(8,128)S(1)}, u32[]{:S(2)}, u32[]{:S(2)}) collective-permute-start(f32[184,128]{1,0:T(8,128)S(1)} %add.463), channel_id=1, source_target_pairs={{0,16},{2,18},{4,20},{6,22},{8,24},{10,26},{12,28},{14,30},{16,0},... | collective-permute-start | bytes 282632 | tf_op jit(solution)/shard_map/ppermute | solution.py:70
  (95 other events, 588.2 us)
Sparse Core Ops, SparseCore 0:
  43.9 98.9 all-gather.1
  183.6 77.5 reduce-scatter.2
  294.8 33.7 reduce-scatter.4
